TPU v7x, 32 devices: a whole 2x2x4 slice. The times are simulated.
32 devices in a mesh: groups: 2 (over y), clip: 4 (over z), strip: 4 (over x, core).
Axes of the slice: x: 2, y: 2, z: 4, core: 2. Of those that a mesh axis runs over, the one named last changes fastest.
Arguments:
- latents: bfloat16 [32, 20, 64, 320], P(('groups', 'clip'), 'strip'), parts along dimension 0, may hold values from -6 to 6
- anchor_index: int32 [8, 1], P(('groups', 'clip')), parts along dimension 0, may hold values from 0 to 3
- window: int32 [1], replicated, may hold values from 2 to 4
- gain_one: float32 [320], replicated, may hold values from 0.5 to 1.5
- spatial_w: bfloat16 [3, 3, 320, 320], replicated, may hold values from -0.109375 to 0.109375
- gain_two: float32 [320], replicated, may hold values from 0.5 to 1.5
- temporal_w: bfloat16 [3, 320, 320], replicated, may hold values from -0.1875 to 0.1875
- gain_three: float32 [320], replicated, may hold values from 0.5 to 1.5
- w_query: bfloat16 [320, 320], replicated
- w_keyval: bfloat16 [320, 640], replicated
- w_out: bfloat16 [320, 320], replicated, may hold values from -0.3125 to 0.3125
Outputs:
- block_out: bfloat16 [32, 20, 64, 320], P(('groups', 'clip'), 'strip'), parts along dimension 0
There are 2 independent parts, one for each index of `groups`. A program takes and returns all parts, laid end to end along the dimension named above; an argument that names none is the same for every part. Nothing has to cross between parts.
Inputs may be any that keep to these rules, and one draw needn't show every extreme that they name: `anchor_index`: indices of anchor frames within their clip of 4 frames. Frames closer than window[0] within one clip attend to each other.
All inputs are finite; a program needn't handle non-finite values.
Results may differ from a plain program's by a relative error of at most 0.0085.
Values may be sent and summed in bfloat16 or wider, within the bound.
No kernel may reach another device: no remote copies, remote signals or barrier semaphores. Data moves between devices by JAX's collectives and lax.ppermute only.
A program may use at most 128 MiB of HBM per device.

v0:
```python
import functools
import math

import jax
import jax.numpy as jnp
from jax import lax
from jax.experimental import pallas as pl
from jax.experimental.pallas import tpu as pltpu
from jax.sharding import PartitionSpec as P

HEADS = 5
HEAD_DIM = 64
LANES = 128
BF = jnp.bfloat16
F32 = jnp.float32
VMEM = pl.BlockSpec(memory_space=pltpu.VMEM)
HBM = pl.BlockSpec(memory_space=pltpu.HBM)
MIB = 1 << 20


def call(body, outs, specs, scratch=(), flops=0, limit=24, out_specs=None):
    return pl.pallas_call(
        body,
        out_shape=tuple(jax.ShapeDtypeStruct(s, d) for s, d in outs),
        in_specs=specs,
        out_specs=out_specs or tuple(VMEM for _ in outs),
        scratch_shapes=list(scratch),
        cost_estimate=pl.CostEstimate(flops=flops, bytes_accessed=2 * MIB, transcendentals=0),
        compiler_params=pltpu.CompilerParams(vmem_limit_bytes=limit * MIB),
    )


def dot(a, b):
    return jnp.dot(a, b, preferred_element_type=F32)


def norm(v, gain_ref):
    wide = v.astype(F32)
    centred = wide - jnp.mean(wide, axis=-1, keepdims=True)
    variance = jnp.mean(centred * centred, axis=-1, keepdims=True)
    return centred * lax.rsqrt(variance + 1e-05) * gain_ref[...].reshape(1, v.shape[1])


def silu(u):
    half = 0.5 * u
    return half + half * jnp.tanh(half)


def pack_into(ref, h):
    cells, channels = h.shape
    full = channels // LANES
    for t in range(full):
        ref[t * cells : (t + 1) * cells, :] = h[:, t * LANES : (t + 1) * LANES]
    rest = channels - full * LANES
    if rest:
        share = LANES // rest
        part = cells // share
        ref[full * cells :, :] = jnp.concatenate(
            [h[s * part : (s + 1) * part, full * LANES :] for s in range(share)], axis=1
        )


def unpacked(p, channels):
    cells = p.shape[0] * LANES // channels
    full = channels // LANES
    pieces = [p[t * cells : (t + 1) * cells, :] for t in range(full)]
    rest = channels - full * LANES
    if rest:
        share = LANES // rest
        tail = p[full * cells :, :]
        pieces.append(
            jnp.concatenate([tail[:, s * rest : (s + 1) * rest] for s in range(share)], axis=0)
        )
    return jnp.concatenate(pieces, axis=1)


def columns(h, width):
    cells = h.shape[0]
    place = lax.rem(lax.broadcasted_iota(jnp.int32, h.shape, 0), width)
    left = jnp.where(place == 0, 0.0, pltpu.roll(h, 1, 0))
    right = jnp.where(place == width - 1, 0.0, pltpu.roll(h, cells - 1, 0))
    return jnp.concatenate([left.astype(BF), h.astype(BF), right.astype(BF)], axis=1)


def scalar(ref, n):
    values = ref[...].astype(F32)
    place = lax.broadcasted_iota(jnp.int32, values.shape, 1)
    return jnp.sum(jnp.where(place == n, values, 0.0)).astype(jnp.int32)


def edge_kernel(x_ref, top_ref, bottom_ref):
    frames, height, width, channels = x_ref.shape
    pack_into(top_ref, x_ref[:, 0].reshape(frames * width, channels))
    pack_into(bottom_ref, x_ref[:, height - 1].reshape(frames * width, channels))


def rests_into(rem_ref, w_ref):
    full = w_ref.shape[2] // 256 * 256
    rest = w_ref.shape[2] - full
    for a in range(3):
        rem_ref[:, a * rest : (a + 1) * rest] = w_ref[a, :, full:]


def frame_rows(f, x_ref, col_ref, g1_ref, w_ref, rem_ref):
    _, height, width, channels = x_ref.shape
    cells = height * width
    full = channels // 256 * 256
    rest = channels - full
    col_ref[...] = columns(silu(norm(x_ref[f].reshape(cells, channels), g1_ref)), width)
    centre = dot(col_ref[...], w_ref[1, :, :full])
    above = dot(col_ref[: cells - width], w_ref[0, :, :full])
    below = dot(col_ref[width:], w_ref[2, :, :full])
    tails = dot(col_ref[...], rem_ref[...])
    rows = []
    for row in range(height):
        lo, hi = row * width, (row + 1) * width
        wide = centre[lo:hi]
        tail = tails[lo:hi, rest : 2 * rest]
        if row > 0:
            wide = wide + above[lo - width : lo]
            tail = tail + tails[lo - width : lo, :rest]
        if row < height - 1:
            wide = wide + below[lo:hi]
            tail = tail + tails[hi : hi + width, 2 * rest : 3 * rest]
        rows.append(x_ref[f, row].astype(F32) + jnp.concatenate([wide, tail], axis=1))
    return rows


def rim_terms(refs, frames, width, channels, g1_ref, w_ref):
    terms = []
    for ref, a in zip(refs, (0, 2)):
        rows = unpacked(ref[...], channels)
        rows = jnp.concatenate([rows[f * width : (f + 1) * width] for f in frames], axis=0)
        terms.append(dot(columns(silu(norm(rows, g1_ref)), width), w_ref[a]))
    return terms


def outer_kernel(x_ref, g1_ref, g2_ref, w_ref, mid_ref, mid2_ref, edge_ref, rem_ref, order_ref, col_ref):
    frames, height, width, channels = x_ref.shape
    order_ref[...] = jnp.zeros_like(order_ref)
    rests_into(rem_ref, w_ref)

    def frame(s, _):
        rows = frame_rows(s * (frames - 1), x_ref, col_ref, g1_ref, w_ref, rem_ref)
        edge_ref[s, 0] = rows[0]
        edge_ref[s, 1] = rows[-1]
        for row, total in enumerate(rows[1:-1]):
            rounded = total.astype(BF)
            mid_ref[s, row * width : (row + 1) * width] = rounded
            hidden = silu(norm(rounded, g2_ref)).astype(BF)
            mid2_ref[s, row * width : (row + 1) * width] = hidden
        return 0

    lax.fori_loop(0, 2, frame, 0)


def outer_edge_kernel(
    frames, edge_ref, above_ref, below_ref, order_ref, mid_ref, mid2_ref, g1_ref, g2_ref, w_ref,
    spatial_ref, hidden_ref, first_ref, last_ref,
):
    _, cells, channels = spatial_ref.shape
    width = edge_ref.shape[2]
    spatial_ref[:, width : cells - width] = mid_ref[...]
    hidden_ref[:, width : cells - width] = mid2_ref[...]
    terms = rim_terms((above_ref, below_ref), (0, frames - 1), width, channels, g1_ref, w_ref)
    for side, lo in ((0, 0), (1, cells - width)):
        rounded = (edge_ref[:, side].reshape(2 * width, channels) + terms[side]).astype(BF)
        hidden = silu(norm(rounded, g2_ref)).astype(BF)
        spatial_ref[:, lo : lo + width] = rounded.reshape(2, width, channels)
        hidden_ref[:, lo : lo + width] = hidden.reshape(2, width, channels)
    pack_into(first_ref, hidden_ref[0])
    pack_into(last_ref, hidden_ref[1])


def inner_kernel(
    x_ref, above_ref, below_ref, g1_ref, g2_ref, w_ref, rem_ref, outer_spatial_ref, outer_hidden_ref,
    spatial_ref, hidden_ref, col_ref, add_ref,
):
    frames, height, width, channels = x_ref.shape
    for s, f in ((0, 0), (1, frames - 1)):
        spatial_ref[f] = outer_spatial_ref[s]
        hidden_ref[f] = outer_hidden_ref[s]
    inside = range(1, frames - 1)
    terms = rim_terms((above_ref, below_ref), inside, width, channels, g1_ref, w_ref)
    for side in range(2):
        add_ref[side, 1 : frames - 1] = terms[side].reshape(frames - 2, width, channels)

    def frame(f, _):
        rows = frame_rows(f, x_ref, col_ref, g1_ref, w_ref, rem_ref)
        rows[0] = rows[0] + add_ref[0, f]
        rows[-1] = rows[-1] + add_ref[1, f]
        for row, total in enumerate(rows):
            rounded = total.astype(BF)
            spatial_ref[f, row * width : (row + 1) * width] = rounded
            hidden = silu(norm(rounded, g2_ref)).astype(BF)
            hidden_ref[f, row * width : (row + 1) * width] = hidden
        return 0

    lax.fori_loop(1, frames - 1, frame, 0)


def chosen_kernel(
    picks_ref, before_ref, after_ref, spatial_ref, hidden_ref, g3_ref, wt_ref, chosen_ref
):
    frames, cells, channels = spatial_ref.shape
    before = unpacked(before_ref[...], channels)
    after = unpacked(after_ref[...], channels)
    for n in range(chosen_ref.shape[0]):
        pick = scalar(picks_ref, n)
        earlier = jnp.where(pick == 0, before, hidden_ref[jnp.maximum(pick - 1, 0)])
        later = jnp.where(pick == frames - 1, after, hidden_ref[jnp.minimum(pick + 1, frames - 1)])
        total = spatial_ref[pick].astype(F32) + dot(hidden_ref[pick], wt_ref[1])
        total = total + dot(earlier, wt_ref[0]) + dot(later, wt_ref[2])
        pack_into(chosen_ref.at[n], norm(total.astype(BF), g3_ref).astype(BF))


def temporal_kernel(
    before_ref, after_ref, spatial_ref, hidden_ref, g3_ref, wt_ref, wq_ref, wkv_ref,
    temporal_ref, query_ref, keyval_ref,
):
    frames, cells, channels = spatial_ref.shape
    size = frames * cells
    before = unpacked(before_ref[...], channels)
    after = unpacked(after_ref[...], channels)
    hidden = hidden_ref[...].reshape(size, channels)
    total = spatial_ref[...].reshape(size, channels).astype(F32) + dot(hidden, wt_ref[1])
    total = total + dot(jnp.concatenate([before, hidden[: size - cells]], axis=0), wt_ref[0])
    total = total + dot(jnp.concatenate([hidden[cells:], after], axis=0), wt_ref[2])
    temporal = total.astype(BF)
    temporal_ref[...] = temporal.reshape(frames, cells, channels)
    normed = norm(temporal, g3_ref).astype(BF)
    query_ref[...] = dot(normed, wq_ref[...]).astype(BF).reshape(frames, cells, channels)
    keyval_ref[...] = dot(normed, wkv_ref[...]).astype(BF).reshape(frames, cells, 2 * channels)


def lane_map(shape, channel_dim, count, channels, value, everywhere=False):
    full = channels // LANES * LANES
    rest = channels - full
    c = lax.broadcasted_iota(jnp.int32, shape, channel_dim)
    lane = lax.broadcasted_iota(jnp.int32, shape, 1 - channel_dim)
    stride = LANES // 4
    wide = c < count * full
    source = jnp.where(wide, lax.div(c, full), lax.div(c - count * full, max(rest, 1)))
    channel = jnp.where(
        wide, lax.rem(c, full), full + lax.rem(jnp.maximum(c - count * full, 0), max(rest, 1))
    )
    head = lax.div(channel, HEAD_DIM)
    if everywhere:
        hit = lax.rem(lane, stride) == head
    else:
        hit = lane == source * stride + head
    return jnp.where(hit, value, 0.0).astype(BF)


def local_kernel(
    picks_ref, window_ref, query_ref, keyval_ref, top_ref, sum_ref, mix_ref,
):
    frames, cells, channels = query_ref.shape
    count = picks_ref.shape[1]
    full = channels // LANES * LANES
    stride = LANES // 4
    queries = [query_ref[f] for f in range(frames)]
    keyvals = [keyval_ref[f] for f in range(frames)]
    keys = [kv[:, :full] for kv in keyvals] + [
        jnp.concatenate([kv[:, full:channels] for kv in keyvals], axis=1)
    ]
    values = [kv[:, channels : channels + full].astype(F32) for kv in keyvals] + [
        jnp.concatenate([kv[:, channels + full :] for kv in keyvals], axis=1).astype(F32)
    ]
    products = []
    for q in queries:
        again = jnp.concatenate([q[:, full:]] * frames, axis=1)
        row = [q[:, :full] * k for k in keys[:frames]] + [again * keys[frames]]
        products.append(jnp.concatenate(row, axis=1))
    to_lanes = lane_map(
        (frames * channels, LANES), 0, frames, channels, 1.0 / math.sqrt(HEAD_DIM)
    )
    to_channels = lane_map((LANES, frames * channels), 1, frames, channels, 1.0)
    scores = dot(jnp.concatenate(products, axis=0), to_lanes)
    source = lax.div(lax.broadcasted_iota(jnp.int32, (1, LANES), 1), stride)
    window = window_ref[...].reshape(1, 1)
    copies = jnp.zeros((1, LANES), F32)
    for n in range(count):
        copies = copies + jnp.where(source == picks_ref[:, n : n + 1], 1.0, 0.0)
    weights = []
    for i in range(frames):
        times = copies + jnp.where(jnp.abs(source - i) < window, 1.0, 0.0)
        s = jnp.where(times > 0.0, scores[i * cells : (i + 1) * cells], -jnp.inf)
        top = jnp.maximum(s, pltpu.roll(s, stride, 1))
        top = jnp.maximum(top, pltpu.roll(top, 2 * stride, 1))
        w = jnp.exp(s - top) * times
        total = w + pltpu.roll(w, stride, 1)
        total = total + pltpu.roll(total, 2 * stride, 1)
        top_ref[i] = top
        sum_ref[i] = total
        weights.append(w.astype(BF))
    spread = dot(jnp.concatenate(weights, axis=0), to_channels)
    for i in range(frames):
        part = spread[i * cells : (i + 1) * cells]
        wide = part[:, :full] * values[0]
        for j in range(1, frames):
            wide = wide + part[:, j * full : (j + 1) * full] * values[j]
        tail = part[:, frames * full :] * values[frames]
        tail = tail[:, :LANES] + tail[:, LANES:]
        tail = tail + pltpu.roll(tail, LANES // 2, 1)
        mix_ref[i] = jnp.concatenate([wide, tail], axis=1)


def updated(anchor_ref, wkv_ref, query_ref, top_ref, sum_ref, mix_ref, last):
    frames, cells, channels = query_ref.shape
    full = channels // LANES * LANES
    count = anchor_ref.shape[0]
    state = (top_ref[...], sum_ref[...], mix_ref[...])
    size = frames * cells
    top, total, mix = (v.reshape(size, v.shape[-1]) for v in state)
    query = query_ref[...].reshape(size, channels)
    to_lanes = lane_map(
        (channels, LANES), 0, 1, channels, 1.0 / math.sqrt(HEAD_DIM), everywhere=True
    )
    to_channels = lane_map((LANES, 2 * channels), 1, 2, channels, 1.0)
    low = lax.broadcasted_iota(jnp.int32, (1, LANES), 1) < LANES // 4
    for n in range(count):
        keyval = dot(unpacked(anchor_ref[n], channels), wkv_ref[...]).astype(BF)
        key = jnp.concatenate([keyval[:, :channels]] * frames, axis=0)
        scores = dot(query * key, to_lanes)
        higher = jnp.maximum(top, scores)
        weight = jnp.exp(scores - higher)
        fade = jnp.exp(top - higher)
        total = total * fade + weight
        both = jnp.where(low, weight, fade)
        if last and n == count - 1:
            both = both / total
        spread = dot(both.astype(BF), to_channels)
        value = keyval[:, channels:].astype(F32)
        value = jnp.concatenate([value] * frames, axis=0)
        wide = spread[:, :full] * value[:, :full] + spread[:, full : 2 * full] * mix[:, :full]
        tail = jnp.concatenate([value[:, full:], mix[:, full + LANES // 2 :]], axis=1)
        tail = spread[:, 2 * full :] * tail
        tail = tail + pltpu.roll(tail, LANES // 2, 1)
        mix = jnp.concatenate([wide, tail], axis=1)
        top = higher
    return top, total, mix


def anchor_kernel(
    anchor_ref, wkv_ref, query_ref, top_ref, sum_ref, mix_ref, top_out, sum_out, mix_out
):
    new = updated(anchor_ref, wkv_ref, query_ref, top_ref, sum_ref, mix_ref, False)
    for ref, v in zip((top_out, sum_out, mix_out), new):
        ref[...] = v.reshape(ref.shape)


def last_kernel(
    anchor_ref, wkv_ref, query_ref, top_ref, sum_ref, mix_ref, temporal_ref, wo_ref,
    out_ref, out_buf, sems,
):
    frames, cells, channels = query_ref.shape
    height, width = out_ref.shape[1:3]
    _, _, mix = updated(anchor_ref, wkv_ref, query_ref, top_ref, sum_ref, mix_ref, True)
    attended = mix[:, :channels].astype(BF)
    result = dot(attended, wo_ref[...])
    copies = []
    for i in range(frames):
        total = temporal_ref[i].astype(F32) + result[i * cells : (i + 1) * cells]
        out_buf[i] = total.astype(BF).reshape(height, width, channels)
        copies.append(pltpu.make_async_copy(out_buf.at[i], out_ref.at[i], sems.at[i]))
        copies[i].start()
    for copy in copies:
        copy.wait()


def neighbours(leading, last, axis):
    count = lax.axis_size(axis)
    up = [(i, i + 1) for i in range(count - 1)]
    down = [(j, i) for i, j in up]
    return lax.ppermute(last, axis, up), lax.ppermute(leading, axis, down)


def on_device(
    latents, anchor_index, window, gain_one, spatial_w, gain_two, temporal_w, gain_three,
    w_query, w_keyval, w_out,
):
    frames, height, width, channels = latents.shape
    cells = height * width
    count = anchor_index.shape[1]
    ws = spatial_w.reshape(3, 3 * channels, channels)
    one = 2 * channels * channels
    packed = cells * channels // LANES
    edge_packed = frames * width * channels // LANES
    lanes_up = (channels + LANES - 1) // LANES * LANES
    sem = pltpu.SemaphoreType.DMA
    some = (frames, cells, channels)

    x, g1, g2, g3, w = latents, gain_one, gain_two, gain_three, ws

    top, bottom = call(
        edge_kernel, [((edge_packed, LANES), BF)] * 2, [VMEM], flops=8 * frames * cells * one
    )(x)
    above, below = neighbours(top, bottom, "strip")
    col = pltpu.VMEM((cells, 3 * channels), BF)
    middle = (2, cells - 2 * width, channels)
    mid, mid2, edge, w_rem, order = call(
        outer_kernel,
        [
            (middle, BF),
            (middle, BF),
            ((2, 2, width, channels), F32),
            ((3 * channels, 3 * (channels % 256)), BF),
            ((8, LANES), F32),
        ],
        [VMEM] * 4,
        [col],
        flops=9 * 2 * cells * one,
    )(x, g1, g2, w)
    outer_spatial, outer_hidden, first, last = call(
        functools.partial(outer_edge_kernel, frames),
        [((2, cells, channels), BF)] * 2 + [((packed, LANES), BF)] * 2,
        [VMEM] * 9,
        flops=6 * 2 * width * one,
    )(edge, above, below, order, mid, mid2, g1, g2, w)
    before, after = neighbours(first, last, "clip")
    spatial, hidden = call(
        inner_kernel,
        [(some, BF), (some, BF)],
        [VMEM] * 9,
        [col, pltpu.VMEM((2, frames, width, channels), F32)],
        flops=9 * (frames - 2) * cells * one,
    )(x, above, below, g1, g2, w, w_rem, outer_spatial, outer_hidden)
    (chosen,) = call(
        chosen_kernel, [((count, packed, LANES), BF)], [VMEM] * 7, flops=3 * cells * one
    )(anchor_index, before, after, spatial, hidden, g3, temporal_w)
    clips = lax.axis_size("clip")
    arrived = [
        lax.ppermute(chosen, "clip", [(i, (i + s) % clips) for i in range(clips)])
        for s in range(1, clips)
    ]
    temporal, query, keyval = call(
        temporal_kernel,
        [(some, BF), (some, BF), ((frames, cells, 2 * channels), BF)],
        [VMEM] * 8,
        flops=6 * frames * cells * one,
        limit=32,
    )(before, after, spatial, hidden, g3, temporal_w, w_query, w_keyval)
    states = [((frames, cells, LANES), F32)] * 2 + [((frames, cells, lanes_up), F32)]
    state = call(
        local_kernel, states, [VMEM] * 4, flops=10 * frames * cells * one, limit=32
    )(anchor_index, window, query, keyval)
    for arrival in arrived[:-1]:
        state = call(
            anchor_kernel, states, [VMEM] * 6, flops=4 * frames * cells * one, limit=32
        )(arrival, w_keyval, query, *state)
    (out,) = call(
        last_kernel,
        [(latents.shape, BF)],
        [VMEM] * 8,
        [pltpu.VMEM(latents.shape, BF), sem((frames,))],
        flops=5 * frames * cells * one,
        limit=32,
        out_specs=(HBM,),
    )(arrived[-1], w_keyval, query, *state, temporal, w_out)
    return out


def solution(mesh):
    return jax.shard_map(
        on_device,
        mesh=mesh,
        in_specs=(
            P(("groups", "clip"), "strip", None, None),
            P(("groups", "clip"), None),
            P(),
            P(),
            P(),
            P(),
            P(),
            P(),
            P(),
            P(),
            P(),
        ),
        out_specs=P(("groups", "clip"), "strip", None, None),
        check_vma=False,
    )
```

profile of v0, /device:TPU:25, one launch (start us, length us, event | category | flops | bytes accessed | tf_op | source)
XLA Modules:
  0.0 46.5 jit_solution(7140420415063687109)
XLA Ops:
  0.0 0.0 copy-start
  0.0 0.0 copy-start.2
  0.0 1.3 %copy-done.2 = bf16[4,5,64,320]{3,2,1,0:T(8,128)(2,1)S(1)} copy-done((bf16[4,5,64,320]{3,2,1,0:T(8,128)(2,1)S(1)}, bf16[4,5,64,320]{3,2,1,0:T(8,128)(2,1)}, u32[]{:S(2)}) %copy-start.2) | copy-done | bytes 819224
  1.4 0.0 copy-start.6
  1.4 0.0 copy-start.7
  1.4 0.1 shard_map.110
  1.4 3.7 %collective-permute-start = (bf16[640,128]{1,0:T(8,128)(2,1)S(1)}, bf16[640,128]{1,0:T(8,128)(2,1)S(1)}, u32[]{:S(2)}, u32[]{:S(2)}) collective-permute-start(bf16[640,128]{1,0:T(8,128)(2,1)S(1)} %get-tuple-element.31), channel_id=1, source_target_pairs={{0,1},{1,2},{2,3},{4,5},{5,6},{6,7},{8,9},{9,10},{10,11},{12,13},{... | collective-permute-start | bytes 491528 | tf_op jit(solution)/shard_map/ppermute | solution.py:376
  5.1 1.9 %collective-permute-start.1 = (bf16[640,128]{1,0:T(8,128)(2,1)S(1)}, bf16[640,128]{1,0:T(8,128)(2,1)S(1)}, u32[]{:S(2)}, u32[]{:S(2)}) collective-permute-start(bf16[640,128]{1,0:T(8,128)(2,1)S(1)} %get-tuple-element.32), channel_id=1, source_target_pairs={{1,0},{2,1},{3,2},{5,4},{6,5},{7,6},{9,8},{10,9},{11,10},{13,12},{... | collective-permute-start | bytes 491528 | tf_op jit(solution)/shard_map/ppermute | solution.py:376
  7.1 0.0 copy-done
  7.1 0.0 copy-done.6
  7.1 0.0 copy-done.7
  7.1 3.2 %shard_map.109 = (bf16[2,192,320]{2,1,0:T(8,128)(2,1)S(1)}, bf16[2,192,320]{2,1,0:T(8,128)(2,1)S(1)}, f32[2,2,64,320]{3,2,1,0:T(8,128)S(1)}, bf16[960,192]{1,0:T(8,128)(2,1)S(1)}, f32[8,128]{1,0:T(8,128)S(1)}) custom-call(bf16[4,5,64,320]{3,2,1,0:T(8,128)(2,1)S(1)} %copy-done.2, f32[320]{0:T(512)S(1)} %copy-done.6, f32[320]{0:T(512)S(1)} %copy-done.7, ...), custom_call_target="tpu_custom_call" | custom-call | flops 1179648000 | bytes 2097152 | tf_op jit(solution)/shard_map/pallas_call | solution.py:402
  10.3 0.0 copy-start.3
  10.3 0.0 collective-permute-done.above_ref
  10.3 1.5 %collective-permute-done.1.below_ref = bf16[640,128]{1,0:T(8,128)(2,1)S(1)} collective-permute-done((bf16[640,128]{1,0:T(8,128)(2,1)S(1)}, bf16[640,128]{1,0:T(8,128)(2,1)S(1)}, u32[]{:S(2)}, u32[]{:S(2)}) %collective-permute-start.1) | collective-permute-done | bytes 163872 | tf_op jit(solution)/shard_map/ppermute | solution.py:376
  11.8 1.2 %shard_map.111 = (bf16[2,320,320]{2,1,0:T(8,128)(2,1)S(1)}, bf16[2,320,320]{2,1,0:T(8,128)(2,1)S(1)}, bf16[800,128]{1,0:T(8,128)(2,1)S(1)}, bf16[800,128]{1,0:T(8,128)(2,1)S(1)}) custom-call(f32[2,2,64,320]{3,2,1,0:T(8,128)S(1)} %get-tuple-element.30.edge_ref, bf16[640,128]{1,0:T(8,128)(2,1)S(1)} %collective-permute-done.above_ref, ...), custom_call_target="tpu_custom_call" | custom-call | flops 157286400 | bytes 2097152 | tf_op jit(solution)/shard_map/pallas_call | solution.py:415
  13.0 1.3 %collective-permute-start.2 = (bf16[800,128]{1,0:T(8,128)(2,1)S(1)}, bf16[800,128]{1,0:T(8,128)(2,1)S(1)}, u32[]{:S(2)}, u32[]{:S(2)}) collective-permute-start(bf16[800,128]{1,0:T(8,128)(2,1)S(1)} %get-tuple-element.36), channel_id=1, source_target_pairs={{0,4},{4,8},{8,12},{1,5},{5,9},{9,13},{2,6},{6,10},{10,14},{3,7},{... | collective-permute-start | bytes 614408 | tf_op jit(solution)/shard_map/ppermute | solution.py:376
  14.3 4.0 %collective-permute-start.3 = (bf16[800,128]{1,0:T(8,128)(2,1)S(1)}, bf16[800,128]{1,0:T(8,128)(2,1)S(1)}, u32[]{:S(2)}, u32[]{:S(2)}) collective-permute-start(bf16[800,128]{1,0:T(8,128)(2,1)S(1)} %get-tuple-element.37), channel_id=1, source_target_pairs={{4,0},{8,4},{12,8},{5,1},{9,5},{13,9},{6,2},{10,6},{14,10},{7,3},{... | collective-permute-start | bytes 614408 | tf_op jit(solution)/shard_map/ppermute | solution.py:376
  19.6 0.0 copy-done.3
  19.6 0.0 copy-start.4
  19.7 0.0 copy-start.8
  19.7 3.9 %shard_map.112 = (bf16[4,320,320]{2,1,0:T(8,128)(2,1)S(1)}, bf16[4,320,320]{2,1,0:T(8,128)(2,1)S(1)}) custom-call(bf16[4,5,64,320]{3,2,1,0:T(8,128)(2,1)S(1)} %copy-done.3, bf16[640,128]{1,0:T(8,128)(2,1)S(1)} %collective-permute-done.above_ref, bf16[640,128]{1,0:T(8,128)(2,1)S(1)} %collective-permute-done.1.below_ref, f32[320]{0:T(512)S(1)} %copy-done.6, ...), custom_call_target="tpu_custom_call" | custom-call | flops 1179648000 | bytes 2097152 | tf_op jit(solution)/shard_map/pallas_call | solution.py:422
  23.6 0.0 copy-start.1
  23.6 0.0 copy-start.9
  23.6 0.0 collective-permute-done.2.before_ref
  23.6 0.0 collective-permute-done.3.after_ref
  23.7 0.0 copy-done.4
  23.7 0.0 copy-done.8
  23.7 0.9 %shard_map.113 = bf16[1,800,128]{2,1,0:T(8,128)(2,1)S(1)} custom-call(s32[1,1]{1,0:T(1,128)S(6)} %copy.12.picks_ref, bf16[800,128]{1,0:T(8,128)(2,1)S(1)} %collective-permute-done.2.before_ref, bf16[800,128]{1,0:T(8,128)(2,1)S(1)} %collective-permute-done.3.after_ref, bf16[4,320,320]{2,1,0:T(8,128)(2,1)S(1)} %get-tuple-element.41.spatial_ref, ...), custom_call_target="tpu_custom_call" | custom-call | flops 196608000 | bytes 2097152 | tf_op jit(solution)/shard_map/pallas_call | solution.py:429
  24.6 0.1 collective-permute-start.6
  24.7 1.3 %collective-permute-start.5 = (bf16[1,800,128]{2,1,0:T(8,128)(2,1)S(1)}, bf16[1,800,128]{2,1,0:T(8,128)(2,1)S(1)}, u32[]{:S(2)}, u32[]{:S(2)}) collective-permute-start(bf16[1,800,128]{2,1,0:T(8,128)(2,1)S(1)} %shard_map.113), channel_id=1, source_target_pairs={{0,8},{4,12},{8,0},{12,4},{1,9},{5,13},{9,1},{13,5},{2,10},{6,14},... | collective-permute-start | bytes 614408 | tf_op jit(solution)/shard_map/ppermute | solution.py:434
  26.0 0.2 collective-permute-start.4
  26.2 0.0 copy-done.1
  26.2 0.0 copy-done.9
  26.2 4.2 %shard_map.114 = (bf16[4,320,320]{2,1,0:T(8,128)(2,1)S(1)}, bf16[4,320,320]{2,1,0:T(8,128)(2,1)S(1)}, bf16[4,320,640]{2,1,0:T(8,128)(2,1)S(1)}) custom-call(bf16[800,128]{1,0:T(8,128)(2,1)S(1)} %collective-permute-done.2.before_ref, bf16[800,128]{1,0:T(8,128)(2,1)S(1)} %collective-permute-done.3.after_ref, ...), custom_call_target="tpu_custom_call" | custom-call | flops 1572864000 | bytes 2097152 | tf_op jit(solution)/shard_map/pallas_call | solution.py:437
  30.4 3.9 %shard_map.115 = (f32[4,320,128]{2,1,0:T(8,128)S(1)}, f32[4,320,128]{2,1,0:T(8,128)S(1)}, f32[4,320,384]{2,1,0:T(8,128)S(1)}) custom-call(s32[1,1]{1,0:T(1,128)S(6)} %copy.12.picks_ref, s32[1]{0:T(128)S(6)} %copy.13.window_ref, bf16[4,320,320]{2,1,0:T(8,128)(2,1)S(1)} %get-tuple-element.43.query_ref, bf16[4,320,640]{2,1,0:T(8,128)(2,1)S(1)} %get-tuple-element.44.keyval_ref), custom_call_target="tpu_custom_call" | custom-call | flops 2621440000 | bytes 2097152 | tf_op jit(solution)/shard_map/pallas_call | solution.py:445
  34.3 0.0 collective-permute-done.6.anchor_ref
  34.3 1.3 %shard_map.116 = (f32[4,320,128]{2,1,0:T(8,128)S(1)}, f32[4,320,128]{2,1,0:T(8,128)S(1)}, f32[4,320,384]{2,1,0:T(8,128)S(1)}) custom-call(bf16[1,800,128]{2,1,0:T(8,128)(2,1)S(1)} %collective-permute-done.6.anchor_ref, bf16[320,640]{1,0:T(8,128)(2,1)S(1)} %copy-done.1, bf16[4,320,320]{2,1,0:T(8,128)(2,1)S(1)} %get-tuple-element.43.query_ref, ...), custom_call_target="tpu_custom_call" | custom-call | flops 1048576000 | bytes 2097152 | tf_op jit(solution)/shard_map/pallas_call | solution.py:449
  35.6 6.6 %collective-permute-done.5.anchor_ref = bf16[1,800,128]{2,1,0:T(8,128)(2,1)S(1)} collective-permute-done((bf16[1,800,128]{2,1,0:T(8,128)(2,1)S(1)}, bf16[1,800,128]{2,1,0:T(8,128)(2,1)S(1)}, u32[]{:S(2)}, u32[]{:S(2)}) %collective-permute-start.5) | collective-permute-done | bytes 204832 | tf_op jit(solution)/shard_map/ppermute | solution.py:434
  42.2 0.0 copy-start.5
  42.2 1.3 %shard_map.117 = (f32[4,320,128]{2,1,0:T(8,128)S(1)}, f32[4,320,128]{2,1,0:T(8,128)S(1)}, f32[4,320,384]{2,1,0:T(8,128)S(1)}) custom-call(bf16[1,800,128]{2,1,0:T(8,128)(2,1)S(1)} %collective-permute-done.5.anchor_ref, bf16[320,640]{1,0:T(8,128)(2,1)S(1)} %copy-done.1, bf16[4,320,320]{2,1,0:T(8,128)(2,1)S(1)} %get-tuple-element.43.query_ref, ...), custom_call_target="tpu_custom_call" | custom-call | flops 1048576000 | bytes 2097152 | tf_op jit(solution)/shard_map/pallas_call | solution.py:449
  43.5 0.0 collective-permute-done.4.anchor_ref
  43.5 0.0 copy-done.5
  43.5 2.8 %shard_map.118 = bf16[4,5,64,320]{3,2,1,0:T(8,128)(2,1)} custom-call(bf16[1,800,128]{2,1,0:T(8,128)(2,1)S(1)} %collective-permute-done.4.anchor_ref, bf16[320,640]{1,0:T(8,128)(2,1)S(1)} %copy-done.1, bf16[4,320,320]{2,1,0:T(8,128)(2,1)S(1)} %get-tuple-element.43.query_ref, f32[4,320,128]{2,1,0:T(8,128)S(1)} %get-tuple-element.51.top_ref, ...), custom_call_target="tpu_custom_call" | custom-call | flops 1310720000 | bytes 2097152 | tf_op jit(solution)/shard_map/pallas_call | solution.py:452
Async XLA Ops:
  0.0 7.1 %copy-start = (bf16[3,3,320,320]{3,2,1,0:T(8,128)(2,1)S(1)}, bf16[3,3,320,320]{3,2,1,0:T(8,128)(2,1)}, u32[]{:S(2)}) copy-start(bf16[3,3,320,320]{3,2,1,0:T(8,128)(2,1)} %param.15) | copy-start | bytes 5529604
  0.0 1.4 %copy-start.2 = (bf16[4,5,64,320]{3,2,1,0:T(8,128)(2,1)S(1)}, bf16[4,5,64,320]{3,2,1,0:T(8,128)(2,1)}, u32[]{:S(2)}) copy-start(bf16[4,5,64,320]{3,2,1,0:T(8,128)(2,1)} %x_ref.5) | copy-start | bytes 2457604
  1.4 5.7 %copy-start.6 = (f32[320]{0:T(512)S(1)}, f32[320]{0:T(512)}, u32[]{:S(2)}) copy-start(f32[320]{0:T(512)} %g1_ref.5) | copy-start | bytes 3844
  1.4 5.7 %copy-start.7 = (f32[320]{0:T(512)S(1)}, f32[320]{0:T(512)}, u32[]{:S(2)}) copy-start(f32[320]{0:T(512)} %g2_ref.5) | copy-start | bytes 3844
  1.4 8.8 %collective-permute-start = (bf16[640,128]{1,0:T(8,128)(2,1)S(1)}, bf16[640,128]{1,0:T(8,128)(2,1)S(1)}, u32[]{:S(2)}, u32[]{:S(2)}) collective-permute-start(bf16[640,128]{1,0:T(8,128)(2,1)S(1)} %get-tuple-element.31), channel_id=1, source_target_pairs={{0,1},{1,2},{2,3},{4,5},{5,6},{6,7},{8,9},{9,10},{10,11},{12,13},{... | collective-permute-start | bytes 491528 | tf_op jit(solution)/shard_map/ppermute | solution.py:376
  5.1 6.6 %collective-permute-start.1 = (bf16[640,128]{1,0:T(8,128)(2,1)S(1)}, bf16[640,128]{1,0:T(8,128)(2,1)S(1)}, u32[]{:S(2)}, u32[]{:S(2)}) collective-permute-start(bf16[640,128]{1,0:T(8,128)(2,1)S(1)} %get-tuple-element.32), channel_id=1, source_target_pairs={{1,0},{2,1},{3,2},{5,4},{6,5},{7,6},{9,8},{10,9},{11,10},{13,12},{... | collective-permute-start | bytes 491528 | tf_op jit(solution)/shard_map/ppermute | solution.py:376
  10.3 9.4 %copy-start.3 = (bf16[4,5,64,320]{3,2,1,0:T(8,128)(2,1)S(1)}, bf16[4,5,64,320]{3,2,1,0:T(8,128)(2,1)}, u32[]{:S(2)}) copy-start(bf16[4,5,64,320]{3,2,1,0:T(8,128)(2,1)} %x_ref.5) | copy-start | bytes 2457604
  13.0 10.6 %collective-permute-start.2 = (bf16[800,128]{1,0:T(8,128)(2,1)S(1)}, bf16[800,128]{1,0:T(8,128)(2,1)S(1)}, u32[]{:S(2)}, u32[]{:S(2)}) collective-permute-start(bf16[800,128]{1,0:T(8,128)(2,1)S(1)} %get-tuple-element.36), channel_id=1, source_target_pairs={{0,4},{4,8},{8,12},{1,5},{5,9},{9,13},{2,6},{6,10},{10,14},{3,7},{... | collective-permute-start | bytes 614408 | tf_op jit(solution)/shard_map/ppermute | solution.py:376
  14.3 9.3 %collective-permute-start.3 = (bf16[800,128]{1,0:T(8,128)(2,1)S(1)}, bf16[800,128]{1,0:T(8,128)(2,1)S(1)}, u32[]{:S(2)}, u32[]{:S(2)}) collective-permute-start(bf16[800,128]{1,0:T(8,128)(2,1)S(1)} %get-tuple-element.37), channel_id=1, source_target_pairs={{4,0},{8,4},{12,8},{5,1},{9,5},{13,9},{6,2},{10,6},{14,10},{7,3},{... | collective-permute-start | bytes 614408 | tf_op jit(solution)/shard_map/ppermute | solution.py:376
  19.6 4.0 %copy-start.4 = (bf16[3,320,320]{2,1,0:T(8,128)(2,1)S(1)}, bf16[3,320,320]{2,1,0:T(8,128)(2,1)}, u32[]{:S(2)}) copy-start(bf16[3,320,320]{2,1,0:T(8,128)(2,1)} %wt_ref.3) | copy-start | bytes 1843204
  19.7 4.0 %copy-start.8 = (f32[320]{0:T(512)S(1)}, f32[320]{0:T(512)}, u32[]{:S(2)}) copy-start(f32[320]{0:T(512)} %g3_ref.3) | copy-start | bytes 3844
  23.6 2.6 %copy-start.1 = (bf16[320,640]{1,0:T(8,128)(2,1)S(1)}, bf16[320,640]{1,0:T(8,128)(2,1)}, u32[]{:S(2)}) copy-start(bf16[320,640]{1,0:T(8,128)(2,1)} %wkv_ref.7) | copy-start | bytes 1228804
  23.6 2.6 %copy-start.9 = (bf16[320,320]{1,0:T(8,128)(2,1)S(1)}, bf16[320,320]{1,0:T(8,128)(2,1)}, u32[]{:S(2)}) copy-start(bf16[320,320]{1,0:T(8,128)(2,1)} %wq_ref.1) | copy-start | bytes 614404
  24.6 9.7 %collective-permute-start.6 = (bf16[1,800,128]{2,1,0:T(8,128)(2,1)S(1)}, bf16[1,800,128]{2,1,0:T(8,128)(2,1)S(1)}, u32[]{:S(2)}, u32[]{:S(2)}) collective-permute-start(bf16[1,800,128]{2,1,0:T(8,128)(2,1)S(1)} %shard_map.113), channel_id=1, source_target_pairs={{0,4},{4,8},{8,12},{12,0},{1,5},{5,9},{9,13},{13,1},{2,6},{6,10},{... | collective-permute-start | bytes 614408 | tf_op jit(solution)/shard_map/ppermute | solution.py:434
  24.7 17.5 %collective-permute-start.5 = (bf16[1,800,128]{2,1,0:T(8,128)(2,1)S(1)}, bf16[1,800,128]{2,1,0:T(8,128)(2,1)S(1)}, u32[]{:S(2)}, u32[]{:S(2)}) collective-permute-start(bf16[1,800,128]{2,1,0:T(8,128)(2,1)S(1)} %shard_map.113), channel_id=1, source_target_pairs={{0,8},{4,12},{8,0},{12,4},{1,9},{5,13},{9,1},{13,5},{2,10},{6,14},... | collective-permute-start | bytes 614408 | tf_op jit(solution)/shard_map/ppermute | solution.py:434
  26.0 17.5 %collective-permute-start.4 = (bf16[1,800,128]{2,1,0:T(8,128)(2,1)S(1)}, bf16[1,800,128]{2,1,0:T(8,128)(2,1)S(1)}, u32[]{:S(2)}, u32[]{:S(2)}) collective-permute-start(bf16[1,800,128]{2,1,0:T(8,128)(2,1)S(1)} %shard_map.113), channel_id=1, source_target_pairs={{0,12},{4,0},{8,4},{12,8},{1,13},{5,1},{9,5},{13,9},{2,14},{6,2},{... | collective-permute-start | bytes 614408 | tf_op jit(solution)/shard_map/ppermute | solution.py:434
  42.2 1.3 %copy-start.5 = (bf16[320,320]{1,0:T(8,128)(2,1)S(1)}, bf16[320,320]{1,0:T(8,128)(2,1)}, u32[]{:S(2)}) copy-start(bf16[320,320]{1,0:T(8,128)(2,1)} %wo_ref.1) | copy-start | bytes 614404
where the time goes:
time: 46.7 us; the launch traced here: 46.5 us
  Pallas kernels  22.9 us (49%)
  starting transfers between devices  12.5 us (27%)
  waiting for transfers between devices  8.08 us (17%)
  between operations  1.69 us (4%)
  local copies, waits for them, and re-layouts  1.4 us (3%)
    ppermute x4, starting transfers between devices, neighbours(): return (lax.ppermute(last, axis, up), lax.ppermute(leading, axis, down))  10.9 us
    ppermute x3, waiting for transfers between devices, on_device(): lax.ppermute(chosen, 'clip', [(i, (i + s) % clips) for i in range(clips)])  6.59 us
    pallas_call x1, Pallas kernels, on_device(): call(temporal_kernel, [(some, BF), (some, BF), ((frames, cells, 2 * chann...  4.21 us
    pallas_call x1, Pallas kernels, on_device(): call(inner_kernel, [(some, BF), (some, BF)], [VMEM] * 9, [col, pltpu.VMEM...  3.93 us
    pallas_call x1, Pallas kernels, on_device(): call(local_kernel, states, [VMEM] * 4, flops=10 * frames * cells * one, l...  3.9 us
    pallas_call x1, Pallas kernels, on_device(): call(outer_kernel, [(middle, BF), (middle, BF), ((2, 2, width, channels),...  3.17 us
    pallas_call x1, Pallas kernels, on_device(): call(last_kernel, [(latents.shape, BF)], [VMEM] * 8, [pltpu.VMEM(latents....  2.8 us
    pallas_call x2, Pallas kernels, on_device(): call(anchor_kernel, states, [VMEM] * 6, flops=4 * frames * cells * one, l...  2.58 us
  transfers between devices with their start and end apart: 7, of which 2 were waited for; matrix products, arithmetic and copies ran while one was open for 0% of the time, Pallas kernels for 38%

commit v1 on v0

--- a/solution.py
+++ b/solution.py
@@ -101,70 +101,87 @@
         rem_ref[:, a * rest : (a + 1) * rest] = w_ref[a, :, full:]
 
 
-def frame_rows(f, x_ref, col_ref, g1_ref, w_ref, rem_ref):
-    _, height, width, channels = x_ref.shape
+def hidden_columns(v, g1_ref, width):
+    return columns(silu(norm(v, g1_ref)), width)
+
+
+def stacked_rows(col_ref, count, height, width, w_ref, rem_ref):
     cells = height * width
+    rims = (col_ref.shape[0] - count * cells) // 2
+    channels = w_ref.shape[2]
     full = channels // 256 * 256
     rest = channels - full
-    col_ref[...] = columns(silu(norm(x_ref[f].reshape(cells, channels), g1_ref)), width)
-    centre = dot(col_ref[...], w_ref[1, :, :full])
-    above = dot(col_ref[: cells - width], w_ref[0, :, :full])
-    below = dot(col_ref[width:], w_ref[2, :, :full])
+    size = count * cells
+    above = dot(col_ref[: rims + size], w_ref[0, :, :full])
+    centre = dot(col_ref[rims : rims + size], w_ref[1, :, :full])
+    below = dot(col_ref[rims:], w_ref[2, :, :full])
     tails = dot(col_ref[...], rem_ref[...])
-    rows = []
-    for row in range(height):
-        lo, hi = row * width, (row + 1) * width
-        wide = centre[lo:hi]
-        tail = tails[lo:hi, rest : 2 * rest]
-        if row > 0:
-            wide = wide + above[lo - width : lo]
-            tail = tail + tails[lo - width : lo, :rest]
-        if row < height - 1:
-            wide = wide + below[lo:hi]
-            tail = tail + tails[hi : hi + width, 2 * rest : 3 * rest]
-        rows.append(x_ref[f, row].astype(F32) + jnp.concatenate([wide, tail], axis=1))
-    return rows
-
-
-def rim_terms(refs, frames, width, channels, g1_ref, w_ref):
-    terms = []
-    for ref, a in zip(refs, (0, 2)):
-        rows = unpacked(ref[...], channels)
-        rows = jnp.concatenate([rows[f * width : (f + 1) * width] for f in frames], axis=0)
-        terms.append(dot(columns(silu(norm(rows, g1_ref)), width), w_ref[a]))
+
+    def terms(place, row):
+        own = place * cells + row * width
+        wide = centre[own : own + width]
+        tail = tails[rims + own : rims + own + width, rest : 2 * rest]
+        if row > 0 or rims:
+            at = rims + own - width if row > 0 else place * width
+            wide = wide + above[at : at + width]
+            tail = tail + tails[at : at + width, :rest]
+        if row < height - 1 or rims:
+            at = own + width if row < height - 1 else size + place * width
+            wide = wide + below[at : at + width]
+            tail = tail + tails[rims + at : rims + at + width, 2 * rest :]
+        return jnp.concatenate([wide, tail], axis=1)
+
     return terms
+
+
+def rim_rows(ref, frames, width, channels):
+    rows = unpacked(ref[...], channels)
+    return jnp.concatenate([rows[f * width : (f + 1) * width] for f in frames], axis=0)
 
 
 def outer_kernel(x_ref, g1_ref, g2_ref, w_ref, mid_ref, mid2_ref, edge_ref, rem_ref, order_ref, col_ref):
     frames, height, width, channels = x_ref.shape
+    cells = height * width
     order_ref[...] = jnp.zeros_like(order_ref)
     rests_into(rem_ref, w_ref)
-
-    def frame(s, _):
-        rows = frame_rows(s * (frames - 1), x_ref, col_ref, g1_ref, w_ref, rem_ref)
-        edge_ref[s, 0] = rows[0]
-        edge_ref[s, 1] = rows[-1]
-        for row, total in enumerate(rows[1:-1]):
-            rounded = total.astype(BF)
-            mid_ref[s, row * width : (row + 1) * width] = rounded
-            hidden = silu(norm(rounded, g2_ref)).astype(BF)
-            mid2_ref[s, row * width : (row + 1) * width] = hidden
-        return 0
-
-    lax.fori_loop(0, 2, frame, 0)
+    outer = (0, frames - 1)
+    for s, f in enumerate(outer):
+        x = x_ref[f].reshape(cells, channels)
+        col_ref[s * cells : (s + 1) * cells] = hidden_columns(x, g1_ref, width)
+    terms = stacked_rows(col_ref, 2, height, width, w_ref, rem_ref)
+    for s, f in enumerate(outer):
+        for row in range(height):
+            total = x_ref[f, row].astype(F32) + terms(s, row)
+            if 0 < row < height - 1:
+                rounded = total.astype(BF)
+                lo = (row - 1) * width
+                mid_ref[s, lo : lo + width] = rounded
+                mid2_ref[s, lo : lo + width] = silu(norm(rounded, g2_ref)).astype(BF)
+            else:
+                edge_ref[s, 0 if row == 0 else 1] = total
 
 
 def outer_edge_kernel(
-    frames, edge_ref, above_ref, below_ref, order_ref, mid_ref, mid2_ref, g1_ref, g2_ref, w_ref,
+    frames, edge_ref, above_ref, below_ref, order_ref, mid_ref, mid2_ref, g1_ref, g2_ref, w_ref, rem_ref,
     spatial_ref, hidden_ref, first_ref, last_ref,
 ):
     _, cells, channels = spatial_ref.shape
     width = edge_ref.shape[2]
+    full = channels // 256 * 256
+    rest = channels - full
     spatial_ref[:, width : cells - width] = mid_ref[...]
     hidden_ref[:, width : cells - width] = mid2_ref[...]
-    terms = rim_terms((above_ref, below_ref), (0, frames - 1), width, channels, g1_ref, w_ref)
+    cols = [
+        hidden_columns(rim_rows(ref, (0, frames - 1), width, channels), g1_ref, width)
+        for ref in (above_ref, below_ref)
+    ]
+    tails = dot(jnp.concatenate(cols, axis=0), rem_ref[...])
+    size = 2 * width
     for side, lo in ((0, 0), (1, cells - width)):
-        rounded = (edge_ref[:, side].reshape(2 * width, channels) + terms[side]).astype(BF)
+        tail = tails[:size, :rest] if side == 0 else tails[size:, 2 * rest :]
+        wide = dot(cols[side], w_ref[2 * side, :, :full])
+        term = jnp.concatenate([wide, tail], axis=1)
+        rounded = (edge_ref[:, side].reshape(size, channels) + term).astype(BF)
         hidden = silu(norm(rounded, g2_ref)).astype(BF)
         spatial_ref[:, lo : lo + width] = rounded.reshape(2, width, channels)
         hidden_ref[:, lo : lo + width] = hidden.reshape(2, width, channels)
@@ -174,29 +191,29 @@
 
 def inner_kernel(
     x_ref, above_ref, below_ref, g1_ref, g2_ref, w_ref, rem_ref, outer_spatial_ref, outer_hidden_ref,
-    spatial_ref, hidden_ref, col_ref, add_ref,
+    spatial_ref, hidden_ref, col_ref,
 ):
     frames, height, width, channels = x_ref.shape
+    cells = height * width
     for s, f in ((0, 0), (1, frames - 1)):
         spatial_ref[f] = outer_spatial_ref[s]
         hidden_ref[f] = outer_hidden_ref[s]
     inside = range(1, frames - 1)
-    terms = rim_terms((above_ref, below_ref), inside, width, channels, g1_ref, w_ref)
-    for side in range(2):
-        add_ref[side, 1 : frames - 1] = terms[side].reshape(frames - 2, width, channels)
-
-    def frame(f, _):
-        rows = frame_rows(f, x_ref, col_ref, g1_ref, w_ref, rem_ref)
-        rows[0] = rows[0] + add_ref[0, f]
-        rows[-1] = rows[-1] + add_ref[1, f]
-        for row, total in enumerate(rows):
-            rounded = total.astype(BF)
-            spatial_ref[f, row * width : (row + 1) * width] = rounded
-            hidden = silu(norm(rounded, g2_ref)).astype(BF)
-            hidden_ref[f, row * width : (row + 1) * width] = hidden
-        return 0
-
-    lax.fori_loop(1, frames - 1, frame, 0)
+    rims = len(inside) * width
+    end = rims + len(inside) * cells
+    col_ref[:rims] = hidden_columns(rim_rows(above_ref, inside, width, channels), g1_ref, width)
+    for s, f in enumerate(inside):
+        x = x_ref[f].reshape(cells, channels)
+        lo = rims + s * cells
+        col_ref[lo : lo + cells] = hidden_columns(x, g1_ref, width)
+    col_ref[end:] = hidden_columns(rim_rows(below_ref, inside, width, channels), g1_ref, width)
+    terms = stacked_rows(col_ref, len(inside), height, width, w_ref, rem_ref)
+    for s, f in enumerate(inside):
+        for row in range(height):
+            rounded = (x_ref[f, row].astype(F32) + terms(s, row)).astype(BF)
+            lo = row * width
+            spatial_ref[f, lo : lo + width] = rounded
+            hidden_ref[f, lo : lo + width] = silu(norm(rounded, g2_ref)).astype(BF)
 
 
 def chosen_kernel(
@@ -397,7 +414,8 @@
         edge_kernel, [((edge_packed, LANES), BF)] * 2, [VMEM], flops=8 * frames * cells * one
     )(x)
     above, below = neighbours(top, bottom, "strip")
-    col = pltpu.VMEM((cells, 3 * channels), BF)
+    outer_col = pltpu.VMEM((2 * cells, 3 * channels), BF)
+    inner_col = pltpu.VMEM(((frames - 2) * (cells + 2 * width), 3 * channels), BF)
     middle = (2, cells - 2 * width, channels)
     mid, mid2, edge, w_rem, order = call(
         outer_kernel,
@@ -409,21 +427,21 @@
             ((8, LANES), F32),
         ],
         [VMEM] * 4,
-        [col],
+        [outer_col],
         flops=9 * 2 * cells * one,
     )(x, g1, g2, w)
     outer_spatial, outer_hidden, first, last = call(
         functools.partial(outer_edge_kernel, frames),
         [((2, cells, channels), BF)] * 2 + [((packed, LANES), BF)] * 2,
-        [VMEM] * 9,
+        [VMEM] * 10,
         flops=6 * 2 * width * one,
-    )(edge, above, below, order, mid, mid2, g1, g2, w)
+    )(edge, above, below, order, mid, mid2, g1, g2, w, w_rem)
     before, after = neighbours(first, last, "clip")
     spatial, hidden = call(
         inner_kernel,
         [(some, BF), (some, BF)],
         [VMEM] * 9,
-        [col, pltpu.VMEM((2, frames, width, channels), F32)],
+        [inner_col],
         flops=9 * (frames - 2) * cells * one,
     )(x, above, below, g1, g2, w, w_rem, outer_spatial, outer_hidden)
     (chosen,) = call(

time: 46.7 us -> 46.5 us (level)
  Pallas kernels: 22.9 us -> 22.1 us
  waiting for transfers between devices: 8.08 us -> 8.6 us
  transfers between devices with their start and end apart: 7 -> 7, of which waited for: 2 -> 2; matrix products, arithmetic and copies ran while one was open for 0% -> 0% of each run, Pallas kernels for 38% -> 37%
where the time goes in v1:
time: 46.5 us; the launch traced here: 46.3 us
  Pallas kernels  22.1 us (48%)
  starting transfers between devices  12.4 us (27%)
  waiting for transfers between devices  8.6 us (18%)
  between operations  1.68 us (4%)
  local copies, waits for them, and re-layouts  1.39 us (3%)
    ppermute x4, starting transfers between devices, neighbours(): return (lax.ppermute(last, axis, up), lax.ppermute(leading, axis, down))  10.9 us
    ppermute x3, waiting for transfers between devices, on_device(): lax.ppermute(chosen, 'clip', [(i, (i + s) % clips) for i in range(clips)])  6.81 us
    pallas_call x1, Pallas kernels, on_device(): call(temporal_kernel, [(some, BF), (some, BF), ((frames, cells, 2 * chann...  4.21 us
    pallas_call x1, Pallas kernels, on_device(): call(local_kernel, states, [VMEM] * 4, flops=10 * frames * cells * one, l...  3.9 us
    pallas_call x1, Pallas kernels, on_device(): call(inner_kernel, [(some, BF), (some, BF)], [VMEM] * 9, [inner_col], flo...  3.68 us
    pallas_call x1, Pallas kernels, on_device(): call(outer_kernel, [(middle, BF), (middle, BF), ((2, 2, width, channels),...  2.88 us
    pallas_call x1, Pallas kernels, on_device(): call(last_kernel, [(latents.shape, BF)], [VMEM] * 8, [pltpu.VMEM(latents....  2.77 us
    pallas_call x2, Pallas kernels, on_device(): call(anchor_kernel, states, [VMEM] * 6, flops=4 * frames * cells * one, l...  2.57 us
  transfers between devices with their start and end apart: 7, of which 2 were waited for; matrix products, arithmetic and copies ran while one was open for 0% of the time, Pallas kernels for 37%

profile of v1, /device:TPU:25, one launch (start us, length us, event | category | flops | bytes accessed | tf_op | source)
XLA Modules:
  0.0 46.3 jit_solution(2745813245131732167)
XLA Ops:
  0.0 0.0 copy-start
  0.0 0.0 copy-start.2
  0.0 1.3 %copy-done.2 = bf16[4,5,64,320]{3,2,1,0:T(8,128)(2,1)S(1)} copy-done((bf16[4,5,64,320]{3,2,1,0:T(8,128)(2,1)S(1)}, bf16[4,5,64,320]{3,2,1,0:T(8,128)(2,1)}, u32[]{:S(2)}) %copy-start.2) | copy-done | bytes 819224
  1.4 0.0 copy-start.6
  1.4 0.0 copy-start.7
  1.4 0.1 shard_map.110
  1.4 3.7 %collective-permute-start = (bf16[640,128]{1,0:T(8,128)(2,1)S(1)}, bf16[640,128]{1,0:T(8,128)(2,1)S(1)}, u32[]{:S(2)}, u32[]{:S(2)}) collective-permute-start(bf16[640,128]{1,0:T(8,128)(2,1)S(1)} %get-tuple-element.31), channel_id=1, source_target_pairs={{0,1},{1,2},{2,3},{4,5},{5,6},{6,7},{8,9},{9,10},{10,11},{12,13},{... | collective-permute-start | bytes 491528 | tf_op jit(solution)/shard_map/ppermute | solution.py:393
  5.1 1.9 %collective-permute-start.1 = (bf16[640,128]{1,0:T(8,128)(2,1)S(1)}, bf16[640,128]{1,0:T(8,128)(2,1)S(1)}, u32[]{:S(2)}, u32[]{:S(2)}) collective-permute-start(bf16[640,128]{1,0:T(8,128)(2,1)S(1)} %get-tuple-element.32), channel_id=1, source_target_pairs={{1,0},{2,1},{3,2},{5,4},{6,5},{7,6},{9,8},{10,9},{11,10},{13,12},{... | collective-permute-start | bytes 491528 | tf_op jit(solution)/shard_map/ppermute | solution.py:393
  7.1 0.0 copy-done
  7.1 0.0 copy-done.6
  7.1 0.0 copy-done.7
  7.1 2.9 %shard_map.109 = (bf16[2,192,320]{2,1,0:T(8,128)(2,1)S(1)}, bf16[2,192,320]{2,1,0:T(8,128)(2,1)S(1)}, f32[2,2,64,320]{3,2,1,0:T(8,128)S(1)}, bf16[960,192]{1,0:T(8,128)(2,1)S(1)}, f32[8,128]{1,0:T(8,128)S(1)}) custom-call(bf16[4,5,64,320]{3,2,1,0:T(8,128)(2,1)S(1)} %copy-done.2, f32[320]{0:T(512)S(1)} %copy-done.6, f32[320]{0:T(512)S(1)} %copy-done.7, ...), custom_call_target="tpu_custom_call" | custom-call | flops 1179648000 | bytes 2097152 | tf_op jit(solution)/shard_map/pallas_call | solution.py:420
  10.0 0.0 collective-permute-done.above_ref
  10.0 1.8 %collective-permute-done.1.below_ref = bf16[640,128]{1,0:T(8,128)(2,1)S(1)} collective-permute-done((bf16[640,128]{1,0:T(8,128)(2,1)S(1)}, bf16[640,128]{1,0:T(8,128)(2,1)S(1)}, u32[]{:S(2)}, u32[]{:S(2)}) %collective-permute-start.1) | collective-permute-done | bytes 163872 | tf_op jit(solution)/shard_map/ppermute | solution.py:393
  11.8 0.0 copy-start.3
  11.8 1.1 %shard_map.111 = (bf16[2,320,320]{2,1,0:T(8,128)(2,1)S(1)}, bf16[2,320,320]{2,1,0:T(8,128)(2,1)S(1)}, bf16[800,128]{1,0:T(8,128)(2,1)S(1)}, bf16[800,128]{1,0:T(8,128)(2,1)S(1)}) custom-call(f32[2,2,64,320]{3,2,1,0:T(8,128)S(1)} %get-tuple-element.30.edge_ref, bf16[640,128]{1,0:T(8,128)(2,1)S(1)} %collective-permute-done.above_ref, ...), custom_call_target="tpu_custom_call" | custom-call | flops 157286400 | bytes 2097152 | tf_op jit(solution)/shard_map/pallas_call | solution.py:433
  12.9 1.3 %collective-permute-start.2 = (bf16[800,128]{1,0:T(8,128)(2,1)S(1)}, bf16[800,128]{1,0:T(8,128)(2,1)S(1)}, u32[]{:S(2)}, u32[]{:S(2)}) collective-permute-start(bf16[800,128]{1,0:T(8,128)(2,1)S(1)} %get-tuple-element.37), channel_id=1, source_target_pairs={{0,4},{4,8},{8,12},{1,5},{5,9},{9,13},{2,6},{6,10},{10,14},{3,7},{... | collective-permute-start | bytes 614408 | tf_op jit(solution)/shard_map/ppermute | solution.py:393
  14.2 4.0 %collective-permute-start.3 = (bf16[800,128]{1,0:T(8,128)(2,1)S(1)}, bf16[800,128]{1,0:T(8,128)(2,1)S(1)}, u32[]{:S(2)}, u32[]{:S(2)}) collective-permute-start(bf16[800,128]{1,0:T(8,128)(2,1)S(1)} %get-tuple-element.38), channel_id=1, source_target_pairs={{4,0},{8,4},{12,8},{5,1},{9,5},{13,9},{6,2},{10,6},{14,10},{7,3},{... | collective-permute-start | bytes 614408 | tf_op jit(solution)/shard_map/ppermute | solution.py:393
  19.5 0.0 copy-done.3
  19.5 0.0 copy-start.4
  19.5 0.0 copy-start.8
  19.5 3.7 %shard_map.112 = (bf16[4,320,320]{2,1,0:T(8,128)(2,1)S(1)}, bf16[4,320,320]{2,1,0:T(8,128)(2,1)S(1)}) custom-call(bf16[4,5,64,320]{3,2,1,0:T(8,128)(2,1)S(1)} %copy-done.3, bf16[640,128]{1,0:T(8,128)(2,1)S(1)} %collective-permute-done.above_ref, bf16[640,128]{1,0:T(8,128)(2,1)S(1)} %collective-permute-done.1.below_ref, f32[320]{0:T(512)S(1)} %copy-done.6, ...), custom_call_target="tpu_custom_call" | custom-call | flops 1179648000 | bytes 2097152 | tf_op jit(solution)/shard_map/pallas_call | solution.py:440
  23.2 0.0 copy-start.1
  23.2 0.0 copy-start.9
  23.2 0.0 collective-permute-done.2.before_ref
  23.2 0.0 collective-permute-done.3.after_ref
  23.3 0.0 copy-done.4
  23.3 0.0 copy-done.8
  23.3 0.9 %shard_map.113 = bf16[1,800,128]{2,1,0:T(8,128)(2,1)S(1)} custom-call(s32[1,1]{1,0:T(1,128)S(6)} %copy.12.picks_ref, bf16[800,128]{1,0:T(8,128)(2,1)S(1)} %collective-permute-done.2.before_ref, bf16[800,128]{1,0:T(8,128)(2,1)S(1)} %collective-permute-done.3.after_ref, bf16[4,320,320]{2,1,0:T(8,128)(2,1)S(1)} %get-tuple-element.41.spatial_ref, ...), custom_call_target="tpu_custom_call" | custom-call | flops 196608000 | bytes 2097152 | tf_op jit(solution)/shard_map/pallas_call | solution.py:447
  24.2 0.1 collective-permute-start.6
  24.3 1.3 %collective-permute-start.5 = (bf16[1,800,128]{2,1,0:T(8,128)(2,1)S(1)}, bf16[1,800,128]{2,1,0:T(8,128)(2,1)S(1)}, u32[]{:S(2)}, u32[]{:S(2)}) collective-permute-start(bf16[1,800,128]{2,1,0:T(8,128)(2,1)S(1)} %shard_map.113), channel_id=1, source_target_pairs={{0,8},{4,12},{8,0},{12,4},{1,9},{5,13},{9,1},{13,5},{2,10},{6,14},... | collective-permute-start | bytes 614408 | tf_op jit(solution)/shard_map/ppermute | solution.py:452
  25.6 0.2 collective-permute-start.4
  25.8 0.0 copy-done.1
  25.8 0.0 copy-done.9
  25.8 4.2 %shard_map.114 = (bf16[4,320,320]{2,1,0:T(8,128)(2,1)S(1)}, bf16[4,320,320]{2,1,0:T(8,128)(2,1)S(1)}, bf16[4,320,640]{2,1,0:T(8,128)(2,1)S(1)}) custom-call(bf16[800,128]{1,0:T(8,128)(2,1)S(1)} %collective-permute-done.2.before_ref, bf16[800,128]{1,0:T(8,128)(2,1)S(1)} %collective-permute-done.3.after_ref, ...), custom_call_target="tpu_custom_call" | custom-call | flops 1572864000 | bytes 2097152 | tf_op jit(solution)/shard_map/pallas_call | solution.py:455
  30.0 3.9 %shard_map.115 = (f32[4,320,128]{2,1,0:T(8,128)S(1)}, f32[4,320,128]{2,1,0:T(8,128)S(1)}, f32[4,320,384]{2,1,0:T(8,128)S(1)}) custom-call(s32[1,1]{1,0:T(1,128)S(6)} %copy.12.picks_ref, s32[1]{0:T(128)S(6)} %copy.13.window_ref, bf16[4,320,320]{2,1,0:T(8,128)(2,1)S(1)} %get-tuple-element.43.query_ref, bf16[4,320,640]{2,1,0:T(8,128)(2,1)S(1)} %get-tuple-element.44.keyval_ref), custom_call_target="tpu_custom_call" | custom-call | flops 2621440000 | bytes 2097152 | tf_op jit(solution)/shard_map/pallas_call | solution.py:463
  33.9 0.0 collective-permute-done.6.anchor_ref
  33.9 1.3 %shard_map.116 = (f32[4,320,128]{2,1,0:T(8,128)S(1)}, f32[4,320,128]{2,1,0:T(8,128)S(1)}, f32[4,320,384]{2,1,0:T(8,128)S(1)}) custom-call(bf16[1,800,128]{2,1,0:T(8,128)(2,1)S(1)} %collective-permute-done.6.anchor_ref, bf16[320,640]{1,0:T(8,128)(2,1)S(1)} %copy-done.1, bf16[4,320,320]{2,1,0:T(8,128)(2,1)S(1)} %get-tuple-element.43.query_ref, ...), custom_call_target="tpu_custom_call" | custom-call | flops 1048576000 | bytes 2097152 | tf_op jit(solution)/shard_map/pallas_call | solution.py:467
  35.2 6.8 %collective-permute-done.5.anchor_ref = bf16[1,800,128]{2,1,0:T(8,128)(2,1)S(1)} collective-permute-done((bf16[1,800,128]{2,1,0:T(8,128)(2,1)S(1)}, bf16[1,800,128]{2,1,0:T(8,128)(2,1)S(1)}, u32[]{:S(2)}, u32[]{:S(2)}) %collective-permute-start.5) | collective-permute-done | bytes 204832 | tf_op jit(solution)/shard_map/ppermute | solution.py:452
  42.0 0.0 copy-start.5
  42.0 1.3 %shard_map.117 = (f32[4,320,128]{2,1,0:T(8,128)S(1)}, f32[4,320,128]{2,1,0:T(8,128)S(1)}, f32[4,320,384]{2,1,0:T(8,128)S(1)}) custom-call(bf16[1,800,128]{2,1,0:T(8,128)(2,1)S(1)} %collective-permute-done.5.anchor_ref, bf16[320,640]{1,0:T(8,128)(2,1)S(1)} %copy-done.1, bf16[4,320,320]{2,1,0:T(8,128)(2,1)S(1)} %get-tuple-element.43.query_ref, ...), custom_call_target="tpu_custom_call" | custom-call | flops 1048576000 | bytes 2097152 | tf_op jit(solution)/shard_map/pallas_call | solution.py:467
  43.3 0.0 collective-permute-done.4.anchor_ref
  43.3 0.0 copy-done.5
  43.3 2.8 %shard_map.118 = bf16[4,5,64,320]{3,2,1,0:T(8,128)(2,1)} custom-call(bf16[1,800,128]{2,1,0:T(8,128)(2,1)S(1)} %collective-permute-done.4.anchor_ref, bf16[320,640]{1,0:T(8,128)(2,1)S(1)} %copy-done.1, bf16[4,320,320]{2,1,0:T(8,128)(2,1)S(1)} %get-tuple-element.43.query_ref, f32[4,320,128]{2,1,0:T(8,128)S(1)} %get-tuple-element.51.top_ref, ...), custom_call_target="tpu_custom_call" | custom-call | flops 1310720000 | bytes 2097152 | tf_op jit(solution)/shard_map/pallas_call | solution.py:470
Async XLA Ops:
  0.0 7.1 %copy-start = (bf16[3,3,320,320]{3,2,1,0:T(8,128)(2,1)S(1)}, bf16[3,3,320,320]{3,2,1,0:T(8,128)(2,1)}, u32[]{:S(2)}) copy-start(bf16[3,3,320,320]{3,2,1,0:T(8,128)(2,1)} %param.15) | copy-start | bytes 5529604
  0.0 1.4 %copy-start.2 = (bf16[4,5,64,320]{3,2,1,0:T(8,128)(2,1)S(1)}, bf16[4,5,64,320]{3,2,1,0:T(8,128)(2,1)}, u32[]{:S(2)}) copy-start(bf16[4,5,64,320]{3,2,1,0:T(8,128)(2,1)} %x_ref.5) | copy-start | bytes 2457604
  1.4 5.7 %copy-start.6 = (f32[320]{0:T(512)S(1)}, f32[320]{0:T(512)}, u32[]{:S(2)}) copy-start(f32[320]{0:T(512)} %g1_ref.5) | copy-start | bytes 3844
  1.4 5.7 %copy-start.7 = (f32[320]{0:T(512)S(1)}, f32[320]{0:T(512)}, u32[]{:S(2)}) copy-start(f32[320]{0:T(512)} %g2_ref.5) | copy-start | bytes 3844
  1.4 8.5 %collective-permute-start = (bf16[640,128]{1,0:T(8,128)(2,1)S(1)}, bf16[640,128]{1,0:T(8,128)(2,1)S(1)}, u32[]{:S(2)}, u32[]{:S(2)}) collective-permute-start(bf16[640,128]{1,0:T(8,128)(2,1)S(1)} %get-tuple-element.31), channel_id=1, source_target_pairs={{0,1},{1,2},{2,3},{4,5},{5,6},{6,7},{8,9},{9,10},{10,11},{12,13},{... | collective-permute-start | bytes 491528 | tf_op jit(solution)/shard_map/ppermute | solution.py:393
  5.1 6.6 %collective-permute-start.1 = (bf16[640,128]{1,0:T(8,128)(2,1)S(1)}, bf16[640,128]{1,0:T(8,128)(2,1)S(1)}, u32[]{:S(2)}, u32[]{:S(2)}) collective-permute-start(bf16[640,128]{1,0:T(8,128)(2,1)S(1)} %get-tuple-element.32), channel_id=1, source_target_pairs={{1,0},{2,1},{3,2},{5,4},{6,5},{7,6},{9,8},{10,9},{11,10},{13,12},{... | collective-permute-start | bytes 491528 | tf_op jit(solution)/shard_map/ppermute | solution.py:393
  11.8 7.7 %copy-start.3 = (bf16[4,5,64,320]{3,2,1,0:T(8,128)(2,1)S(1)}, bf16[4,5,64,320]{3,2,1,0:T(8,128)(2,1)}, u32[]{:S(2)}) copy-start(bf16[4,5,64,320]{3,2,1,0:T(8,128)(2,1)} %x_ref.5) | copy-start | bytes 2457604
  12.9 10.4 %collective-permute-start.2 = (bf16[800,128]{1,0:T(8,128)(2,1)S(1)}, bf16[800,128]{1,0:T(8,128)(2,1)S(1)}, u32[]{:S(2)}, u32[]{:S(2)}) collective-permute-start(bf16[800,128]{1,0:T(8,128)(2,1)S(1)} %get-tuple-element.37), channel_id=1, source_target_pairs={{0,4},{4,8},{8,12},{1,5},{5,9},{9,13},{2,6},{6,10},{10,14},{3,7},{... | collective-permute-start | bytes 614408 | tf_op jit(solution)/shard_map/ppermute | solution.py:393
  14.2 9.1 %collective-permute-start.3 = (bf16[800,128]{1,0:T(8,128)(2,1)S(1)}, bf16[800,128]{1,0:T(8,128)(2,1)S(1)}, u32[]{:S(2)}, u32[]{:S(2)}) collective-permute-start(bf16[800,128]{1,0:T(8,128)(2,1)S(1)} %get-tuple-element.38), channel_id=1, source_target_pairs={{4,0},{8,4},{12,8},{5,1},{9,5},{13,9},{6,2},{10,6},{14,10},{7,3},{... | collective-permute-start | bytes 614408 | tf_op jit(solution)/shard_map/ppermute | solution.py:393
  19.5 3.8 %copy-start.4 = (bf16[3,320,320]{2,1,0:T(8,128)(2,1)S(1)}, bf16[3,320,320]{2,1,0:T(8,128)(2,1)}, u32[]{:S(2)}) copy-start(bf16[3,320,320]{2,1,0:T(8,128)(2,1)} %wt_ref.3) | copy-start | bytes 1843204
  19.5 3.8 %copy-start.8 = (f32[320]{0:T(512)S(1)}, f32[320]{0:T(512)}, u32[]{:S(2)}) copy-start(f32[320]{0:T(512)} %g3_ref.3) | copy-start | bytes 3844
  23.2 2.6 %copy-start.1 = (bf16[320,640]{1,0:T(8,128)(2,1)S(1)}, bf16[320,640]{1,0:T(8,128)(2,1)}, u32[]{:S(2)}) copy-start(bf16[320,640]{1,0:T(8,128)(2,1)} %wkv_ref.7) | copy-start | bytes 1228804
  23.2 2.6 %copy-start.9 = (bf16[320,320]{1,0:T(8,128)(2,1)S(1)}, bf16[320,320]{1,0:T(8,128)(2,1)}, u32[]{:S(2)}) copy-start(bf16[320,320]{1,0:T(8,128)(2,1)} %wq_ref.1) | copy-start | bytes 614404
  24.2 9.7 %collective-permute-start.6 = (bf16[1,800,128]{2,1,0:T(8,128)(2,1)S(1)}, bf16[1,800,128]{2,1,0:T(8,128)(2,1)S(1)}, u32[]{:S(2)}, u32[]{:S(2)}) collective-permute-start(bf16[1,800,128]{2,1,0:T(8,128)(2,1)S(1)} %shard_map.113), channel_id=1, source_target_pairs={{0,4},{4,8},{8,12},{12,0},{1,5},{5,9},{9,13},{13,1},{2,6},{6,10},{... | collective-permute-start | bytes 614408 | tf_op jit(solution)/shard_map/ppermute | solution.py:452
  24.3 17.7 %collective-permute-start.5 = (bf16[1,800,128]{2,1,0:T(8,128)(2,1)S(1)}, bf16[1,800,128]{2,1,0:T(8,128)(2,1)S(1)}, u32[]{:S(2)}, u32[]{:S(2)}) collective-permute-start(bf16[1,800,128]{2,1,0:T(8,128)(2,1)S(1)} %shard_map.113), channel_id=1, source_target_pairs={{0,8},{4,12},{8,0},{12,4},{1,9},{5,13},{9,1},{13,5},{2,10},{6,14},... | collective-permute-start | bytes 614408 | tf_op jit(solution)/shard_map/ppermute | solution.py:452
  25.6 17.7 %collective-permute-start.4 = (bf16[1,800,128]{2,1,0:T(8,128)(2,1)S(1)}, bf16[1,800,128]{2,1,0:T(8,128)(2,1)S(1)}, u32[]{:S(2)}, u32[]{:S(2)}) collective-permute-start(bf16[1,800,128]{2,1,0:T(8,128)(2,1)S(1)} %shard_map.113), channel_id=1, source_target_pairs={{0,12},{4,0},{8,4},{12,8},{1,13},{5,1},{9,5},{13,9},{2,14},{6,2},{... | collective-permute-start | bytes 614408 | tf_op jit(solution)/shard_map/ppermute | solution.py:452
  42.0 1.3 %copy-start.5 = (bf16[320,320]{1,0:T(8,128)(2,1)S(1)}, bf16[320,320]{1,0:T(8,128)(2,1)}, u32[]{:S(2)}) copy-start(bf16[320,320]{1,0:T(8,128)(2,1)} %wo_ref.1) | copy-start | bytes 614404

commit v2 on v1

--- a/solution.py
+++ b/solution.py
@@ -3,6 +3,7 @@
 
 import jax
 import jax.numpy as jnp
+import numpy as np
 from jax import lax
 from jax.experimental import pallas as pl
 from jax.experimental.pallas import tpu as pltpu
@@ -75,11 +76,17 @@
 
 
 def columns(h, width):
-    cells = h.shape[0]
-    place = lax.rem(lax.broadcasted_iota(jnp.int32, h.shape, 0), width)
-    left = jnp.where(place == 0, 0.0, pltpu.roll(h, 1, 0))
-    right = jnp.where(place == width - 1, 0.0, pltpu.roll(h, cells - 1, 0))
-    return jnp.concatenate([left.astype(BF), h.astype(BF), right.astype(BF)], axis=1)
+    cells, channels = h.shape
+    left = pltpu.roll(h, 1, 0)
+    right = pltpu.roll(h, cells - 1, 0)
+    place = lax.broadcasted_iota(jnp.int32, (8, channels), 0)
+    lefts, rights = [], []
+    for lo in range(0, cells, width):
+        hi = lo + width
+        lefts += [jnp.where(place == 0, 0.0, left[lo : lo + 8]), left[lo + 8 : hi]]
+        rights += [right[lo : hi - 8], jnp.where(place == 7, 0.0, right[hi - 8 : hi])]
+    sides = [jnp.concatenate(lefts, axis=0), h, jnp.concatenate(rights, axis=0)]
+    return jnp.concatenate([v.astype(BF) for v in sides], axis=1)
 
 
 def scalar(ref, n):
@@ -250,27 +257,31 @@
     keyval_ref[...] = dot(normed, wkv_ref[...]).astype(BF).reshape(frames, cells, 2 * channels)
 
 
-def lane_map(shape, channel_dim, count, channels, value, everywhere=False):
+def head_maps(count, channels, everywhere=False):
     full = channels // LANES * LANES
     rest = channels - full
-    c = lax.broadcasted_iota(jnp.int32, shape, channel_dim)
-    lane = lax.broadcasted_iota(jnp.int32, shape, 1 - channel_dim)
     stride = LANES // 4
-    wide = c < count * full
-    source = jnp.where(wide, lax.div(c, full), lax.div(c - count * full, max(rest, 1)))
-    channel = jnp.where(
-        wide, lax.rem(c, full), full + lax.rem(jnp.maximum(c - count * full, 0), max(rest, 1))
-    )
-    head = lax.div(channel, HEAD_DIM)
-    if everywhere:
-        hit = lax.rem(lane, stride) == head
-    else:
-        hit = lane == source * stride + head
-    return jnp.where(hit, value, 0.0).astype(BF)
+    hits = np.zeros((count * channels, LANES), np.float32)
+    for j in range(count):
+        for c in range(channels):
+            at = j * full + c if c < full else count * full + j * rest + c - full
+            lanes = range(0, LANES, stride) if everywhere else (j * stride,)
+            for lane in lanes:
+                hits[at, lane + c // HEAD_DIM] = 1.0
+    padded = np.zeros((-(-hits.shape[0] // LANES) * LANES, LANES), np.float32)
+    padded[: hits.shape[0]] = hits
+    blocks = padded.reshape(-1, LANES, LANES).transpose(0, 2, 1).reshape(-1, LANES)
+    return jnp.asarray(hits / math.sqrt(HEAD_DIM), BF), jnp.asarray(blocks, BF)
+
+
+def beside(ref):
+    count = ref.shape[0] // LANES
+    return jnp.concatenate([ref[b * LANES : (b + 1) * LANES] for b in range(count)], axis=1)
 
 
 def local_kernel(
-    picks_ref, window_ref, query_ref, keyval_ref, top_ref, sum_ref, mix_ref,
+    picks_ref, window_ref, query_ref, keyval_ref, to_lanes_ref, to_channels_ref,
+    top_ref, sum_ref, mix_ref,
 ):
     frames, cells, channels = query_ref.shape
     count = picks_ref.shape[1]
@@ -289,11 +300,7 @@
         again = jnp.concatenate([q[:, full:]] * frames, axis=1)
         row = [q[:, :full] * k for k in keys[:frames]] + [again * keys[frames]]
         products.append(jnp.concatenate(row, axis=1))
-    to_lanes = lane_map(
-        (frames * channels, LANES), 0, frames, channels, 1.0 / math.sqrt(HEAD_DIM)
-    )
-    to_channels = lane_map((LANES, frames * channels), 1, frames, channels, 1.0)
-    scores = dot(jnp.concatenate(products, axis=0), to_lanes)
+    scores = dot(jnp.concatenate(products, axis=0), to_lanes_ref[...])
     source = lax.div(lax.broadcasted_iota(jnp.int32, (1, LANES), 1), stride)
     window = window_ref[...].reshape(1, 1)
     copies = jnp.zeros((1, LANES), F32)
@@ -311,7 +318,7 @@
         top_ref[i] = top
         sum_ref[i] = total
         weights.append(w.astype(BF))
-    spread = dot(jnp.concatenate(weights, axis=0), to_channels)
+    spread = dot(jnp.concatenate(weights, axis=0), beside(to_channels_ref))
     for i in range(frames):
         part = spread[i * cells : (i + 1) * cells]
         wide = part[:, :full] * values[0]
@@ -323,7 +330,9 @@
         mix_ref[i] = jnp.concatenate([wide, tail], axis=1)
 
 
-def updated(anchor_ref, wkv_ref, query_ref, top_ref, sum_ref, mix_ref, last):
+def updated(
+    anchor_ref, wkv_ref, to_lanes_ref, to_channels_ref, query_ref, top_ref, sum_ref, mix_ref, last
+):
     frames, cells, channels = query_ref.shape
     full = channels // LANES * LANES
     count = anchor_ref.shape[0]
@@ -331,15 +340,11 @@
     size = frames * cells
     top, total, mix = (v.reshape(size, v.shape[-1]) for v in state)
     query = query_ref[...].reshape(size, channels)
-    to_lanes = lane_map(
-        (channels, LANES), 0, 1, channels, 1.0 / math.sqrt(HEAD_DIM), everywhere=True
-    )
-    to_channels = lane_map((LANES, 2 * channels), 1, 2, channels, 1.0)
     low = lax.broadcasted_iota(jnp.int32, (1, LANES), 1) < LANES // 4
     for n in range(count):
         keyval = dot(unpacked(anchor_ref[n], channels), wkv_ref[...]).astype(BF)
         key = jnp.concatenate([keyval[:, :channels]] * frames, axis=0)
-        scores = dot(query * key, to_lanes)
+        scores = dot(query * key, to_lanes_ref[...])
         higher = jnp.maximum(top, scores)
         weight = jnp.exp(scores - higher)
         fade = jnp.exp(top - higher)
@@ -347,7 +352,7 @@
         both = jnp.where(low, weight, fade)
         if last and n == count - 1:
             both = both / total
-        spread = dot(both.astype(BF), to_channels)
+        spread = dot(both.astype(BF), beside(to_channels_ref))
         value = keyval[:, channels:].astype(F32)
         value = jnp.concatenate([value] * frames, axis=0)
         wide = spread[:, :full] * value[:, :full] + spread[:, full : 2 * full] * mix[:, :full]
@@ -360,20 +365,25 @@
 
 
 def anchor_kernel(
-    anchor_ref, wkv_ref, query_ref, top_ref, sum_ref, mix_ref, top_out, sum_out, mix_out
-):
-    new = updated(anchor_ref, wkv_ref, query_ref, top_ref, sum_ref, mix_ref, False)
+    anchor_ref, wkv_ref, to_lanes_ref, to_channels_ref, query_ref, top_ref, sum_ref, mix_ref,
+    top_out, sum_out, mix_out,
+):
+    new = updated(
+        anchor_ref, wkv_ref, to_lanes_ref, to_channels_ref, query_ref, top_ref, sum_ref, mix_ref, False
+    )
     for ref, v in zip((top_out, sum_out, mix_out), new):
         ref[...] = v.reshape(ref.shape)
 
 
 def last_kernel(
-    anchor_ref, wkv_ref, query_ref, top_ref, sum_ref, mix_ref, temporal_ref, wo_ref,
-    out_ref, out_buf, sems,
+    anchor_ref, wkv_ref, to_lanes_ref, to_channels_ref, query_ref, top_ref, sum_ref, mix_ref,
+    temporal_ref, wo_ref, out_ref, out_buf, sems,
 ):
     frames, cells, channels = query_ref.shape
     height, width = out_ref.shape[1:3]
-    _, _, mix = updated(anchor_ref, wkv_ref, query_ref, top_ref, sum_ref, mix_ref, True)
+    _, _, mix = updated(
+        anchor_ref, wkv_ref, to_lanes_ref, to_channels_ref, query_ref, top_ref, sum_ref, mix_ref, True
+    )
     attended = mix[:, :channels].astype(BF)
     result = dot(attended, wo_ref[...])
     copies = []
@@ -461,21 +471,23 @@
     )(before, after, spatial, hidden, g3, temporal_w, w_query, w_keyval)
     states = [((frames, cells, LANES), F32)] * 2 + [((frames, cells, lanes_up), F32)]
     state = call(
-        local_kernel, states, [VMEM] * 4, flops=10 * frames * cells * one, limit=32
-    )(anchor_index, window, query, keyval)
+        local_kernel, states, [VMEM] * 6, flops=10 * frames * cells * one, limit=32
+    )(anchor_index, window, query, keyval, *head_maps(frames, channels))
+    to_lanes, _ = head_maps(1, channels, everywhere=True)
+    _, to_channels = head_maps(2, channels)
     for arrival in arrived[:-1]:
         state = call(
-            anchor_kernel, states, [VMEM] * 6, flops=4 * frames * cells * one, limit=32
-        )(arrival, w_keyval, query, *state)
+            anchor_kernel, states, [VMEM] * 8, flops=4 * frames * cells * one, limit=32
+        )(arrival, w_keyval, to_lanes, to_channels, query, *state)
     (out,) = call(
         last_kernel,
         [(latents.shape, BF)],
-        [VMEM] * 8,
+        [VMEM] * 10,
         [pltpu.VMEM(latents.shape, BF), sem((frames,))],
         flops=5 * frames * cells * one,
         limit=32,
         out_specs=(HBM,),
-    )(arrived[-1], w_keyval, query, *state, temporal, w_out)
+    )(arrived[-1], w_keyval, to_lanes, to_channels, query, *state, temporal, w_out)
     return out
 
 

time: 46.5 us -> 46.5 us (level)
  the two profiles are of different devices: /device:TPU:25 before, /device:TPU:29 now
where the time goes in v2:
time: 46.5 us; the launch traced here: 46.3 us
  Pallas kernels  22.2 us (48%)
  starting transfers between devices  12.5 us (27%)
  waiting for transfers between devices  8.51 us (18%)
  between operations  1.74 us (4%)
  local copies, waits for them, and re-layouts  1.42 us (3%)
    ppermute x4, starting transfers between devices, neighbours(): return (lax.ppermute(last, axis, up), lax.ppermute(leading, axis, down))  10.9 us
    ppermute x3, waiting for transfers between devices, on_device(): lax.ppermute(chosen, 'clip', [(i, (i + s) % clips) for i in range(clips)])  6.71 us
    pallas_call x1, Pallas kernels, on_device(): call(temporal_kernel, [(some, BF), (some, BF), ((frames, cells, 2 * chann...  4.21 us
    pallas_call x1, Pallas kernels, on_device(): call(local_kernel, states, [VMEM] * 6, flops=10 * frames * cells * one, l...  3.91 us
    pallas_call x1, Pallas kernels, on_device(): call(inner_kernel, [(some, BF), (some, BF)], [VMEM] * 9, [inner_col], flo...  3.67 us
    pallas_call x1, Pallas kernels, on_device(): call(outer_kernel, [(middle, BF), (middle, BF), ((2, 2, width, channels),...  2.87 us
    pallas_call x1, Pallas kernels, on_device(): call(last_kernel, [(latents.shape, BF)], [VMEM] * 10, [pltpu.VMEM(latents...  2.78 us
    pallas_call x2, Pallas kernels, on_device(): call(anchor_kernel, states, [VMEM] * 8, flops=4 * frames * cells * one, l...  2.6 us
  transfers between devices with their start and end apart: 7, of which 2 were waited for; matrix products, arithmetic and copies ran while one was open for 0% of the time, Pallas kernels for 37%

profile of v2, /device:TPU:29, one launch (start us, length us, event | category | flops | bytes accessed | tf_op | source)
XLA Modules:
  0.0 46.3 jit_solution(4291274479010077024)
XLA Ops:
  0.0 0.0 copy-start
  0.0 0.0 copy-start.3
  0.0 1.3 %copy-done.3 = bf16[4,5,64,320]{3,2,1,0:T(8,128)(2,1)S(1)} copy-done((bf16[4,5,64,320]{3,2,1,0:T(8,128)(2,1)S(1)}, bf16[4,5,64,320]{3,2,1,0:T(8,128)(2,1)}, u32[]{:S(2)}) %copy-start.3) | copy-done | bytes 819224
  1.4 0.1 shard_map.146
  1.4 3.7 %collective-permute-start = (bf16[640,128]{1,0:T(8,128)(2,1)S(1)}, bf16[640,128]{1,0:T(8,128)(2,1)S(1)}, u32[]{:S(2)}, u32[]{:S(2)}) collective-permute-start(bf16[640,128]{1,0:T(8,128)(2,1)S(1)} %get-tuple-element.31), channel_id=1, source_target_pairs={{0,1},{1,2},{2,3},{4,5},{5,6},{6,7},{8,9},{9,10},{10,11},{12,13},{... | collective-permute-start | bytes 491528 | tf_op jit(solution)/shard_map/ppermute | solution.py:403
  5.1 1.9 %collective-permute-start.1 = (bf16[640,128]{1,0:T(8,128)(2,1)S(1)}, bf16[640,128]{1,0:T(8,128)(2,1)S(1)}, u32[]{:S(2)}, u32[]{:S(2)}) collective-permute-start(bf16[640,128]{1,0:T(8,128)(2,1)S(1)} %get-tuple-element.32), channel_id=1, source_target_pairs={{1,0},{2,1},{3,2},{5,4},{6,5},{7,6},{9,8},{10,9},{11,10},{13,12},{... | collective-permute-start | bytes 491528 | tf_op jit(solution)/shard_map/ppermute | solution.py:403
  7.1 0.0 copy-done
  7.1 0.0 copy-done.8
  7.1 0.0 copy-done.9
  7.1 2.9 %shard_map.145 = (bf16[2,192,320]{2,1,0:T(8,128)(2,1)S(1)}, bf16[2,192,320]{2,1,0:T(8,128)(2,1)S(1)}, f32[2,2,64,320]{3,2,1,0:T(8,128)S(1)}, bf16[960,192]{1,0:T(8,128)(2,1)S(1)}, f32[8,128]{1,0:T(8,128)S(1)}) custom-call(bf16[4,5,64,320]{3,2,1,0:T(8,128)(2,1)S(1)} %copy-done.3, f32[320]{0:T(512)S(1)} %copy-done.8, f32[320]{0:T(512)S(1)} %copy-done.9, ...), custom_call_target="tpu_custom_call" | custom-call | flops 1179648000 | bytes 2097152 | tf_op jit(solution)/shard_map/pallas_call | solution.py:430
  10.0 0.0 collective-permute-done.above_ref
  10.0 1.8 %collective-permute-done.1.below_ref = bf16[640,128]{1,0:T(8,128)(2,1)S(1)} collective-permute-done((bf16[640,128]{1,0:T(8,128)(2,1)S(1)}, bf16[640,128]{1,0:T(8,128)(2,1)S(1)}, u32[]{:S(2)}, u32[]{:S(2)}) %collective-permute-start.1) | collective-permute-done | bytes 163872 | tf_op jit(solution)/shard_map/ppermute | solution.py:403
  11.8 1.1 %shard_map.147 = (bf16[2,320,320]{2,1,0:T(8,128)(2,1)S(1)}, bf16[2,320,320]{2,1,0:T(8,128)(2,1)S(1)}, bf16[800,128]{1,0:T(8,128)(2,1)S(1)}, bf16[800,128]{1,0:T(8,128)(2,1)S(1)}) custom-call(f32[2,2,64,320]{3,2,1,0:T(8,128)S(1)} %get-tuple-element.30.edge_ref, bf16[640,128]{1,0:T(8,128)(2,1)S(1)} %collective-permute-done.above_ref, ...), custom_call_target="tpu_custom_call" | custom-call | flops 157286400 | bytes 2097152 | tf_op jit(solution)/shard_map/pallas_call | solution.py:443
  12.9 1.3 %collective-permute-start.2 = (bf16[800,128]{1,0:T(8,128)(2,1)S(1)}, bf16[800,128]{1,0:T(8,128)(2,1)S(1)}, u32[]{:S(2)}, u32[]{:S(2)}) collective-permute-start(bf16[800,128]{1,0:T(8,128)(2,1)S(1)} %get-tuple-element.37), channel_id=1, source_target_pairs={{0,4},{4,8},{8,12},{1,5},{5,9},{9,13},{2,6},{6,10},{10,14},{3,7},{... | collective-permute-start | bytes 614408 | tf_op jit(solution)/shard_map/ppermute | solution.py:403
  14.2 4.0 %collective-permute-start.3 = (bf16[800,128]{1,0:T(8,128)(2,1)S(1)}, bf16[800,128]{1,0:T(8,128)(2,1)S(1)}, u32[]{:S(2)}, u32[]{:S(2)}) collective-permute-start(bf16[800,128]{1,0:T(8,128)(2,1)S(1)} %get-tuple-element.38), channel_id=1, source_target_pairs={{4,0},{8,4},{12,8},{5,1},{9,5},{13,9},{6,2},{10,6},{14,10},{7,3},{... | collective-permute-start | bytes 614408 | tf_op jit(solution)/shard_map/ppermute | solution.py:403
  19.5 0.0 copy-done.4
  19.5 0.0 copy-start.5
  19.5 0.0 copy-start.10
  19.5 3.7 %shard_map.148 = (bf16[4,320,320]{2,1,0:T(8,128)(2,1)S(1)}, bf16[4,320,320]{2,1,0:T(8,128)(2,1)S(1)}) custom-call(bf16[4,5,64,320]{3,2,1,0:T(8,128)(2,1)S(1)} %copy-done.4, bf16[640,128]{1,0:T(8,128)(2,1)S(1)} %collective-permute-done.above_ref, bf16[640,128]{1,0:T(8,128)(2,1)S(1)} %collective-permute-done.1.below_ref, f32[320]{0:T(512)S(1)} %copy-done.8, ...), custom_call_target="tpu_custom_call" | custom-call | flops 1179648000 | bytes 2097152 | tf_op jit(solution)/shard_map/pallas_call | solution.py:450
  23.2 0.0 copy-start.1
  23.2 0.0 copy-start.11
  23.2 0.0 collective-permute-done.2.before_ref
  23.2 0.0 collective-permute-done.3.after_ref
  23.2 0.0 copy-done.5
  23.3 0.0 copy-done.10
  23.3 0.9 %shard_map.149 = bf16[1,800,128]{2,1,0:T(8,128)(2,1)S(1)} custom-call(s32[1,1]{1,0:T(1,128)S(6)} %copy.16.picks_ref, bf16[800,128]{1,0:T(8,128)(2,1)S(1)} %collective-permute-done.2.before_ref, bf16[800,128]{1,0:T(8,128)(2,1)S(1)} %collective-permute-done.3.after_ref, bf16[4,320,320]{2,1,0:T(8,128)(2,1)S(1)} %get-tuple-element.41.spatial_ref, ...), custom_call_target="tpu_custom_call" | custom-call | flops 196608000 | bytes 2097152 | tf_op jit(solution)/shard_map/pallas_call | solution.py:457
  24.2 0.0 copy-start.12
  24.2 0.0 copy-start.13
  24.2 0.1 collective-permute-start.6
  24.3 1.3 %collective-permute-start.5 = (bf16[1,800,128]{2,1,0:T(8,128)(2,1)S(1)}, bf16[1,800,128]{2,1,0:T(8,128)(2,1)S(1)}, u32[]{:S(2)}, u32[]{:S(2)}) collective-permute-start(bf16[1,800,128]{2,1,0:T(8,128)(2,1)S(1)} %shard_map.149), channel_id=1, source_target_pairs={{0,8},{4,12},{8,0},{12,4},{1,9},{5,13},{9,1},{13,5},{2,10},{6,14},... | collective-permute-start | bytes 614408 | tf_op jit(solution)/shard_map/ppermute | solution.py:462
  25.6 0.2 collective-permute-start.4
  25.8 0.0 copy-done.1
  25.8 0.0 copy-done.11
  25.8 4.2 %shard_map.150 = (bf16[4,320,320]{2,1,0:T(8,128)(2,1)S(1)}, bf16[4,320,320]{2,1,0:T(8,128)(2,1)S(1)}, bf16[4,320,640]{2,1,0:T(8,128)(2,1)S(1)}) custom-call(bf16[800,128]{1,0:T(8,128)(2,1)S(1)} %collective-permute-done.2.before_ref, bf16[800,128]{1,0:T(8,128)(2,1)S(1)} %collective-permute-done.3.after_ref, ...), custom_call_target="tpu_custom_call" | custom-call | flops 1572864000 | bytes 2097152 | tf_op jit(solution)/shard_map/pallas_call | solution.py:465
  30.0 0.0 copy-done.12
  30.0 0.0 copy-done.13
  30.0 0.0 copy-start.2
  30.1 0.0 copy-start.6
  30.1 3.9 %shard_map.151 = (f32[4,320,128]{2,1,0:T(8,128)S(1)}, f32[4,320,128]{2,1,0:T(8,128)S(1)}, f32[4,320,384]{2,1,0:T(8,128)S(1)}) custom-call(s32[1,1]{1,0:T(1,128)S(6)} %copy.16.picks_ref, s32[1]{0:T(128)S(6)} %copy.17.window_ref, bf16[4,320,320]{2,1,0:T(8,128)(2,1)S(1)} %get-tuple-element.43.query_ref, bf16[4,320,640]{2,1,0:T(8,128)(2,1)S(1)} %get-tuple-element.44.keyval_ref, ...), custom_call_target="tpu_custom_call" | custom-call | flops 2621440000 | bytes 2097152 | tf_op jit(solution)/shard_map/pallas_call | solution.py:473
  34.0 0.0 collective-permute-done.6.anchor_ref
  34.0 0.0 copy-done.2
  34.0 0.0 copy-done.6
  34.0 1.3 %shard_map.152 = (f32[4,320,128]{2,1,0:T(8,128)S(1)}, f32[4,320,128]{2,1,0:T(8,128)S(1)}, f32[4,320,384]{2,1,0:T(8,128)S(1)}) custom-call(bf16[1,800,128]{2,1,0:T(8,128)(2,1)S(1)} %collective-permute-done.6.anchor_ref, bf16[320,640]{1,0:T(8,128)(2,1)S(1)} %copy-done.1, bf16[320,128]{1,0:T(8,128)(2,1)S(1)} %copy-done.6, bf16[640,128]{1,0:T(8,128)(2,1)S(1)} %copy-done.2, ...), custom_call_target="tpu_custom_call" | custom-call | flops 1048576000 | bytes 2097152 | tf_op jit(solution)/shard_map/pallas_call | solution.py:479
  35.3 6.7 %collective-permute-done.5.anchor_ref = bf16[1,800,128]{2,1,0:T(8,128)(2,1)S(1)} collective-permute-done((bf16[1,800,128]{2,1,0:T(8,128)(2,1)S(1)}, bf16[1,800,128]{2,1,0:T(8,128)(2,1)S(1)}, u32[]{:S(2)}, u32[]{:S(2)}) %collective-permute-start.5) | collective-permute-done | bytes 204832 | tf_op jit(solution)/shard_map/ppermute | solution.py:462
  42.0 1.3 %shard_map.153 = (f32[4,320,128]{2,1,0:T(8,128)S(1)}, f32[4,320,128]{2,1,0:T(8,128)S(1)}, f32[4,320,384]{2,1,0:T(8,128)S(1)}) custom-call(bf16[1,800,128]{2,1,0:T(8,128)(2,1)S(1)} %collective-permute-done.5.anchor_ref, bf16[320,640]{1,0:T(8,128)(2,1)S(1)} %copy-done.1, bf16[320,128]{1,0:T(8,128)(2,1)S(1)} %copy-done.6, bf16[640,128]{1,0:T(8,128)(2,1)S(1)} %copy-done.2, ...), custom_call_target="tpu_custom_call" | custom-call | flops 1048576000 | bytes 2097152 | tf_op jit(solution)/shard_map/pallas_call | solution.py:479
  43.3 0.0 collective-permute-done.4.anchor_ref
  43.3 0.0 copy-done.7
  43.3 2.8 %shard_map.154 = bf16[4,5,64,320]{3,2,1,0:T(8,128)(2,1)} custom-call(bf16[1,800,128]{2,1,0:T(8,128)(2,1)S(1)} %collective-permute-done.4.anchor_ref, bf16[320,640]{1,0:T(8,128)(2,1)S(1)} %copy-done.1, bf16[320,128]{1,0:T(8,128)(2,1)S(1)} %copy-done.6, bf16[640,128]{1,0:T(8,128)(2,1)S(1)} %copy-done.2, bf16[4,320,320]{2,1,0:T(8,128)(2,1)S(1)} %get-tuple-element.43.query_ref, ...), custom_call_target="tpu_custom_call" | custom-call | flops 1310720000 | bytes 2097152 | tf_op jit(solution)/shard_map/pallas_call | solution.py:482
  (4 shorter events, 0.0 us)
Async XLA Ops:
  0.0 7.1 %copy-start = (bf16[3,3,320,320]{3,2,1,0:T(8,128)(2,1)S(1)}, bf16[3,3,320,320]{3,2,1,0:T(8,128)(2,1)}, u32[]{:S(2)}) copy-start(bf16[3,3,320,320]{3,2,1,0:T(8,128)(2,1)} %param.19) | copy-start | bytes 5529604
  0.0 1.4 %copy-start.3 = (bf16[4,5,64,320]{3,2,1,0:T(8,128)(2,1)S(1)}, bf16[4,5,64,320]{3,2,1,0:T(8,128)(2,1)}, u32[]{:S(2)}) copy-start(bf16[4,5,64,320]{3,2,1,0:T(8,128)(2,1)} %x_ref.5) | copy-start | bytes 2457604
  1.4 5.7 %copy-start.8 = (f32[320]{0:T(512)S(1)}, f32[320]{0:T(512)}, u32[]{:S(2)}) copy-start(f32[320]{0:T(512)} %g1_ref.5) | copy-start | bytes 3844
  1.4 5.7 %copy-start.9 = (f32[320]{0:T(512)S(1)}, f32[320]{0:T(512)}, u32[]{:S(2)}) copy-start(f32[320]{0:T(512)} %g2_ref.5) | copy-start | bytes 3844
  1.4 8.5 %collective-permute-start = (bf16[640,128]{1,0:T(8,128)(2,1)S(1)}, bf16[640,128]{1,0:T(8,128)(2,1)S(1)}, u32[]{:S(2)}, u32[]{:S(2)}) collective-permute-start(bf16[640,128]{1,0:T(8,128)(2,1)S(1)} %get-tuple-element.31), channel_id=1, source_target_pairs={{0,1},{1,2},{2,3},{4,5},{5,6},{6,7},{8,9},{9,10},{10,11},{12,13},{... | collective-permute-start | bytes 491528 | tf_op jit(solution)/shard_map/ppermute | solution.py:403
  5.1 6.6 %collective-permute-start.1 = (bf16[640,128]{1,0:T(8,128)(2,1)S(1)}, bf16[640,128]{1,0:T(8,128)(2,1)S(1)}, u32[]{:S(2)}, u32[]{:S(2)}) collective-permute-start(bf16[640,128]{1,0:T(8,128)(2,1)S(1)} %get-tuple-element.32), channel_id=1, source_target_pairs={{1,0},{2,1},{3,2},{5,4},{6,5},{7,6},{9,8},{10,9},{11,10},{13,12},{... | collective-permute-start | bytes 491528 | tf_op jit(solution)/shard_map/ppermute | solution.py:403
  11.8 7.7 %copy-start.4 = (bf16[4,5,64,320]{3,2,1,0:T(8,128)(2,1)S(1)}, bf16[4,5,64,320]{3,2,1,0:T(8,128)(2,1)}, u32[]{:S(2)}) copy-start(bf16[4,5,64,320]{3,2,1,0:T(8,128)(2,1)} %x_ref.5) | copy-start | bytes 2457604
  12.9 10.3 %collective-permute-start.2 = (bf16[800,128]{1,0:T(8,128)(2,1)S(1)}, bf16[800,128]{1,0:T(8,128)(2,1)S(1)}, u32[]{:S(2)}, u32[]{:S(2)}) collective-permute-start(bf16[800,128]{1,0:T(8,128)(2,1)S(1)} %get-tuple-element.37), channel_id=1, source_target_pairs={{0,4},{4,8},{8,12},{1,5},{5,9},{9,13},{2,6},{6,10},{10,14},{3,7},{... | collective-permute-start | bytes 614408 | tf_op jit(solution)/shard_map/ppermute | solution.py:403
  14.2 9.1 %collective-permute-start.3 = (bf16[800,128]{1,0:T(8,128)(2,1)S(1)}, bf16[800,128]{1,0:T(8,128)(2,1)S(1)}, u32[]{:S(2)}, u32[]{:S(2)}) collective-permute-start(bf16[800,128]{1,0:T(8,128)(2,1)S(1)} %get-tuple-element.38), channel_id=1, source_target_pairs={{4,0},{8,4},{12,8},{5,1},{9,5},{13,9},{6,2},{10,6},{14,10},{7,3},{... | collective-permute-start | bytes 614408 | tf_op jit(solution)/shard_map/ppermute | solution.py:403
  19.5 3.8 %copy-start.5 = (bf16[3,320,320]{2,1,0:T(8,128)(2,1)S(1)}, bf16[3,320,320]{2,1,0:T(8,128)(2,1)}, u32[]{:S(2)}) copy-start(bf16[3,320,320]{2,1,0:T(8,128)(2,1)} %wt_ref.3) | copy-start | bytes 1843204
  19.5 3.8 %copy-start.10 = (f32[320]{0:T(512)S(1)}, f32[320]{0:T(512)}, u32[]{:S(2)}) copy-start(f32[320]{0:T(512)} %g3_ref.3) | copy-start | bytes 3844
  23.2 2.6 %copy-start.1 = (bf16[320,640]{1,0:T(8,128)(2,1)S(1)}, bf16[320,640]{1,0:T(8,128)(2,1)}, u32[]{:S(2)}) copy-start(bf16[320,640]{1,0:T(8,128)(2,1)} %wkv_ref.7) | copy-start | bytes 1228804
  23.2 2.6 %copy-start.11 = (bf16[320,320]{1,0:T(8,128)(2,1)S(1)}, bf16[320,320]{1,0:T(8,128)(2,1)}, u32[]{:S(2)}) copy-start(bf16[320,320]{1,0:T(8,128)(2,1)} %wq_ref.1) | copy-start | bytes 614404
  24.2 5.8 %copy-start.12 = (bf16[1280,128]{1,0:T(8,128)(2,1)S(1)}, bf16[1280,128]{1,0:T(8,128)(2,1)}, u32[]{:S(2)}) copy-start(bf16[1280,128]{1,0:T(8,128)(2,1)} %constant.9.clone.to_channels_ref) | copy-start | bytes 983044
  24.2 5.8 %copy-start.13 = (bf16[1280,128]{1,0:T(8,128)(2,1)S(1)}, bf16[1280,128]{1,0:T(8,128)(2,1)}, u32[]{:S(2)}) copy-start(bf16[1280,128]{1,0:T(8,128)(2,1)} %constant.8.clone.to_lanes_ref) | copy-start | bytes 983044
  24.2 9.8 %collective-permute-start.6 = (bf16[1,800,128]{2,1,0:T(8,128)(2,1)S(1)}, bf16[1,800,128]{2,1,0:T(8,128)(2,1)S(1)}, u32[]{:S(2)}, u32[]{:S(2)}) collective-permute-start(bf16[1,800,128]{2,1,0:T(8,128)(2,1)S(1)} %shard_map.149), channel_id=1, source_target_pairs={{0,4},{4,8},{8,12},{12,0},{1,5},{5,9},{9,13},{13,1},{2,6},{6,10},{... | collective-permute-start | bytes 614408 | tf_op jit(solution)/shard_map/ppermute | solution.py:462
  24.3 17.7 %collective-permute-start.5 = (bf16[1,800,128]{2,1,0:T(8,128)(2,1)S(1)}, bf16[1,800,128]{2,1,0:T(8,128)(2,1)S(1)}, u32[]{:S(2)}, u32[]{:S(2)}) collective-permute-start(bf16[1,800,128]{2,1,0:T(8,128)(2,1)S(1)} %shard_map.149), channel_id=1, source_target_pairs={{0,8},{4,12},{8,0},{12,4},{1,9},{5,13},{9,1},{13,5},{2,10},{6,14},... | collective-permute-start | bytes 614408 | tf_op jit(solution)/shard_map/ppermute | solution.py:462
  25.6 17.7 %collective-permute-start.4 = (bf16[1,800,128]{2,1,0:T(8,128)(2,1)S(1)}, bf16[1,800,128]{2,1,0:T(8,128)(2,1)S(1)}, u32[]{:S(2)}, u32[]{:S(2)}) collective-permute-start(bf16[1,800,128]{2,1,0:T(8,128)(2,1)S(1)} %shard_map.149), channel_id=1, source_target_pairs={{0,12},{4,0},{8,4},{12,8},{1,13},{5,1},{9,5},{13,9},{2,14},{6,2},{... | collective-permute-start | bytes 614408 | tf_op jit(solution)/shard_map/ppermute | solution.py:462
  30.0 4.0 %copy-start.2 = (bf16[640,128]{1,0:T(8,128)(2,1)S(1)}, bf16[640,128]{1,0:T(8,128)(2,1)}, u32[]{:S(2)}) copy-start(bf16[640,128]{1,0:T(8,128)(2,1)} %constant.11.clone.to_channels_ref) | copy-start | bytes 491524
  30.1 4.0 %copy-start.6 = (bf16[320,128]{1,0:T(8,128)(2,1)S(1)}, bf16[320,128]{1,0:T(8,128)(2,1)}, u32[]{:S(2)}) copy-start(bf16[320,128]{1,0:T(8,128)(2,1)} %constant.10.clone.to_lanes_ref) | copy-start | bytes 245764
  42.0 1.3 %copy-start.7 = (bf16[320,320]{1,0:T(8,128)(2,1)S(1)}, bf16[320,320]{1,0:T(8,128)(2,1)}, u32[]{:S(2)}) copy-start(bf16[320,320]{1,0:T(8,128)(2,1)} %wo_ref.1) | copy-start | bytes 614404

commit v3 on v2

--- a/solution.py
+++ b/solution.py
@@ -364,9 +364,15 @@
     return top, total, mix
 
 
+def relay_kernel(from_below_ref, from_above_ref, out_ref, order_ref):
+    even = lax.rem(lax.axis_index("clip"), 2) == 0
+    out_ref[...] = jnp.where(even, from_below_ref[...], from_above_ref[...])
+    order_ref[...] = jnp.zeros_like(order_ref)
+
+
 def anchor_kernel(
     anchor_ref, wkv_ref, to_lanes_ref, to_channels_ref, query_ref, top_ref, sum_ref, mix_ref,
-    top_out, sum_out, mix_out,
+    order_ref, top_out, sum_out, mix_out,
 ):
     new = updated(
         anchor_ref, wkv_ref, to_lanes_ref, to_channels_ref, query_ref, top_ref, sum_ref, mix_ref, False
@@ -458,10 +464,20 @@
         chosen_kernel, [((count, packed, LANES), BF)], [VMEM] * 7, flops=3 * cells * one
     )(anchor_index, before, after, spatial, hidden, g3, temporal_w)
     clips = lax.axis_size("clip")
-    arrived = [
-        lax.ppermute(chosen, "clip", [(i, (i + s) % clips) for i in range(clips)])
-        for s in range(1, clips)
-    ]
+
+    def rotated(step):
+        return lax.ppermute(chosen, "clip", [(i, (i + step) % clips) for i in range(clips)])
+
+    if clips == 4:
+        arrived = [rotated(1), rotated(clips - 1)]
+        relayed, anchors_order = call(
+            relay_kernel, [(chosen.shape, BF), ((8, LANES), F32)], [VMEM] * 2
+        )(*arrived)
+        pairs = [(i, i + 1 - 2 * (i % 2)) for i in range(clips)]
+        arrived.append(lax.ppermute(relayed, "clip", pairs))
+    else:
+        arrived = [rotated(s) for s in range(1, clips)]
+        anchors_order = order
     temporal, query, keyval = call(
         temporal_kernel,
         [(some, BF), (some, BF), ((frames, cells, 2 * channels), BF)],
@@ -477,8 +493,8 @@
     _, to_channels = head_maps(2, channels)
     for arrival in arrived[:-1]:
         state = call(
-            anchor_kernel, states, [VMEM] * 8, flops=4 * frames * cells * one, limit=32
-        )(arrival, w_keyval, to_lanes, to_channels, query, *state)
+            anchor_kernel, states, [VMEM] * 9, flops=4 * frames * cells * one, limit=32
+        )(arrival, w_keyval, to_lanes, to_channels, query, *state, anchors_order)
     (out,) = call(
         last_kernel,
         [(latents.shape, BF)],

time: 46.5 us -> 46.7 us (level)
  the two profiles are of different devices: /device:TPU:29 before, /device:TPU:0 now
where the time goes in v3:
time: 46.7 us; the launch traced here: 46.1 us
  Pallas kernels  22.2 us (48%)
  starting transfers between devices  11.3 us (24%)
  waiting for transfers between devices  9.38 us (20%)
  between operations  1.73 us (4%)
  local copies, waits for them, and re-layouts  1.42 us (3%)
    ppermute x4, starting transfers between devices, neighbours(): return (lax.ppermute(last, axis, up), lax.ppermute(leading, axis, down))  8.44 us
    ppermute x2, waiting for transfers between devices, rotated(): lax.ppermute(chosen, 'clip', [(i, (i + step) % clips) for i in range(clip...  5.18 us
    pallas_call x1, Pallas kernels, on_device(): call(temporal_kernel, [(some, BF), (some, BF), ((frames, cells, 2 * chann...  4.21 us
    pallas_call x1, Pallas kernels, on_device(): call(local_kernel, states, [VMEM] * 6, flops=10 * frames * cells * one, l...  3.91 us
    pallas_call x1, Pallas kernels, on_device(): call(inner_kernel, [(some, BF), (some, BF)], [VMEM] * 9, [inner_col], flo...  3.67 us
    ppermute x4, waiting for transfers between devices, neighbours(): return (lax.ppermute(last, axis, up), lax.ppermute(leading, axis, down))  3.13 us
    pallas_call x1, Pallas kernels, on_device(): call(outer_kernel, [(middle, BF), (middle, BF), ((2, 2, width, channels),...  2.87 us
    ppermute x2, starting transfers between devices, rotated(): lax.ppermute(chosen, 'clip', [(i, (i + step) % clips) for i in range(clip...  2.8 us
  transfers between devices with their start and end apart: 7, of which 4 were waited for; matrix products, arithmetic and copies ran while one was open for 0% of the time, Pallas kernels for 37%

profile of v3, /device:TPU:0, one launch (start us, length us, event | category | flops | bytes accessed | tf_op | source)
XLA Modules:
  0.0 46.1 jit_solution(289175968365002763)
XLA Ops:
  0.0 1.3 %copy-done.3 = bf16[4,5,64,320]{3,2,1,0:T(8,128)(2,1)S(1)} copy-done((bf16[4,5,64,320]{3,2,1,0:T(8,128)(2,1)S(1)}, bf16[4,5,64,320]{3,2,1,0:T(8,128)(2,1)}, u32[]{:S(2)}) %copy-start.3) | copy-done | bytes 819224
  1.4 0.1 shard_map.146
  1.4 2.4 %collective-permute-start = (bf16[640,128]{1,0:T(8,128)(2,1)S(1)}, bf16[640,128]{1,0:T(8,128)(2,1)S(1)}, u32[]{:S(2)}, u32[]{:S(2)}) collective-permute-start(bf16[640,128]{1,0:T(8,128)(2,1)S(1)} %get-tuple-element.33), channel_id=1, source_target_pairs={{0,1},{1,2},{2,3},{4,5},{5,6},{6,7},{8,9},{9,10},{10,11},{12,13},{... | collective-permute-start | bytes 491528 | tf_op jit(solution)/shard_map/ppermute | solution.py:409
  3.8 1.3 %collective-permute-start.1 = (bf16[640,128]{1,0:T(8,128)(2,1)S(1)}, bf16[640,128]{1,0:T(8,128)(2,1)S(1)}, u32[]{:S(2)}, u32[]{:S(2)}) collective-permute-start(bf16[640,128]{1,0:T(8,128)(2,1)S(1)} %get-tuple-element.34), channel_id=1, source_target_pairs={{1,0},{2,1},{3,2},{5,4},{6,5},{7,6},{9,8},{10,9},{11,10},{13,12},{... | collective-permute-start | bytes 491528 | tf_op jit(solution)/shard_map/ppermute | solution.py:409
  5.1 0.0 copy-done
  5.1 0.0 copy-done.8
  5.1 0.0 copy-done.9
  5.2 2.9 %shard_map.145 = (bf16[2,192,320]{2,1,0:T(8,128)(2,1)S(1)}, bf16[2,192,320]{2,1,0:T(8,128)(2,1)S(1)}, f32[2,2,64,320]{3,2,1,0:T(8,128)S(1)}, bf16[960,192]{1,0:T(8,128)(2,1)S(1)}, f32[8,128]{1,0:T(8,128)S(1)}) custom-call(bf16[4,5,64,320]{3,2,1,0:T(8,128)(2,1)S(1)} %copy-done.3, f32[320]{0:T(512)S(1)} %copy-done.8, f32[320]{0:T(512)S(1)} %copy-done.9, ...), custom_call_target="tpu_custom_call" | custom-call | flops 1179648000 | bytes 2097152 | tf_op jit(solution)/shard_map/pallas_call | solution.py:436
  8.0 0.0 collective-permute-done.above_ref
  8.0 1.2 %collective-permute-done.1.below_ref = bf16[640,128]{1,0:T(8,128)(2,1)S(1)} collective-permute-done((bf16[640,128]{1,0:T(8,128)(2,1)S(1)}, bf16[640,128]{1,0:T(8,128)(2,1)S(1)}, u32[]{:S(2)}, u32[]{:S(2)}) %collective-permute-start.1) | collective-permute-done | bytes 163872 | tf_op jit(solution)/shard_map/ppermute | solution.py:409
  9.2 1.1 %shard_map.147 = (bf16[2,320,320]{2,1,0:T(8,128)(2,1)S(1)}, bf16[2,320,320]{2,1,0:T(8,128)(2,1)S(1)}, bf16[800,128]{1,0:T(8,128)(2,1)S(1)}, bf16[800,128]{1,0:T(8,128)(2,1)S(1)}) custom-call(f32[2,2,64,320]{3,2,1,0:T(8,128)S(1)} %get-tuple-element.32.edge_ref, bf16[640,128]{1,0:T(8,128)(2,1)S(1)} %collective-permute-done.above_ref, ...), custom_call_target="tpu_custom_call" | custom-call | flops 157286400 | bytes 2097152 | tf_op jit(solution)/shard_map/pallas_call | solution.py:449
  10.3 3.5 %collective-permute-start.2 = (bf16[800,128]{1,0:T(8,128)(2,1)S(1)}, bf16[800,128]{1,0:T(8,128)(2,1)S(1)}, u32[]{:S(2)}, u32[]{:S(2)}) collective-permute-start(bf16[800,128]{1,0:T(8,128)(2,1)S(1)} %get-tuple-element.39), channel_id=1, source_target_pairs={{0,4},{4,8},{8,12},{1,5},{5,9},{9,13},{2,6},{6,10},{10,14},{3,7},{... | collective-permute-start | bytes 614408 | tf_op jit(solution)/shard_map/ppermute | solution.py:409
  13.8 1.3 %collective-permute-start.3 = (bf16[800,128]{1,0:T(8,128)(2,1)S(1)}, bf16[800,128]{1,0:T(8,128)(2,1)S(1)}, u32[]{:S(2)}, u32[]{:S(2)}) collective-permute-start(bf16[800,128]{1,0:T(8,128)(2,1)S(1)} %get-tuple-element.40), channel_id=1, source_target_pairs={{4,0},{8,4},{12,8},{5,1},{9,5},{13,9},{6,2},{10,6},{14,10},{7,3},{... | collective-permute-start | bytes 614408 | tf_op jit(solution)/shard_map/ppermute | solution.py:409
  15.8 0.0 copy-done.4
  15.8 0.0 copy-start.5
  15.8 0.0 copy-start.10
  15.8 3.7 %shard_map.148 = (bf16[4,320,320]{2,1,0:T(8,128)(2,1)S(1)}, bf16[4,320,320]{2,1,0:T(8,128)(2,1)S(1)}) custom-call(bf16[4,5,64,320]{3,2,1,0:T(8,128)(2,1)S(1)} %copy-done.4, bf16[640,128]{1,0:T(8,128)(2,1)S(1)} %collective-permute-done.above_ref, bf16[640,128]{1,0:T(8,128)(2,1)S(1)} %collective-permute-done.1.below_ref, f32[320]{0:T(512)S(1)} %copy-done.8, ...), custom_call_target="tpu_custom_call" | custom-call | flops 1179648000 | bytes 2097152 | tf_op jit(solution)/shard_map/pallas_call | solution.py:456
  19.5 0.0 copy-start.1
  19.5 0.0 copy-start.11
  19.5 0.0 collective-permute-done.2.before_ref
  19.5 2.0 %collective-permute-done.3.after_ref = bf16[800,128]{1,0:T(8,128)(2,1)S(1)} collective-permute-done((bf16[800,128]{1,0:T(8,128)(2,1)S(1)}, bf16[800,128]{1,0:T(8,128)(2,1)S(1)}, u32[]{:S(2)}, u32[]{:S(2)}) %collective-permute-start.3) | collective-permute-done | bytes 204832 | tf_op jit(solution)/shard_map/ppermute | solution.py:409
  21.5 0.0 copy-done.5
  21.5 0.0 copy-done.10
  21.5 0.9 %shard_map.149 = bf16[1,800,128]{2,1,0:T(8,128)(2,1)S(1)} custom-call(s32[1,1]{1,0:T(1,128)S(6)} %copy.16.picks_ref, bf16[800,128]{1,0:T(8,128)(2,1)S(1)} %collective-permute-done.2.before_ref, bf16[800,128]{1,0:T(8,128)(2,1)S(1)} %collective-permute-done.3.after_ref, bf16[4,320,320]{2,1,0:T(8,128)(2,1)S(1)} %get-tuple-element.43.spatial_ref, ...), custom_call_target="tpu_custom_call" | custom-call | flops 196608000 | bytes 2097152 | tf_op jit(solution)/shard_map/pallas_call | solution.py:463
  22.4 2.8 %collective-permute-start.5 = (bf16[1,800,128]{2,1,0:T(8,128)(2,1)S(1)}, bf16[1,800,128]{2,1,0:T(8,128)(2,1)S(1)}, u32[]{:S(2)}, u32[]{:S(2)}) collective-permute-start(bf16[1,800,128]{2,1,0:T(8,128)(2,1)S(1)} %shard_map.149), channel_id=1, source_target_pairs={{0,12},{4,0},{8,4},{12,8},{1,13},{5,1},{9,5},{13,9},{2,14},{6,2},{... | collective-permute-start | bytes 614408 | tf_op jit(solution)/shard_map/ppermute | solution.py:469
  25.2 0.0 collective-permute-start.4
  25.9 0.0 copy-done.1
  25.9 0.0 copy-done.11
  25.9 0.0 copy-start.12
  25.9 0.0 copy-start.13
  25.9 4.2 %shard_map.151 = (bf16[4,320,320]{2,1,0:T(8,128)(2,1)S(1)}, bf16[4,320,320]{2,1,0:T(8,128)(2,1)S(1)}, bf16[4,320,640]{2,1,0:T(8,128)(2,1)S(1)}) custom-call(bf16[800,128]{1,0:T(8,128)(2,1)S(1)} %collective-permute-done.2.before_ref, bf16[800,128]{1,0:T(8,128)(2,1)S(1)} %collective-permute-done.3.after_ref, ...), custom_call_target="tpu_custom_call" | custom-call | flops 1572864000 | bytes 2097152 | tf_op jit(solution)/shard_map/pallas_call | solution.py:481
  30.1 0.0 collective-permute-done.5.from_above_ref.anchor_ref
  30.1 5.2 %collective-permute-done.4.from_below_ref.anchor_ref = bf16[1,800,128]{2,1,0:T(8,128)(2,1)S(1)} collective-permute-done((bf16[1,800,128]{2,1,0:T(8,128)(2,1)S(1)}, bf16[1,800,128]{2,1,0:T(8,128)(2,1)S(1)}, u32[]{:S(2)}, u32[]{:S(2)}) %collective-permute-start.4) | collective-permute-done | bytes 204832 | tf_op jit(solution)/shard_map/ppermute | solution.py:469
  35.3 0.1 shard_map.150
  35.4 0.1 collective-permute-start.6
  35.5 0.0 copy-done.12
  35.5 0.0 copy-done.13
  35.5 0.0 copy-start.2
  35.5 0.0 copy-start.6
  35.5 3.9 %shard_map.152 = (f32[4,320,128]{2,1,0:T(8,128)S(1)}, f32[4,320,128]{2,1,0:T(8,128)S(1)}, f32[4,320,384]{2,1,0:T(8,128)S(1)}) custom-call(s32[1,1]{1,0:T(1,128)S(6)} %copy.16.picks_ref, s32[1]{0:T(128)S(6)} %copy.17.window_ref, bf16[4,320,320]{2,1,0:T(8,128)(2,1)S(1)} %get-tuple-element.46.query_ref, bf16[4,320,640]{2,1,0:T(8,128)(2,1)S(1)} %get-tuple-element.47.keyval_ref, ...), custom_call_target="tpu_custom_call" | custom-call | flops 2621440000 | bytes 2097152 | tf_op jit(solution)/shard_map/pallas_call | solution.py:489
  39.4 0.0 copy-done.2
  39.4 0.0 copy-done.6
  39.4 1.3 %shard_map.153 = (f32[4,320,128]{2,1,0:T(8,128)S(1)}, f32[4,320,128]{2,1,0:T(8,128)S(1)}, f32[4,320,384]{2,1,0:T(8,128)S(1)}) custom-call(bf16[1,800,128]{2,1,0:T(8,128)(2,1)S(1)} %collective-permute-done.4.from_below_ref.anchor_ref, bf16[320,640]{1,0:T(8,128)(2,1)S(1)} %copy-done.1, bf16[320,128]{1,0:T(8,128)(2,1)S(1)} %copy-done.6, ...), custom_call_target="tpu_custom_call" | custom-call | flops 1048576000 | bytes 2097152 | tf_op jit(solution)/shard_map/pallas_call | solution.py:495
  40.7 0.0 copy-start.7
  40.7 1.3 %shard_map.154 = (f32[4,320,128]{2,1,0:T(8,128)S(1)}, f32[4,320,128]{2,1,0:T(8,128)S(1)}, f32[4,320,384]{2,1,0:T(8,128)S(1)}) custom-call(bf16[1,800,128]{2,1,0:T(8,128)(2,1)S(1)} %collective-permute-done.5.from_above_ref.anchor_ref, bf16[320,640]{1,0:T(8,128)(2,1)S(1)} %copy-done.1, bf16[320,128]{1,0:T(8,128)(2,1)S(1)} %copy-done.6, ...), custom_call_target="tpu_custom_call" | custom-call | flops 1048576000 | bytes 2097152 | tf_op jit(solution)/shard_map/pallas_call | solution.py:495
  42.1 1.1 %collective-permute-done.6.anchor_ref = bf16[1,800,128]{2,1,0:T(8,128)(2,1)S(1)} collective-permute-done((bf16[1,800,128]{2,1,0:T(8,128)(2,1)S(1)}, bf16[1,800,128]{2,1,0:T(8,128)(2,1)S(1)}, u32[]{:S(2)}, u32[]{:S(2)}) %collective-permute-start.6) | collective-permute-done | bytes 204832 | tf_op jit(solution)/shard_map/ppermute | solution.py:477
  43.1 0.0 copy-done.7
  43.1 2.8 %shard_map.155 = bf16[4,5,64,320]{3,2,1,0:T(8,128)(2,1)} custom-call(bf16[1,800,128]{2,1,0:T(8,128)(2,1)S(1)} %collective-permute-done.6.anchor_ref, bf16[320,640]{1,0:T(8,128)(2,1)S(1)} %copy-done.1, bf16[320,128]{1,0:T(8,128)(2,1)S(1)} %copy-done.6, bf16[640,128]{1,0:T(8,128)(2,1)S(1)} %copy-done.2, bf16[4,320,320]{2,1,0:T(8,128)(2,1)S(1)} %get-tuple-element.46.query_ref, ...), custom_call_target="tpu_custom_call" | custom-call | flops 1310720000 | bytes 2097152 | tf_op jit(solution)/shard_map/pallas_call | solution.py:498
  (5 shorter events, 0.0 us)
Async XLA Ops:
  0.0 5.1 %copy-start = (bf16[3,3,320,320]{3,2,1,0:T(8,128)(2,1)S(1)}, bf16[3,3,320,320]{3,2,1,0:T(8,128)(2,1)}, u32[]{:S(2)}) copy-start(bf16[3,3,320,320]{3,2,1,0:T(8,128)(2,1)} %param.19) | copy-start | bytes 5529604
  0.0 1.4 %copy-start.3 = (bf16[4,5,64,320]{3,2,1,0:T(8,128)(2,1)S(1)}, bf16[4,5,64,320]{3,2,1,0:T(8,128)(2,1)}, u32[]{:S(2)}) copy-start(bf16[4,5,64,320]{3,2,1,0:T(8,128)(2,1)} %x_ref.5) | copy-start | bytes 2457604
  1.4 3.8 %copy-start.8 = (f32[320]{0:T(512)S(1)}, f32[320]{0:T(512)}, u32[]{:S(2)}) copy-start(f32[320]{0:T(512)} %g1_ref.5) | copy-start | bytes 3844
  1.4 3.8 %copy-start.9 = (f32[320]{0:T(512)S(1)}, f32[320]{0:T(512)}, u32[]{:S(2)}) copy-start(f32[320]{0:T(512)} %g2_ref.5) | copy-start | bytes 3844
  1.4 6.6 %collective-permute-start = (bf16[640,128]{1,0:T(8,128)(2,1)S(1)}, bf16[640,128]{1,0:T(8,128)(2,1)S(1)}, u32[]{:S(2)}, u32[]{:S(2)}) collective-permute-start(bf16[640,128]{1,0:T(8,128)(2,1)S(1)} %get-tuple-element.33), channel_id=1, source_target_pairs={{0,1},{1,2},{2,3},{4,5},{5,6},{6,7},{8,9},{9,10},{10,11},{12,13},{... | collective-permute-start | bytes 491528 | tf_op jit(solution)/shard_map/ppermute | solution.py:409
  3.8 5.4 %collective-permute-start.1 = (bf16[640,128]{1,0:T(8,128)(2,1)S(1)}, bf16[640,128]{1,0:T(8,128)(2,1)S(1)}, u32[]{:S(2)}, u32[]{:S(2)}) collective-permute-start(bf16[640,128]{1,0:T(8,128)(2,1)S(1)} %get-tuple-element.34), channel_id=1, source_target_pairs={{1,0},{2,1},{3,2},{5,4},{6,5},{7,6},{9,8},{10,9},{11,10},{13,12},{... | collective-permute-start | bytes 491528 | tf_op jit(solution)/shard_map/ppermute | solution.py:409
  9.2 6.6 %copy-start.4 = (bf16[4,5,64,320]{3,2,1,0:T(8,128)(2,1)S(1)}, bf16[4,5,64,320]{3,2,1,0:T(8,128)(2,1)}, u32[]{:S(2)}) copy-start(bf16[4,5,64,320]{3,2,1,0:T(8,128)(2,1)} %x_ref.5) | copy-start | bytes 2457604
  10.3 9.2 %collective-permute-start.2 = (bf16[800,128]{1,0:T(8,128)(2,1)S(1)}, bf16[800,128]{1,0:T(8,128)(2,1)S(1)}, u32[]{:S(2)}, u32[]{:S(2)}) collective-permute-start(bf16[800,128]{1,0:T(8,128)(2,1)S(1)} %get-tuple-element.39), channel_id=1, source_target_pairs={{0,4},{4,8},{8,12},{1,5},{5,9},{9,13},{2,6},{6,10},{10,14},{3,7},{... | collective-permute-start | bytes 614408 | tf_op jit(solution)/shard_map/ppermute | solution.py:409
  13.8 7.7 %collective-permute-start.3 = (bf16[800,128]{1,0:T(8,128)(2,1)S(1)}, bf16[800,128]{1,0:T(8,128)(2,1)S(1)}, u32[]{:S(2)}, u32[]{:S(2)}) collective-permute-start(bf16[800,128]{1,0:T(8,128)(2,1)S(1)} %get-tuple-element.40), channel_id=1, source_target_pairs={{4,0},{8,4},{12,8},{5,1},{9,5},{13,9},{6,2},{10,6},{14,10},{7,3},{... | collective-permute-start | bytes 614408 | tf_op jit(solution)/shard_map/ppermute | solution.py:409
  15.8 5.7 %copy-start.5 = (bf16[3,320,320]{2,1,0:T(8,128)(2,1)S(1)}, bf16[3,320,320]{2,1,0:T(8,128)(2,1)}, u32[]{:S(2)}) copy-start(bf16[3,320,320]{2,1,0:T(8,128)(2,1)} %wt_ref.3) | copy-start | bytes 1843204
  15.8 5.7 %copy-start.10 = (f32[320]{0:T(512)S(1)}, f32[320]{0:T(512)}, u32[]{:S(2)}) copy-start(f32[320]{0:T(512)} %g3_ref.3) | copy-start | bytes 3844
  19.5 6.4 %copy-start.1 = (bf16[320,640]{1,0:T(8,128)(2,1)S(1)}, bf16[320,640]{1,0:T(8,128)(2,1)}, u32[]{:S(2)}) copy-start(bf16[320,640]{1,0:T(8,128)(2,1)} %wkv_ref.7) | copy-start | bytes 1228804
  19.5 6.4 %copy-start.11 = (bf16[320,320]{1,0:T(8,128)(2,1)S(1)}, bf16[320,320]{1,0:T(8,128)(2,1)}, u32[]{:S(2)}) copy-start(bf16[320,320]{1,0:T(8,128)(2,1)} %wq_ref.1) | copy-start | bytes 614404
  22.4 7.7 %collective-permute-start.5 = (bf16[1,800,128]{2,1,0:T(8,128)(2,1)S(1)}, bf16[1,800,128]{2,1,0:T(8,128)(2,1)S(1)}, u32[]{:S(2)}, u32[]{:S(2)}) collective-permute-start(bf16[1,800,128]{2,1,0:T(8,128)(2,1)S(1)} %shard_map.149), channel_id=1, source_target_pairs={{0,12},{4,0},{8,4},{12,8},{1,13},{5,1},{9,5},{13,9},{2,14},{6,2},{... | collective-permute-start | bytes 614408 | tf_op jit(solution)/shard_map/ppermute | solution.py:469
  25.2 10.1 %collective-permute-start.4 = (bf16[1,800,128]{2,1,0:T(8,128)(2,1)S(1)}, bf16[1,800,128]{2,1,0:T(8,128)(2,1)S(1)}, u32[]{:S(2)}, u32[]{:S(2)}) collective-permute-start(bf16[1,800,128]{2,1,0:T(8,128)(2,1)S(1)} %shard_map.149), channel_id=1, source_target_pairs={{0,4},{4,8},{8,12},{12,0},{1,5},{5,9},{9,13},{13,1},{2,6},{6,10},{... | collective-permute-start | bytes 614408 | tf_op jit(solution)/shard_map/ppermute | solution.py:469
  25.9 9.6 %copy-start.12 = (bf16[1280,128]{1,0:T(8,128)(2,1)S(1)}, bf16[1280,128]{1,0:T(8,128)(2,1)}, u32[]{:S(2)}) copy-start(bf16[1280,128]{1,0:T(8,128)(2,1)} %constant.9.clone.to_channels_ref) | copy-start | bytes 983044
  25.9 9.6 %copy-start.13 = (bf16[1280,128]{1,0:T(8,128)(2,1)S(1)}, bf16[1280,128]{1,0:T(8,128)(2,1)}, u32[]{:S(2)}) copy-start(bf16[1280,128]{1,0:T(8,128)(2,1)} %constant.8.clone.to_lanes_ref) | copy-start | bytes 983044
  35.4 7.7 %collective-permute-start.6 = (bf16[1,800,128]{2,1,0:T(8,128)(2,1)S(1)}, bf16[1,800,128]{2,1,0:T(8,128)(2,1)S(1)}, u32[]{:S(2)}, u32[]{:S(2)}) collective-permute-start(bf16[1,800,128]{2,1,0:T(8,128)(2,1)S(1)} %get-tuple-element.45), channel_id=1, source_target_pairs={{0,4},{4,0},{8,12},{12,8},{1,5},{5,1},{9,13},{13,9},{2,6},{6,2},{1... | collective-permute-start | bytes 614408 | tf_op jit(solution)/shard_map/ppermute | solution.py:477
  35.5 3.9 %copy-start.2 = (bf16[640,128]{1,0:T(8,128)(2,1)S(1)}, bf16[640,128]{1,0:T(8,128)(2,1)}, u32[]{:S(2)}) copy-start(bf16[640,128]{1,0:T(8,128)(2,1)} %constant.11.clone.to_channels_ref) | copy-start | bytes 491524
  35.5 3.9 %copy-start.6 = (bf16[320,128]{1,0:T(8,128)(2,1)S(1)}, bf16[320,128]{1,0:T(8,128)(2,1)}, u32[]{:S(2)}) copy-start(bf16[320,128]{1,0:T(8,128)(2,1)} %constant.10.clone.to_lanes_ref) | copy-start | bytes 245764
  40.7 2.4 %copy-start.7 = (bf16[320,320]{1,0:T(8,128)(2,1)S(1)}, bf16[320,320]{1,0:T(8,128)(2,1)}, u32[]{:S(2)}) copy-start(bf16[320,320]{1,0:T(8,128)(2,1)} %wo_ref.1) | copy-start | bytes 614404

commit v4 on v2

--- a/solution.py
+++ b/solution.py
@@ -330,19 +330,20 @@
         mix_ref[i] = jnp.concatenate([wide, tail], axis=1)
 
 
-def updated(
-    anchor_ref, wkv_ref, to_lanes_ref, to_channels_ref, query_ref, top_ref, sum_ref, mix_ref, last
-):
-    frames, cells, channels = query_ref.shape
+def keys_and_values(anchor_ref, wkv_ref, channels):
+    return [
+        dot(unpacked(anchor_ref[n], channels), wkv_ref[...]).astype(BF)
+        for n in range(anchor_ref.shape[0])
+    ]
+
+
+def updated(keyvals, to_lanes_ref, to_channels_ref, query, top, total, mix, last):
+    frames, cells, channels = query.shape
     full = channels // LANES * LANES
-    count = anchor_ref.shape[0]
-    state = (top_ref[...], sum_ref[...], mix_ref[...])
     size = frames * cells
-    top, total, mix = (v.reshape(size, v.shape[-1]) for v in state)
-    query = query_ref[...].reshape(size, channels)
+    query, top, total, mix = (v.reshape(size, v.shape[-1]) for v in (query, top, total, mix))
     low = lax.broadcasted_iota(jnp.int32, (1, LANES), 1) < LANES // 4
-    for n in range(count):
-        keyval = dot(unpacked(anchor_ref[n], channels), wkv_ref[...]).astype(BF)
+    for n, keyval in enumerate(keyvals):
         key = jnp.concatenate([keyval[:, :channels]] * frames, axis=0)
         scores = dot(query * key, to_lanes_ref[...])
         higher = jnp.maximum(top, scores)
@@ -350,7 +351,7 @@
         fade = jnp.exp(top - higher)
         total = total * fade + weight
         both = jnp.where(low, weight, fade)
-        if last and n == count - 1:
+        if last and n == len(keyvals) - 1:
             both = both / total
         spread = dot(both.astype(BF), beside(to_channels_ref))
         value = keyval[:, channels:].astype(F32)
@@ -369,7 +370,8 @@
     top_out, sum_out, mix_out,
 ):
     new = updated(
-        anchor_ref, wkv_ref, to_lanes_ref, to_channels_ref, query_ref, top_ref, sum_ref, mix_ref, False
+        keys_and_values(anchor_ref, wkv_ref, query_ref.shape[2]), to_lanes_ref, to_channels_ref,
+        query_ref[...], top_ref[...], sum_ref[...], mix_ref[...], False,
     )
     for ref, v in zip((top_out, sum_out, mix_out), new):
         ref[...] = v.reshape(ref.shape)
@@ -381,17 +383,20 @@
 ):
     frames, cells, channels = query_ref.shape
     height, width = out_ref.shape[1:3]
-    _, _, mix = updated(
-        anchor_ref, wkv_ref, to_lanes_ref, to_channels_ref, query_ref, top_ref, sum_ref, mix_ref, True
-    )
-    attended = mix[:, :channels].astype(BF)
-    result = dot(attended, wo_ref[...])
+    keyvals = keys_and_values(anchor_ref, wkv_ref, channels)
     copies = []
-    for i in range(frames):
-        total = temporal_ref[i].astype(F32) + result[i * cells : (i + 1) * cells]
-        out_buf[i] = total.astype(BF).reshape(height, width, channels)
-        copies.append(pltpu.make_async_copy(out_buf.at[i], out_ref.at[i], sems.at[i]))
-        copies[i].start()
+    group = 2 if frames % 2 == 0 else 1
+    for lo in range(0, frames, group):
+        at = slice(lo, lo + group)
+        _, _, mix = updated(
+            keyvals, to_lanes_ref, to_channels_ref,
+            query_ref[at], top_ref[at], sum_ref[at], mix_ref[at], True,
+        )
+        result = dot(mix[:, :channels].astype(BF), wo_ref[...])
+        total = temporal_ref[at].astype(F32) + result.reshape(group, cells, channels)
+        out_buf[at] = total.astype(BF).reshape(group, height, width, channels)
+        copies.append(pltpu.make_async_copy(out_buf.at[at], out_ref.at[at], sems.at[lo // group]))
+        copies[-1].start()
     for copy in copies:
         copy.wait()
 

time: 46.5 us -> 46.5 us (level)
  no operation moved by 1% of the time
where the time goes in v4:
time: 46.5 us; the launch traced here: 46.2 us
  Pallas kernels  22.1 us (48%)
  starting transfers between devices  12.5 us (27%)
  waiting for transfers between devices  8.51 us (18%)
  between operations  1.74 us (4%)
  local copies, waits for them, and re-layouts  1.42 us (3%)
    ppermute x4, starting transfers between devices, neighbours(): return (lax.ppermute(last, axis, up), lax.ppermute(leading, axis, down))  10.9 us
    ppermute x3, waiting for transfers between devices, on_device(): lax.ppermute(chosen, 'clip', [(i, (i + s) % clips) for i in range(clips)])  6.71 us
    pallas_call x1, Pallas kernels, on_device(): call(temporal_kernel, [(some, BF), (some, BF), ((frames, cells, 2 * chann...  4.21 us
    pallas_call x1, Pallas kernels, on_device(): call(local_kernel, states, [VMEM] * 6, flops=10 * frames * cells * one, l...  3.91 us
    pallas_call x1, Pallas kernels, on_device(): call(inner_kernel, [(some, BF), (some, BF)], [VMEM] * 9, [inner_col], flo...  3.67 us
    pallas_call x1, Pallas kernels, on_device(): call(outer_kernel, [(middle, BF), (middle, BF), ((2, 2, width, channels),...  2.87 us
    pallas_call x1, Pallas kernels, on_device(): call(last_kernel, [(latents.shape, BF)], [VMEM] * 10, [pltpu.VMEM(latents...  2.73 us
    pallas_call x2, Pallas kernels, on_device(): call(anchor_kernel, states, [VMEM] * 8, flops=4 * frames * cells * one, l...  2.59 us
  transfers between devices with their start and end apart: 7, of which 2 were waited for; matrix products, arithmetic and copies ran while one was open for 0% of the time, Pallas kernels for 37%

profile of v4, /device:TPU:29, one launch (start us, length us, event | category | flops | bytes accessed | tf_op | source)
XLA Modules:
  0.0 46.2 jit_solution(6241465901570488675)
XLA Ops:
  0.0 0.0 copy-start
  0.0 0.0 copy-start.3
  0.0 1.3 %copy-done.3 = bf16[4,5,64,320]{3,2,1,0:T(8,128)(2,1)S(1)} copy-done((bf16[4,5,64,320]{3,2,1,0:T(8,128)(2,1)S(1)}, bf16[4,5,64,320]{3,2,1,0:T(8,128)(2,1)}, u32[]{:S(2)}) %copy-start.3) | copy-done | bytes 819224
  1.4 0.1 shard_map.146
  1.4 3.7 %collective-permute-start = (bf16[640,128]{1,0:T(8,128)(2,1)S(1)}, bf16[640,128]{1,0:T(8,128)(2,1)S(1)}, u32[]{:S(2)}, u32[]{:S(2)}) collective-permute-start(bf16[640,128]{1,0:T(8,128)(2,1)S(1)} %get-tuple-element.31), channel_id=1, source_target_pairs={{0,1},{1,2},{2,3},{4,5},{5,6},{6,7},{8,9},{9,10},{10,11},{12,13},{... | collective-permute-start | bytes 491528 | tf_op jit(solution)/shard_map/ppermute | solution.py:408
  5.1 1.9 %collective-permute-start.1 = (bf16[640,128]{1,0:T(8,128)(2,1)S(1)}, bf16[640,128]{1,0:T(8,128)(2,1)S(1)}, u32[]{:S(2)}, u32[]{:S(2)}) collective-permute-start(bf16[640,128]{1,0:T(8,128)(2,1)S(1)} %get-tuple-element.32), channel_id=1, source_target_pairs={{1,0},{2,1},{3,2},{5,4},{6,5},{7,6},{9,8},{10,9},{11,10},{13,12},{... | collective-permute-start | bytes 491528 | tf_op jit(solution)/shard_map/ppermute | solution.py:408
  7.1 0.0 copy-done
  7.1 0.0 copy-done.8
  7.1 0.0 copy-done.9
  7.1 2.9 %shard_map.145 = (bf16[2,192,320]{2,1,0:T(8,128)(2,1)S(1)}, bf16[2,192,320]{2,1,0:T(8,128)(2,1)S(1)}, f32[2,2,64,320]{3,2,1,0:T(8,128)S(1)}, bf16[960,192]{1,0:T(8,128)(2,1)S(1)}, f32[8,128]{1,0:T(8,128)S(1)}) custom-call(bf16[4,5,64,320]{3,2,1,0:T(8,128)(2,1)S(1)} %copy-done.3, f32[320]{0:T(512)S(1)} %copy-done.8, f32[320]{0:T(512)S(1)} %copy-done.9, ...), custom_call_target="tpu_custom_call" | custom-call | flops 1179648000 | bytes 2097152 | tf_op jit(solution)/shard_map/pallas_call | solution.py:435
  10.0 0.0 collective-permute-done.above_ref
  10.0 1.8 %collective-permute-done.1.below_ref = bf16[640,128]{1,0:T(8,128)(2,1)S(1)} collective-permute-done((bf16[640,128]{1,0:T(8,128)(2,1)S(1)}, bf16[640,128]{1,0:T(8,128)(2,1)S(1)}, u32[]{:S(2)}, u32[]{:S(2)}) %collective-permute-start.1) | collective-permute-done | bytes 163872 | tf_op jit(solution)/shard_map/ppermute | solution.py:408
  11.8 1.1 %shard_map.147 = (bf16[2,320,320]{2,1,0:T(8,128)(2,1)S(1)}, bf16[2,320,320]{2,1,0:T(8,128)(2,1)S(1)}, bf16[800,128]{1,0:T(8,128)(2,1)S(1)}, bf16[800,128]{1,0:T(8,128)(2,1)S(1)}) custom-call(f32[2,2,64,320]{3,2,1,0:T(8,128)S(1)} %get-tuple-element.30.edge_ref, bf16[640,128]{1,0:T(8,128)(2,1)S(1)} %collective-permute-done.above_ref, ...), custom_call_target="tpu_custom_call" | custom-call | flops 157286400 | bytes 2097152 | tf_op jit(solution)/shard_map/pallas_call | solution.py:448
  12.9 1.3 %collective-permute-start.2 = (bf16[800,128]{1,0:T(8,128)(2,1)S(1)}, bf16[800,128]{1,0:T(8,128)(2,1)S(1)}, u32[]{:S(2)}, u32[]{:S(2)}) collective-permute-start(bf16[800,128]{1,0:T(8,128)(2,1)S(1)} %get-tuple-element.37), channel_id=1, source_target_pairs={{0,4},{4,8},{8,12},{1,5},{5,9},{9,13},{2,6},{6,10},{10,14},{3,7},{... | collective-permute-start | bytes 614408 | tf_op jit(solution)/shard_map/ppermute | solution.py:408
  14.2 4.0 %collective-permute-start.3 = (bf16[800,128]{1,0:T(8,128)(2,1)S(1)}, bf16[800,128]{1,0:T(8,128)(2,1)S(1)}, u32[]{:S(2)}, u32[]{:S(2)}) collective-permute-start(bf16[800,128]{1,0:T(8,128)(2,1)S(1)} %get-tuple-element.38), channel_id=1, source_target_pairs={{4,0},{8,4},{12,8},{5,1},{9,5},{13,9},{6,2},{10,6},{14,10},{7,3},{... | collective-permute-start | bytes 614408 | tf_op jit(solution)/shard_map/ppermute | solution.py:408
  19.5 0.0 copy-done.4
  19.5 0.0 copy-start.5
  19.5 0.0 copy-start.10
  19.5 3.7 %shard_map.148 = (bf16[4,320,320]{2,1,0:T(8,128)(2,1)S(1)}, bf16[4,320,320]{2,1,0:T(8,128)(2,1)S(1)}) custom-call(bf16[4,5,64,320]{3,2,1,0:T(8,128)(2,1)S(1)} %copy-done.4, bf16[640,128]{1,0:T(8,128)(2,1)S(1)} %collective-permute-done.above_ref, bf16[640,128]{1,0:T(8,128)(2,1)S(1)} %collective-permute-done.1.below_ref, f32[320]{0:T(512)S(1)} %copy-done.8, ...), custom_call_target="tpu_custom_call" | custom-call | flops 1179648000 | bytes 2097152 | tf_op jit(solution)/shard_map/pallas_call | solution.py:455
  23.2 0.0 copy-start.1
  23.2 0.0 copy-start.11
  23.2 0.0 collective-permute-done.2.before_ref
  23.2 0.0 collective-permute-done.3.after_ref
  23.2 0.0 copy-done.5
  23.3 0.0 copy-done.10
  23.3 0.9 %shard_map.149 = bf16[1,800,128]{2,1,0:T(8,128)(2,1)S(1)} custom-call(s32[1,1]{1,0:T(1,128)S(6)} %copy.16.picks_ref, bf16[800,128]{1,0:T(8,128)(2,1)S(1)} %collective-permute-done.2.before_ref, bf16[800,128]{1,0:T(8,128)(2,1)S(1)} %collective-permute-done.3.after_ref, bf16[4,320,320]{2,1,0:T(8,128)(2,1)S(1)} %get-tuple-element.41.spatial_ref, ...), custom_call_target="tpu_custom_call" | custom-call | flops 196608000 | bytes 2097152 | tf_op jit(solution)/shard_map/pallas_call | solution.py:462
  24.2 0.0 copy-start.12
  24.2 0.0 copy-start.13
  24.2 0.1 collective-permute-start.6
  24.3 1.3 %collective-permute-start.5 = (bf16[1,800,128]{2,1,0:T(8,128)(2,1)S(1)}, bf16[1,800,128]{2,1,0:T(8,128)(2,1)S(1)}, u32[]{:S(2)}, u32[]{:S(2)}) collective-permute-start(bf16[1,800,128]{2,1,0:T(8,128)(2,1)S(1)} %shard_map.149), channel_id=1, source_target_pairs={{0,8},{4,12},{8,0},{12,4},{1,9},{5,13},{9,1},{13,5},{2,10},{6,14},... | collective-permute-start | bytes 614408 | tf_op jit(solution)/shard_map/ppermute | solution.py:467
  25.6 0.2 collective-permute-start.4
  25.8 0.0 copy-done.1
  25.8 0.0 copy-done.11
  25.8 4.2 %shard_map.150 = (bf16[4,320,320]{2,1,0:T(8,128)(2,1)S(1)}, bf16[4,320,320]{2,1,0:T(8,128)(2,1)S(1)}, bf16[4,320,640]{2,1,0:T(8,128)(2,1)S(1)}) custom-call(bf16[800,128]{1,0:T(8,128)(2,1)S(1)} %collective-permute-done.2.before_ref, bf16[800,128]{1,0:T(8,128)(2,1)S(1)} %collective-permute-done.3.after_ref, ...), custom_call_target="tpu_custom_call" | custom-call | flops 1572864000 | bytes 2097152 | tf_op jit(solution)/shard_map/pallas_call | solution.py:470
  30.0 0.0 copy-done.12
  30.0 0.0 copy-done.13
  30.0 0.0 copy-start.2
  30.1 0.0 copy-start.6
  30.1 3.9 %shard_map.151 = (f32[4,320,128]{2,1,0:T(8,128)S(1)}, f32[4,320,128]{2,1,0:T(8,128)S(1)}, f32[4,320,384]{2,1,0:T(8,128)S(1)}) custom-call(s32[1,1]{1,0:T(1,128)S(6)} %copy.16.picks_ref, s32[1]{0:T(128)S(6)} %copy.17.window_ref, bf16[4,320,320]{2,1,0:T(8,128)(2,1)S(1)} %get-tuple-element.43.query_ref, bf16[4,320,640]{2,1,0:T(8,128)(2,1)S(1)} %get-tuple-element.44.keyval_ref, ...), custom_call_target="tpu_custom_call" | custom-call | flops 2621440000 | bytes 2097152 | tf_op jit(solution)/shard_map/pallas_call | solution.py:478
  34.0 0.0 collective-permute-done.6.anchor_ref
  34.0 0.0 copy-done.2
  34.0 0.0 copy-done.6
  34.0 1.3 %shard_map.152 = (f32[4,320,128]{2,1,0:T(8,128)S(1)}, f32[4,320,128]{2,1,0:T(8,128)S(1)}, f32[4,320,384]{2,1,0:T(8,128)S(1)}) custom-call(bf16[1,800,128]{2,1,0:T(8,128)(2,1)S(1)} %collective-permute-done.6.anchor_ref, bf16[320,640]{1,0:T(8,128)(2,1)S(1)} %copy-done.1, bf16[320,128]{1,0:T(8,128)(2,1)S(1)} %copy-done.6, bf16[640,128]{1,0:T(8,128)(2,1)S(1)} %copy-done.2, ...), custom_call_target="tpu_custom_call" | custom-call | flops 1048576000 | bytes 2097152 | tf_op jit(solution)/shard_map/pallas_call | solution.py:484
  35.3 6.7 %collective-permute-done.5.anchor_ref = bf16[1,800,128]{2,1,0:T(8,128)(2,1)S(1)} collective-permute-done((bf16[1,800,128]{2,1,0:T(8,128)(2,1)S(1)}, bf16[1,800,128]{2,1,0:T(8,128)(2,1)S(1)}, u32[]{:S(2)}, u32[]{:S(2)}) %collective-permute-start.5) | collective-permute-done | bytes 204832 | tf_op jit(solution)/shard_map/ppermute | solution.py:467
  42.0 1.3 %shard_map.153 = (f32[4,320,128]{2,1,0:T(8,128)S(1)}, f32[4,320,128]{2,1,0:T(8,128)S(1)}, f32[4,320,384]{2,1,0:T(8,128)S(1)}) custom-call(bf16[1,800,128]{2,1,0:T(8,128)(2,1)S(1)} %collective-permute-done.5.anchor_ref, bf16[320,640]{1,0:T(8,128)(2,1)S(1)} %copy-done.1, bf16[320,128]{1,0:T(8,128)(2,1)S(1)} %copy-done.6, bf16[640,128]{1,0:T(8,128)(2,1)S(1)} %copy-done.2, ...), custom_call_target="tpu_custom_call" | custom-call | flops 1048576000 | bytes 2097152 | tf_op jit(solution)/shard_map/pallas_call | solution.py:484
  43.3 0.0 collective-permute-done.4.anchor_ref
  43.3 0.0 copy-done.7
  43.3 2.7 %shard_map.154 = bf16[4,5,64,320]{3,2,1,0:T(8,128)(2,1)} custom-call(bf16[1,800,128]{2,1,0:T(8,128)(2,1)S(1)} %collective-permute-done.4.anchor_ref, bf16[320,640]{1,0:T(8,128)(2,1)S(1)} %copy-done.1, bf16[320,128]{1,0:T(8,128)(2,1)S(1)} %copy-done.6, bf16[640,128]{1,0:T(8,128)(2,1)S(1)} %copy-done.2, bf16[4,320,320]{2,1,0:T(8,128)(2,1)S(1)} %get-tuple-element.43.query_ref, ...), custom_call_target="tpu_custom_call" | custom-call | flops 1310720000 | bytes 2097152 | tf_op jit(solution)/shard_map/pallas_call | solution.py:487
  (4 shorter events, 0.0 us)
Async XLA Ops:
  0.0 7.1 %copy-start = (bf16[3,3,320,320]{3,2,1,0:T(8,128)(2,1)S(1)}, bf16[3,3,320,320]{3,2,1,0:T(8,128)(2,1)}, u32[]{:S(2)}) copy-start(bf16[3,3,320,320]{3,2,1,0:T(8,128)(2,1)} %param.19) | copy-start | bytes 5529604
  0.0 1.4 %copy-start.3 = (bf16[4,5,64,320]{3,2,1,0:T(8,128)(2,1)S(1)}, bf16[4,5,64,320]{3,2,1,0:T(8,128)(2,1)}, u32[]{:S(2)}) copy-start(bf16[4,5,64,320]{3,2,1,0:T(8,128)(2,1)} %x_ref.5) | copy-start | bytes 2457604
  1.4 5.7 %copy-start.8 = (f32[320]{0:T(512)S(1)}, f32[320]{0:T(512)}, u32[]{:S(2)}) copy-start(f32[320]{0:T(512)} %g1_ref.5) | copy-start | bytes 3844
  1.4 5.7 %copy-start.9 = (f32[320]{0:T(512)S(1)}, f32[320]{0:T(512)}, u32[]{:S(2)}) copy-start(f32[320]{0:T(512)} %g2_ref.5) | copy-start | bytes 3844
  1.4 8.5 %collective-permute-start = (bf16[640,128]{1,0:T(8,128)(2,1)S(1)}, bf16[640,128]{1,0:T(8,128)(2,1)S(1)}, u32[]{:S(2)}, u32[]{:S(2)}) collective-permute-start(bf16[640,128]{1,0:T(8,128)(2,1)S(1)} %get-tuple-element.31), channel_id=1, source_target_pairs={{0,1},{1,2},{2,3},{4,5},{5,6},{6,7},{8,9},{9,10},{10,11},{12,13},{... | collective-permute-start | bytes 491528 | tf_op jit(solution)/shard_map/ppermute | solution.py:408
  5.1 6.6 %collective-permute-start.1 = (bf16[640,128]{1,0:T(8,128)(2,1)S(1)}, bf16[640,128]{1,0:T(8,128)(2,1)S(1)}, u32[]{:S(2)}, u32[]{:S(2)}) collective-permute-start(bf16[640,128]{1,0:T(8,128)(2,1)S(1)} %get-tuple-element.32), channel_id=1, source_target_pairs={{1,0},{2,1},{3,2},{5,4},{6,5},{7,6},{9,8},{10,9},{11,10},{13,12},{... | collective-permute-start | bytes 491528 | tf_op jit(solution)/shard_map/ppermute | solution.py:408
  11.8 7.7 %copy-start.4 = (bf16[4,5,64,320]{3,2,1,0:T(8,128)(2,1)S(1)}, bf16[4,5,64,320]{3,2,1,0:T(8,128)(2,1)}, u32[]{:S(2)}) copy-start(bf16[4,5,64,320]{3,2,1,0:T(8,128)(2,1)} %x_ref.5) | copy-start | bytes 2457604
  12.9 10.3 %collective-permute-start.2 = (bf16[800,128]{1,0:T(8,128)(2,1)S(1)}, bf16[800,128]{1,0:T(8,128)(2,1)S(1)}, u32[]{:S(2)}, u32[]{:S(2)}) collective-permute-start(bf16[800,128]{1,0:T(8,128)(2,1)S(1)} %get-tuple-element.37), channel_id=1, source_target_pairs={{0,4},{4,8},{8,12},{1,5},{5,9},{9,13},{2,6},{6,10},{10,14},{3,7},{... | collective-permute-start | bytes 614408 | tf_op jit(solution)/shard_map/ppermute | solution.py:408
  14.2 9.1 %collective-permute-start.3 = (bf16[800,128]{1,0:T(8,128)(2,1)S(1)}, bf16[800,128]{1,0:T(8,128)(2,1)S(1)}, u32[]{:S(2)}, u32[]{:S(2)}) collective-permute-start(bf16[800,128]{1,0:T(8,128)(2,1)S(1)} %get-tuple-element.38), channel_id=1, source_target_pairs={{4,0},{8,4},{12,8},{5,1},{9,5},{13,9},{6,2},{10,6},{14,10},{7,3},{... | collective-permute-start | bytes 614408 | tf_op jit(solution)/shard_map/ppermute | solution.py:408
  19.5 3.8 %copy-start.5 = (bf16[3,320,320]{2,1,0:T(8,128)(2,1)S(1)}, bf16[3,320,320]{2,1,0:T(8,128)(2,1)}, u32[]{:S(2)}) copy-start(bf16[3,320,320]{2,1,0:T(8,128)(2,1)} %wt_ref.3) | copy-start | bytes 1843204
  19.5 3.8 %copy-start.10 = (f32[320]{0:T(512)S(1)}, f32[320]{0:T(512)}, u32[]{:S(2)}) copy-start(f32[320]{0:T(512)} %g3_ref.3) | copy-start | bytes 3844
  23.2 2.6 %copy-start.1 = (bf16[320,640]{1,0:T(8,128)(2,1)S(1)}, bf16[320,640]{1,0:T(8,128)(2,1)}, u32[]{:S(2)}) copy-start(bf16[320,640]{1,0:T(8,128)(2,1)} %wkv_ref.7) | copy-start | bytes 1228804
  23.2 2.6 %copy-start.11 = (bf16[320,320]{1,0:T(8,128)(2,1)S(1)}, bf16[320,320]{1,0:T(8,128)(2,1)}, u32[]{:S(2)}) copy-start(bf16[320,320]{1,0:T(8,128)(2,1)} %wq_ref.1) | copy-start | bytes 614404
  24.2 5.8 %copy-start.12 = (bf16[1280,128]{1,0:T(8,128)(2,1)S(1)}, bf16[1280,128]{1,0:T(8,128)(2,1)}, u32[]{:S(2)}) copy-start(bf16[1280,128]{1,0:T(8,128)(2,1)} %constant.9.clone.to_channels_ref) | copy-start | bytes 983044
  24.2 5.8 %copy-start.13 = (bf16[1280,128]{1,0:T(8,128)(2,1)S(1)}, bf16[1280,128]{1,0:T(8,128)(2,1)}, u32[]{:S(2)}) copy-start(bf16[1280,128]{1,0:T(8,128)(2,1)} %constant.8.clone.to_lanes_ref) | copy-start | bytes 983044
  24.2 9.8 %collective-permute-start.6 = (bf16[1,800,128]{2,1,0:T(8,128)(2,1)S(1)}, bf16[1,800,128]{2,1,0:T(8,128)(2,1)S(1)}, u32[]{:S(2)}, u32[]{:S(2)}) collective-permute-start(bf16[1,800,128]{2,1,0:T(8,128)(2,1)S(1)} %shard_map.149), channel_id=1, source_target_pairs={{0,4},{4,8},{8,12},{12,0},{1,5},{5,9},{9,13},{13,1},{2,6},{6,10},{... | collective-permute-start | bytes 614408 | tf_op jit(solution)/shard_map/ppermute | solution.py:467
  24.3 17.7 %collective-permute-start.5 = (bf16[1,800,128]{2,1,0:T(8,128)(2,1)S(1)}, bf16[1,800,128]{2,1,0:T(8,128)(2,1)S(1)}, u32[]{:S(2)}, u32[]{:S(2)}) collective-permute-start(bf16[1,800,128]{2,1,0:T(8,128)(2,1)S(1)} %shard_map.149), channel_id=1, source_target_pairs={{0,8},{4,12},{8,0},{12,4},{1,9},{5,13},{9,1},{13,5},{2,10},{6,14},... | collective-permute-start | bytes 614408 | tf_op jit(solution)/shard_map/ppermute | solution.py:467
  25.6 17.7 %collective-permute-start.4 = (bf16[1,800,128]{2,1,0:T(8,128)(2,1)S(1)}, bf16[1,800,128]{2,1,0:T(8,128)(2,1)S(1)}, u32[]{:S(2)}, u32[]{:S(2)}) collective-permute-start(bf16[1,800,128]{2,1,0:T(8,128)(2,1)S(1)} %shard_map.149), channel_id=1, source_target_pairs={{0,12},{4,0},{8,4},{12,8},{1,13},{5,1},{9,5},{13,9},{2,14},{6,2},{... | collective-permute-start | bytes 614408 | tf_op jit(solution)/shard_map/ppermute | solution.py:467
  30.0 4.0 %copy-start.2 = (bf16[640,128]{1,0:T(8,128)(2,1)S(1)}, bf16[640,128]{1,0:T(8,128)(2,1)}, u32[]{:S(2)}) copy-start(bf16[640,128]{1,0:T(8,128)(2,1)} %constant.11.clone.to_channels_ref) | copy-start | bytes 491524
  30.1 4.0 %copy-start.6 = (bf16[320,128]{1,0:T(8,128)(2,1)S(1)}, bf16[320,128]{1,0:T(8,128)(2,1)}, u32[]{:S(2)}) copy-start(bf16[320,128]{1,0:T(8,128)(2,1)} %constant.10.clone.to_lanes_ref) | copy-start | bytes 245764
  42.0 1.3 %copy-start.7 = (bf16[320,320]{1,0:T(8,128)(2,1)S(1)}, bf16[320,320]{1,0:T(8,128)(2,1)}, u32[]{:S(2)}) copy-start(bf16[320,320]{1,0:T(8,128)(2,1)} %wo_ref.1) | copy-start | bytes 614404

commit v5 on v4

--- a/solution.py
+++ b/solution.py
@@ -95,10 +95,23 @@
     return jnp.sum(jnp.where(place == n, values, 0.0)).astype(jnp.int32)
 
 
-def edge_kernel(x_ref, top_ref, bottom_ref):
+def at_odd(axis):
+    return lax.rem(lax.axis_index(axis), 2) == 1
+
+
+def sorted_pair(odd_ref, even_ref, axis):
+    odd = at_odd(axis)
+    first, second = odd_ref[...], even_ref[...]
+    return jnp.where(odd, second, first), jnp.where(odd, first, second)
+
+
+def edge_kernel(x_ref, odd_ref, even_ref):
     frames, height, width, channels = x_ref.shape
-    pack_into(top_ref, x_ref[:, 0].reshape(frames * width, channels))
-    pack_into(bottom_ref, x_ref[:, height - 1].reshape(frames * width, channels))
+    odd = at_odd("strip")
+    top = x_ref[:, 0].reshape(frames * width, channels)
+    bottom = x_ref[:, height - 1].reshape(frames * width, channels)
+    pack_into(odd_ref, jnp.where(odd, bottom, top))
+    pack_into(even_ref, jnp.where(odd, top, bottom))
 
 
 def rests_into(rem_ref, w_ref):
@@ -141,8 +154,8 @@
     return terms
 
 
-def rim_rows(ref, frames, width, channels):
-    rows = unpacked(ref[...], channels)
+def rim_rows(packed, frames, width, channels):
+    rows = unpacked(packed, channels)
     return jnp.concatenate([rows[f * width : (f + 1) * width] for f in frames], axis=0)
 
 
@@ -169,8 +182,8 @@
 
 
 def outer_edge_kernel(
-    frames, edge_ref, above_ref, below_ref, order_ref, mid_ref, mid2_ref, g1_ref, g2_ref, w_ref, rem_ref,
-    spatial_ref, hidden_ref, first_ref, last_ref,
+    frames, edge_ref, odd_ref, even_ref, order_ref, mid_ref, mid2_ref, g1_ref, g2_ref, w_ref, rem_ref,
+    spatial_ref, hidden_ref, odd_clip_ref, even_clip_ref,
 ):
     _, cells, channels = spatial_ref.shape
     width = edge_ref.shape[2]
@@ -179,8 +192,8 @@
     spatial_ref[:, width : cells - width] = mid_ref[...]
     hidden_ref[:, width : cells - width] = mid2_ref[...]
     cols = [
-        hidden_columns(rim_rows(ref, (0, frames - 1), width, channels), g1_ref, width)
-        for ref in (above_ref, below_ref)
+        hidden_columns(rim_rows(packed, (0, frames - 1), width, channels), g1_ref, width)
+        for packed in sorted_pair(odd_ref, even_ref, "strip")
     ]
     tails = dot(jnp.concatenate(cols, axis=0), rem_ref[...])
     size = 2 * width
@@ -192,12 +205,13 @@
         hidden = silu(norm(rounded, g2_ref)).astype(BF)
         spatial_ref[:, lo : lo + width] = rounded.reshape(2, width, channels)
         hidden_ref[:, lo : lo + width] = hidden.reshape(2, width, channels)
-    pack_into(first_ref, hidden_ref[0])
-    pack_into(last_ref, hidden_ref[1])
+    odd = at_odd("clip")
+    pack_into(odd_clip_ref, jnp.where(odd, hidden_ref[1], hidden_ref[0]))
+    pack_into(even_clip_ref, jnp.where(odd, hidden_ref[0], hidden_ref[1]))
 
 
 def inner_kernel(
-    x_ref, above_ref, below_ref, g1_ref, g2_ref, w_ref, rem_ref, outer_spatial_ref, outer_hidden_ref,
+    x_ref, odd_ref, even_ref, g1_ref, g2_ref, w_ref, rem_ref, outer_spatial_ref, outer_hidden_ref,
     spatial_ref, hidden_ref, col_ref,
 ):
     frames, height, width, channels = x_ref.shape
@@ -206,14 +220,15 @@
         spatial_ref[f] = outer_spatial_ref[s]
         hidden_ref[f] = outer_hidden_ref[s]
     inside = range(1, frames - 1)
+    above, below = sorted_pair(odd_ref, even_ref, "strip")
     rims = len(inside) * width
     end = rims + len(inside) * cells
-    col_ref[:rims] = hidden_columns(rim_rows(above_ref, inside, width, channels), g1_ref, width)
+    col_ref[:rims] = hidden_columns(rim_rows(above, inside, width, channels), g1_ref, width)
     for s, f in enumerate(inside):
         x = x_ref[f].reshape(cells, channels)
         lo = rims + s * cells
         col_ref[lo : lo + cells] = hidden_columns(x, g1_ref, width)
-    col_ref[end:] = hidden_columns(rim_rows(below_ref, inside, width, channels), g1_ref, width)
+    col_ref[end:] = hidden_columns(rim_rows(below, inside, width, channels), g1_ref, width)
     terms = stacked_rows(col_ref, len(inside), height, width, w_ref, rem_ref)
     for s, f in enumerate(inside):
         for row in range(height):
@@ -224,11 +239,10 @@
 
 
 def chosen_kernel(
-    picks_ref, before_ref, after_ref, spatial_ref, hidden_ref, g3_ref, wt_ref, chosen_ref
+    picks_ref, odd_ref, even_ref, spatial_ref, hidden_ref, g3_ref, wt_ref, chosen_ref
 ):
     frames, cells, channels = spatial_ref.shape
-    before = unpacked(before_ref[...], channels)
-    after = unpacked(after_ref[...], channels)
+    before, after = (unpacked(v, channels) for v in sorted_pair(odd_ref, even_ref, "clip"))
     for n in range(chosen_ref.shape[0]):
         pick = scalar(picks_ref, n)
         earlier = jnp.where(pick == 0, before, hidden_ref[jnp.maximum(pick - 1, 0)])
@@ -239,13 +253,12 @@
 
 
 def temporal_kernel(
-    before_ref, after_ref, spatial_ref, hidden_ref, g3_ref, wt_ref, wq_ref, wkv_ref,
+    odd_ref, even_ref, spatial_ref, hidden_ref, g3_ref, wt_ref, wq_ref, wkv_ref,
     temporal_ref, query_ref, keyval_ref,
 ):
     frames, cells, channels = spatial_ref.shape
     size = frames * cells
-    before = unpacked(before_ref[...], channels)
-    after = unpacked(after_ref[...], channels)
+    before, after = (unpacked(v, channels) for v in sorted_pair(odd_ref, even_ref, "clip"))
     hidden = hidden_ref[...].reshape(size, channels)
     total = spatial_ref[...].reshape(size, channels).astype(F32) + dot(hidden, wt_ref[1])
     total = total + dot(jnp.concatenate([before, hidden[: size - cells]], axis=0), wt_ref[0])
@@ -401,11 +414,11 @@
         copy.wait()
 
 
-def neighbours(leading, last, axis):
+def swapped(odd, even, axis):
     count = lax.axis_size(axis)
-    up = [(i, i + 1) for i in range(count - 1)]
-    down = [(j, i) for i, j in up]
-    return lax.ppermute(last, axis, up), lax.ppermute(leading, axis, down)
+    pairs = [[(i, i + 1) for i in range(start, count - 1, 2)] for start in (1, 0)]
+    pairs = [up + [(j, i) for i, j in up] for up in pairs]
+    return lax.ppermute(odd, axis, pairs[0]), lax.ppermute(even, axis, pairs[1])
 
 
 def on_device(
@@ -425,10 +438,10 @@
 
     x, g1, g2, g3, w = latents, gain_one, gain_two, gain_three, ws
 
-    top, bottom = call(
+    strip_odd, strip_even = call(
         edge_kernel, [((edge_packed, LANES), BF)] * 2, [VMEM], flops=8 * frames * cells * one
     )(x)
-    above, below = neighbours(top, bottom, "strip")
+    strip_odd, strip_even = swapped(strip_odd, strip_even, "strip")
     outer_col = pltpu.VMEM((2 * cells, 3 * channels), BF)
     inner_col = pltpu.VMEM(((frames - 2) * (cells + 2 * width), 3 * channels), BF)
     middle = (2, cells - 2 * width, channels)
@@ -445,23 +458,23 @@
         [outer_col],
         flops=9 * 2 * cells * one,
     )(x, g1, g2, w)
-    outer_spatial, outer_hidden, first, last = call(
+    outer_spatial, outer_hidden, clip_odd, clip_even = call(
         functools.partial(outer_edge_kernel, frames),
         [((2, cells, channels), BF)] * 2 + [((packed, LANES), BF)] * 2,
         [VMEM] * 10,
         flops=6 * 2 * width * one,
-    )(edge, above, below, order, mid, mid2, g1, g2, w, w_rem)
-    before, after = neighbours(first, last, "clip")
+    )(edge, strip_odd, strip_even, order, mid, mid2, g1, g2, w, w_rem)
+    clip_odd, clip_even = swapped(clip_odd, clip_even, "clip")
     spatial, hidden = call(
         inner_kernel,
         [(some, BF), (some, BF)],
         [VMEM] * 9,
         [inner_col],
         flops=9 * (frames - 2) * cells * one,
-    )(x, above, below, g1, g2, w, w_rem, outer_spatial, outer_hidden)
+    )(x, strip_odd, strip_even, g1, g2, w, w_rem, outer_spatial, outer_hidden)
     (chosen,) = call(
         chosen_kernel, [((count, packed, LANES), BF)], [VMEM] * 7, flops=3 * cells * one
-    )(anchor_index, before, after, spatial, hidden, g3, temporal_w)
+    )(anchor_index, clip_odd, clip_even, spatial, hidden, g3, temporal_w)
     clips = lax.axis_size("clip")
     arrived = [
         lax.ppermute(chosen, "clip", [(i, (i + s) % clips) for i in range(clips)])
@@ -473,7 +486,7 @@
         [VMEM] * 8,
         flops=6 * frames * cells * one,
         limit=32,
-    )(before, after, spatial, hidden, g3, temporal_w, w_query, w_keyval)
+    )(clip_odd, clip_even, spatial, hidden, g3, temporal_w, w_query, w_keyval)
     states = [((frames, cells, LANES), F32)] * 2 + [((frames, cells, lanes_up), F32)]
     state = call(
         local_kernel, states, [VMEM] * 6, flops=10 * frames * cells * one, limit=32

time: 46.5 us -> 43.8 us (0.942)
  the two profiles are of different devices: /device:TPU:29 before, /device:TPU:0 now
where the time goes in v5:
time: 43.8 us; the launch traced here: 43.2 us
  Pallas kernels  22.2 us (51%)
  starting transfers between devices  14.7 us (34%)
  waiting for transfers between devices  3.21 us (7%)
  between operations  1.71 us (4%)
  local copies, waits for them, and re-layouts  1.42 us (3%)
    ppermute x2, starting transfers between devices, swapped(): lax.ppermute(even, axis, pairs[1])  8.81 us
    ppermute x3, starting transfers between devices, on_device(): lax.ppermute(chosen, 'clip', [(i, (i + s) % clips) for i in range(clips)])  4.51 us
    pallas_call x1, Pallas kernels, on_device(): call(temporal_kernel, [(some, BF), (some, BF), ((frames, cells, 2 * chann...  4.2 us
    pallas_call x1, Pallas kernels, on_device(): call(local_kernel, states, [VMEM] * 6, flops=10 * frames * cells * one, l...  3.91 us
    pallas_call x1, Pallas kernels, on_device(): call(inner_kernel, [(some, BF), (some, BF)], [VMEM] * 9, [inner_col], flo...  3.69 us
    ppermute x3, waiting for transfers between devices, on_device(): lax.ppermute(chosen, 'clip', [(i, (i + s) % clips) for i in range(clips)])  3.2 us
    pallas_call x1, Pallas kernels, on_device(): call(outer_kernel, [(middle, BF), (middle, BF), ((2, 2, width, channels),...  2.87 us
    pallas_call x1, Pallas kernels, on_device(): call(last_kernel, [(latents.shape, BF)], [VMEM] * 10, [pltpu.VMEM(latents...  2.73 us
  transfers between devices with their start and end apart: 7, of which 1 were waited for; matrix products, arithmetic and copies ran while one was open for 0% of the time, Pallas kernels for 40%

profile of v5, /device:TPU:0, one launch (start us, length us, event | category | flops | bytes accessed | tf_op | source)
XLA Modules:
  0.0 43.2 jit_solution(12363724201378572608)
XLA Ops:
  0.0 0.0 copy-start
  0.0 1.3 %copy-done.3 = bf16[4,5,64,320]{3,2,1,0:T(8,128)(2,1)S(1)} copy-done((bf16[4,5,64,320]{3,2,1,0:T(8,128)(2,1)S(1)}, bf16[4,5,64,320]{3,2,1,0:T(8,128)(2,1)}, u32[]{:S(2)}) %copy-start.3) | copy-done | bytes 819224
  1.4 0.1 shard_map.146
  1.5 0.7 %collective-permute-start = (bf16[640,128]{1,0:T(8,128)(2,1)S(1)}, bf16[640,128]{1,0:T(8,128)(2,1)S(1)}, u32[]{:S(2)}, u32[]{:S(2)}) collective-permute-start(bf16[640,128]{1,0:T(8,128)(2,1)S(1)} %get-tuple-element.31), channel_id=1, source_target_pairs={{1,2},{2,1},{5,6},{6,5},{9,10},{10,9},{13,14},{14,13},{17,18},{18,... | collective-permute-start | bytes 491528 | tf_op jit(solution)/shard_map/ppermute | solution.py:421
  2.1 4.4 %collective-permute-start.1 = (bf16[640,128]{1,0:T(8,128)(2,1)S(1)}, bf16[640,128]{1,0:T(8,128)(2,1)S(1)}, u32[]{:S(2)}, u32[]{:S(2)}) collective-permute-start(bf16[640,128]{1,0:T(8,128)(2,1)S(1)} %get-tuple-element.32), channel_id=1, source_target_pairs={{0,1},{2,3},{1,0},{3,2},{4,5},{6,7},{5,4},{7,6},{8,9},{10,11},{9,8... | collective-permute-start | bytes 491528 | tf_op jit(solution)/shard_map/ppermute | solution.py:421
  6.5 0.0 copy-done
  6.5 0.0 copy-done.8
  6.5 0.0 copy-done.9
  6.5 2.9 %shard_map.145 = (bf16[2,192,320]{2,1,0:T(8,128)(2,1)S(1)}, bf16[2,192,320]{2,1,0:T(8,128)(2,1)S(1)}, f32[2,2,64,320]{3,2,1,0:T(8,128)S(1)}, bf16[960,192]{1,0:T(8,128)(2,1)S(1)}, f32[8,128]{1,0:T(8,128)S(1)}) custom-call(bf16[4,5,64,320]{3,2,1,0:T(8,128)(2,1)S(1)} %copy-done.3, f32[320]{0:T(512)S(1)} %copy-done.8, f32[320]{0:T(512)S(1)} %copy-done.9, ...), custom_call_target="tpu_custom_call" | custom-call | flops 1179648000 | bytes 2097152 | tf_op jit(solution)/shard_map/pallas_call | solution.py:448
  9.4 0.0 collective-permute-done.odd_ref
  9.4 0.0 collective-permute-done.1.even_ref
  9.4 0.0 copy-start.4
  9.4 1.2 %shard_map.147 = (bf16[2,320,320]{2,1,0:T(8,128)(2,1)S(1)}, bf16[2,320,320]{2,1,0:T(8,128)(2,1)S(1)}, bf16[800,128]{1,0:T(8,128)(2,1)S(1)}, bf16[800,128]{1,0:T(8,128)(2,1)S(1)}) custom-call(f32[2,2,64,320]{3,2,1,0:T(8,128)S(1)} %get-tuple-element.30.edge_ref, bf16[640,128]{1,0:T(8,128)(2,1)S(1)} %collective-permute-done.odd_ref, ...), custom_call_target="tpu_custom_call" | custom-call | flops 157286400 | bytes 2097152 | tf_op jit(solution)/shard_map/pallas_call | solution.py:461
  10.6 0.7 %collective-permute-start.2 = (bf16[800,128]{1,0:T(8,128)(2,1)S(1)}, bf16[800,128]{1,0:T(8,128)(2,1)S(1)}, u32[]{:S(2)}, u32[]{:S(2)}) collective-permute-start(bf16[800,128]{1,0:T(8,128)(2,1)S(1)} %get-tuple-element.37), channel_id=1, source_target_pairs={{4,8},{8,4},{5,9},{9,5},{6,10},{10,6},{7,11},{11,7},{20,24},{24,20... | collective-permute-start | bytes 614408 | tf_op jit(solution)/shard_map/ppermute | solution.py:421
  11.2 4.5 %collective-permute-start.3 = (bf16[800,128]{1,0:T(8,128)(2,1)S(1)}, bf16[800,128]{1,0:T(8,128)(2,1)S(1)}, u32[]{:S(2)}, u32[]{:S(2)}) collective-permute-start(bf16[800,128]{1,0:T(8,128)(2,1)S(1)} %get-tuple-element.38), channel_id=1, source_target_pairs={{0,4},{8,12},{4,0},{12,8},{1,5},{9,13},{5,1},{13,9},{2,6},{10,14},... | collective-permute-start | bytes 614408 | tf_op jit(solution)/shard_map/ppermute | solution.py:421
  17.0 0.0 copy-done.4
  17.0 0.0 copy-start.5
  17.0 0.0 copy-start.10
  17.0 3.7 %shard_map.148 = (bf16[4,320,320]{2,1,0:T(8,128)(2,1)S(1)}, bf16[4,320,320]{2,1,0:T(8,128)(2,1)S(1)}) custom-call(bf16[4,5,64,320]{3,2,1,0:T(8,128)(2,1)S(1)} %copy-done.4, bf16[640,128]{1,0:T(8,128)(2,1)S(1)} %collective-permute-done.odd_ref, bf16[640,128]{1,0:T(8,128)(2,1)S(1)} %collective-permute-done.1.even_ref, f32[320]{0:T(512)S(1)} %copy-done.8, ...), custom_call_target="tpu_custom_call" | custom-call | flops 1179648000 | bytes 2097152 | tf_op jit(solution)/shard_map/pallas_call | solution.py:468
  20.7 0.0 copy-start.1
  20.7 0.0 copy-start.11
  20.8 0.0 collective-permute-done.2.odd_ref
  20.8 0.0 collective-permute-done.3.even_ref
  20.8 0.0 copy-done.5
  20.8 0.0 copy-done.10
  20.8 0.9 %shard_map.149 = bf16[1,800,128]{2,1,0:T(8,128)(2,1)S(1)} custom-call(s32[1,1]{1,0:T(1,128)S(6)} %copy.16.picks_ref, bf16[800,128]{1,0:T(8,128)(2,1)S(1)} %collective-permute-done.2.odd_ref, bf16[800,128]{1,0:T(8,128)(2,1)S(1)} %collective-permute-done.3.even_ref, bf16[4,320,320]{2,1,0:T(8,128)(2,1)S(1)} %get-tuple-element.41.spatial_ref, ...), custom_call_target="tpu_custom_call" | custom-call | flops 196608000 | bytes 2097152 | tf_op jit(solution)/shard_map/pallas_call | solution.py:475
  21.7 0.0 copy-start.12
  21.7 0.0 copy-start.13
  21.8 1.7 %collective-permute-start.6 = (bf16[1,800,128]{2,1,0:T(8,128)(2,1)S(1)}, bf16[1,800,128]{2,1,0:T(8,128)(2,1)S(1)}, u32[]{:S(2)}, u32[]{:S(2)}) collective-permute-start(bf16[1,800,128]{2,1,0:T(8,128)(2,1)S(1)} %shard_map.149), channel_id=1, source_target_pairs={{0,4},{4,8},{8,12},{12,0},{1,5},{5,9},{9,13},{13,1},{2,6},{6,10},{... | collective-permute-start | bytes 614408 | tf_op jit(solution)/shard_map/ppermute | solution.py:480
  23.4 0.3 collective-permute-start.5
  23.7 2.5 %collective-permute-start.4 = (bf16[1,800,128]{2,1,0:T(8,128)(2,1)S(1)}, bf16[1,800,128]{2,1,0:T(8,128)(2,1)S(1)}, u32[]{:S(2)}, u32[]{:S(2)}) collective-permute-start(bf16[1,800,128]{2,1,0:T(8,128)(2,1)S(1)} %shard_map.149), channel_id=1, source_target_pairs={{0,12},{4,0},{8,4},{12,8},{1,13},{5,1},{9,5},{13,9},{2,14},{6,2},{... | collective-permute-start | bytes 614408 | tf_op jit(solution)/shard_map/ppermute | solution.py:480
  26.3 0.0 copy-done.1
  26.3 0.0 copy-done.11
  26.3 4.2 %shard_map.150 = (bf16[4,320,320]{2,1,0:T(8,128)(2,1)S(1)}, bf16[4,320,320]{2,1,0:T(8,128)(2,1)S(1)}, bf16[4,320,640]{2,1,0:T(8,128)(2,1)S(1)}) custom-call(bf16[800,128]{1,0:T(8,128)(2,1)S(1)} %collective-permute-done.2.odd_ref, bf16[800,128]{1,0:T(8,128)(2,1)S(1)} %collective-permute-done.3.even_ref, ...), custom_call_target="tpu_custom_call" | custom-call | flops 1572864000 | bytes 2097152 | tf_op jit(solution)/shard_map/pallas_call | solution.py:483
  30.5 0.0 copy-done.12
  30.5 0.0 copy-done.13
  30.5 0.0 copy-start.2
  30.5 0.0 copy-start.6
  30.5 3.9 %shard_map.151 = (f32[4,320,128]{2,1,0:T(8,128)S(1)}, f32[4,320,128]{2,1,0:T(8,128)S(1)}, f32[4,320,384]{2,1,0:T(8,128)S(1)}) custom-call(s32[1,1]{1,0:T(1,128)S(6)} %copy.16.picks_ref, s32[1]{0:T(128)S(6)} %copy.17.window_ref, bf16[4,320,320]{2,1,0:T(8,128)(2,1)S(1)} %get-tuple-element.43.query_ref, bf16[4,320,640]{2,1,0:T(8,128)(2,1)S(1)} %get-tuple-element.44.keyval_ref, ...), custom_call_target="tpu_custom_call" | custom-call | flops 2621440000 | bytes 2097152 | tf_op jit(solution)/shard_map/pallas_call | solution.py:491
  34.4 0.0 collective-permute-done.6.anchor_ref
  34.5 0.0 copy-done.2
  34.5 0.0 copy-done.6
  34.5 1.3 %shard_map.152 = (f32[4,320,128]{2,1,0:T(8,128)S(1)}, f32[4,320,128]{2,1,0:T(8,128)S(1)}, f32[4,320,384]{2,1,0:T(8,128)S(1)}) custom-call(bf16[1,800,128]{2,1,0:T(8,128)(2,1)S(1)} %collective-permute-done.6.anchor_ref, bf16[320,640]{1,0:T(8,128)(2,1)S(1)} %copy-done.1, bf16[320,128]{1,0:T(8,128)(2,1)S(1)} %copy-done.6, bf16[640,128]{1,0:T(8,128)(2,1)S(1)} %copy-done.2, ...), custom_call_target="tpu_custom_call" | custom-call | flops 1048576000 | bytes 2097152 | tf_op jit(solution)/shard_map/pallas_call | solution.py:497
  35.8 3.2 %collective-permute-done.5.anchor_ref = bf16[1,800,128]{2,1,0:T(8,128)(2,1)S(1)} collective-permute-done((bf16[1,800,128]{2,1,0:T(8,128)(2,1)S(1)}, bf16[1,800,128]{2,1,0:T(8,128)(2,1)S(1)}, u32[]{:S(2)}, u32[]{:S(2)}) %collective-permute-start.5) | collective-permute-done | bytes 204832 | tf_op jit(solution)/shard_map/ppermute | solution.py:480
  39.0 1.3 %shard_map.153 = (f32[4,320,128]{2,1,0:T(8,128)S(1)}, f32[4,320,128]{2,1,0:T(8,128)S(1)}, f32[4,320,384]{2,1,0:T(8,128)S(1)}) custom-call(bf16[1,800,128]{2,1,0:T(8,128)(2,1)S(1)} %collective-permute-done.5.anchor_ref, bf16[320,640]{1,0:T(8,128)(2,1)S(1)} %copy-done.1, bf16[320,128]{1,0:T(8,128)(2,1)S(1)} %copy-done.6, bf16[640,128]{1,0:T(8,128)(2,1)S(1)} %copy-done.2, ...), custom_call_target="tpu_custom_call" | custom-call | flops 1048576000 | bytes 2097152 | tf_op jit(solution)/shard_map/pallas_call | solution.py:497
  40.3 0.0 collective-permute-done.4.anchor_ref
  40.3 0.0 copy-done.7
  40.3 2.7 %shard_map.154 = bf16[4,5,64,320]{3,2,1,0:T(8,128)(2,1)} custom-call(bf16[1,800,128]{2,1,0:T(8,128)(2,1)S(1)} %collective-permute-done.4.anchor_ref, bf16[320,640]{1,0:T(8,128)(2,1)S(1)} %copy-done.1, bf16[320,128]{1,0:T(8,128)(2,1)S(1)} %copy-done.6, bf16[640,128]{1,0:T(8,128)(2,1)S(1)} %copy-done.2, bf16[4,320,320]{2,1,0:T(8,128)(2,1)S(1)} %get-tuple-element.43.query_ref, ...), custom_call_target="tpu_custom_call" | custom-call | flops 1310720000 | bytes 2097152 | tf_op jit(solution)/shard_map/pallas_call | solution.py:500
  (4 shorter events, 0.0 us)
Async XLA Ops:
  0.0 6.5 %copy-start = (bf16[3,3,320,320]{3,2,1,0:T(8,128)(2,1)S(1)}, bf16[3,3,320,320]{3,2,1,0:T(8,128)(2,1)}, u32[]{:S(2)}) copy-start(bf16[3,3,320,320]{3,2,1,0:T(8,128)(2,1)} %param.19) | copy-start | bytes 5529604
  0.0 1.4 %copy-start.3 = (bf16[4,5,64,320]{3,2,1,0:T(8,128)(2,1)S(1)}, bf16[4,5,64,320]{3,2,1,0:T(8,128)(2,1)}, u32[]{:S(2)}) copy-start(bf16[4,5,64,320]{3,2,1,0:T(8,128)(2,1)} %x_ref.5) | copy-start | bytes 2457604
  1.4 5.1 %copy-start.8 = (f32[320]{0:T(512)S(1)}, f32[320]{0:T(512)}, u32[]{:S(2)}) copy-start(f32[320]{0:T(512)} %g1_ref.5) | copy-start | bytes 3844
  1.4 5.1 %copy-start.9 = (f32[320]{0:T(512)S(1)}, f32[320]{0:T(512)}, u32[]{:S(2)}) copy-start(f32[320]{0:T(512)} %g2_ref.5) | copy-start | bytes 3844
  1.5 7.9 %collective-permute-start = (bf16[640,128]{1,0:T(8,128)(2,1)S(1)}, bf16[640,128]{1,0:T(8,128)(2,1)S(1)}, u32[]{:S(2)}, u32[]{:S(2)}) collective-permute-start(bf16[640,128]{1,0:T(8,128)(2,1)S(1)} %get-tuple-element.31), channel_id=1, source_target_pairs={{1,2},{2,1},{5,6},{6,5},{9,10},{10,9},{13,14},{14,13},{17,18},{18,... | collective-permute-start | bytes 491528 | tf_op jit(solution)/shard_map/ppermute | solution.py:421
  2.1 7.3 %collective-permute-start.1 = (bf16[640,128]{1,0:T(8,128)(2,1)S(1)}, bf16[640,128]{1,0:T(8,128)(2,1)S(1)}, u32[]{:S(2)}, u32[]{:S(2)}) collective-permute-start(bf16[640,128]{1,0:T(8,128)(2,1)S(1)} %get-tuple-element.32), channel_id=1, source_target_pairs={{0,1},{2,3},{1,0},{3,2},{4,5},{6,7},{5,4},{7,6},{8,9},{10,11},{9,8... | collective-permute-start | bytes 491528 | tf_op jit(solution)/shard_map/ppermute | solution.py:421
  9.4 7.6 %copy-start.4 = (bf16[4,5,64,320]{3,2,1,0:T(8,128)(2,1)S(1)}, bf16[4,5,64,320]{3,2,1,0:T(8,128)(2,1)}, u32[]{:S(2)}) copy-start(bf16[4,5,64,320]{3,2,1,0:T(8,128)(2,1)} %x_ref.5) | copy-start | bytes 2457604
  10.6 10.2 %collective-permute-start.2 = (bf16[800,128]{1,0:T(8,128)(2,1)S(1)}, bf16[800,128]{1,0:T(8,128)(2,1)S(1)}, u32[]{:S(2)}, u32[]{:S(2)}) collective-permute-start(bf16[800,128]{1,0:T(8,128)(2,1)S(1)} %get-tuple-element.37), channel_id=1, source_target_pairs={{4,8},{8,4},{5,9},{9,5},{6,10},{10,6},{7,11},{11,7},{20,24},{24,20... | collective-permute-start | bytes 614408 | tf_op jit(solution)/shard_map/ppermute | solution.py:421
  11.2 9.5 %collective-permute-start.3 = (bf16[800,128]{1,0:T(8,128)(2,1)S(1)}, bf16[800,128]{1,0:T(8,128)(2,1)S(1)}, u32[]{:S(2)}, u32[]{:S(2)}) collective-permute-start(bf16[800,128]{1,0:T(8,128)(2,1)S(1)} %get-tuple-element.38), channel_id=1, source_target_pairs={{0,4},{8,12},{4,0},{12,8},{1,5},{9,13},{5,1},{13,9},{2,6},{10,14},... | collective-permute-start | bytes 614408 | tf_op jit(solution)/shard_map/ppermute | solution.py:421
  17.0 3.8 %copy-start.5 = (bf16[3,320,320]{2,1,0:T(8,128)(2,1)S(1)}, bf16[3,320,320]{2,1,0:T(8,128)(2,1)}, u32[]{:S(2)}) copy-start(bf16[3,320,320]{2,1,0:T(8,128)(2,1)} %wt_ref.3) | copy-start | bytes 1843204
  17.0 3.8 %copy-start.10 = (f32[320]{0:T(512)S(1)}, f32[320]{0:T(512)}, u32[]{:S(2)}) copy-start(f32[320]{0:T(512)} %g3_ref.3) | copy-start | bytes 3844
  20.7 5.5 %copy-start.1 = (bf16[320,640]{1,0:T(8,128)(2,1)S(1)}, bf16[320,640]{1,0:T(8,128)(2,1)}, u32[]{:S(2)}) copy-start(bf16[320,640]{1,0:T(8,128)(2,1)} %wkv_ref.7) | copy-start | bytes 1228804
  20.7 5.5 %copy-start.11 = (bf16[320,320]{1,0:T(8,128)(2,1)S(1)}, bf16[320,320]{1,0:T(8,128)(2,1)}, u32[]{:S(2)}) copy-start(bf16[320,320]{1,0:T(8,128)(2,1)} %wq_ref.1) | copy-start | bytes 614404
  21.7 8.8 %copy-start.12 = (bf16[1280,128]{1,0:T(8,128)(2,1)S(1)}, bf16[1280,128]{1,0:T(8,128)(2,1)}, u32[]{:S(2)}) copy-start(bf16[1280,128]{1,0:T(8,128)(2,1)} %constant.9.clone.to_channels_ref) | copy-start | bytes 983044
  21.7 8.8 %copy-start.13 = (bf16[1280,128]{1,0:T(8,128)(2,1)S(1)}, bf16[1280,128]{1,0:T(8,128)(2,1)}, u32[]{:S(2)}) copy-start(bf16[1280,128]{1,0:T(8,128)(2,1)} %constant.8.clone.to_lanes_ref) | copy-start | bytes 983044
  21.8 12.7 %collective-permute-start.6 = (bf16[1,800,128]{2,1,0:T(8,128)(2,1)S(1)}, bf16[1,800,128]{2,1,0:T(8,128)(2,1)S(1)}, u32[]{:S(2)}, u32[]{:S(2)}) collective-permute-start(bf16[1,800,128]{2,1,0:T(8,128)(2,1)S(1)} %shard_map.149), channel_id=1, source_target_pairs={{0,4},{4,8},{8,12},{12,0},{1,5},{5,9},{9,13},{13,1},{2,6},{6,10},{... | collective-permute-start | bytes 614408 | tf_op jit(solution)/shard_map/ppermute | solution.py:480
  23.4 15.5 %collective-permute-start.5 = (bf16[1,800,128]{2,1,0:T(8,128)(2,1)S(1)}, bf16[1,800,128]{2,1,0:T(8,128)(2,1)S(1)}, u32[]{:S(2)}, u32[]{:S(2)}) collective-permute-start(bf16[1,800,128]{2,1,0:T(8,128)(2,1)S(1)} %shard_map.149), channel_id=1, source_target_pairs={{0,8},{4,12},{8,0},{12,4},{1,9},{5,13},{9,1},{13,5},{2,10},{6,14},... | collective-permute-start | bytes 614408 | tf_op jit(solution)/shard_map/ppermute | solution.py:480
  23.7 16.6 %collective-permute-start.4 = (bf16[1,800,128]{2,1,0:T(8,128)(2,1)S(1)}, bf16[1,800,128]{2,1,0:T(8,128)(2,1)S(1)}, u32[]{:S(2)}, u32[]{:S(2)}) collective-permute-start(bf16[1,800,128]{2,1,0:T(8,128)(2,1)S(1)} %shard_map.149), channel_id=1, source_target_pairs={{0,12},{4,0},{8,4},{12,8},{1,13},{5,1},{9,5},{13,9},{2,14},{6,2},{... | collective-permute-start | bytes 614408 | tf_op jit(solution)/shard_map/ppermute | solution.py:480
  30.5 4.0 %copy-start.2 = (bf16[640,128]{1,0:T(8,128)(2,1)S(1)}, bf16[640,128]{1,0:T(8,128)(2,1)}, u32[]{:S(2)}) copy-start(bf16[640,128]{1,0:T(8,128)(2,1)} %constant.11.clone.to_channels_ref) | copy-start | bytes 491524
  30.5 4.0 %copy-start.6 = (bf16[320,128]{1,0:T(8,128)(2,1)S(1)}, bf16[320,128]{1,0:T(8,128)(2,1)}, u32[]{:S(2)}) copy-start(bf16[320,128]{1,0:T(8,128)(2,1)} %constant.10.clone.to_lanes_ref) | copy-start | bytes 245764
  39.0 1.3 %copy-start.7 = (bf16[320,320]{1,0:T(8,128)(2,1)S(1)}, bf16[320,320]{1,0:T(8,128)(2,1)}, u32[]{:S(2)}) copy-start(bf16[320,320]{1,0:T(8,128)(2,1)} %wo_ref.1) | copy-start | bytes 614404

commit v6 on v5

--- a/solution.py
+++ b/solution.py
@@ -421,6 +421,10 @@
     return lax.ppermute(odd, axis, pairs[0]), lax.ppermute(even, axis, pairs[1])
 
 
+def swap_order(s):
+    return (s.bit_length(), -s)
+
+
 def on_device(
     latents, anchor_index, window, gain_one, spatial_w, gain_two, temporal_w, gain_three,
     w_query, w_keyval, w_out,
@@ -476,10 +480,11 @@
         chosen_kernel, [((count, packed, LANES), BF)], [VMEM] * 7, flops=3 * cells * one
     )(anchor_index, clip_odd, clip_even, spatial, hidden, g3, temporal_w)
     clips = lax.axis_size("clip")
-    arrived = [
-        lax.ppermute(chosen, "clip", [(i, (i + s) % clips) for i in range(clips)])
-        for s in range(1, clips)
-    ]
+    if clips & (clips - 1) == 0:
+        routes = [[(i, i ^ s) for i in range(clips)] for s in sorted(range(1, clips), key=swap_order)]
+    else:
+        routes = [[(i, (i + s) % clips) for i in range(clips)] for s in range(1, clips)]
+    arrived = [lax.ppermute(chosen, "clip", route) for route in routes]
     temporal, query, keyval = call(
         temporal_kernel,
         [(some, BF), (some, BF), ((frames, cells, 2 * channels), BF)],

time: 43.8 us -> 45.9 us (1.048)
  waiting for transfers between devices: 3.21 us -> 6.26 us
  starting transfers between devices: 14.7 us -> 13.9 us
    ppermute x3, waiting for transfers between devices: 3.2 us -> 6.25 us  [on_device(): arrived = [lax.ppermute(chosen, 'clip', route) for route in routes]]
    ppermute x3, starting transfers between devices: 4.51 us -> 3.55 us  [on_device(): arrived = [lax.ppermute(chosen, 'clip', route) for route in routes]]
  transfers between devices with their start and end apart: 7 -> 7, of which waited for: 1 -> 2; matrix products, arithmetic and copies ran while one was open for 0% -> 0% of each run, Pallas kernels for 40% -> 38%
where the time goes in v6:
time: 45.9 us; the launch traced here: 45.7 us
  Pallas kernels  22.4 us (49%)
  starting transfers between devices  13.9 us (30%)
  waiting for transfers between devices  6.26 us (14%)
  between operations  1.72 us (4%)
  local copies, waits for them, and re-layouts  1.42 us (3%)
    ppermute x2, starting transfers between devices, swapped(): lax.ppermute(even, axis, pairs[1])  8.81 us
    ppermute x3, waiting for transfers between devices, on_device(): arrived = [lax.ppermute(chosen, 'clip', route) for route in routes]  6.25 us
    pallas_call x1, Pallas kernels, on_device(): call(temporal_kernel, [(some, BF), (some, BF), ((frames, cells, 2 * chann...  4.2 us
    pallas_call x1, Pallas kernels, on_device(): call(local_kernel, states, [VMEM] * 6, flops=10 * frames * cells * one, l...  3.91 us
    pallas_call x1, Pallas kernels, on_device(): call(inner_kernel, [(some, BF), (some, BF)], [VMEM] * 9, [inner_col], flo...  3.69 us
    ppermute x3, starting transfers between devices, on_device(): arrived = [lax.ppermute(chosen, 'clip', route) for route in routes]  3.55 us
    pallas_call x1, Pallas kernels, on_device(): call(outer_kernel, [(middle, BF), (middle, BF), ((2, 2, width, channels),...  2.87 us
    pallas_call x2, Pallas kernels, on_device(): call(anchor_kernel, states, [VMEM] * 8, flops=4 * frames * cells * one, l...  2.84 us
  transfers between devices with their start and end apart: 7, of which 2 were waited for; matrix products, arithmetic and copies ran while one was open for 0% of the time, Pallas kernels for 38%

profile of v6, /device:TPU:0, one launch (start us, length us, event | category | flops | bytes accessed | tf_op | source)
XLA Modules:
  0.0 45.7 jit_solution(9196850099539526037)
XLA Ops:
  0.0 0.0 copy-start
  0.0 1.3 %copy-done.3 = bf16[4,5,64,320]{3,2,1,0:T(8,128)(2,1)S(1)} copy-done((bf16[4,5,64,320]{3,2,1,0:T(8,128)(2,1)S(1)}, bf16[4,5,64,320]{3,2,1,0:T(8,128)(2,1)}, u32[]{:S(2)}) %copy-start.3) | copy-done | bytes 819224
  1.4 0.1 shard_map.146
  1.5 0.7 %collective-permute-start = (bf16[640,128]{1,0:T(8,128)(2,1)S(1)}, bf16[640,128]{1,0:T(8,128)(2,1)S(1)}, u32[]{:S(2)}, u32[]{:S(2)}) collective-permute-start(bf16[640,128]{1,0:T(8,128)(2,1)S(1)} %get-tuple-element.31), channel_id=1, source_target_pairs={{1,2},{2,1},{5,6},{6,5},{9,10},{10,9},{13,14},{14,13},{17,18},{18,... | collective-permute-start | bytes 491528 | tf_op jit(solution)/shard_map/ppermute | solution.py:421
  2.1 4.4 %collective-permute-start.1 = (bf16[640,128]{1,0:T(8,128)(2,1)S(1)}, bf16[640,128]{1,0:T(8,128)(2,1)S(1)}, u32[]{:S(2)}, u32[]{:S(2)}) collective-permute-start(bf16[640,128]{1,0:T(8,128)(2,1)S(1)} %get-tuple-element.32), channel_id=1, source_target_pairs={{0,1},{2,3},{1,0},{3,2},{4,5},{6,7},{5,4},{7,6},{8,9},{10,11},{9,8... | collective-permute-start | bytes 491528 | tf_op jit(solution)/shard_map/ppermute | solution.py:421
  6.5 0.0 copy-done
  6.5 0.0 copy-done.8
  6.5 0.0 copy-done.9
  6.5 2.9 %shard_map.145 = (bf16[2,192,320]{2,1,0:T(8,128)(2,1)S(1)}, bf16[2,192,320]{2,1,0:T(8,128)(2,1)S(1)}, f32[2,2,64,320]{3,2,1,0:T(8,128)S(1)}, bf16[960,192]{1,0:T(8,128)(2,1)S(1)}, f32[8,128]{1,0:T(8,128)S(1)}) custom-call(bf16[4,5,64,320]{3,2,1,0:T(8,128)(2,1)S(1)} %copy-done.3, f32[320]{0:T(512)S(1)} %copy-done.8, f32[320]{0:T(512)S(1)} %copy-done.9, ...), custom_call_target="tpu_custom_call" | custom-call | flops 1179648000 | bytes 2097152 | tf_op jit(solution)/shard_map/pallas_call | solution.py:452
  9.4 0.0 collective-permute-done.odd_ref
  9.4 0.0 collective-permute-done.1.even_ref
  9.4 0.0 copy-start.4
  9.4 1.2 %shard_map.147 = (bf16[2,320,320]{2,1,0:T(8,128)(2,1)S(1)}, bf16[2,320,320]{2,1,0:T(8,128)(2,1)S(1)}, bf16[800,128]{1,0:T(8,128)(2,1)S(1)}, bf16[800,128]{1,0:T(8,128)(2,1)S(1)}) custom-call(f32[2,2,64,320]{3,2,1,0:T(8,128)S(1)} %get-tuple-element.30.edge_ref, bf16[640,128]{1,0:T(8,128)(2,1)S(1)} %collective-permute-done.odd_ref, ...), custom_call_target="tpu_custom_call" | custom-call | flops 157286400 | bytes 2097152 | tf_op jit(solution)/shard_map/pallas_call | solution.py:465
  10.6 0.9 %collective-permute-start.2 = (bf16[800,128]{1,0:T(8,128)(2,1)S(1)}, bf16[800,128]{1,0:T(8,128)(2,1)S(1)}, u32[]{:S(2)}, u32[]{:S(2)}) collective-permute-start(bf16[800,128]{1,0:T(8,128)(2,1)S(1)} %get-tuple-element.37), channel_id=1, source_target_pairs={{4,8},{8,4},{5,9},{9,5},{6,10},{10,6},{7,11},{11,7},{20,24},{24,20... | collective-permute-start | bytes 614408 | tf_op jit(solution)/shard_map/ppermute | solution.py:421
  11.4 4.5 %collective-permute-start.3 = (bf16[800,128]{1,0:T(8,128)(2,1)S(1)}, bf16[800,128]{1,0:T(8,128)(2,1)S(1)}, u32[]{:S(2)}, u32[]{:S(2)}) collective-permute-start(bf16[800,128]{1,0:T(8,128)(2,1)S(1)} %get-tuple-element.38), channel_id=1, source_target_pairs={{0,4},{8,12},{4,0},{12,8},{1,5},{9,13},{5,1},{13,9},{2,6},{10,14},... | collective-permute-start | bytes 614408 | tf_op jit(solution)/shard_map/ppermute | solution.py:421
  17.2 0.0 copy-done.4
  17.2 0.0 copy-start.5
  17.2 0.0 copy-start.10
  17.2 3.7 %shard_map.148 = (bf16[4,320,320]{2,1,0:T(8,128)(2,1)S(1)}, bf16[4,320,320]{2,1,0:T(8,128)(2,1)S(1)}) custom-call(bf16[4,5,64,320]{3,2,1,0:T(8,128)(2,1)S(1)} %copy-done.4, bf16[640,128]{1,0:T(8,128)(2,1)S(1)} %collective-permute-done.odd_ref, bf16[640,128]{1,0:T(8,128)(2,1)S(1)} %collective-permute-done.1.even_ref, f32[320]{0:T(512)S(1)} %copy-done.8, ...), custom_call_target="tpu_custom_call" | custom-call | flops 1179648000 | bytes 2097152 | tf_op jit(solution)/shard_map/pallas_call | solution.py:472
  20.9 0.0 copy-start.1
  20.9 0.0 copy-start.11
  20.9 0.0 collective-permute-done.2.odd_ref
  21.0 0.0 collective-permute-done.3.even_ref
  21.0 0.0 copy-done.5
  21.0 0.0 copy-done.10
  21.0 0.9 %shard_map.149 = bf16[1,800,128]{2,1,0:T(8,128)(2,1)S(1)} custom-call(s32[1,1]{1,0:T(1,128)S(6)} %copy.16.picks_ref, bf16[800,128]{1,0:T(8,128)(2,1)S(1)} %collective-permute-done.2.odd_ref, bf16[800,128]{1,0:T(8,128)(2,1)S(1)} %collective-permute-done.3.even_ref, bf16[4,320,320]{2,1,0:T(8,128)(2,1)S(1)} %get-tuple-element.41.spatial_ref, ...), custom_call_target="tpu_custom_call" | custom-call | flops 196608000 | bytes 2097152 | tf_op jit(solution)/shard_map/pallas_call | solution.py:479
  21.9 0.0 copy-start.12
  21.9 0.0 copy-start.13
  21.9 1.7 %collective-permute-start.6 = (bf16[1,800,128]{2,1,0:T(8,128)(2,1)S(1)}, bf16[1,800,128]{2,1,0:T(8,128)(2,1)S(1)}, u32[]{:S(2)}, u32[]{:S(2)}) collective-permute-start(bf16[1,800,128]{2,1,0:T(8,128)(2,1)S(1)} %shard_map.149), channel_id=1, source_target_pairs={{0,4},{4,0},{8,12},{12,8},{1,5},{5,1},{9,13},{13,9},{2,6},{6,2},{1... | collective-permute-start | bytes 614408 | tf_op jit(solution)/shard_map/ppermute | solution.py:487
  23.6 1.4 %collective-permute-start.5 = (bf16[1,800,128]{2,1,0:T(8,128)(2,1)S(1)}, bf16[1,800,128]{2,1,0:T(8,128)(2,1)S(1)}, u32[]{:S(2)}, u32[]{:S(2)}) collective-permute-start(bf16[1,800,128]{2,1,0:T(8,128)(2,1)S(1)} %shard_map.149), channel_id=1, source_target_pairs={{0,12},{4,8},{8,4},{12,0},{1,13},{5,9},{9,5},{13,1},{2,14},{6,10},... | collective-permute-start | bytes 614408 | tf_op jit(solution)/shard_map/ppermute | solution.py:487
  25.0 0.5 %collective-permute-start.4 = (bf16[1,800,128]{2,1,0:T(8,128)(2,1)S(1)}, bf16[1,800,128]{2,1,0:T(8,128)(2,1)S(1)}, u32[]{:S(2)}, u32[]{:S(2)}) collective-permute-start(bf16[1,800,128]{2,1,0:T(8,128)(2,1)S(1)} %shard_map.149), channel_id=1, source_target_pairs={{0,8},{4,12},{8,0},{12,4},{1,9},{5,13},{9,1},{13,5},{2,10},{6,14},... | collective-permute-start | bytes 614408 | tf_op jit(solution)/shard_map/ppermute | solution.py:487
  25.5 0.0 copy-done.1
  25.5 0.0 copy-done.11
  25.5 4.2 %shard_map.150 = (bf16[4,320,320]{2,1,0:T(8,128)(2,1)S(1)}, bf16[4,320,320]{2,1,0:T(8,128)(2,1)S(1)}, bf16[4,320,640]{2,1,0:T(8,128)(2,1)S(1)}) custom-call(bf16[800,128]{1,0:T(8,128)(2,1)S(1)} %collective-permute-done.2.odd_ref, bf16[800,128]{1,0:T(8,128)(2,1)S(1)} %collective-permute-done.3.even_ref, ...), custom_call_target="tpu_custom_call" | custom-call | flops 1572864000 | bytes 2097152 | tf_op jit(solution)/shard_map/pallas_call | solution.py:488
  29.7 0.0 copy-done.12
  29.7 0.0 copy-done.13
  29.7 0.0 copy-start.2
  29.7 0.0 copy-start.6
  29.8 3.9 %shard_map.151 = (f32[4,320,128]{2,1,0:T(8,128)S(1)}, f32[4,320,128]{2,1,0:T(8,128)S(1)}, f32[4,320,384]{2,1,0:T(8,128)S(1)}) custom-call(s32[1,1]{1,0:T(1,128)S(6)} %copy.16.picks_ref, s32[1]{0:T(128)S(6)} %copy.17.window_ref, bf16[4,320,320]{2,1,0:T(8,128)(2,1)S(1)} %get-tuple-element.43.query_ref, bf16[4,320,640]{2,1,0:T(8,128)(2,1)S(1)} %get-tuple-element.44.keyval_ref, ...), custom_call_target="tpu_custom_call" | custom-call | flops 2621440000 | bytes 2097152 | tf_op jit(solution)/shard_map/pallas_call | solution.py:496
  33.7 0.0 collective-permute-done.6.anchor_ref
  33.7 0.0 copy-done.2
  33.7 0.0 copy-done.6
  33.7 1.5 %shard_map.152 = (f32[4,320,128]{2,1,0:T(8,128)S(1)}, f32[4,320,128]{2,1,0:T(8,128)S(1)}, f32[4,320,384]{2,1,0:T(8,128)S(1)}) custom-call(bf16[1,800,128]{2,1,0:T(8,128)(2,1)S(1)} %collective-permute-done.6.anchor_ref, bf16[320,640]{1,0:T(8,128)(2,1)S(1)} %copy-done.1, bf16[320,128]{1,0:T(8,128)(2,1)S(1)} %copy-done.6, bf16[640,128]{1,0:T(8,128)(2,1)S(1)} %copy-done.2, ...), custom_call_target="tpu_custom_call" | custom-call | flops 1048576000 | bytes 2097152 | tf_op jit(solution)/shard_map/pallas_call | solution.py:502
  35.3 0.2 collective-permute-done.5.anchor_ref
  35.5 1.3 %shard_map.153 = (f32[4,320,128]{2,1,0:T(8,128)S(1)}, f32[4,320,128]{2,1,0:T(8,128)S(1)}, f32[4,320,384]{2,1,0:T(8,128)S(1)}) custom-call(bf16[1,800,128]{2,1,0:T(8,128)(2,1)S(1)} %collective-permute-done.5.anchor_ref, bf16[320,640]{1,0:T(8,128)(2,1)S(1)} %copy-done.1, bf16[320,128]{1,0:T(8,128)(2,1)S(1)} %copy-done.6, bf16[640,128]{1,0:T(8,128)(2,1)S(1)} %copy-done.2, ...), custom_call_target="tpu_custom_call" | custom-call | flops 1048576000 | bytes 2097152 | tf_op jit(solution)/shard_map/pallas_call | solution.py:502
  36.8 6.0 %collective-permute-done.4.anchor_ref = bf16[1,800,128]{2,1,0:T(8,128)(2,1)S(1)} collective-permute-done((bf16[1,800,128]{2,1,0:T(8,128)(2,1)S(1)}, bf16[1,800,128]{2,1,0:T(8,128)(2,1)S(1)}, u32[]{:S(2)}, u32[]{:S(2)}) %collective-permute-start.4) | collective-permute-done | bytes 204832 | tf_op jit(solution)/shard_map/ppermute | solution.py:487
  42.8 0.0 copy-done.7
  42.8 2.7 %shard_map.154 = bf16[4,5,64,320]{3,2,1,0:T(8,128)(2,1)} custom-call(bf16[1,800,128]{2,1,0:T(8,128)(2,1)S(1)} %collective-permute-done.4.anchor_ref, bf16[320,640]{1,0:T(8,128)(2,1)S(1)} %copy-done.1, bf16[320,128]{1,0:T(8,128)(2,1)S(1)} %copy-done.6, bf16[640,128]{1,0:T(8,128)(2,1)S(1)} %copy-done.2, bf16[4,320,320]{2,1,0:T(8,128)(2,1)S(1)} %get-tuple-element.43.query_ref, ...), custom_call_target="tpu_custom_call" | custom-call | flops 1310720000 | bytes 2097152 | tf_op jit(solution)/shard_map/pallas_call | solution.py:505
  (4 shorter events, 0.0 us)
Async XLA Ops:
  0.0 6.5 %copy-start = (bf16[3,3,320,320]{3,2,1,0:T(8,128)(2,1)S(1)}, bf16[3,3,320,320]{3,2,1,0:T(8,128)(2,1)}, u32[]{:S(2)}) copy-start(bf16[3,3,320,320]{3,2,1,0:T(8,128)(2,1)} %param.19) | copy-start | bytes 5529604
  0.0 1.4 %copy-start.3 = (bf16[4,5,64,320]{3,2,1,0:T(8,128)(2,1)S(1)}, bf16[4,5,64,320]{3,2,1,0:T(8,128)(2,1)}, u32[]{:S(2)}) copy-start(bf16[4,5,64,320]{3,2,1,0:T(8,128)(2,1)} %x_ref.5) | copy-start | bytes 2457604
  1.4 5.1 %copy-start.8 = (f32[320]{0:T(512)S(1)}, f32[320]{0:T(512)}, u32[]{:S(2)}) copy-start(f32[320]{0:T(512)} %g1_ref.5) | copy-start | bytes 3844
  1.4 5.1 %copy-start.9 = (f32[320]{0:T(512)S(1)}, f32[320]{0:T(512)}, u32[]{:S(2)}) copy-start(f32[320]{0:T(512)} %g2_ref.5) | copy-start | bytes 3844
  1.5 7.9 %collective-permute-start = (bf16[640,128]{1,0:T(8,128)(2,1)S(1)}, bf16[640,128]{1,0:T(8,128)(2,1)S(1)}, u32[]{:S(2)}, u32[]{:S(2)}) collective-permute-start(bf16[640,128]{1,0:T(8,128)(2,1)S(1)} %get-tuple-element.31), channel_id=1, source_target_pairs={{1,2},{2,1},{5,6},{6,5},{9,10},{10,9},{13,14},{14,13},{17,18},{18,... | collective-permute-start | bytes 491528 | tf_op jit(solution)/shard_map/ppermute | solution.py:421
  2.1 7.3 %collective-permute-start.1 = (bf16[640,128]{1,0:T(8,128)(2,1)S(1)}, bf16[640,128]{1,0:T(8,128)(2,1)S(1)}, u32[]{:S(2)}, u32[]{:S(2)}) collective-permute-start(bf16[640,128]{1,0:T(8,128)(2,1)S(1)} %get-tuple-element.32), channel_id=1, source_target_pairs={{0,1},{2,3},{1,0},{3,2},{4,5},{6,7},{5,4},{7,6},{8,9},{10,11},{9,8... | collective-permute-start | bytes 491528 | tf_op jit(solution)/shard_map/ppermute | solution.py:421
  9.4 7.8 %copy-start.4 = (bf16[4,5,64,320]{3,2,1,0:T(8,128)(2,1)S(1)}, bf16[4,5,64,320]{3,2,1,0:T(8,128)(2,1)}, u32[]{:S(2)}) copy-start(bf16[4,5,64,320]{3,2,1,0:T(8,128)(2,1)} %x_ref.5) | copy-start | bytes 2457604
  10.6 10.4 %collective-permute-start.2 = (bf16[800,128]{1,0:T(8,128)(2,1)S(1)}, bf16[800,128]{1,0:T(8,128)(2,1)S(1)}, u32[]{:S(2)}, u32[]{:S(2)}) collective-permute-start(bf16[800,128]{1,0:T(8,128)(2,1)S(1)} %get-tuple-element.37), channel_id=1, source_target_pairs={{4,8},{8,4},{5,9},{9,5},{6,10},{10,6},{7,11},{11,7},{20,24},{24,20... | collective-permute-start | bytes 614408 | tf_op jit(solution)/shard_map/ppermute | solution.py:421
  11.4 9.5 %collective-permute-start.3 = (bf16[800,128]{1,0:T(8,128)(2,1)S(1)}, bf16[800,128]{1,0:T(8,128)(2,1)S(1)}, u32[]{:S(2)}, u32[]{:S(2)}) collective-permute-start(bf16[800,128]{1,0:T(8,128)(2,1)S(1)} %get-tuple-element.38), channel_id=1, source_target_pairs={{0,4},{8,12},{4,0},{12,8},{1,5},{9,13},{5,1},{13,9},{2,6},{10,14},... | collective-permute-start | bytes 614408 | tf_op jit(solution)/shard_map/ppermute | solution.py:421
  17.2 3.8 %copy-start.5 = (bf16[3,320,320]{2,1,0:T(8,128)(2,1)S(1)}, bf16[3,320,320]{2,1,0:T(8,128)(2,1)}, u32[]{:S(2)}) copy-start(bf16[3,320,320]{2,1,0:T(8,128)(2,1)} %wt_ref.3) | copy-start | bytes 1843204
  17.2 3.8 %copy-start.10 = (f32[320]{0:T(512)S(1)}, f32[320]{0:T(512)}, u32[]{:S(2)}) copy-start(f32[320]{0:T(512)} %g3_ref.3) | copy-start | bytes 3844
  20.9 4.6 %copy-start.1 = (bf16[320,640]{1,0:T(8,128)(2,1)S(1)}, bf16[320,640]{1,0:T(8,128)(2,1)}, u32[]{:S(2)}) copy-start(bf16[320,640]{1,0:T(8,128)(2,1)} %wkv_ref.7) | copy-start | bytes 1228804
  20.9 4.6 %copy-start.11 = (bf16[320,320]{1,0:T(8,128)(2,1)S(1)}, bf16[320,320]{1,0:T(8,128)(2,1)}, u32[]{:S(2)}) copy-start(bf16[320,320]{1,0:T(8,128)(2,1)} %wq_ref.1) | copy-start | bytes 614404
  21.9 7.8 %copy-start.12 = (bf16[1280,128]{1,0:T(8,128)(2,1)S(1)}, bf16[1280,128]{1,0:T(8,128)(2,1)}, u32[]{:S(2)}) copy-start(bf16[1280,128]{1,0:T(8,128)(2,1)} %constant.9.clone.to_channels_ref) | copy-start | bytes 983044
  21.9 7.8 %copy-start.13 = (bf16[1280,128]{1,0:T(8,128)(2,1)S(1)}, bf16[1280,128]{1,0:T(8,128)(2,1)}, u32[]{:S(2)}) copy-start(bf16[1280,128]{1,0:T(8,128)(2,1)} %constant.8.clone.to_lanes_ref) | copy-start | bytes 983044
  21.9 11.7 %collective-permute-start.6 = (bf16[1,800,128]{2,1,0:T(8,128)(2,1)S(1)}, bf16[1,800,128]{2,1,0:T(8,128)(2,1)S(1)}, u32[]{:S(2)}, u32[]{:S(2)}) collective-permute-start(bf16[1,800,128]{2,1,0:T(8,128)(2,1)S(1)} %shard_map.149), channel_id=1, source_target_pairs={{0,4},{4,0},{8,12},{12,8},{1,5},{5,1},{9,13},{13,9},{2,6},{6,2},{1... | collective-permute-start | bytes 614408 | tf_op jit(solution)/shard_map/ppermute | solution.py:487
  23.6 11.8 %collective-permute-start.5 = (bf16[1,800,128]{2,1,0:T(8,128)(2,1)S(1)}, bf16[1,800,128]{2,1,0:T(8,128)(2,1)S(1)}, u32[]{:S(2)}, u32[]{:S(2)}) collective-permute-start(bf16[1,800,128]{2,1,0:T(8,128)(2,1)S(1)} %shard_map.149), channel_id=1, source_target_pairs={{0,12},{4,8},{8,4},{12,0},{1,13},{5,9},{9,5},{13,1},{2,14},{6,10},... | collective-permute-start | bytes 614408 | tf_op jit(solution)/shard_map/ppermute | solution.py:487
  25.0 17.8 %collective-permute-start.4 = (bf16[1,800,128]{2,1,0:T(8,128)(2,1)S(1)}, bf16[1,800,128]{2,1,0:T(8,128)(2,1)S(1)}, u32[]{:S(2)}, u32[]{:S(2)}) collective-permute-start(bf16[1,800,128]{2,1,0:T(8,128)(2,1)S(1)} %shard_map.149), channel_id=1, source_target_pairs={{0,8},{4,12},{8,0},{12,4},{1,9},{5,13},{9,1},{13,5},{2,10},{6,14},... | collective-permute-start | bytes 614408 | tf_op jit(solution)/shard_map/ppermute | solution.py:487
  29.7 4.0 %copy-start.2 = (bf16[640,128]{1,0:T(8,128)(2,1)S(1)}, bf16[640,128]{1,0:T(8,128)(2,1)}, u32[]{:S(2)}) copy-start(bf16[640,128]{1,0:T(8,128)(2,1)} %constant.11.clone.to_channels_ref) | copy-start | bytes 491524
  29.7 4.0 %copy-start.6 = (bf16[320,128]{1,0:T(8,128)(2,1)S(1)}, bf16[320,128]{1,0:T(8,128)(2,1)}, u32[]{:S(2)}) copy-start(bf16[320,128]{1,0:T(8,128)(2,1)} %constant.10.clone.to_lanes_ref) | copy-start | bytes 245764
  35.5 7.3 %copy-start.7 = (bf16[320,320]{1,0:T(8,128)(2,1)S(1)}, bf16[320,320]{1,0:T(8,128)(2,1)}, u32[]{:S(2)}) copy-start(bf16[320,320]{1,0:T(8,128)(2,1)} %wo_ref.1) | copy-start | bytes 614404

commit v7 on v6

--- a/solution.py
+++ b/solution.py
@@ -378,9 +378,16 @@
     return top, total, mix
 
 
+def relay_kernel(*refs):
+    count = len(refs) // 2
+    for n in range(count):
+        refs[count + n][...] = refs[n][...]
+    refs[-1][...] = jnp.zeros_like(refs[-1])
+
+
 def anchor_kernel(
     anchor_ref, wkv_ref, to_lanes_ref, to_channels_ref, query_ref, top_ref, sum_ref, mix_ref,
-    top_out, sum_out, mix_out,
+    order_ref, top_out, sum_out, mix_out,
 ):
     new = updated(
         keys_and_values(anchor_ref, wkv_ref, query_ref.shape[2]), to_lanes_ref, to_channels_ref,
@@ -419,10 +426,6 @@
     pairs = [[(i, i + 1) for i in range(start, count - 1, 2)] for start in (1, 0)]
     pairs = [up + [(j, i) for i, j in up] for up in pairs]
     return lax.ppermute(odd, axis, pairs[0]), lax.ppermute(even, axis, pairs[1])
-
-
-def swap_order(s):
-    return (s.bit_length(), -s)
 
 
 def on_device(
@@ -480,11 +483,19 @@
         chosen_kernel, [((count, packed, LANES), BF)], [VMEM] * 7, flops=3 * cells * one
     )(anchor_index, clip_odd, clip_even, spatial, hidden, g3, temporal_w)
     clips = lax.axis_size("clip")
+    anchors_order = order
     if clips & (clips - 1) == 0:
-        routes = [[(i, i ^ s) for i in range(clips)] for s in sorted(range(1, clips), key=swap_order)]
+        routes = [[(i, i ^ s) for i in range(clips)] for s in range(1, clips, 2)]
+        arrived = [lax.ppermute(chosen, "clip", route) for route in routes]
+        *relayed, anchors_order = call(
+            relay_kernel,
+            [(chosen.shape, BF)] * (clips // 2 - 1) + [((8, LANES), F32)],
+            [VMEM] * (clips // 2 - 1),
+        )(*arrived[1:])
+        arrived += [lax.ppermute(v, "clip", routes[0]) for v in relayed]
     else:
         routes = [[(i, (i + s) % clips) for i in range(clips)] for s in range(1, clips)]
-    arrived = [lax.ppermute(chosen, "clip", route) for route in routes]
+        arrived = [lax.ppermute(chosen, "clip", route) for route in routes]
     temporal, query, keyval = call(
         temporal_kernel,
         [(some, BF), (some, BF), ((frames, cells, 2 * channels), BF)],
@@ -500,8 +511,8 @@
     _, to_channels = head_maps(2, channels)
     for arrival in arrived[:-1]:
         state = call(
-            anchor_kernel, states, [VMEM] * 8, flops=4 * frames * cells * one, limit=32
-        )(arrival, w_keyval, to_lanes, to_channels, query, *state)
+            anchor_kernel, states, [VMEM] * 9, flops=4 * frames * cells * one, limit=32
+        )(arrival, w_keyval, to_lanes, to_channels, query, *state, anchors_order)
     (out,) = call(
         last_kernel,
         [(latents.shape, BF)],

time: 45.9 us -> 43.8 us (0.954)
  waiting for transfers between devices: 6.26 us -> 3.3 us
  starting transfers between devices: 13.9 us -> 14.8 us
    ppermute x3 -> x2, waiting for transfers between devices: 6.25 us -> 2.71 us  [on_device(): arrived = [lax.ppermute(chosen, 'clip', route) for route in routes]]
    ppermute x0 -> x1, starting transfers between devices: none -> 2.19 us  [on_device(): arrived += [lax.ppermute(v, 'clip', routes[0]) for v in relayed]]
    ppermute x3 -> x2, starting transfers between devices: 3.55 us -> 2.32 us  [on_device(): arrived = [lax.ppermute(chosen, 'clip', route) for route in routes]]
    ppermute x2, waiting for transfers between devices: 0.01 us -> 0.58 us  [swapped(): lax.ppermute(even, axis, pairs[1])]
    pallas_call x2 -> x3, Pallas kernels: 2.84 us -> 2.83 us  [the longest x2 2.82 us: on_device(): call(anchor_kernel, states, [VMEM] * 9, flops=4 * frames * cells * one, l...]
  transfers between devices with their start and end apart: 7 -> 7, of which waited for: 2 -> 2; matrix products, arithmetic and copies ran while one was open for 0% -> 0% of each run, Pallas kernels for 38% -> 40%
where the time goes in v7:
time: 43.8 us; the launch traced here: 43.7 us
  Pallas kernels  22.4 us (51%)
  starting transfers between devices  14.8 us (34%)
  waiting for transfers between devices  3.3 us (8%)
  between operations  1.7 us (4%)
  local copies, waits for them, and re-layouts  1.42 us (3%)
    ppermute x2, starting transfers between devices, swapped(): lax.ppermute(even, axis, pairs[1])  8.81 us
    pallas_call x1, Pallas kernels, on_device(): call(temporal_kernel, [(some, BF), (some, BF), ((frames, cells, 2 * chann...  4.2 us
    pallas_call x1, Pallas kernels, on_device(): call(local_kernel, states, [VMEM] * 6, flops=10 * frames * cells * one, l...  3.91 us
    pallas_call x1, Pallas kernels, on_device(): call(inner_kernel, [(some, BF), (some, BF)], [VMEM] * 9, [inner_col], flo...  3.69 us
    pallas_call x1, Pallas kernels, on_device(): call(outer_kernel, [(middle, BF), (middle, BF), ((2, 2, width, channels),...  2.87 us
    pallas_call x2, Pallas kernels, on_device(): call(anchor_kernel, states, [VMEM] * 9, flops=4 * frames * cells * one, l...  2.82 us
    ppermute x2, waiting for transfers between devices, on_device(): arrived = [lax.ppermute(chosen, 'clip', route) for route in routes]  2.71 us
    pallas_call x1, Pallas kernels, on_device(): call(last_kernel, [(latents.shape, BF)], [VMEM] * 10, [pltpu.VMEM(latents...  2.71 us
  transfers between devices with their start and end apart: 7, of which 2 were waited for; matrix products, arithmetic and copies ran while one was open for 0% of the time, Pallas kernels for 40%

profile of v7, /device:TPU:0, one launch (start us, length us, event | category | flops | bytes accessed | tf_op | source)
XLA Modules:
  0.0 43.7 jit_solution(7499290970669447256)
XLA Ops:
  0.0 0.0 copy-start
  0.0 0.0 copy-start.3
  0.0 1.3 %copy-done.3 = bf16[4,5,64,320]{3,2,1,0:T(8,128)(2,1)S(1)} copy-done((bf16[4,5,64,320]{3,2,1,0:T(8,128)(2,1)S(1)}, bf16[4,5,64,320]{3,2,1,0:T(8,128)(2,1)}, u32[]{:S(2)}) %copy-start.3) | copy-done | bytes 819224
  1.4 0.1 shard_map.146
  1.5 0.7 %collective-permute-start = (bf16[640,128]{1,0:T(8,128)(2,1)S(1)}, bf16[640,128]{1,0:T(8,128)(2,1)S(1)}, u32[]{:S(2)}, u32[]{:S(2)}) collective-permute-start(bf16[640,128]{1,0:T(8,128)(2,1)S(1)} %get-tuple-element.33), channel_id=1, source_target_pairs={{1,2},{2,1},{5,6},{6,5},{9,10},{10,9},{13,14},{14,13},{17,18},{18,... | collective-permute-start | bytes 491528 | tf_op jit(solution)/shard_map/ppermute | solution.py:428
  2.1 4.4 %collective-permute-start.1 = (bf16[640,128]{1,0:T(8,128)(2,1)S(1)}, bf16[640,128]{1,0:T(8,128)(2,1)S(1)}, u32[]{:S(2)}, u32[]{:S(2)}) collective-permute-start(bf16[640,128]{1,0:T(8,128)(2,1)S(1)} %get-tuple-element.34), channel_id=1, source_target_pairs={{0,1},{2,3},{1,0},{3,2},{4,5},{6,7},{5,4},{7,6},{8,9},{10,11},{9,8... | collective-permute-start | bytes 491528 | tf_op jit(solution)/shard_map/ppermute | solution.py:428
  6.5 0.0 copy-done
  6.5 0.0 copy-done.8
  6.5 0.0 copy-done.9
  6.5 2.9 %shard_map.145 = (bf16[2,192,320]{2,1,0:T(8,128)(2,1)S(1)}, bf16[2,192,320]{2,1,0:T(8,128)(2,1)S(1)}, f32[2,2,64,320]{3,2,1,0:T(8,128)S(1)}, bf16[960,192]{1,0:T(8,128)(2,1)S(1)}, f32[8,128]{1,0:T(8,128)S(1)}) custom-call(bf16[4,5,64,320]{3,2,1,0:T(8,128)(2,1)S(1)} %copy-done.3, f32[320]{0:T(512)S(1)} %copy-done.8, f32[320]{0:T(512)S(1)} %copy-done.9, ...), custom_call_target="tpu_custom_call" | custom-call | flops 1179648000 | bytes 2097152 | tf_op jit(solution)/shard_map/pallas_call | solution.py:455
  9.4 0.0 collective-permute-done.odd_ref
  9.4 0.0 collective-permute-done.1.even_ref
  9.4 0.0 copy-start.4
  9.4 1.2 %shard_map.147 = (bf16[2,320,320]{2,1,0:T(8,128)(2,1)S(1)}, bf16[2,320,320]{2,1,0:T(8,128)(2,1)S(1)}, bf16[800,128]{1,0:T(8,128)(2,1)S(1)}, bf16[800,128]{1,0:T(8,128)(2,1)S(1)}) custom-call(f32[2,2,64,320]{3,2,1,0:T(8,128)S(1)} %get-tuple-element.32.edge_ref, bf16[640,128]{1,0:T(8,128)(2,1)S(1)} %collective-permute-done.odd_ref, ...), custom_call_target="tpu_custom_call" | custom-call | flops 157286400 | bytes 2097152 | tf_op jit(solution)/shard_map/pallas_call | solution.py:468
  10.6 0.9 %collective-permute-start.2 = (bf16[800,128]{1,0:T(8,128)(2,1)S(1)}, bf16[800,128]{1,0:T(8,128)(2,1)S(1)}, u32[]{:S(2)}, u32[]{:S(2)}) collective-permute-start(bf16[800,128]{1,0:T(8,128)(2,1)S(1)} %get-tuple-element.39), channel_id=1, source_target_pairs={{4,8},{8,4},{5,9},{9,5},{6,10},{10,6},{7,11},{11,7},{20,24},{24,20... | collective-permute-start | bytes 614408 | tf_op jit(solution)/shard_map/ppermute | solution.py:428
  11.4 4.5 %collective-permute-start.3 = (bf16[800,128]{1,0:T(8,128)(2,1)S(1)}, bf16[800,128]{1,0:T(8,128)(2,1)S(1)}, u32[]{:S(2)}, u32[]{:S(2)}) collective-permute-start(bf16[800,128]{1,0:T(8,128)(2,1)S(1)} %get-tuple-element.40), channel_id=1, source_target_pairs={{0,4},{8,12},{4,0},{12,8},{1,5},{9,13},{5,1},{13,9},{2,6},{10,14},... | collective-permute-start | bytes 614408 | tf_op jit(solution)/shard_map/ppermute | solution.py:428
  16.5 0.0 copy-done.4
  16.5 0.0 copy-start.5
  16.6 0.0 copy-start.10
  16.6 3.7 %shard_map.148 = (bf16[4,320,320]{2,1,0:T(8,128)(2,1)S(1)}, bf16[4,320,320]{2,1,0:T(8,128)(2,1)S(1)}) custom-call(bf16[4,5,64,320]{3,2,1,0:T(8,128)(2,1)S(1)} %copy-done.4, bf16[640,128]{1,0:T(8,128)(2,1)S(1)} %collective-permute-done.odd_ref, bf16[640,128]{1,0:T(8,128)(2,1)S(1)} %collective-permute-done.1.even_ref, f32[320]{0:T(512)S(1)} %copy-done.8, ...), custom_call_target="tpu_custom_call" | custom-call | flops 1179648000 | bytes 2097152 | tf_op jit(solution)/shard_map/pallas_call | solution.py:475
  20.3 0.0 copy-start.1
  20.3 0.0 copy-start.11
  20.3 0.0 collective-permute-done.2.odd_ref
  20.3 0.6 %collective-permute-done.3.even_ref = bf16[800,128]{1,0:T(8,128)(2,1)S(1)} collective-permute-done((bf16[800,128]{1,0:T(8,128)(2,1)S(1)}, bf16[800,128]{1,0:T(8,128)(2,1)S(1)}, u32[]{:S(2)}, u32[]{:S(2)}) %collective-permute-start.3) | collective-permute-done | bytes 204832 | tf_op jit(solution)/shard_map/ppermute | solution.py:428
  20.9 0.0 copy-done.5
  20.9 0.0 copy-done.10
  20.9 0.9 %shard_map.149 = bf16[1,800,128]{2,1,0:T(8,128)(2,1)S(1)} custom-call(s32[1,1]{1,0:T(1,128)S(6)} %copy.16.picks_ref, bf16[800,128]{1,0:T(8,128)(2,1)S(1)} %collective-permute-done.2.odd_ref, bf16[800,128]{1,0:T(8,128)(2,1)S(1)} %collective-permute-done.3.even_ref, bf16[4,320,320]{2,1,0:T(8,128)(2,1)S(1)} %get-tuple-element.43.spatial_ref, ...), custom_call_target="tpu_custom_call" | custom-call | flops 196608000 | bytes 2097152 | tf_op jit(solution)/shard_map/pallas_call | solution.py:482
  21.8 1.4 %collective-permute-start.4 = (bf16[1,800,128]{2,1,0:T(8,128)(2,1)S(1)}, bf16[1,800,128]{2,1,0:T(8,128)(2,1)S(1)}, u32[]{:S(2)}, u32[]{:S(2)}) collective-permute-start(bf16[1,800,128]{2,1,0:T(8,128)(2,1)S(1)} %shard_map.149), channel_id=1, source_target_pairs={{0,12},{4,8},{8,4},{12,0},{1,13},{5,9},{9,5},{13,1},{2,14},{6,10},... | collective-permute-start | bytes 614408 | tf_op jit(solution)/shard_map/ppermute | solution.py:489
  23.9 0.0 copy-start.12
  23.9 0.0 copy-start.13
  23.9 0.9 %collective-permute-start.6 = (bf16[1,800,128]{2,1,0:T(8,128)(2,1)S(1)}, bf16[1,800,128]{2,1,0:T(8,128)(2,1)S(1)}, u32[]{:S(2)}, u32[]{:S(2)}) collective-permute-start(bf16[1,800,128]{2,1,0:T(8,128)(2,1)S(1)} %shard_map.149), channel_id=1, source_target_pairs={{0,4},{4,0},{8,12},{12,8},{1,5},{5,1},{9,13},{13,9},{2,6},{6,2},{1... | collective-permute-start | bytes 614408 | tf_op jit(solution)/shard_map/ppermute | solution.py:489
  24.8 0.0 copy-done.1
  24.8 0.0 copy-done.11
  24.8 4.2 %shard_map.151 = (bf16[4,320,320]{2,1,0:T(8,128)(2,1)S(1)}, bf16[4,320,320]{2,1,0:T(8,128)(2,1)S(1)}, bf16[4,320,640]{2,1,0:T(8,128)(2,1)S(1)}) custom-call(bf16[800,128]{1,0:T(8,128)(2,1)S(1)} %collective-permute-done.2.odd_ref, bf16[800,128]{1,0:T(8,128)(2,1)S(1)} %collective-permute-done.3.even_ref, ...), custom_call_target="tpu_custom_call" | custom-call | flops 1572864000 | bytes 2097152 | tf_op jit(solution)/shard_map/pallas_call | solution.py:499
  29.0 2.7 %collective-permute-done.4.refs_0_.anchor_ref = bf16[1,800,128]{2,1,0:T(8,128)(2,1)S(1)} collective-permute-done((bf16[1,800,128]{2,1,0:T(8,128)(2,1)S(1)}, bf16[1,800,128]{2,1,0:T(8,128)(2,1)S(1)}, u32[]{:S(2)}, u32[]{:S(2)}) %collective-permute-start.4) | collective-permute-done | bytes 204832 | tf_op jit(solution)/shard_map/ppermute | solution.py:489
  31.8 2.2 %collective-permute-start.5 = (bf16[1,800,128]{2,1,0:T(8,128)(2,1)S(1)}, bf16[1,800,128]{2,1,0:T(8,128)(2,1)S(1)}, u32[]{:S(2)}, u32[]{:S(2)}) collective-permute-start(bf16[1,800,128]{2,1,0:T(8,128)(2,1)S(1)} %get-tuple-element.45), channel_id=1, source_target_pairs={{0,4},{4,0},{8,12},{12,8},{1,5},{5,1},{9,13},{13,9},{2,6},{6,2},{1... | collective-permute-start | bytes 614408 | tf_op jit(solution)/shard_map/ppermute | solution.py:495
  33.9 0.0 copy-done.12
  33.9 0.0 copy-done.13
  34.0 3.9 %shard_map.152 = (f32[4,320,128]{2,1,0:T(8,128)S(1)}, f32[4,320,128]{2,1,0:T(8,128)S(1)}, f32[4,320,384]{2,1,0:T(8,128)S(1)}) custom-call(s32[1,1]{1,0:T(1,128)S(6)} %copy.16.picks_ref, s32[1]{0:T(128)S(6)} %copy.17.window_ref, bf16[4,320,320]{2,1,0:T(8,128)(2,1)S(1)} %get-tuple-element.46.query_ref, bf16[4,320,640]{2,1,0:T(8,128)(2,1)S(1)} %get-tuple-element.47.keyval_ref, ...), custom_call_target="tpu_custom_call" | custom-call | flops 2621440000 | bytes 2097152 | tf_op jit(solution)/shard_map/pallas_call | solution.py:507
  37.9 0.0 collective-permute-done.6.anchor_ref
  37.9 0.0 copy-done.2
  37.9 0.0 copy-done.6
  37.9 1.5 %shard_map.153 = (f32[4,320,128]{2,1,0:T(8,128)S(1)}, f32[4,320,128]{2,1,0:T(8,128)S(1)}, f32[4,320,384]{2,1,0:T(8,128)S(1)}) custom-call(bf16[1,800,128]{2,1,0:T(8,128)(2,1)S(1)} %collective-permute-done.6.anchor_ref, bf16[320,640]{1,0:T(8,128)(2,1)S(1)} %copy-done.1, bf16[320,128]{1,0:T(8,128)(2,1)S(1)} %copy-done.6, bf16[640,128]{1,0:T(8,128)(2,1)S(1)} %copy-done.2, ...), custom_call_target="tpu_custom_call" | custom-call | flops 1048576000 | bytes 2097152 | tf_op jit(solution)/shard_map/pallas_call | solution.py:513
  39.4 0.0 copy-start.7
  39.5 1.3 %shard_map.154 = (f32[4,320,128]{2,1,0:T(8,128)S(1)}, f32[4,320,128]{2,1,0:T(8,128)S(1)}, f32[4,320,384]{2,1,0:T(8,128)S(1)}) custom-call(bf16[1,800,128]{2,1,0:T(8,128)(2,1)S(1)} %collective-permute-done.4.refs_0_.anchor_ref, bf16[320,640]{1,0:T(8,128)(2,1)S(1)} %copy-done.1, bf16[320,128]{1,0:T(8,128)(2,1)S(1)} %copy-done.6, ...), custom_call_target="tpu_custom_call" | custom-call | flops 1048576000 | bytes 2097152 | tf_op jit(solution)/shard_map/pallas_call | solution.py:513
  40.8 0.0 collective-permute-done.5.anchor_ref
  40.8 0.0 copy-done.7
  40.8 2.7 %shard_map.155 = bf16[4,5,64,320]{3,2,1,0:T(8,128)(2,1)} custom-call(bf16[1,800,128]{2,1,0:T(8,128)(2,1)S(1)} %collective-permute-done.5.anchor_ref, bf16[320,640]{1,0:T(8,128)(2,1)S(1)} %copy-done.1, bf16[320,128]{1,0:T(8,128)(2,1)S(1)} %copy-done.6, bf16[640,128]{1,0:T(8,128)(2,1)S(1)} %copy-done.2, bf16[4,320,320]{2,1,0:T(8,128)(2,1)S(1)} %get-tuple-element.46.query_ref, ...), custom_call_target="tpu_custom_call" | custom-call | flops 1310720000 | bytes 2097152 | tf_op jit(solution)/shard_map/pallas_call | solution.py:516
  (5 shorter events, 0.0 us)
Async XLA Ops:
  0.0 6.5 %copy-start = (bf16[3,3,320,320]{3,2,1,0:T(8,128)(2,1)S(1)}, bf16[3,3,320,320]{3,2,1,0:T(8,128)(2,1)}, u32[]{:S(2)}) copy-start(bf16[3,3,320,320]{3,2,1,0:T(8,128)(2,1)} %param.19) | copy-start | bytes 5529604
  0.0 1.4 %copy-start.3 = (bf16[4,5,64,320]{3,2,1,0:T(8,128)(2,1)S(1)}, bf16[4,5,64,320]{3,2,1,0:T(8,128)(2,1)}, u32[]{:S(2)}) copy-start(bf16[4,5,64,320]{3,2,1,0:T(8,128)(2,1)} %x_ref.5) | copy-start | bytes 2457604
  1.4 5.1 %copy-start.8 = (f32[320]{0:T(512)S(1)}, f32[320]{0:T(512)}, u32[]{:S(2)}) copy-start(f32[320]{0:T(512)} %g1_ref.5) | copy-start | bytes 3844
  1.4 5.1 %copy-start.9 = (f32[320]{0:T(512)S(1)}, f32[320]{0:T(512)}, u32[]{:S(2)}) copy-start(f32[320]{0:T(512)} %g2_ref.5) | copy-start | bytes 3844
  1.5 7.9 %collective-permute-start = (bf16[640,128]{1,0:T(8,128)(2,1)S(1)}, bf16[640,128]{1,0:T(8,128)(2,1)S(1)}, u32[]{:S(2)}, u32[]{:S(2)}) collective-permute-start(bf16[640,128]{1,0:T(8,128)(2,1)S(1)} %get-tuple-element.33), channel_id=1, source_target_pairs={{1,2},{2,1},{5,6},{6,5},{9,10},{10,9},{13,14},{14,13},{17,18},{18,... | collective-permute-start | bytes 491528 | tf_op jit(solution)/shard_map/ppermute | solution.py:428
  2.1 7.3 %collective-permute-start.1 = (bf16[640,128]{1,0:T(8,128)(2,1)S(1)}, bf16[640,128]{1,0:T(8,128)(2,1)S(1)}, u32[]{:S(2)}, u32[]{:S(2)}) collective-permute-start(bf16[640,128]{1,0:T(8,128)(2,1)S(1)} %get-tuple-element.34), channel_id=1, source_target_pairs={{0,1},{2,3},{1,0},{3,2},{4,5},{6,7},{5,4},{7,6},{8,9},{10,11},{9,8... | collective-permute-start | bytes 491528 | tf_op jit(solution)/shard_map/ppermute | solution.py:428
  9.4 7.1 %copy-start.4 = (bf16[4,5,64,320]{3,2,1,0:T(8,128)(2,1)S(1)}, bf16[4,5,64,320]{3,2,1,0:T(8,128)(2,1)}, u32[]{:S(2)}) copy-start(bf16[4,5,64,320]{3,2,1,0:T(8,128)(2,1)} %x_ref.5) | copy-start | bytes 2457604
  10.6 9.7 %collective-permute-start.2 = (bf16[800,128]{1,0:T(8,128)(2,1)S(1)}, bf16[800,128]{1,0:T(8,128)(2,1)S(1)}, u32[]{:S(2)}, u32[]{:S(2)}) collective-permute-start(bf16[800,128]{1,0:T(8,128)(2,1)S(1)} %get-tuple-element.39), channel_id=1, source_target_pairs={{4,8},{8,4},{5,9},{9,5},{6,10},{10,6},{7,11},{11,7},{20,24},{24,20... | collective-permute-start | bytes 614408 | tf_op jit(solution)/shard_map/ppermute | solution.py:428
  11.4 9.4 %collective-permute-start.3 = (bf16[800,128]{1,0:T(8,128)(2,1)S(1)}, bf16[800,128]{1,0:T(8,128)(2,1)S(1)}, u32[]{:S(2)}, u32[]{:S(2)}) collective-permute-start(bf16[800,128]{1,0:T(8,128)(2,1)S(1)} %get-tuple-element.40), channel_id=1, source_target_pairs={{0,4},{8,12},{4,0},{12,8},{1,5},{9,13},{5,1},{13,9},{2,6},{10,14},... | collective-permute-start | bytes 614408 | tf_op jit(solution)/shard_map/ppermute | solution.py:428
  16.5 4.3 %copy-start.5 = (bf16[3,320,320]{2,1,0:T(8,128)(2,1)S(1)}, bf16[3,320,320]{2,1,0:T(8,128)(2,1)}, u32[]{:S(2)}) copy-start(bf16[3,320,320]{2,1,0:T(8,128)(2,1)} %wt_ref.3) | copy-start | bytes 1843204
  16.6 4.3 %copy-start.10 = (f32[320]{0:T(512)S(1)}, f32[320]{0:T(512)}, u32[]{:S(2)}) copy-start(f32[320]{0:T(512)} %g3_ref.3) | copy-start | bytes 3844
  20.3 4.5 %copy-start.1 = (bf16[320,640]{1,0:T(8,128)(2,1)S(1)}, bf16[320,640]{1,0:T(8,128)(2,1)}, u32[]{:S(2)}) copy-start(bf16[320,640]{1,0:T(8,128)(2,1)} %wkv_ref.7) | copy-start | bytes 1228804
  20.3 4.5 %copy-start.11 = (bf16[320,320]{1,0:T(8,128)(2,1)S(1)}, bf16[320,320]{1,0:T(8,128)(2,1)}, u32[]{:S(2)}) copy-start(bf16[320,320]{1,0:T(8,128)(2,1)} %wq_ref.1) | copy-start | bytes 614404
  21.8 9.9 %collective-permute-start.4 = (bf16[1,800,128]{2,1,0:T(8,128)(2,1)S(1)}, bf16[1,800,128]{2,1,0:T(8,128)(2,1)S(1)}, u32[]{:S(2)}, u32[]{:S(2)}) collective-permute-start(bf16[1,800,128]{2,1,0:T(8,128)(2,1)S(1)} %shard_map.149), channel_id=1, source_target_pairs={{0,12},{4,8},{8,4},{12,0},{1,13},{5,9},{9,5},{13,1},{2,14},{6,10},... | collective-permute-start | bytes 614408 | tf_op jit(solution)/shard_map/ppermute | solution.py:489
  23.9 10.1 %copy-start.12 = (bf16[1280,128]{1,0:T(8,128)(2,1)S(1)}, bf16[1280,128]{1,0:T(8,128)(2,1)}, u32[]{:S(2)}) copy-start(bf16[1280,128]{1,0:T(8,128)(2,1)} %constant.9.clone.to_channels_ref) | copy-start | bytes 983044
  23.9 10.1 %copy-start.13 = (bf16[1280,128]{1,0:T(8,128)(2,1)S(1)}, bf16[1280,128]{1,0:T(8,128)(2,1)}, u32[]{:S(2)}) copy-start(bf16[1280,128]{1,0:T(8,128)(2,1)} %constant.8.clone.to_lanes_ref) | copy-start | bytes 983044
  23.9 14.0 %collective-permute-start.6 = (bf16[1,800,128]{2,1,0:T(8,128)(2,1)S(1)}, bf16[1,800,128]{2,1,0:T(8,128)(2,1)S(1)}, u32[]{:S(2)}, u32[]{:S(2)}) collective-permute-start(bf16[1,800,128]{2,1,0:T(8,128)(2,1)S(1)} %shard_map.149), channel_id=1, source_target_pairs={{0,4},{4,0},{8,12},{12,8},{1,5},{5,1},{9,13},{13,9},{2,6},{6,2},{1... | collective-permute-start | bytes 614408 | tf_op jit(solution)/shard_map/ppermute | solution.py:489
  31.8 9.0 %collective-permute-start.5 = (bf16[1,800,128]{2,1,0:T(8,128)(2,1)S(1)}, bf16[1,800,128]{2,1,0:T(8,128)(2,1)S(1)}, u32[]{:S(2)}, u32[]{:S(2)}) collective-permute-start(bf16[1,800,128]{2,1,0:T(8,128)(2,1)S(1)} %get-tuple-element.45), channel_id=1, source_target_pairs={{0,4},{4,0},{8,12},{12,8},{1,5},{5,1},{9,13},{13,9},{2,6},{6,2},{1... | collective-permute-start | bytes 614408 | tf_op jit(solution)/shard_map/ppermute | solution.py:495
  34.0 3.9 %copy-start.2 = (bf16[640,128]{1,0:T(8,128)(2,1)S(1)}, bf16[640,128]{1,0:T(8,128)(2,1)}, u32[]{:S(2)}) copy-start(bf16[640,128]{1,0:T(8,128)(2,1)} %constant.11.clone.to_channels_ref) | copy-start | bytes 491524
  34.0 3.9 %copy-start.6 = (bf16[320,128]{1,0:T(8,128)(2,1)S(1)}, bf16[320,128]{1,0:T(8,128)(2,1)}, u32[]{:S(2)}) copy-start(bf16[320,128]{1,0:T(8,128)(2,1)} %constant.10.clone.to_lanes_ref) | copy-start | bytes 245764
  39.4 1.3 %copy-start.7 = (bf16[320,320]{1,0:T(8,128)(2,1)S(1)}, bf16[320,320]{1,0:T(8,128)(2,1)}, u32[]{:S(2)}) copy-start(bf16[320,320]{1,0:T(8,128)(2,1)} %wo_ref.1) | copy-start | bytes 614404

commit v8 on v6

--- a/solution.py
+++ b/solution.py
@@ -293,14 +293,16 @@
 
 
 def local_kernel(
-    picks_ref, window_ref, query_ref, keyval_ref, to_lanes_ref, to_channels_ref,
-    top_ref, sum_ref, mix_ref,
-):
+    start, picks_ref, window_ref, query_ref, keyval_ref, to_lanes_ref, to_channels_ref, order_ref,
+    top_ref, sum_ref, mix_ref, next_ref,
+):
+    next_ref[...] = jnp.zeros_like(next_ref)
     frames, cells, channels = query_ref.shape
     count = picks_ref.shape[1]
     full = channels // LANES * LANES
     stride = LANES // 4
-    queries = [query_ref[f] for f in range(frames)]
+    part = top_ref.shape[0]
+    queries = [query_ref[start + f] for f in range(part)]
     keyvals = [keyval_ref[f] for f in range(frames)]
     keys = [kv[:, :full] for kv in keyvals] + [
         jnp.concatenate([kv[:, full:channels] for kv in keyvals], axis=1)
@@ -320,8 +322,8 @@
     for n in range(count):
         copies = copies + jnp.where(source == picks_ref[:, n : n + 1], 1.0, 0.0)
     weights = []
-    for i in range(frames):
-        times = copies + jnp.where(jnp.abs(source - i) < window, 1.0, 0.0)
+    for i in range(part):
+        times = copies + jnp.where(jnp.abs(source - (start + i)) < window, 1.0, 0.0)
         s = jnp.where(times > 0.0, scores[i * cells : (i + 1) * cells], -jnp.inf)
         top = jnp.maximum(s, pltpu.roll(s, stride, 1))
         top = jnp.maximum(top, pltpu.roll(top, 2 * stride, 1))
@@ -332,12 +334,12 @@
         sum_ref[i] = total
         weights.append(w.astype(BF))
     spread = dot(jnp.concatenate(weights, axis=0), beside(to_channels_ref))
-    for i in range(frames):
-        part = spread[i * cells : (i + 1) * cells]
-        wide = part[:, :full] * values[0]
+    for i in range(part):
+        share = spread[i * cells : (i + 1) * cells]
+        wide = share[:, :full] * values[0]
         for j in range(1, frames):
-            wide = wide + part[:, j * full : (j + 1) * full] * values[j]
-        tail = part[:, frames * full :] * values[frames]
+            wide = wide + share[:, j * full : (j + 1) * full] * values[j]
+        tail = share[:, frames * full :] * values[frames]
         tail = tail[:, :LANES] + tail[:, LANES:]
         tail = tail + pltpu.roll(tail, LANES // 2, 1)
         mix_ref[i] = jnp.concatenate([wide, tail], axis=1)
@@ -378,15 +380,23 @@
     return top, total, mix
 
 
-def anchor_kernel(
-    anchor_ref, wkv_ref, to_lanes_ref, to_channels_ref, query_ref, top_ref, sum_ref, mix_ref,
-    top_out, sum_out, mix_out,
-):
+def relay_kernel(order_ref, *refs):
+    count = len(refs) // 2
+    for n in range(count):
+        refs[count + n][...] = refs[n][...]
+    refs[-1][...] = jnp.zeros_like(refs[-1])
+
+
+def anchor_kernel(pieces, anchor_ref, wkv_ref, to_lanes_ref, to_channels_ref, query_ref, *refs):
+    top, total, mix = (
+        jnp.concatenate([ref[...] for ref in refs[v * pieces : (v + 1) * pieces]], axis=0)
+        for v in range(3)
+    )
     new = updated(
         keys_and_values(anchor_ref, wkv_ref, query_ref.shape[2]), to_lanes_ref, to_channels_ref,
-        query_ref[...], top_ref[...], sum_ref[...], mix_ref[...], False,
+        query_ref[...], top, total, mix, False,
     )
-    for ref, v in zip((top_out, sum_out, mix_out), new):
+    for ref, v in zip(refs[3 * pieces :], new):
         ref[...] = v.reshape(ref.shape)
 
 
@@ -419,10 +429,6 @@
     pairs = [[(i, i + 1) for i in range(start, count - 1, 2)] for start in (1, 0)]
     pairs = [up + [(j, i) for i, j in up] for up in pairs]
     return lax.ppermute(odd, axis, pairs[0]), lax.ppermute(even, axis, pairs[1])
-
-
-def swap_order(s):
-    return (s.bit_length(), -s)
 
 
 def on_device(
@@ -480,8 +486,9 @@
         chosen_kernel, [((count, packed, LANES), BF)], [VMEM] * 7, flops=3 * cells * one
     )(anchor_index, clip_odd, clip_even, spatial, hidden, g3, temporal_w)
     clips = lax.axis_size("clip")
-    if clips & (clips - 1) == 0:
-        routes = [[(i, i ^ s) for i in range(clips)] for s in sorted(range(1, clips), key=swap_order)]
+    powers = clips & (clips - 1) == 0
+    if powers:
+        routes = [[(i, i ^ s) for i in range(clips)] for s in range(1, clips, 2)]
     else:
         routes = [[(i, (i + s) % clips) for i in range(clips)] for s in range(1, clips)]
     arrived = [lax.ppermute(chosen, "clip", route) for route in routes]
@@ -492,16 +499,42 @@
         flops=6 * frames * cells * one,
         limit=32,
     )(clip_odd, clip_even, spatial, hidden, g3, temporal_w, w_query, w_keyval)
+    maps = head_maps(frames, channels)
+    split = frames // 2 if frames > 1 else frames
+
+    def local(start, part, after):
+        shape = (part, cells)
+        return call(
+            functools.partial(local_kernel, start),
+            [(shape + (LANES,), F32)] * 2 + [(shape + (lanes_up,), F32), ((8, LANES), F32)],
+            [VMEM] * 7,
+            flops=10 * part * cells * one,
+            limit=32,
+        )(anchor_index, window, query, keyval, *maps, after)
+
+    *early, after = local(0, split, order)
+    if powers and clips > 2:
+        *relayed, after = call(
+            relay_kernel,
+            [(chosen.shape, BF)] * (clips // 2 - 1) + [((8, LANES), F32)],
+            [VMEM] * (clips // 2),
+        )(after, *arrived[1:])
+        arrived += [lax.ppermute(v, "clip", routes[0]) for v in relayed]
+    *late, after = local(split, frames - split, after)
+    pieces = 2
+    state = [v for pair in zip(early, late) for v in pair]
     states = [((frames, cells, LANES), F32)] * 2 + [((frames, cells, lanes_up), F32)]
-    state = call(
-        local_kernel, states, [VMEM] * 6, flops=10 * frames * cells * one, limit=32
-    )(anchor_index, window, query, keyval, *head_maps(frames, channels))
     to_lanes, _ = head_maps(1, channels, everywhere=True)
     _, to_channels = head_maps(2, channels)
     for arrival in arrived[:-1]:
         state = call(
-            anchor_kernel, states, [VMEM] * 8, flops=4 * frames * cells * one, limit=32
+            functools.partial(anchor_kernel, pieces),
+            states,
+            [VMEM] * (5 + 3 * pieces),
+            flops=4 * frames * cells * one,
+            limit=32,
         )(arrival, w_keyval, to_lanes, to_channels, query, *state)
+        pieces = 1
     (out,) = call(
         last_kernel,
         [(latents.shape, BF)],

time: 45.9 us -> 42.9 us (0.935)
  waiting for transfers between devices: 6.26 us -> 1.86 us
  starting transfers between devices: 13.9 us -> 14.7 us
  Pallas kernels: 22.4 us -> 23 us
    ppermute x3 -> x2, waiting for transfers between devices: 6.25 us -> 1.84 us  [on_device(): arrived = [lax.ppermute(chosen, 'clip', route) for route in routes]]
    ppermute x0 -> x1, starting transfers between devices: none -> 1.34 us  [on_device(): arrived += [lax.ppermute(v, 'clip', routes[0]) for v in relayed]]
    pallas_call x3 -> x5, Pallas kernels: 6.75 us -> 7.32 us  [the longest x2 4.5 us: local(): call(functools.partial(local_kernel, start), [(shape + (LANES,), F32)] *...]
    ppermute x3 -> x2, starting transfers between devices: 3.55 us -> 3.06 us  [on_device(): arrived = [lax.ppermute(chosen, 'clip', route) for route in routes]]
  transfers between devices with their start and end apart: 7 -> 7, of which waited for: 2 -> 1; matrix products, arithmetic and copies ran while one was open for 0% -> 0% of each run, Pallas kernels for 38% -> 42%
where the time goes in v8:
time: 42.9 us; the launch traced here: 42.7 us
  Pallas kernels  23 us (54%)
  starting transfers between devices  14.7 us (34%)
  waiting for transfers between devices  1.86 us (4%)
  between operations  1.73 us (4%)
  local copies, waits for them, and re-layouts  1.42 us (3%)
    ppermute x2, starting transfers between devices, swapped(): lax.ppermute(even, axis, pairs[1])  8.81 us
    pallas_call x2, Pallas kernels, local(): call(functools.partial(local_kernel, start), [(shape + (LANES,), F32)] *...  4.5 us
    pallas_call x1, Pallas kernels, on_device(): call(temporal_kernel, [(some, BF), (some, BF), ((frames, cells, 2 * chann...  4.2 us
    pallas_call x1, Pallas kernels, on_device(): call(inner_kernel, [(some, BF), (some, BF)], [VMEM] * 9, [inner_col], flo...  3.69 us
    ppermute x2, starting transfers between devices, on_device(): arrived = [lax.ppermute(chosen, 'clip', route) for route in routes]  3.06 us
    pallas_call x1, Pallas kernels, on_device(): call(outer_kernel, [(middle, BF), (middle, BF), ((2, 2, width, channels),...  2.87 us
    pallas_call x2, Pallas kernels, on_device(): call(functools.partial(anchor_kernel, pieces), states, [VMEM] * (5 + 3 *...  2.81 us
    pallas_call x1, Pallas kernels, on_device(): call(last_kernel, [(latents.shape, BF)], [VMEM] * 10, [pltpu.VMEM(latents...  2.74 us
  transfers between devices with their start and end apart: 7, of which 1 were waited for; matrix products, arithmetic and copies ran while one was open for 0% of the time, Pallas kernels for 42%

profile of v8, /device:TPU:0, one launch (start us, length us, event | category | flops | bytes accessed | tf_op | source)
XLA Modules:
  0.0 42.7 jit_solution(7526967498400187745)
XLA Ops:
  0.0 0.0 copy-start
  0.0 1.3 %copy-done.3 = bf16[4,5,64,320]{3,2,1,0:T(8,128)(2,1)S(1)} copy-done((bf16[4,5,64,320]{3,2,1,0:T(8,128)(2,1)S(1)}, bf16[4,5,64,320]{3,2,1,0:T(8,128)(2,1)}, u32[]{:S(2)}) %copy-start.3) | copy-done | bytes 819224
  1.4 0.1 shard_map.146
  1.5 0.7 %collective-permute-start = (bf16[640,128]{1,0:T(8,128)(2,1)S(1)}, bf16[640,128]{1,0:T(8,128)(2,1)S(1)}, u32[]{:S(2)}, u32[]{:S(2)}) collective-permute-start(bf16[640,128]{1,0:T(8,128)(2,1)S(1)} %get-tuple-element.37), channel_id=1, source_target_pairs={{1,2},{2,1},{5,6},{6,5},{9,10},{10,9},{13,14},{14,13},{17,18},{18,... | collective-permute-start | bytes 491528 | tf_op jit(solution)/shard_map/ppermute | solution.py:431
  2.1 4.4 %collective-permute-start.1 = (bf16[640,128]{1,0:T(8,128)(2,1)S(1)}, bf16[640,128]{1,0:T(8,128)(2,1)S(1)}, u32[]{:S(2)}, u32[]{:S(2)}) collective-permute-start(bf16[640,128]{1,0:T(8,128)(2,1)S(1)} %get-tuple-element.38), channel_id=1, source_target_pairs={{0,1},{2,3},{1,0},{3,2},{4,5},{6,7},{5,4},{7,6},{8,9},{10,11},{9,8... | collective-permute-start | bytes 491528 | tf_op jit(solution)/shard_map/ppermute | solution.py:431
  6.5 0.0 copy-done
  6.5 0.0 copy-done.8
  6.5 0.0 copy-done.9
  6.5 2.9 %shard_map.145 = (bf16[2,192,320]{2,1,0:T(8,128)(2,1)S(1)}, bf16[2,192,320]{2,1,0:T(8,128)(2,1)S(1)}, f32[2,2,64,320]{3,2,1,0:T(8,128)S(1)}, bf16[960,192]{1,0:T(8,128)(2,1)S(1)}, f32[8,128]{1,0:T(8,128)S(1)}) custom-call(bf16[4,5,64,320]{3,2,1,0:T(8,128)(2,1)S(1)} %copy-done.3, f32[320]{0:T(512)S(1)} %copy-done.8, f32[320]{0:T(512)S(1)} %copy-done.9, ...), custom_call_target="tpu_custom_call" | custom-call | flops 1179648000 | bytes 2097152 | tf_op jit(solution)/shard_map/pallas_call | solution.py:458
  9.4 0.0 collective-permute-done.odd_ref
  9.4 0.0 collective-permute-done.1.even_ref
  9.4 0.0 copy-start.4
  9.4 1.2 %shard_map.147 = (bf16[2,320,320]{2,1,0:T(8,128)(2,1)S(1)}, bf16[2,320,320]{2,1,0:T(8,128)(2,1)S(1)}, bf16[800,128]{1,0:T(8,128)(2,1)S(1)}, bf16[800,128]{1,0:T(8,128)(2,1)S(1)}) custom-call(f32[2,2,64,320]{3,2,1,0:T(8,128)S(1)} %get-tuple-element.36.edge_ref, bf16[640,128]{1,0:T(8,128)(2,1)S(1)} %collective-permute-done.odd_ref, ...), custom_call_target="tpu_custom_call" | custom-call | flops 157286400 | bytes 2097152 | tf_op jit(solution)/shard_map/pallas_call | solution.py:471
  10.6 0.9 %collective-permute-start.2 = (bf16[800,128]{1,0:T(8,128)(2,1)S(1)}, bf16[800,128]{1,0:T(8,128)(2,1)S(1)}, u32[]{:S(2)}, u32[]{:S(2)}) collective-permute-start(bf16[800,128]{1,0:T(8,128)(2,1)S(1)} %get-tuple-element.43), channel_id=1, source_target_pairs={{4,8},{8,4},{5,9},{9,5},{6,10},{10,6},{7,11},{11,7},{20,24},{24,20... | collective-permute-start | bytes 614408 | tf_op jit(solution)/shard_map/ppermute | solution.py:431
  11.4 4.5 %collective-permute-start.3 = (bf16[800,128]{1,0:T(8,128)(2,1)S(1)}, bf16[800,128]{1,0:T(8,128)(2,1)S(1)}, u32[]{:S(2)}, u32[]{:S(2)}) collective-permute-start(bf16[800,128]{1,0:T(8,128)(2,1)S(1)} %get-tuple-element.44), channel_id=1, source_target_pairs={{0,4},{8,12},{4,0},{12,8},{1,5},{9,13},{5,1},{13,9},{2,6},{10,14},... | collective-permute-start | bytes 614408 | tf_op jit(solution)/shard_map/ppermute | solution.py:431
  17.2 0.0 copy-done.4
  17.2 0.0 copy-start.5
  17.2 0.0 copy-start.10
  17.2 3.7 %shard_map.148 = (bf16[4,320,320]{2,1,0:T(8,128)(2,1)S(1)}, bf16[4,320,320]{2,1,0:T(8,128)(2,1)S(1)}) custom-call(bf16[4,5,64,320]{3,2,1,0:T(8,128)(2,1)S(1)} %copy-done.4, bf16[640,128]{1,0:T(8,128)(2,1)S(1)} %collective-permute-done.odd_ref, bf16[640,128]{1,0:T(8,128)(2,1)S(1)} %collective-permute-done.1.even_ref, f32[320]{0:T(512)S(1)} %copy-done.8, ...), custom_call_target="tpu_custom_call" | custom-call | flops 1179648000 | bytes 2097152 | tf_op jit(solution)/shard_map/pallas_call | solution.py:478
  20.9 0.0 copy-start.1
  20.9 0.0 copy-start.11
  20.9 0.0 collective-permute-done.2.odd_ref
  21.0 0.0 collective-permute-done.3.even_ref
  21.0 0.0 copy-done.5
  21.0 0.0 copy-done.10
  21.0 0.9 %shard_map.151 = bf16[1,800,128]{2,1,0:T(8,128)(2,1)S(1)} custom-call(s32[1,1]{1,0:T(1,128)S(6)} %copy.16.picks_ref, bf16[800,128]{1,0:T(8,128)(2,1)S(1)} %collective-permute-done.2.odd_ref, bf16[800,128]{1,0:T(8,128)(2,1)S(1)} %collective-permute-done.3.even_ref, bf16[4,320,320]{2,1,0:T(8,128)(2,1)S(1)} %get-tuple-element.47.spatial_ref, ...), custom_call_target="tpu_custom_call" | custom-call | flops 196608000 | bytes 2097152 | tf_op jit(solution)/shard_map/pallas_call | solution.py:485
  21.9 0.0 copy-start.12
  21.9 0.0 copy-start.13
  21.9 1.7 %collective-permute-start.6 = (bf16[1,800,128]{2,1,0:T(8,128)(2,1)S(1)}, bf16[1,800,128]{2,1,0:T(8,128)(2,1)S(1)}, u32[]{:S(2)}, u32[]{:S(2)}) collective-permute-start(bf16[1,800,128]{2,1,0:T(8,128)(2,1)S(1)} %shard_map.151), channel_id=1, source_target_pairs={{0,4},{4,0},{8,12},{12,8},{1,5},{5,1},{9,13},{13,9},{2,6},{6,2},{1... | collective-permute-start | bytes 614408 | tf_op jit(solution)/shard_map/ppermute | solution.py:494
  23.6 1.3 %collective-permute-start.4 = (bf16[1,800,128]{2,1,0:T(8,128)(2,1)S(1)}, bf16[1,800,128]{2,1,0:T(8,128)(2,1)S(1)}, u32[]{:S(2)}, u32[]{:S(2)}) collective-permute-start(bf16[1,800,128]{2,1,0:T(8,128)(2,1)S(1)} %shard_map.151), channel_id=1, source_target_pairs={{0,12},{4,8},{8,4},{12,0},{1,13},{5,9},{9,5},{13,1},{2,14},{6,10},... | collective-permute-start | bytes 614408 | tf_op jit(solution)/shard_map/ppermute | solution.py:494
  25.0 0.0 copy-done.1
  25.0 0.0 copy-done.11
  25.0 4.2 %shard_map.149 = (bf16[4,320,320]{2,1,0:T(8,128)(2,1)S(1)}, bf16[4,320,320]{2,1,0:T(8,128)(2,1)S(1)}, bf16[4,320,640]{2,1,0:T(8,128)(2,1)S(1)}) custom-call(bf16[800,128]{1,0:T(8,128)(2,1)S(1)} %collective-permute-done.2.odd_ref, bf16[800,128]{1,0:T(8,128)(2,1)S(1)} %collective-permute-done.3.even_ref, ...), custom_call_target="tpu_custom_call" | custom-call | flops 1572864000 | bytes 2097152 | tf_op jit(solution)/shard_map/pallas_call | solution.py:495
  29.2 0.0 copy-done.12
  29.2 0.0 copy-done.13
  29.2 2.2 %shard_map.150 = (f32[2,320,128]{2,1,0:T(8,128)S(1)}, f32[2,320,128]{2,1,0:T(8,128)S(1)}, f32[2,320,384]{2,1,0:T(8,128)S(1)}, f32[8,128]{1,0:T(8,128)S(1)}) custom-call(s32[1,1]{1,0:T(1,128)S(6)} %copy.16.picks_ref, s32[1]{0:T(128)S(6)} %copy.17.window_ref, bf16[4,320,320]{2,1,0:T(8,128)(2,1)S(1)} %get-tuple-element.49.query_ref, ...), custom_call_target="tpu_custom_call" | custom-call | flops 1310720000 | bytes 2097152 | tf_op jit(solution)/shard_map/pallas_call | solution.py:507
  31.5 1.8 %collective-permute-done.4.refs_0_.anchor_ref = bf16[1,800,128]{2,1,0:T(8,128)(2,1)S(1)} collective-permute-done((bf16[1,800,128]{2,1,0:T(8,128)(2,1)S(1)}, bf16[1,800,128]{2,1,0:T(8,128)(2,1)S(1)}, u32[]{:S(2)}, u32[]{:S(2)}) %collective-permute-start.4) | collective-permute-done | bytes 204832 | tf_op jit(solution)/shard_map/ppermute | solution.py:494
  33.3 1.3 %collective-permute-start.5 = (bf16[1,800,128]{2,1,0:T(8,128)(2,1)S(1)}, bf16[1,800,128]{2,1,0:T(8,128)(2,1)S(1)}, u32[]{:S(2)}, u32[]{:S(2)}) collective-permute-start(bf16[1,800,128]{2,1,0:T(8,128)(2,1)S(1)} %get-tuple-element.52), channel_id=1, source_target_pairs={{0,4},{4,0},{8,12},{12,8},{1,5},{5,1},{9,13},{13,9},{2,6},{6,2},{1... | collective-permute-start | bytes 614408 | tf_op jit(solution)/shard_map/ppermute | solution.py:522
  34.7 2.2 %shard_map.153 = (f32[2,320,128]{2,1,0:T(8,128)S(1)}, f32[2,320,128]{2,1,0:T(8,128)S(1)}, f32[2,320,384]{2,1,0:T(8,128)S(1)}, f32[8,128]{1,0:T(8,128)}) custom-call(s32[1,1]{1,0:T(1,128)S(6)} %copy.16.picks_ref, s32[1]{0:T(128)S(6)} %copy.17.window_ref, bf16[4,320,320]{2,1,0:T(8,128)(2,1)S(1)} %get-tuple-element.49.query_ref, ...), custom_call_target="tpu_custom_call" | custom-call | flops 1310720000 | bytes 2097152 | tf_op jit(solution)/shard_map/pallas_call | solution.py:507
  36.9 0.0 collective-permute-done.6.anchor_ref
  36.9 0.0 copy-done.2
  37.0 0.0 copy-done.6
  37.0 1.5 %shard_map.154 = (f32[4,320,128]{2,1,0:T(8,128)S(1)}, f32[4,320,128]{2,1,0:T(8,128)S(1)}, f32[4,320,384]{2,1,0:T(8,128)S(1)}) custom-call(bf16[1,800,128]{2,1,0:T(8,128)(2,1)S(1)} %collective-permute-done.6.anchor_ref, bf16[320,640]{1,0:T(8,128)(2,1)S(1)} %copy-done.1, bf16[320,128]{1,0:T(8,128)(2,1)S(1)} %copy-done.6, bf16[640,128]{1,0:T(8,128)(2,1)S(1)} %copy-done.2, ...), custom_call_target="tpu_custom_call" | custom-call | flops 1048576000 | bytes 2097152 | tf_op jit(solution)/shard_map/pallas_call | solution.py:530
  38.5 0.0 copy-start.7
  38.5 1.3 %shard_map.155 = (f32[4,320,128]{2,1,0:T(8,128)S(1)}, f32[4,320,128]{2,1,0:T(8,128)S(1)}, f32[4,320,384]{2,1,0:T(8,128)S(1)}) custom-call(bf16[1,800,128]{2,1,0:T(8,128)(2,1)S(1)} %collective-permute-done.4.refs_0_.anchor_ref, bf16[320,640]{1,0:T(8,128)(2,1)S(1)} %copy-done.1, bf16[320,128]{1,0:T(8,128)(2,1)S(1)} %copy-done.6, ...), custom_call_target="tpu_custom_call" | custom-call | flops 1048576000 | bytes 2097152 | tf_op jit(solution)/shard_map/pallas_call | solution.py:530
  39.8 0.0 collective-permute-done.5.anchor_ref
  39.8 0.0 copy-done.7
  39.8 2.7 %shard_map.156 = bf16[4,5,64,320]{3,2,1,0:T(8,128)(2,1)} custom-call(bf16[1,800,128]{2,1,0:T(8,128)(2,1)S(1)} %collective-permute-done.5.anchor_ref, bf16[320,640]{1,0:T(8,128)(2,1)S(1)} %copy-done.1, bf16[320,128]{1,0:T(8,128)(2,1)S(1)} %copy-done.6, bf16[640,128]{1,0:T(8,128)(2,1)S(1)} %copy-done.2, bf16[4,320,320]{2,1,0:T(8,128)(2,1)S(1)} %get-tuple-element.49.query_ref, ...), custom_call_target="tpu_custom_call" | custom-call | flops 1310720000 | bytes 2097152 | tf_op jit(solution)/shard_map/pallas_call | solution.py:538
  (6 shorter events, 0.0 us)
Async XLA Ops:
  0.0 6.5 %copy-start = (bf16[3,3,320,320]{3,2,1,0:T(8,128)(2,1)S(1)}, bf16[3,3,320,320]{3,2,1,0:T(8,128)(2,1)}, u32[]{:S(2)}) copy-start(bf16[3,3,320,320]{3,2,1,0:T(8,128)(2,1)} %param.19) | copy-start | bytes 5529604
  0.0 1.4 %copy-start.3 = (bf16[4,5,64,320]{3,2,1,0:T(8,128)(2,1)S(1)}, bf16[4,5,64,320]{3,2,1,0:T(8,128)(2,1)}, u32[]{:S(2)}) copy-start(bf16[4,5,64,320]{3,2,1,0:T(8,128)(2,1)} %x_ref.5) | copy-start | bytes 2457604
  1.4 5.1 %copy-start.8 = (f32[320]{0:T(512)S(1)}, f32[320]{0:T(512)}, u32[]{:S(2)}) copy-start(f32[320]{0:T(512)} %g1_ref.5) | copy-start | bytes 3844
  1.4 5.1 %copy-start.9 = (f32[320]{0:T(512)S(1)}, f32[320]{0:T(512)}, u32[]{:S(2)}) copy-start(f32[320]{0:T(512)} %g2_ref.5) | copy-start | bytes 3844
  1.5 7.9 %collective-permute-start = (bf16[640,128]{1,0:T(8,128)(2,1)S(1)}, bf16[640,128]{1,0:T(8,128)(2,1)S(1)}, u32[]{:S(2)}, u32[]{:S(2)}) collective-permute-start(bf16[640,128]{1,0:T(8,128)(2,1)S(1)} %get-tuple-element.37), channel_id=1, source_target_pairs={{1,2},{2,1},{5,6},{6,5},{9,10},{10,9},{13,14},{14,13},{17,18},{18,... | collective-permute-start | bytes 491528 | tf_op jit(solution)/shard_map/ppermute | solution.py:431
  2.1 7.3 %collective-permute-start.1 = (bf16[640,128]{1,0:T(8,128)(2,1)S(1)}, bf16[640,128]{1,0:T(8,128)(2,1)S(1)}, u32[]{:S(2)}, u32[]{:S(2)}) collective-permute-start(bf16[640,128]{1,0:T(8,128)(2,1)S(1)} %get-tuple-element.38), channel_id=1, source_target_pairs={{0,1},{2,3},{1,0},{3,2},{4,5},{6,7},{5,4},{7,6},{8,9},{10,11},{9,8... | collective-permute-start | bytes 491528 | tf_op jit(solution)/shard_map/ppermute | solution.py:431
  9.4 7.8 %copy-start.4 = (bf16[4,5,64,320]{3,2,1,0:T(8,128)(2,1)S(1)}, bf16[4,5,64,320]{3,2,1,0:T(8,128)(2,1)}, u32[]{:S(2)}) copy-start(bf16[4,5,64,320]{3,2,1,0:T(8,128)(2,1)} %x_ref.5) | copy-start | bytes 2457604
  10.6 10.4 %collective-permute-start.2 = (bf16[800,128]{1,0:T(8,128)(2,1)S(1)}, bf16[800,128]{1,0:T(8,128)(2,1)S(1)}, u32[]{:S(2)}, u32[]{:S(2)}) collective-permute-start(bf16[800,128]{1,0:T(8,128)(2,1)S(1)} %get-tuple-element.43), channel_id=1, source_target_pairs={{4,8},{8,4},{5,9},{9,5},{6,10},{10,6},{7,11},{11,7},{20,24},{24,20... | collective-permute-start | bytes 614408 | tf_op jit(solution)/shard_map/ppermute | solution.py:431
  11.4 9.5 %collective-permute-start.3 = (bf16[800,128]{1,0:T(8,128)(2,1)S(1)}, bf16[800,128]{1,0:T(8,128)(2,1)S(1)}, u32[]{:S(2)}, u32[]{:S(2)}) collective-permute-start(bf16[800,128]{1,0:T(8,128)(2,1)S(1)} %get-tuple-element.44), channel_id=1, source_target_pairs={{0,4},{8,12},{4,0},{12,8},{1,5},{9,13},{5,1},{13,9},{2,6},{10,14},... | collective-permute-start | bytes 614408 | tf_op jit(solution)/shard_map/ppermute | solution.py:431
  17.2 3.8 %copy-start.5 = (bf16[3,320,320]{2,1,0:T(8,128)(2,1)S(1)}, bf16[3,320,320]{2,1,0:T(8,128)(2,1)}, u32[]{:S(2)}) copy-start(bf16[3,320,320]{2,1,0:T(8,128)(2,1)} %wt_ref.3) | copy-start | bytes 1843204
  17.2 3.8 %copy-start.10 = (f32[320]{0:T(512)S(1)}, f32[320]{0:T(512)}, u32[]{:S(2)}) copy-start(f32[320]{0:T(512)} %g3_ref.3) | copy-start | bytes 3844
  20.9 4.1 %copy-start.1 = (bf16[320,640]{1,0:T(8,128)(2,1)S(1)}, bf16[320,640]{1,0:T(8,128)(2,1)}, u32[]{:S(2)}) copy-start(bf16[320,640]{1,0:T(8,128)(2,1)} %wkv_ref.7) | copy-start | bytes 1228804
  20.9 4.1 %copy-start.11 = (bf16[320,320]{1,0:T(8,128)(2,1)S(1)}, bf16[320,320]{1,0:T(8,128)(2,1)}, u32[]{:S(2)}) copy-start(bf16[320,320]{1,0:T(8,128)(2,1)} %wq_ref.1) | copy-start | bytes 614404
  21.9 7.3 %copy-start.12 = (bf16[1280,128]{1,0:T(8,128)(2,1)S(1)}, bf16[1280,128]{1,0:T(8,128)(2,1)}, u32[]{:S(2)}) copy-start(bf16[1280,128]{1,0:T(8,128)(2,1)} %constant.9.clone.to_channels_ref) | copy-start | bytes 983044
  21.9 7.3 %copy-start.13 = (bf16[1280,128]{1,0:T(8,128)(2,1)S(1)}, bf16[1280,128]{1,0:T(8,128)(2,1)}, u32[]{:S(2)}) copy-start(bf16[1280,128]{1,0:T(8,128)(2,1)} %constant.8.clone.to_lanes_ref) | copy-start | bytes 983044
  21.9 15.0 %collective-permute-start.6 = (bf16[1,800,128]{2,1,0:T(8,128)(2,1)S(1)}, bf16[1,800,128]{2,1,0:T(8,128)(2,1)S(1)}, u32[]{:S(2)}, u32[]{:S(2)}) collective-permute-start(bf16[1,800,128]{2,1,0:T(8,128)(2,1)S(1)} %shard_map.151), channel_id=1, source_target_pairs={{0,4},{4,0},{8,12},{12,8},{1,5},{5,1},{9,13},{13,9},{2,6},{6,2},{1... | collective-permute-start | bytes 614408 | tf_op jit(solution)/shard_map/ppermute | solution.py:494
  23.6 9.7 %collective-permute-start.4 = (bf16[1,800,128]{2,1,0:T(8,128)(2,1)S(1)}, bf16[1,800,128]{2,1,0:T(8,128)(2,1)S(1)}, u32[]{:S(2)}, u32[]{:S(2)}) collective-permute-start(bf16[1,800,128]{2,1,0:T(8,128)(2,1)S(1)} %shard_map.151), channel_id=1, source_target_pairs={{0,12},{4,8},{8,4},{12,0},{1,13},{5,9},{9,5},{13,1},{2,14},{6,10},... | collective-permute-start | bytes 614408 | tf_op jit(solution)/shard_map/ppermute | solution.py:494
  33.3 6.5 %collective-permute-start.5 = (bf16[1,800,128]{2,1,0:T(8,128)(2,1)S(1)}, bf16[1,800,128]{2,1,0:T(8,128)(2,1)S(1)}, u32[]{:S(2)}, u32[]{:S(2)}) collective-permute-start(bf16[1,800,128]{2,1,0:T(8,128)(2,1)S(1)} %get-tuple-element.52), channel_id=1, source_target_pairs={{0,4},{4,0},{8,12},{12,8},{1,5},{5,1},{9,13},{13,9},{2,6},{6,2},{1... | collective-permute-start | bytes 614408 | tf_op jit(solution)/shard_map/ppermute | solution.py:522
  34.7 2.3 %copy-start.2 = (bf16[640,128]{1,0:T(8,128)(2,1)S(1)}, bf16[640,128]{1,0:T(8,128)(2,1)}, u32[]{:S(2)}) copy-start(bf16[640,128]{1,0:T(8,128)(2,1)} %constant.11.clone.to_channels_ref) | copy-start | bytes 491524
  34.7 2.3 %copy-start.6 = (bf16[320,128]{1,0:T(8,128)(2,1)S(1)}, bf16[320,128]{1,0:T(8,128)(2,1)}, u32[]{:S(2)}) copy-start(bf16[320,128]{1,0:T(8,128)(2,1)} %constant.10.clone.to_lanes_ref) | copy-start | bytes 245764
  38.5 1.3 %copy-start.7 = (bf16[320,320]{1,0:T(8,128)(2,1)S(1)}, bf16[320,320]{1,0:T(8,128)(2,1)}, u32[]{:S(2)}) copy-start(bf16[320,320]{1,0:T(8,128)(2,1)} %wo_ref.1) | copy-start | bytes 614404

commit v9 on v8

--- a/solution.py
+++ b/solution.py
@@ -380,6 +380,10 @@
     return top, total, mix
 
 
+def copy_kernel(from_ref, to_ref):
+    to_ref[...] = from_ref[...]
+
+
 def relay_kernel(order_ref, *refs):
     count = len(refs) // 2
     for n in range(count):
@@ -491,7 +495,9 @@
         routes = [[(i, i ^ s) for i in range(clips)] for s in range(1, clips, 2)]
     else:
         routes = [[(i, (i + s) % clips) for i in range(clips)] for s in range(1, clips)]
-    arrived = [lax.ppermute(chosen, "clip", route) for route in routes]
+    (near,) = call(copy_kernel, [(chosen.shape, BF)], [VMEM])(chosen)
+    sent = [near] + [chosen] * (len(routes) - 1)
+    arrived = [lax.ppermute(v, "clip", route) for v, route in zip(sent, routes)]
     temporal, query, keyval = call(
         temporal_kernel,
         [(some, BF), (some, BF), ((frames, cells, 2 * channels), BF)],

time: 42.9 us -> 42.2 us (0.984)
  waiting for transfers between devices: 1.86 us -> 1.23 us
    ppermute x2, starting transfers between devices: 3.06 us -> 2.17 us  [on_device(): arrived = [lax.ppermute(v, 'clip', route) for v, route in zip(sent, routes)]]
    ppermute x1, starting transfers between devices: 1.34 us -> 2.14 us  [on_device(): arrived += [lax.ppermute(v, 'clip', routes[0]) for v in relayed]]
    ppermute x2, waiting for transfers between devices: 1.84 us -> 1.22 us  [on_device(): arrived = [lax.ppermute(v, 'clip', route) for v, route in zip(sent, routes)]]
  transfers between devices with their start and end apart: 7 -> 7, of which waited for: 1 -> 1; matrix products, arithmetic and copies ran while one was open for 0% -> 0% of each run, Pallas kernels for 42% -> 43%
where the time goes in v9:
time: 42.2 us; the launch traced here: 42.1 us
  Pallas kernels  23 us (55%)
  starting transfers between devices  14.6 us (35%)
  between operations  1.74 us (4%)
  local copies, waits for them, and re-layouts  1.42 us (3%)
  waiting for transfers between devices  1.23 us (3%)
    ppermute x2, starting transfers between devices, swapped(): lax.ppermute(even, axis, pairs[1])  8.81 us
    pallas_call x2, Pallas kernels, local(): call(functools.partial(local_kernel, start), [(shape + (LANES,), F32)] *...  4.5 us
    pallas_call x1, Pallas kernels, on_device(): call(temporal_kernel, [(some, BF), (some, BF), ((frames, cells, 2 * chann...  4.21 us
    pallas_call x1, Pallas kernels, on_device(): call(inner_kernel, [(some, BF), (some, BF)], [VMEM] * 9, [inner_col], flo...  3.69 us
    pallas_call x1, Pallas kernels, on_device(): call(outer_kernel, [(middle, BF), (middle, BF), ((2, 2, width, channels),...  2.87 us
    pallas_call x2, Pallas kernels, on_device(): call(functools.partial(anchor_kernel, pieces), states, [VMEM] * (5 + 3 *...  2.82 us
    pallas_call x1, Pallas kernels, on_device(): call(last_kernel, [(latents.shape, BF)], [VMEM] * 10, [pltpu.VMEM(latents...  2.74 us
    ppermute x2, starting transfers between devices, on_device(): arrived = [lax.ppermute(v, 'clip', route) for v, route in zip(sent, routes)]  2.17 us
  transfers between devices with their start and end apart: 7, of which 1 were waited for; matrix products, arithmetic and copies ran while one was open for 0% of the time, Pallas kernels for 43%

profile of v9, /device:TPU:0, one launch (start us, length us, event | category | flops | bytes accessed | tf_op | source)
XLA Modules:
  0.0 42.1 jit_solution(9077327227655056)
XLA Ops:
  0.0 0.0 copy-start
  0.0 1.3 %copy-done.3 = bf16[4,5,64,320]{3,2,1,0:T(8,128)(2,1)S(1)} copy-done((bf16[4,5,64,320]{3,2,1,0:T(8,128)(2,1)S(1)}, bf16[4,5,64,320]{3,2,1,0:T(8,128)(2,1)}, u32[]{:S(2)}) %copy-start.3) | copy-done | bytes 819224
  1.4 0.1 shard_map.146
  1.5 0.7 %collective-permute-start = (bf16[640,128]{1,0:T(8,128)(2,1)S(1)}, bf16[640,128]{1,0:T(8,128)(2,1)S(1)}, u32[]{:S(2)}, u32[]{:S(2)}) collective-permute-start(bf16[640,128]{1,0:T(8,128)(2,1)S(1)} %get-tuple-element.37), channel_id=1, source_target_pairs={{1,2},{2,1},{5,6},{6,5},{9,10},{10,9},{13,14},{14,13},{17,18},{18,... | collective-permute-start | bytes 491528 | tf_op jit(solution)/shard_map/ppermute | solution.py:435
  2.1 4.4 %collective-permute-start.1 = (bf16[640,128]{1,0:T(8,128)(2,1)S(1)}, bf16[640,128]{1,0:T(8,128)(2,1)S(1)}, u32[]{:S(2)}, u32[]{:S(2)}) collective-permute-start(bf16[640,128]{1,0:T(8,128)(2,1)S(1)} %get-tuple-element.38), channel_id=1, source_target_pairs={{0,1},{2,3},{1,0},{3,2},{4,5},{6,7},{5,4},{7,6},{8,9},{10,11},{9,8... | collective-permute-start | bytes 491528 | tf_op jit(solution)/shard_map/ppermute | solution.py:435
  6.5 0.0 copy-done
  6.5 0.0 copy-done.8
  6.5 0.0 copy-done.9
  6.5 2.9 %shard_map.145 = (bf16[2,192,320]{2,1,0:T(8,128)(2,1)S(1)}, bf16[2,192,320]{2,1,0:T(8,128)(2,1)S(1)}, f32[2,2,64,320]{3,2,1,0:T(8,128)S(1)}, bf16[960,192]{1,0:T(8,128)(2,1)S(1)}, f32[8,128]{1,0:T(8,128)S(1)}) custom-call(bf16[4,5,64,320]{3,2,1,0:T(8,128)(2,1)S(1)} %copy-done.3, f32[320]{0:T(512)S(1)} %copy-done.8, f32[320]{0:T(512)S(1)} %copy-done.9, ...), custom_call_target="tpu_custom_call" | custom-call | flops 1179648000 | bytes 2097152 | tf_op jit(solution)/shard_map/pallas_call | solution.py:462
  9.4 0.0 collective-permute-done.odd_ref
  9.4 0.0 collective-permute-done.1.even_ref
  9.4 0.0 copy-start.4
  9.4 1.2 %shard_map.147 = (bf16[2,320,320]{2,1,0:T(8,128)(2,1)S(1)}, bf16[2,320,320]{2,1,0:T(8,128)(2,1)S(1)}, bf16[800,128]{1,0:T(8,128)(2,1)S(1)}, bf16[800,128]{1,0:T(8,128)(2,1)S(1)}) custom-call(f32[2,2,64,320]{3,2,1,0:T(8,128)S(1)} %get-tuple-element.36.edge_ref, bf16[640,128]{1,0:T(8,128)(2,1)S(1)} %collective-permute-done.odd_ref, ...), custom_call_target="tpu_custom_call" | custom-call | flops 157286400 | bytes 2097152 | tf_op jit(solution)/shard_map/pallas_call | solution.py:475
  10.6 0.9 %collective-permute-start.2 = (bf16[800,128]{1,0:T(8,128)(2,1)S(1)}, bf16[800,128]{1,0:T(8,128)(2,1)S(1)}, u32[]{:S(2)}, u32[]{:S(2)}) collective-permute-start(bf16[800,128]{1,0:T(8,128)(2,1)S(1)} %get-tuple-element.43), channel_id=1, source_target_pairs={{4,8},{8,4},{5,9},{9,5},{6,10},{10,6},{7,11},{11,7},{20,24},{24,20... | collective-permute-start | bytes 614408 | tf_op jit(solution)/shard_map/ppermute | solution.py:435
  11.4 4.5 %collective-permute-start.3 = (bf16[800,128]{1,0:T(8,128)(2,1)S(1)}, bf16[800,128]{1,0:T(8,128)(2,1)S(1)}, u32[]{:S(2)}, u32[]{:S(2)}) collective-permute-start(bf16[800,128]{1,0:T(8,128)(2,1)S(1)} %get-tuple-element.44), channel_id=1, source_target_pairs={{0,4},{8,12},{4,0},{12,8},{1,5},{9,13},{5,1},{13,9},{2,6},{10,14},... | collective-permute-start | bytes 614408 | tf_op jit(solution)/shard_map/ppermute | solution.py:435
  17.2 0.0 copy-done.4
  17.2 0.0 copy-start.5
  17.2 0.0 copy-start.10
  17.2 3.7 %shard_map.148 = (bf16[4,320,320]{2,1,0:T(8,128)(2,1)S(1)}, bf16[4,320,320]{2,1,0:T(8,128)(2,1)S(1)}) custom-call(bf16[4,5,64,320]{3,2,1,0:T(8,128)(2,1)S(1)} %copy-done.4, bf16[640,128]{1,0:T(8,128)(2,1)S(1)} %collective-permute-done.odd_ref, bf16[640,128]{1,0:T(8,128)(2,1)S(1)} %collective-permute-done.1.even_ref, f32[320]{0:T(512)S(1)} %copy-done.8, ...), custom_call_target="tpu_custom_call" | custom-call | flops 1179648000 | bytes 2097152 | tf_op jit(solution)/shard_map/pallas_call | solution.py:482
  20.9 0.0 copy-start.1
  20.9 0.0 copy-start.11
  20.9 0.0 collective-permute-done.2.odd_ref
  21.0 0.0 collective-permute-done.3.even_ref
  21.0 0.0 copy-done.5
  21.0 0.0 copy-done.10
  21.0 0.9 %shard_map.151.from_ref = bf16[1,800,128]{2,1,0:T(8,128)(2,1)S(1)} custom-call(s32[1,1]{1,0:T(1,128)S(6)} %copy.16.picks_ref, bf16[800,128]{1,0:T(8,128)(2,1)S(1)} %collective-permute-done.2.odd_ref, bf16[800,128]{1,0:T(8,128)(2,1)S(1)} %collective-permute-done.3.even_ref, bf16[4,320,320]{2,1,0:T(8,128)(2,1)S(1)} %get-tuple-element.47.spatial_ref, ...), custom_call_target="tpu_custom_call" | custom-call | flops 196608000 | bytes 2097152 | tf_op jit(solution)/shard_map/pallas_call | solution.py:489
  21.9 0.0 copy-start.12
  21.9 0.0 copy-start.13
  22.0 1.4 %collective-permute-start.4 = (bf16[1,800,128]{2,1,0:T(8,128)(2,1)S(1)}, bf16[1,800,128]{2,1,0:T(8,128)(2,1)S(1)}, u32[]{:S(2)}, u32[]{:S(2)}) collective-permute-start(bf16[1,800,128]{2,1,0:T(8,128)(2,1)S(1)} %shard_map.151.from_ref), channel_id=1, source_target_pairs={{0,12},{4,8},{8,4},{12,0},{1,13},{5,9},{9,5},{13,1},{2,14},{6,10},... | collective-permute-start | bytes 614408 | tf_op jit(solution)/shard_map/ppermute | solution.py:500
  23.4 0.7 %collective-permute-start.6 = (bf16[1,800,128]{2,1,0:T(8,128)(2,1)S(1)}, bf16[1,800,128]{2,1,0:T(8,128)(2,1)S(1)}, u32[]{:S(2)}, u32[]{:S(2)}) collective-permute-start(bf16[1,800,128]{2,1,0:T(8,128)(2,1)S(1)} %shard_map.153), channel_id=1, source_target_pairs={{0,4},{4,0},{8,12},{12,8},{1,5},{5,1},{9,13},{13,9},{2,6},{6,2},{1... | collective-permute-start | bytes 614408 | tf_op jit(solution)/shard_map/ppermute | solution.py:500
  24.1 0.0 copy-done.1
  24.1 0.0 copy-done.11
  24.1 4.2 %shard_map.149 = (bf16[4,320,320]{2,1,0:T(8,128)(2,1)S(1)}, bf16[4,320,320]{2,1,0:T(8,128)(2,1)S(1)}, bf16[4,320,640]{2,1,0:T(8,128)(2,1)S(1)}) custom-call(bf16[800,128]{1,0:T(8,128)(2,1)S(1)} %collective-permute-done.2.odd_ref, bf16[800,128]{1,0:T(8,128)(2,1)S(1)} %collective-permute-done.3.even_ref, ...), custom_call_target="tpu_custom_call" | custom-call | flops 1572864000 | bytes 2097152 | tf_op jit(solution)/shard_map/pallas_call | solution.py:501
  28.3 0.0 copy-done.12
  28.4 0.0 copy-done.13
  28.4 2.3 %shard_map.150 = (f32[2,320,128]{2,1,0:T(8,128)S(1)}, f32[2,320,128]{2,1,0:T(8,128)S(1)}, f32[2,320,384]{2,1,0:T(8,128)S(1)}, f32[8,128]{1,0:T(8,128)S(1)}) custom-call(s32[1,1]{1,0:T(1,128)S(6)} %copy.16.picks_ref, s32[1]{0:T(128)S(6)} %copy.17.window_ref, bf16[4,320,320]{2,1,0:T(8,128)(2,1)S(1)} %get-tuple-element.49.query_ref, ...), custom_call_target="tpu_custom_call" | custom-call | flops 1310720000 | bytes 2097152 | tf_op jit(solution)/shard_map/pallas_call | solution.py:513
  30.6 1.2 %collective-permute-done.4.refs_0_.anchor_ref = bf16[1,800,128]{2,1,0:T(8,128)(2,1)S(1)} collective-permute-done((bf16[1,800,128]{2,1,0:T(8,128)(2,1)S(1)}, bf16[1,800,128]{2,1,0:T(8,128)(2,1)S(1)}, u32[]{:S(2)}, u32[]{:S(2)}) %collective-permute-start.4) | collective-permute-done | bytes 204832 | tf_op jit(solution)/shard_map/ppermute | solution.py:500
  31.9 2.1 %collective-permute-start.5 = (bf16[1,800,128]{2,1,0:T(8,128)(2,1)S(1)}, bf16[1,800,128]{2,1,0:T(8,128)(2,1)S(1)}, u32[]{:S(2)}, u32[]{:S(2)}) collective-permute-start(bf16[1,800,128]{2,1,0:T(8,128)(2,1)S(1)} %get-tuple-element.52), channel_id=1, source_target_pairs={{0,4},{4,0},{8,12},{12,8},{1,5},{5,1},{9,13},{13,9},{2,6},{6,2},{1... | collective-permute-start | bytes 614408 | tf_op jit(solution)/shard_map/ppermute | solution.py:528
  34.0 2.2 %shard_map.154 = (f32[2,320,128]{2,1,0:T(8,128)S(1)}, f32[2,320,128]{2,1,0:T(8,128)S(1)}, f32[2,320,384]{2,1,0:T(8,128)S(1)}, f32[8,128]{1,0:T(8,128)}) custom-call(s32[1,1]{1,0:T(1,128)S(6)} %copy.16.picks_ref, s32[1]{0:T(128)S(6)} %copy.17.window_ref, bf16[4,320,320]{2,1,0:T(8,128)(2,1)S(1)} %get-tuple-element.49.query_ref, ...), custom_call_target="tpu_custom_call" | custom-call | flops 1310720000 | bytes 2097152 | tf_op jit(solution)/shard_map/pallas_call | solution.py:513
  36.2 0.0 collective-permute-done.6.anchor_ref
  36.3 0.0 copy-done.2
  36.3 0.0 copy-done.6
  36.3 1.5 %shard_map.155 = (f32[4,320,128]{2,1,0:T(8,128)S(1)}, f32[4,320,128]{2,1,0:T(8,128)S(1)}, f32[4,320,384]{2,1,0:T(8,128)S(1)}) custom-call(bf16[1,800,128]{2,1,0:T(8,128)(2,1)S(1)} %collective-permute-done.6.anchor_ref, bf16[320,640]{1,0:T(8,128)(2,1)S(1)} %copy-done.1, bf16[320,128]{1,0:T(8,128)(2,1)S(1)} %copy-done.6, bf16[640,128]{1,0:T(8,128)(2,1)S(1)} %copy-done.2, ...), custom_call_target="tpu_custom_call" | custom-call | flops 1048576000 | bytes 2097152 | tf_op jit(solution)/shard_map/pallas_call | solution.py:536
  37.8 0.0 copy-start.7
  37.8 1.3 %shard_map.156 = (f32[4,320,128]{2,1,0:T(8,128)S(1)}, f32[4,320,128]{2,1,0:T(8,128)S(1)}, f32[4,320,384]{2,1,0:T(8,128)S(1)}) custom-call(bf16[1,800,128]{2,1,0:T(8,128)(2,1)S(1)} %collective-permute-done.4.refs_0_.anchor_ref, bf16[320,640]{1,0:T(8,128)(2,1)S(1)} %copy-done.1, bf16[320,128]{1,0:T(8,128)(2,1)S(1)} %copy-done.6, ...), custom_call_target="tpu_custom_call" | custom-call | flops 1048576000 | bytes 2097152 | tf_op jit(solution)/shard_map/pallas_call | solution.py:536
  39.1 0.0 collective-permute-done.5.anchor_ref
  39.1 0.0 copy-done.7
  39.1 2.7 %shard_map.157 = bf16[4,5,64,320]{3,2,1,0:T(8,128)(2,1)} custom-call(bf16[1,800,128]{2,1,0:T(8,128)(2,1)S(1)} %collective-permute-done.5.anchor_ref, bf16[320,640]{1,0:T(8,128)(2,1)S(1)} %copy-done.1, bf16[320,128]{1,0:T(8,128)(2,1)S(1)} %copy-done.6, bf16[640,128]{1,0:T(8,128)(2,1)S(1)} %copy-done.2, bf16[4,320,320]{2,1,0:T(8,128)(2,1)S(1)} %get-tuple-element.49.query_ref, ...), custom_call_target="tpu_custom_call" | custom-call | flops 1310720000 | bytes 2097152 | tf_op jit(solution)/shard_map/pallas_call | solution.py:544
  (7 shorter events, 0.0 us)
Async XLA Ops:
  0.0 6.5 %copy-start = (bf16[3,3,320,320]{3,2,1,0:T(8,128)(2,1)S(1)}, bf16[3,3,320,320]{3,2,1,0:T(8,128)(2,1)}, u32[]{:S(2)}) copy-start(bf16[3,3,320,320]{3,2,1,0:T(8,128)(2,1)} %param.19) | copy-start | bytes 5529604
  0.0 1.4 %copy-start.3 = (bf16[4,5,64,320]{3,2,1,0:T(8,128)(2,1)S(1)}, bf16[4,5,64,320]{3,2,1,0:T(8,128)(2,1)}, u32[]{:S(2)}) copy-start(bf16[4,5,64,320]{3,2,1,0:T(8,128)(2,1)} %x_ref.5) | copy-start | bytes 2457604
  1.4 5.1 %copy-start.8 = (f32[320]{0:T(512)S(1)}, f32[320]{0:T(512)}, u32[]{:S(2)}) copy-start(f32[320]{0:T(512)} %g1_ref.5) | copy-start | bytes 3844
  1.4 5.1 %copy-start.9 = (f32[320]{0:T(512)S(1)}, f32[320]{0:T(512)}, u32[]{:S(2)}) copy-start(f32[320]{0:T(512)} %g2_ref.5) | copy-start | bytes 3844
  1.5 7.9 %collective-permute-start = (bf16[640,128]{1,0:T(8,128)(2,1)S(1)}, bf16[640,128]{1,0:T(8,128)(2,1)S(1)}, u32[]{:S(2)}, u32[]{:S(2)}) collective-permute-start(bf16[640,128]{1,0:T(8,128)(2,1)S(1)} %get-tuple-element.37), channel_id=1, source_target_pairs={{1,2},{2,1},{5,6},{6,5},{9,10},{10,9},{13,14},{14,13},{17,18},{18,... | collective-permute-start | bytes 491528 | tf_op jit(solution)/shard_map/ppermute | solution.py:435
  2.1 7.3 %collective-permute-start.1 = (bf16[640,128]{1,0:T(8,128)(2,1)S(1)}, bf16[640,128]{1,0:T(8,128)(2,1)S(1)}, u32[]{:S(2)}, u32[]{:S(2)}) collective-permute-start(bf16[640,128]{1,0:T(8,128)(2,1)S(1)} %get-tuple-element.38), channel_id=1, source_target_pairs={{0,1},{2,3},{1,0},{3,2},{4,5},{6,7},{5,4},{7,6},{8,9},{10,11},{9,8... | collective-permute-start | bytes 491528 | tf_op jit(solution)/shard_map/ppermute | solution.py:435
  9.4 7.8 %copy-start.4 = (bf16[4,5,64,320]{3,2,1,0:T(8,128)(2,1)S(1)}, bf16[4,5,64,320]{3,2,1,0:T(8,128)(2,1)}, u32[]{:S(2)}) copy-start(bf16[4,5,64,320]{3,2,1,0:T(8,128)(2,1)} %x_ref.5) | copy-start | bytes 2457604
  10.6 10.4 %collective-permute-start.2 = (bf16[800,128]{1,0:T(8,128)(2,1)S(1)}, bf16[800,128]{1,0:T(8,128)(2,1)S(1)}, u32[]{:S(2)}, u32[]{:S(2)}) collective-permute-start(bf16[800,128]{1,0:T(8,128)(2,1)S(1)} %get-tuple-element.43), channel_id=1, source_target_pairs={{4,8},{8,4},{5,9},{9,5},{6,10},{10,6},{7,11},{11,7},{20,24},{24,20... | collective-permute-start | bytes 614408 | tf_op jit(solution)/shard_map/ppermute | solution.py:435
  11.4 9.5 %collective-permute-start.3 = (bf16[800,128]{1,0:T(8,128)(2,1)S(1)}, bf16[800,128]{1,0:T(8,128)(2,1)S(1)}, u32[]{:S(2)}, u32[]{:S(2)}) collective-permute-start(bf16[800,128]{1,0:T(8,128)(2,1)S(1)} %get-tuple-element.44), channel_id=1, source_target_pairs={{0,4},{8,12},{4,0},{12,8},{1,5},{9,13},{5,1},{13,9},{2,6},{10,14},... | collective-permute-start | bytes 614408 | tf_op jit(solution)/shard_map/ppermute | solution.py:435
  17.2 3.8 %copy-start.5 = (bf16[3,320,320]{2,1,0:T(8,128)(2,1)S(1)}, bf16[3,320,320]{2,1,0:T(8,128)(2,1)}, u32[]{:S(2)}) copy-start(bf16[3,320,320]{2,1,0:T(8,128)(2,1)} %wt_ref.3) | copy-start | bytes 1843204
  17.2 3.8 %copy-start.10 = (f32[320]{0:T(512)S(1)}, f32[320]{0:T(512)}, u32[]{:S(2)}) copy-start(f32[320]{0:T(512)} %g3_ref.3) | copy-start | bytes 3844
  20.9 3.2 %copy-start.1 = (bf16[320,640]{1,0:T(8,128)(2,1)S(1)}, bf16[320,640]{1,0:T(8,128)(2,1)}, u32[]{:S(2)}) copy-start(bf16[320,640]{1,0:T(8,128)(2,1)} %wkv_ref.7) | copy-start | bytes 1228804
  20.9 3.2 %copy-start.11 = (bf16[320,320]{1,0:T(8,128)(2,1)S(1)}, bf16[320,320]{1,0:T(8,128)(2,1)}, u32[]{:S(2)}) copy-start(bf16[320,320]{1,0:T(8,128)(2,1)} %wq_ref.1) | copy-start | bytes 614404
  21.9 6.4 %copy-start.12 = (bf16[1280,128]{1,0:T(8,128)(2,1)S(1)}, bf16[1280,128]{1,0:T(8,128)(2,1)}, u32[]{:S(2)}) copy-start(bf16[1280,128]{1,0:T(8,128)(2,1)} %constant.9.clone.to_channels_ref) | copy-start | bytes 983044
  21.9 6.4 %copy-start.13 = (bf16[1280,128]{1,0:T(8,128)(2,1)S(1)}, bf16[1280,128]{1,0:T(8,128)(2,1)}, u32[]{:S(2)}) copy-start(bf16[1280,128]{1,0:T(8,128)(2,1)} %constant.8.clone.to_lanes_ref) | copy-start | bytes 983044
  22.0 9.9 %collective-permute-start.4 = (bf16[1,800,128]{2,1,0:T(8,128)(2,1)S(1)}, bf16[1,800,128]{2,1,0:T(8,128)(2,1)S(1)}, u32[]{:S(2)}, u32[]{:S(2)}) collective-permute-start(bf16[1,800,128]{2,1,0:T(8,128)(2,1)S(1)} %shard_map.151.from_ref), channel_id=1, source_target_pairs={{0,12},{4,8},{8,4},{12,0},{1,13},{5,9},{9,5},{13,1},{2,14},{6,10},... | collective-permute-start | bytes 614408 | tf_op jit(solution)/shard_map/ppermute | solution.py:500
  23.4 12.9 %collective-permute-start.6 = (bf16[1,800,128]{2,1,0:T(8,128)(2,1)S(1)}, bf16[1,800,128]{2,1,0:T(8,128)(2,1)S(1)}, u32[]{:S(2)}, u32[]{:S(2)}) collective-permute-start(bf16[1,800,128]{2,1,0:T(8,128)(2,1)S(1)} %shard_map.153), channel_id=1, source_target_pairs={{0,4},{4,0},{8,12},{12,8},{1,5},{5,1},{9,13},{13,9},{2,6},{6,2},{1... | collective-permute-start | bytes 614408 | tf_op jit(solution)/shard_map/ppermute | solution.py:500
  31.9 7.3 %collective-permute-start.5 = (bf16[1,800,128]{2,1,0:T(8,128)(2,1)S(1)}, bf16[1,800,128]{2,1,0:T(8,128)(2,1)S(1)}, u32[]{:S(2)}, u32[]{:S(2)}) collective-permute-start(bf16[1,800,128]{2,1,0:T(8,128)(2,1)S(1)} %get-tuple-element.52), channel_id=1, source_target_pairs={{0,4},{4,0},{8,12},{12,8},{1,5},{5,1},{9,13},{13,9},{2,6},{6,2},{1... | collective-permute-start | bytes 614408 | tf_op jit(solution)/shard_map/ppermute | solution.py:528
  34.0 2.3 %copy-start.2 = (bf16[640,128]{1,0:T(8,128)(2,1)S(1)}, bf16[640,128]{1,0:T(8,128)(2,1)}, u32[]{:S(2)}) copy-start(bf16[640,128]{1,0:T(8,128)(2,1)} %constant.11.clone.to_channels_ref) | copy-start | bytes 491524
  34.0 2.3 %copy-start.6 = (bf16[320,128]{1,0:T(8,128)(2,1)S(1)}, bf16[320,128]{1,0:T(8,128)(2,1)}, u32[]{:S(2)}) copy-start(bf16[320,128]{1,0:T(8,128)(2,1)} %constant.10.clone.to_lanes_ref) | copy-start | bytes 245764
  37.8 1.3 %copy-start.7 = (bf16[320,320]{1,0:T(8,128)(2,1)S(1)}, bf16[320,320]{1,0:T(8,128)(2,1)}, u32[]{:S(2)}) copy-start(bf16[320,320]{1,0:T(8,128)(2,1)} %wo_ref.1) | copy-start | bytes 614404

commit v10 on v9

--- a/solution.py
+++ b/solution.py
@@ -183,7 +183,7 @@
 
 def outer_edge_kernel(
     frames, edge_ref, odd_ref, even_ref, order_ref, mid_ref, mid2_ref, g1_ref, g2_ref, w_ref, rem_ref,
-    spatial_ref, hidden_ref, odd_clip_ref, even_clip_ref,
+    spatial_ref, hidden_ref, even_clip_ref, odd_clip_ref,
 ):
     _, cells, channels = spatial_ref.shape
     width = edge_ref.shape[2]
@@ -239,7 +239,7 @@
 
 
 def chosen_kernel(
-    picks_ref, odd_ref, even_ref, spatial_ref, hidden_ref, g3_ref, wt_ref, chosen_ref
+    picks_ref, even_ref, odd_ref, spatial_ref, hidden_ref, g3_ref, wt_ref, chosen_ref
 ):
     frames, cells, channels = spatial_ref.shape
     before, after = (unpacked(v, channels) for v in sorted_pair(odd_ref, even_ref, "clip"))
@@ -253,7 +253,7 @@
 
 
 def temporal_kernel(
-    odd_ref, even_ref, spatial_ref, hidden_ref, g3_ref, wt_ref, wq_ref, wkv_ref,
+    even_ref, odd_ref, spatial_ref, hidden_ref, g3_ref, wt_ref, wq_ref, wkv_ref,
     temporal_ref, query_ref, keyval_ref,
 ):
     frames, cells, channels = spatial_ref.shape
@@ -428,11 +428,15 @@
         copy.wait()
 
 
-def swapped(odd, even, axis):
+def swapped(odd, even, axis, even_first):
     count = lax.axis_size(axis)
     pairs = [[(i, i + 1) for i in range(start, count - 1, 2)] for start in (1, 0)]
     pairs = [up + [(j, i) for i, j in up] for up in pairs]
-    return lax.ppermute(odd, axis, pairs[0]), lax.ppermute(even, axis, pairs[1])
+    if even_first:
+        even = lax.ppermute(even, axis, pairs[1])
+        return lax.ppermute(odd, axis, pairs[0]), even
+    odd = lax.ppermute(odd, axis, pairs[0])
+    return odd, lax.ppermute(even, axis, pairs[1])
 
 
 def on_device(
@@ -455,7 +459,7 @@
     strip_odd, strip_even = call(
         edge_kernel, [((edge_packed, LANES), BF)] * 2, [VMEM], flops=8 * frames * cells * one
     )(x)
-    strip_odd, strip_even = swapped(strip_odd, strip_even, "strip")
+    strip_odd, strip_even = swapped(strip_odd, strip_even, "strip", False)
     outer_col = pltpu.VMEM((2 * cells, 3 * channels), BF)
     inner_col = pltpu.VMEM(((frames - 2) * (cells + 2 * width), 3 * channels), BF)
     middle = (2, cells - 2 * width, channels)
@@ -472,13 +476,13 @@
         [outer_col],
         flops=9 * 2 * cells * one,
     )(x, g1, g2, w)
-    outer_spatial, outer_hidden, clip_odd, clip_even = call(
+    outer_spatial, outer_hidden, clip_even, clip_odd = call(
         functools.partial(outer_edge_kernel, frames),
         [((2, cells, channels), BF)] * 2 + [((packed, LANES), BF)] * 2,
         [VMEM] * 10,
         flops=6 * 2 * width * one,
     )(edge, strip_odd, strip_even, order, mid, mid2, g1, g2, w, w_rem)
-    clip_odd, clip_even = swapped(clip_odd, clip_even, "clip")
+    clip_odd, clip_even = swapped(clip_odd, clip_even, "clip", True)
     spatial, hidden = call(
         inner_kernel,
         [(some, BF), (some, BF)],
@@ -488,7 +492,7 @@
     )(x, strip_odd, strip_even, g1, g2, w, w_rem, outer_spatial, outer_hidden)
     (chosen,) = call(
         chosen_kernel, [((count, packed, LANES), BF)], [VMEM] * 7, flops=3 * cells * one
-    )(anchor_index, clip_odd, clip_even, spatial, hidden, g3, temporal_w)
+    )(anchor_index, clip_even, clip_odd, spatial, hidden, g3, temporal_w)
     clips = lax.axis_size("clip")
     powers = clips & (clips - 1) == 0
     if powers:
@@ -504,7 +508,7 @@
         [VMEM] * 8,
         flops=6 * frames * cells * one,
         limit=32,
-    )(clip_odd, clip_even, spatial, hidden, g3, temporal_w, w_query, w_keyval)
+    )(clip_even, clip_odd, spatial, hidden, g3, temporal_w, w_query, w_keyval)
     maps = head_maps(frames, channels)
     split = frames // 2 if frames > 1 else frames
 

time: 42.2 us -> 41.1 us (0.974)
  waiting for transfers between devices: 1.23 us -> 0.14 us
    ppermute x2, starting transfers between devices: 2.17 us -> 5.9 us  [on_device(): arrived = [lax.ppermute(v, 'clip', route) for v, route in zip(sent, routes)]]
    ppermute x4, starting transfers between devices: 10.3 us -> 7.51 us  [the longest x1 4.36 us: swapped(): return (odd, lax.ppermute(even, axis, pairs[1]))]
    ppermute x2, waiting for transfers between devices: 1.22 us -> 0.01 us  [on_device(): arrived = [lax.ppermute(v, 'clip', route) for v, route in zip(sent, routes)]]
    ppermute x1, starting transfers between devices: 2.14 us -> 1.21 us  [on_device(): arrived += [lax.ppermute(v, 'clip', routes[0]) for v in relayed]]
  transfers between devices with their start and end apart: 7 -> 7, of which waited for: 1 -> 1; matrix products, arithmetic and copies ran while one was open for 0% -> 0% of each run, Pallas kernels for 43% -> 44%
where the time goes in v10:
time: 41.1 us; the launch traced here: 41 us
  Pallas kernels  23 us (56%)
  starting transfers between devices  14.6 us (36%)
  between operations  1.73 us (4%)
  local copies, waits for them, and re-layouts  1.42 us (3%)
    ppermute x2, starting transfers between devices, on_device(): arrived = [lax.ppermute(v, 'clip', route) for v, route in zip(sent, routes)]  5.9 us
    pallas_call x2, Pallas kernels, local(): call(functools.partial(local_kernel, start), [(shape + (LANES,), F32)] *...  4.5 us
    ppermute x1, starting transfers between devices, swapped(): return (odd, lax.ppermute(even, axis, pairs[1]))  4.36 us
    pallas_call x1, Pallas kernels, on_device(): call(temporal_kernel, [(some, BF), (some, BF), ((frames, cells, 2 * chann...  4.22 us
    pallas_call x1, Pallas kernels, on_device(): call(inner_kernel, [(some, BF), (some, BF)], [VMEM] * 9, [inner_col], flo...  3.69 us
    pallas_call x1, Pallas kernels, on_device(): call(outer_kernel, [(middle, BF), (middle, BF), ((2, 2, width, channels),...  2.87 us
    pallas_call x2, Pallas kernels, on_device(): call(functools.partial(anchor_kernel, pieces), states, [VMEM] * (5 + 3 *...  2.82 us
    pallas_call x1, Pallas kernels, on_device(): call(last_kernel, [(latents.shape, BF)], [VMEM] * 10, [pltpu.VMEM(latents...  2.74 us
  transfers between devices with their start and end apart: 7, of which 1 were waited for; matrix products, arithmetic and copies ran while one was open for 0% of the time, Pallas kernels for 44%

profile of v10, /device:TPU:0, one launch (start us, length us, event | category | flops | bytes accessed | tf_op | source)
XLA Modules:
  0.0 41.0 jit_solution(16093775825729350124)
XLA Ops:
  0.0 0.0 copy-start
  0.0 1.3 %copy-done.3 = bf16[4,5,64,320]{3,2,1,0:T(8,128)(2,1)S(1)} copy-done((bf16[4,5,64,320]{3,2,1,0:T(8,128)(2,1)S(1)}, bf16[4,5,64,320]{3,2,1,0:T(8,128)(2,1)}, u32[]{:S(2)}) %copy-start.3) | copy-done | bytes 819224
  1.4 0.1 shard_map.146
  1.5 0.7 %collective-permute-start = (bf16[640,128]{1,0:T(8,128)(2,1)S(1)}, bf16[640,128]{1,0:T(8,128)(2,1)S(1)}, u32[]{:S(2)}, u32[]{:S(2)}) collective-permute-start(bf16[640,128]{1,0:T(8,128)(2,1)S(1)} %get-tuple-element.37), channel_id=1, source_target_pairs={{1,2},{2,1},{5,6},{6,5},{9,10},{10,9},{13,14},{14,13},{17,18},{18,... | collective-permute-start | bytes 491528 | tf_op jit(solution)/shard_map/ppermute | solution.py:438
  2.1 4.4 %collective-permute-start.1 = (bf16[640,128]{1,0:T(8,128)(2,1)S(1)}, bf16[640,128]{1,0:T(8,128)(2,1)S(1)}, u32[]{:S(2)}, u32[]{:S(2)}) collective-permute-start(bf16[640,128]{1,0:T(8,128)(2,1)S(1)} %get-tuple-element.38), channel_id=1, source_target_pairs={{0,1},{2,3},{1,0},{3,2},{4,5},{6,7},{5,4},{7,6},{8,9},{10,11},{9,8... | collective-permute-start | bytes 491528 | tf_op jit(solution)/shard_map/ppermute | solution.py:439
  6.5 0.0 copy-done
  6.5 0.0 copy-done.8
  6.5 0.0 copy-done.9
  6.5 2.9 %shard_map.145 = (bf16[2,192,320]{2,1,0:T(8,128)(2,1)S(1)}, bf16[2,192,320]{2,1,0:T(8,128)(2,1)S(1)}, f32[2,2,64,320]{3,2,1,0:T(8,128)S(1)}, bf16[960,192]{1,0:T(8,128)(2,1)S(1)}, f32[8,128]{1,0:T(8,128)S(1)}) custom-call(bf16[4,5,64,320]{3,2,1,0:T(8,128)(2,1)S(1)} %copy-done.3, f32[320]{0:T(512)S(1)} %copy-done.8, f32[320]{0:T(512)S(1)} %copy-done.9, ...), custom_call_target="tpu_custom_call" | custom-call | flops 1179648000 | bytes 2097152 | tf_op jit(solution)/shard_map/pallas_call | solution.py:466
  9.4 0.0 collective-permute-done.odd_ref
  9.4 0.0 collective-permute-done.1.even_ref
  9.4 0.0 copy-start.4
  9.4 1.2 %shard_map.147 = (bf16[2,320,320]{2,1,0:T(8,128)(2,1)S(1)}, bf16[2,320,320]{2,1,0:T(8,128)(2,1)S(1)}, bf16[800,128]{1,0:T(8,128)(2,1)S(1)}, bf16[800,128]{1,0:T(8,128)(2,1)S(1)}) custom-call(f32[2,2,64,320]{3,2,1,0:T(8,128)S(1)} %get-tuple-element.36.edge_ref, bf16[640,128]{1,0:T(8,128)(2,1)S(1)} %collective-permute-done.odd_ref, ...), custom_call_target="tpu_custom_call" | custom-call | flops 157286400 | bytes 2097152 | tf_op jit(solution)/shard_map/pallas_call | solution.py:479
  10.6 1.6 %collective-permute-start.2 = (bf16[800,128]{1,0:T(8,128)(2,1)S(1)}, bf16[800,128]{1,0:T(8,128)(2,1)S(1)}, u32[]{:S(2)}, u32[]{:S(2)}) collective-permute-start(bf16[800,128]{1,0:T(8,128)(2,1)S(1)} %get-tuple-element.43), channel_id=1, source_target_pairs={{0,4},{8,12},{4,0},{12,8},{1,5},{9,13},{5,1},{13,9},{2,6},{10,14},... | collective-permute-start | bytes 614408 | tf_op jit(solution)/shard_map/ppermute | solution.py:436
  12.2 0.8 %collective-permute-start.3 = (bf16[800,128]{1,0:T(8,128)(2,1)S(1)}, bf16[800,128]{1,0:T(8,128)(2,1)S(1)}, u32[]{:S(2)}, u32[]{:S(2)}) collective-permute-start(bf16[800,128]{1,0:T(8,128)(2,1)S(1)} %get-tuple-element.44), channel_id=1, source_target_pairs={{4,8},{8,4},{5,9},{9,5},{6,10},{10,6},{7,11},{11,7},{20,24},{24,20... | collective-permute-start | bytes 614408 | tf_op jit(solution)/shard_map/ppermute | solution.py:437
  14.4 0.0 copy-done.4
  14.4 0.0 copy-start.5
  14.4 0.0 copy-start.10
  14.4 3.7 %shard_map.148 = (bf16[4,320,320]{2,1,0:T(8,128)(2,1)S(1)}, bf16[4,320,320]{2,1,0:T(8,128)(2,1)S(1)}) custom-call(bf16[4,5,64,320]{3,2,1,0:T(8,128)(2,1)S(1)} %copy-done.4, bf16[640,128]{1,0:T(8,128)(2,1)S(1)} %collective-permute-done.odd_ref, bf16[640,128]{1,0:T(8,128)(2,1)S(1)} %collective-permute-done.1.even_ref, f32[320]{0:T(512)S(1)} %copy-done.8, ...), custom_call_target="tpu_custom_call" | custom-call | flops 1179648000 | bytes 2097152 | tf_op jit(solution)/shard_map/pallas_call | solution.py:486
  18.1 0.0 copy-start.1
  18.1 0.0 copy-start.11
  18.1 0.0 collective-permute-done.2.even_ref
  18.1 0.0 collective-permute-done.3.odd_ref
  18.1 0.0 copy-done.5
  18.1 0.0 copy-done.10
  18.2 0.9 %shard_map.151.from_ref = bf16[1,800,128]{2,1,0:T(8,128)(2,1)S(1)} custom-call(s32[1,1]{1,0:T(1,128)S(6)} %copy.16.picks_ref, bf16[800,128]{1,0:T(8,128)(2,1)S(1)} %collective-permute-done.2.even_ref, bf16[800,128]{1,0:T(8,128)(2,1)S(1)} %collective-permute-done.3.odd_ref, bf16[4,320,320]{2,1,0:T(8,128)(2,1)S(1)} %get-tuple-element.47.spatial_ref, ...), custom_call_target="tpu_custom_call" | custom-call | flops 196608000 | bytes 2097152 | tf_op jit(solution)/shard_map/pallas_call | solution.py:493
  19.1 0.0 copy-start.12
  19.1 0.0 copy-start.13
  19.1 3.2 %collective-permute-start.4 = (bf16[1,800,128]{2,1,0:T(8,128)(2,1)S(1)}, bf16[1,800,128]{2,1,0:T(8,128)(2,1)S(1)}, u32[]{:S(2)}, u32[]{:S(2)}) collective-permute-start(bf16[1,800,128]{2,1,0:T(8,128)(2,1)S(1)} %shard_map.151.from_ref), channel_id=1, source_target_pairs={{0,12},{4,8},{8,4},{12,0},{1,13},{5,9},{9,5},{13,1},{2,14},{6,10},... | collective-permute-start | bytes 614408 | tf_op jit(solution)/shard_map/ppermute | solution.py:504
  22.3 2.7 %collective-permute-start.6 = (bf16[1,800,128]{2,1,0:T(8,128)(2,1)S(1)}, bf16[1,800,128]{2,1,0:T(8,128)(2,1)S(1)}, u32[]{:S(2)}, u32[]{:S(2)}) collective-permute-start(bf16[1,800,128]{2,1,0:T(8,128)(2,1)S(1)} %shard_map.153), channel_id=1, source_target_pairs={{0,4},{4,0},{8,12},{12,8},{1,5},{5,1},{9,13},{13,9},{2,6},{6,2},{1... | collective-permute-start | bytes 614408 | tf_op jit(solution)/shard_map/ppermute | solution.py:504
  25.0 0.0 copy-done.1
  25.0 0.0 copy-done.11
  25.0 4.2 %shard_map.149 = (bf16[4,320,320]{2,1,0:T(8,128)(2,1)S(1)}, bf16[4,320,320]{2,1,0:T(8,128)(2,1)S(1)}, bf16[4,320,640]{2,1,0:T(8,128)(2,1)S(1)}) custom-call(bf16[800,128]{1,0:T(8,128)(2,1)S(1)} %collective-permute-done.2.even_ref, bf16[800,128]{1,0:T(8,128)(2,1)S(1)} %collective-permute-done.3.odd_ref, ...), custom_call_target="tpu_custom_call" | custom-call | flops 1572864000 | bytes 2097152 | tf_op jit(solution)/shard_map/pallas_call | solution.py:505
  29.3 0.0 copy-done.12
  29.3 0.0 copy-done.13
  29.3 2.3 %shard_map.150 = (f32[2,320,128]{2,1,0:T(8,128)S(1)}, f32[2,320,128]{2,1,0:T(8,128)S(1)}, f32[2,320,384]{2,1,0:T(8,128)S(1)}, f32[8,128]{1,0:T(8,128)S(1)}) custom-call(s32[1,1]{1,0:T(1,128)S(6)} %copy.16.picks_ref, s32[1]{0:T(128)S(6)} %copy.17.window_ref, bf16[4,320,320]{2,1,0:T(8,128)(2,1)S(1)} %get-tuple-element.49.query_ref, ...), custom_call_target="tpu_custom_call" | custom-call | flops 1310720000 | bytes 2097152 | tf_op jit(solution)/shard_map/pallas_call | solution.py:517
  31.5 0.0 collective-permute-done.4.refs_0_.anchor_ref
  31.6 1.2 %collective-permute-start.5 = (bf16[1,800,128]{2,1,0:T(8,128)(2,1)S(1)}, bf16[1,800,128]{2,1,0:T(8,128)(2,1)S(1)}, u32[]{:S(2)}, u32[]{:S(2)}) collective-permute-start(bf16[1,800,128]{2,1,0:T(8,128)(2,1)S(1)} %get-tuple-element.52), channel_id=1, source_target_pairs={{0,4},{4,0},{8,12},{12,8},{1,5},{5,1},{9,13},{13,9},{2,6},{6,2},{1... | collective-permute-start | bytes 614408 | tf_op jit(solution)/shard_map/ppermute | solution.py:532
  32.8 2.2 %shard_map.154 = (f32[2,320,128]{2,1,0:T(8,128)S(1)}, f32[2,320,128]{2,1,0:T(8,128)S(1)}, f32[2,320,384]{2,1,0:T(8,128)S(1)}, f32[8,128]{1,0:T(8,128)}) custom-call(s32[1,1]{1,0:T(1,128)S(6)} %copy.16.picks_ref, s32[1]{0:T(128)S(6)} %copy.17.window_ref, bf16[4,320,320]{2,1,0:T(8,128)(2,1)S(1)} %get-tuple-element.49.query_ref, ...), custom_call_target="tpu_custom_call" | custom-call | flops 1310720000 | bytes 2097152 | tf_op jit(solution)/shard_map/pallas_call | solution.py:517
  35.0 0.0 collective-permute-done.6.anchor_ref
  35.0 0.0 copy-done.2
  35.1 0.0 copy-done.6
  35.1 1.5 %shard_map.155 = (f32[4,320,128]{2,1,0:T(8,128)S(1)}, f32[4,320,128]{2,1,0:T(8,128)S(1)}, f32[4,320,384]{2,1,0:T(8,128)S(1)}) custom-call(bf16[1,800,128]{2,1,0:T(8,128)(2,1)S(1)} %collective-permute-done.6.anchor_ref, bf16[320,640]{1,0:T(8,128)(2,1)S(1)} %copy-done.1, bf16[320,128]{1,0:T(8,128)(2,1)S(1)} %copy-done.6, bf16[640,128]{1,0:T(8,128)(2,1)S(1)} %copy-done.2, ...), custom_call_target="tpu_custom_call" | custom-call | flops 1048576000 | bytes 2097152 | tf_op jit(solution)/shard_map/pallas_call | solution.py:540
  36.6 0.0 copy-start.7
  36.6 1.3 %shard_map.156 = (f32[4,320,128]{2,1,0:T(8,128)S(1)}, f32[4,320,128]{2,1,0:T(8,128)S(1)}, f32[4,320,384]{2,1,0:T(8,128)S(1)}) custom-call(bf16[1,800,128]{2,1,0:T(8,128)(2,1)S(1)} %collective-permute-done.4.refs_0_.anchor_ref, bf16[320,640]{1,0:T(8,128)(2,1)S(1)} %copy-done.1, bf16[320,128]{1,0:T(8,128)(2,1)S(1)} %copy-done.6, ...), custom_call_target="tpu_custom_call" | custom-call | flops 1048576000 | bytes 2097152 | tf_op jit(solution)/shard_map/pallas_call | solution.py:540
  37.9 0.1 collective-permute-done.5.anchor_ref
  38.0 0.0 copy-done.7
  38.0 2.7 %shard_map.157 = bf16[4,5,64,320]{3,2,1,0:T(8,128)(2,1)} custom-call(bf16[1,800,128]{2,1,0:T(8,128)(2,1)S(1)} %collective-permute-done.5.anchor_ref, bf16[320,640]{1,0:T(8,128)(2,1)S(1)} %copy-done.1, bf16[320,128]{1,0:T(8,128)(2,1)S(1)} %copy-done.6, bf16[640,128]{1,0:T(8,128)(2,1)S(1)} %copy-done.2, bf16[4,320,320]{2,1,0:T(8,128)(2,1)S(1)} %get-tuple-element.49.query_ref, ...), custom_call_target="tpu_custom_call" | custom-call | flops 1310720000 | bytes 2097152 | tf_op jit(solution)/shard_map/pallas_call | solution.py:548
  (7 shorter events, 0.0 us)
Async XLA Ops:
  0.0 6.5 %copy-start = (bf16[3,3,320,320]{3,2,1,0:T(8,128)(2,1)S(1)}, bf16[3,3,320,320]{3,2,1,0:T(8,128)(2,1)}, u32[]{:S(2)}) copy-start(bf16[3,3,320,320]{3,2,1,0:T(8,128)(2,1)} %param.19) | copy-start | bytes 5529604
  0.0 1.4 %copy-start.3 = (bf16[4,5,64,320]{3,2,1,0:T(8,128)(2,1)S(1)}, bf16[4,5,64,320]{3,2,1,0:T(8,128)(2,1)}, u32[]{:S(2)}) copy-start(bf16[4,5,64,320]{3,2,1,0:T(8,128)(2,1)} %x_ref.5) | copy-start | bytes 2457604
  1.4 5.1 %copy-start.8 = (f32[320]{0:T(512)S(1)}, f32[320]{0:T(512)}, u32[]{:S(2)}) copy-start(f32[320]{0:T(512)} %g1_ref.5) | copy-start | bytes 3844
  1.4 5.1 %copy-start.9 = (f32[320]{0:T(512)S(1)}, f32[320]{0:T(512)}, u32[]{:S(2)}) copy-start(f32[320]{0:T(512)} %g2_ref.5) | copy-start | bytes 3844
  1.5 7.9 %collective-permute-start = (bf16[640,128]{1,0:T(8,128)(2,1)S(1)}, bf16[640,128]{1,0:T(8,128)(2,1)S(1)}, u32[]{:S(2)}, u32[]{:S(2)}) collective-permute-start(bf16[640,128]{1,0:T(8,128)(2,1)S(1)} %get-tuple-element.37), channel_id=1, source_target_pairs={{1,2},{2,1},{5,6},{6,5},{9,10},{10,9},{13,14},{14,13},{17,18},{18,... | collective-permute-start | bytes 491528 | tf_op jit(solution)/shard_map/ppermute | solution.py:438
  2.1 7.3 %collective-permute-start.1 = (bf16[640,128]{1,0:T(8,128)(2,1)S(1)}, bf16[640,128]{1,0:T(8,128)(2,1)S(1)}, u32[]{:S(2)}, u32[]{:S(2)}) collective-permute-start(bf16[640,128]{1,0:T(8,128)(2,1)S(1)} %get-tuple-element.38), channel_id=1, source_target_pairs={{0,1},{2,3},{1,0},{3,2},{4,5},{6,7},{5,4},{7,6},{8,9},{10,11},{9,8... | collective-permute-start | bytes 491528 | tf_op jit(solution)/shard_map/ppermute | solution.py:439
  9.4 5.0 %copy-start.4 = (bf16[4,5,64,320]{3,2,1,0:T(8,128)(2,1)S(1)}, bf16[4,5,64,320]{3,2,1,0:T(8,128)(2,1)}, u32[]{:S(2)}) copy-start(bf16[4,5,64,320]{3,2,1,0:T(8,128)(2,1)} %x_ref.5) | copy-start | bytes 2457604
  10.6 7.5 %collective-permute-start.2 = (bf16[800,128]{1,0:T(8,128)(2,1)S(1)}, bf16[800,128]{1,0:T(8,128)(2,1)S(1)}, u32[]{:S(2)}, u32[]{:S(2)}) collective-permute-start(bf16[800,128]{1,0:T(8,128)(2,1)S(1)} %get-tuple-element.43), channel_id=1, source_target_pairs={{0,4},{8,12},{4,0},{12,8},{1,5},{9,13},{5,1},{13,9},{2,6},{10,14},... | collective-permute-start | bytes 614408 | tf_op jit(solution)/shard_map/ppermute | solution.py:436
  12.2 5.9 %collective-permute-start.3 = (bf16[800,128]{1,0:T(8,128)(2,1)S(1)}, bf16[800,128]{1,0:T(8,128)(2,1)S(1)}, u32[]{:S(2)}, u32[]{:S(2)}) collective-permute-start(bf16[800,128]{1,0:T(8,128)(2,1)S(1)} %get-tuple-element.44), channel_id=1, source_target_pairs={{4,8},{8,4},{5,9},{9,5},{6,10},{10,6},{7,11},{11,7},{20,24},{24,20... | collective-permute-start | bytes 614408 | tf_op jit(solution)/shard_map/ppermute | solution.py:437
  14.4 3.8 %copy-start.5 = (bf16[3,320,320]{2,1,0:T(8,128)(2,1)S(1)}, bf16[3,320,320]{2,1,0:T(8,128)(2,1)}, u32[]{:S(2)}) copy-start(bf16[3,320,320]{2,1,0:T(8,128)(2,1)} %wt_ref.3) | copy-start | bytes 1843204
  14.4 3.8 %copy-start.10 = (f32[320]{0:T(512)S(1)}, f32[320]{0:T(512)}, u32[]{:S(2)}) copy-start(f32[320]{0:T(512)} %g3_ref.3) | copy-start | bytes 3844
  18.1 7.0 %copy-start.1 = (bf16[320,640]{1,0:T(8,128)(2,1)S(1)}, bf16[320,640]{1,0:T(8,128)(2,1)}, u32[]{:S(2)}) copy-start(bf16[320,640]{1,0:T(8,128)(2,1)} %wkv_ref.7) | copy-start | bytes 1228804
  18.1 6.9 %copy-start.11 = (bf16[320,320]{1,0:T(8,128)(2,1)S(1)}, bf16[320,320]{1,0:T(8,128)(2,1)}, u32[]{:S(2)}) copy-start(bf16[320,320]{1,0:T(8,128)(2,1)} %wq_ref.1) | copy-start | bytes 614404
  19.1 10.2 %copy-start.12 = (bf16[1280,128]{1,0:T(8,128)(2,1)S(1)}, bf16[1280,128]{1,0:T(8,128)(2,1)}, u32[]{:S(2)}) copy-start(bf16[1280,128]{1,0:T(8,128)(2,1)} %constant.9.clone.to_channels_ref) | copy-start | bytes 983044
  19.1 10.2 %copy-start.13 = (bf16[1280,128]{1,0:T(8,128)(2,1)S(1)}, bf16[1280,128]{1,0:T(8,128)(2,1)}, u32[]{:S(2)}) copy-start(bf16[1280,128]{1,0:T(8,128)(2,1)} %constant.8.clone.to_lanes_ref) | copy-start | bytes 983044
  19.1 12.4 %collective-permute-start.4 = (bf16[1,800,128]{2,1,0:T(8,128)(2,1)S(1)}, bf16[1,800,128]{2,1,0:T(8,128)(2,1)S(1)}, u32[]{:S(2)}, u32[]{:S(2)}) collective-permute-start(bf16[1,800,128]{2,1,0:T(8,128)(2,1)S(1)} %shard_map.151.from_ref), channel_id=1, source_target_pairs={{0,12},{4,8},{8,4},{12,0},{1,13},{5,9},{9,5},{13,1},{2,14},{6,10},... | collective-permute-start | bytes 614408 | tf_op jit(solution)/shard_map/ppermute | solution.py:504
  22.3 12.7 %collective-permute-start.6 = (bf16[1,800,128]{2,1,0:T(8,128)(2,1)S(1)}, bf16[1,800,128]{2,1,0:T(8,128)(2,1)S(1)}, u32[]{:S(2)}, u32[]{:S(2)}) collective-permute-start(bf16[1,800,128]{2,1,0:T(8,128)(2,1)S(1)} %shard_map.153), channel_id=1, source_target_pairs={{0,4},{4,0},{8,12},{12,8},{1,5},{5,1},{9,13},{13,9},{2,6},{6,2},{1... | collective-permute-start | bytes 614408 | tf_op jit(solution)/shard_map/ppermute | solution.py:504
  31.6 6.5 %collective-permute-start.5 = (bf16[1,800,128]{2,1,0:T(8,128)(2,1)S(1)}, bf16[1,800,128]{2,1,0:T(8,128)(2,1)S(1)}, u32[]{:S(2)}, u32[]{:S(2)}) collective-permute-start(bf16[1,800,128]{2,1,0:T(8,128)(2,1)S(1)} %get-tuple-element.52), channel_id=1, source_target_pairs={{0,4},{4,0},{8,12},{12,8},{1,5},{5,1},{9,13},{13,9},{2,6},{6,2},{1... | collective-permute-start | bytes 614408 | tf_op jit(solution)/shard_map/ppermute | solution.py:532
  32.8 2.3 %copy-start.2 = (bf16[640,128]{1,0:T(8,128)(2,1)S(1)}, bf16[640,128]{1,0:T(8,128)(2,1)}, u32[]{:S(2)}) copy-start(bf16[640,128]{1,0:T(8,128)(2,1)} %constant.11.clone.to_channels_ref) | copy-start | bytes 491524
  32.8 2.3 %copy-start.6 = (bf16[320,128]{1,0:T(8,128)(2,1)S(1)}, bf16[320,128]{1,0:T(8,128)(2,1)}, u32[]{:S(2)}) copy-start(bf16[320,128]{1,0:T(8,128)(2,1)} %constant.10.clone.to_lanes_ref) | copy-start | bytes 245764
  36.6 1.5 %copy-start.7 = (bf16[320,320]{1,0:T(8,128)(2,1)S(1)}, bf16[320,320]{1,0:T(8,128)(2,1)}, u32[]{:S(2)}) copy-start(bf16[320,320]{1,0:T(8,128)(2,1)} %wo_ref.1) | copy-start | bytes 614404

commit v11 on v10

--- a/solution.py
+++ b/solution.py
@@ -380,7 +380,7 @@
     return top, total, mix
 
 
-def copy_kernel(from_ref, to_ref):
+def copy_kernel(from_ref, order_ref, to_ref):
     to_ref[...] = from_ref[...]
 
 
@@ -499,9 +499,7 @@
         routes = [[(i, i ^ s) for i in range(clips)] for s in range(1, clips, 2)]
     else:
         routes = [[(i, (i + s) % clips) for i in range(clips)] for s in range(1, clips)]
-    (near,) = call(copy_kernel, [(chosen.shape, BF)], [VMEM])(chosen)
-    sent = [near] + [chosen] * (len(routes) - 1)
-    arrived = [lax.ppermute(v, "clip", route) for v, route in zip(sent, routes)]
+    far = [lax.ppermute(chosen, "clip", route) for route in routes[1:]]
     temporal, query, keyval = call(
         temporal_kernel,
         [(some, BF), (some, BF), ((frames, cells, 2 * channels), BF)],
@@ -509,6 +507,8 @@
         flops=6 * frames * cells * one,
         limit=32,
     )(clip_even, clip_odd, spatial, hidden, g3, temporal_w, w_query, w_keyval)
+    (near,) = call(copy_kernel, [(chosen.shape, BF)], [VMEM] * 2)(chosen, temporal)
+    arrived = [lax.ppermute(near, "clip", routes[0])] + far
     maps = head_maps(frames, channels)
     split = frames // 2 if frames > 1 else frames
 

time: 41.1 us -> 41.1 us (level)
  no operation moved by 1% of the time
where the time goes in v11:
time: 41.1 us; the launch traced here: 40.9 us
  Pallas kernels  23 us (56%)
  starting transfers between devices  14.6 us (36%)
  between operations  1.72 us (4%)
  local copies, waits for them, and re-layouts  1.42 us (3%)
    pallas_call x2, Pallas kernels, local(): call(functools.partial(local_kernel, start), [(shape + (LANES,), F32)] *...  4.44 us
    ppermute x1, starting transfers between devices, swapped(): return (odd, lax.ppermute(even, axis, pairs[1]))  4.36 us
    pallas_call x1, Pallas kernels, on_device(): call(temporal_kernel, [(some, BF), (some, BF), ((frames, cells, 2 * chann...  4.21 us
    pallas_call x1, Pallas kernels, on_device(): call(inner_kernel, [(some, BF), (some, BF)], [VMEM] * 9, [inner_col], flo...  3.7 us
    ppermute x1, starting transfers between devices, on_device(): far = [lax.ppermute(chosen, 'clip', route) for route in routes[1:]]  3.17 us
    pallas_call x1, Pallas kernels, on_device(): call(outer_kernel, [(middle, BF), (middle, BF), ((2, 2, width, channels),...  2.87 us
    pallas_call x2, Pallas kernels, on_device(): call(functools.partial(anchor_kernel, pieces), states, [VMEM] * (5 + 3 *...  2.82 us
    ppermute x1, starting transfers between devices, on_device(): arrived = [lax.ppermute(near, 'clip', routes[0])] + far  2.78 us
  transfers between devices with their start and end apart: 7, of which 1 were waited for; matrix products, arithmetic and copies ran while one was open for 0% of the time, Pallas kernels for 44%

profile of v11, /device:TPU:0, one launch (start us, length us, event | category | flops | bytes accessed | tf_op | source)
XLA Modules:
  0.0 40.9 jit_solution(13183454526051999458)
XLA Ops:
  0.0 0.0 copy-start
  0.0 1.3 %copy-done.3 = bf16[4,5,64,320]{3,2,1,0:T(8,128)(2,1)S(1)} copy-done((bf16[4,5,64,320]{3,2,1,0:T(8,128)(2,1)S(1)}, bf16[4,5,64,320]{3,2,1,0:T(8,128)(2,1)}, u32[]{:S(2)}) %copy-start.3) | copy-done | bytes 819224
  1.4 0.1 shard_map.146
  1.5 0.7 %collective-permute-start = (bf16[640,128]{1,0:T(8,128)(2,1)S(1)}, bf16[640,128]{1,0:T(8,128)(2,1)S(1)}, u32[]{:S(2)}, u32[]{:S(2)}) collective-permute-start(bf16[640,128]{1,0:T(8,128)(2,1)S(1)} %get-tuple-element.37), channel_id=1, source_target_pairs={{1,2},{2,1},{5,6},{6,5},{9,10},{10,9},{13,14},{14,13},{17,18},{18,... | collective-permute-start | bytes 491528 | tf_op jit(solution)/shard_map/ppermute | solution.py:438
  2.1 4.4 %collective-permute-start.1 = (bf16[640,128]{1,0:T(8,128)(2,1)S(1)}, bf16[640,128]{1,0:T(8,128)(2,1)S(1)}, u32[]{:S(2)}, u32[]{:S(2)}) collective-permute-start(bf16[640,128]{1,0:T(8,128)(2,1)S(1)} %get-tuple-element.38), channel_id=1, source_target_pairs={{0,1},{2,3},{1,0},{3,2},{4,5},{6,7},{5,4},{7,6},{8,9},{10,11},{9,8... | collective-permute-start | bytes 491528 | tf_op jit(solution)/shard_map/ppermute | solution.py:439
  6.5 0.0 copy-done
  6.5 0.0 copy-done.8
  6.5 0.0 copy-done.9
  6.5 2.9 %shard_map.145 = (bf16[2,192,320]{2,1,0:T(8,128)(2,1)S(1)}, bf16[2,192,320]{2,1,0:T(8,128)(2,1)S(1)}, f32[2,2,64,320]{3,2,1,0:T(8,128)S(1)}, bf16[960,192]{1,0:T(8,128)(2,1)S(1)}, f32[8,128]{1,0:T(8,128)S(1)}) custom-call(bf16[4,5,64,320]{3,2,1,0:T(8,128)(2,1)S(1)} %copy-done.3, f32[320]{0:T(512)S(1)} %copy-done.8, f32[320]{0:T(512)S(1)} %copy-done.9, ...), custom_call_target="tpu_custom_call" | custom-call | flops 1179648000 | bytes 2097152 | tf_op jit(solution)/shard_map/pallas_call | solution.py:466
  9.4 0.0 collective-permute-done.odd_ref
  9.4 0.0 collective-permute-done.1.even_ref
  9.4 0.0 copy-start.4
  9.4 1.2 %shard_map.147 = (bf16[2,320,320]{2,1,0:T(8,128)(2,1)S(1)}, bf16[2,320,320]{2,1,0:T(8,128)(2,1)S(1)}, bf16[800,128]{1,0:T(8,128)(2,1)S(1)}, bf16[800,128]{1,0:T(8,128)(2,1)S(1)}) custom-call(f32[2,2,64,320]{3,2,1,0:T(8,128)S(1)} %get-tuple-element.36.edge_ref, bf16[640,128]{1,0:T(8,128)(2,1)S(1)} %collective-permute-done.odd_ref, ...), custom_call_target="tpu_custom_call" | custom-call | flops 157286400 | bytes 2097152 | tf_op jit(solution)/shard_map/pallas_call | solution.py:479
  10.6 1.6 %collective-permute-start.2 = (bf16[800,128]{1,0:T(8,128)(2,1)S(1)}, bf16[800,128]{1,0:T(8,128)(2,1)S(1)}, u32[]{:S(2)}, u32[]{:S(2)}) collective-permute-start(bf16[800,128]{1,0:T(8,128)(2,1)S(1)} %get-tuple-element.43), channel_id=1, source_target_pairs={{0,4},{8,12},{4,0},{12,8},{1,5},{9,13},{5,1},{13,9},{2,6},{10,14},... | collective-permute-start | bytes 614408 | tf_op jit(solution)/shard_map/ppermute | solution.py:436
  12.2 0.8 %collective-permute-start.3 = (bf16[800,128]{1,0:T(8,128)(2,1)S(1)}, bf16[800,128]{1,0:T(8,128)(2,1)S(1)}, u32[]{:S(2)}, u32[]{:S(2)}) collective-permute-start(bf16[800,128]{1,0:T(8,128)(2,1)S(1)} %get-tuple-element.44), channel_id=1, source_target_pairs={{4,8},{8,4},{5,9},{9,5},{6,10},{10,6},{7,11},{11,7},{20,24},{24,20... | collective-permute-start | bytes 614408 | tf_op jit(solution)/shard_map/ppermute | solution.py:437
  14.4 0.0 copy-done.4
  14.4 0.0 copy-start.5
  14.4 0.0 copy-start.10
  14.4 3.7 %shard_map.148 = (bf16[4,320,320]{2,1,0:T(8,128)(2,1)S(1)}, bf16[4,320,320]{2,1,0:T(8,128)(2,1)S(1)}) custom-call(bf16[4,5,64,320]{3,2,1,0:T(8,128)(2,1)S(1)} %copy-done.4, bf16[640,128]{1,0:T(8,128)(2,1)S(1)} %collective-permute-done.odd_ref, bf16[640,128]{1,0:T(8,128)(2,1)S(1)} %collective-permute-done.1.even_ref, f32[320]{0:T(512)S(1)} %copy-done.8, ...), custom_call_target="tpu_custom_call" | custom-call | flops 1179648000 | bytes 2097152 | tf_op jit(solution)/shard_map/pallas_call | solution.py:486
  18.1 0.0 copy-start.1
  18.1 0.0 copy-start.11
  18.1 0.0 collective-permute-done.2.even_ref
  18.1 0.0 collective-permute-done.3.odd_ref
  18.1 0.0 copy-done.5
  18.1 0.0 copy-done.10
  18.2 0.9 %shard_map.151.from_ref = bf16[1,800,128]{2,1,0:T(8,128)(2,1)S(1)} custom-call(s32[1,1]{1,0:T(1,128)S(6)} %copy.16.picks_ref, bf16[800,128]{1,0:T(8,128)(2,1)S(1)} %collective-permute-done.2.even_ref, bf16[800,128]{1,0:T(8,128)(2,1)S(1)} %collective-permute-done.3.odd_ref, bf16[4,320,320]{2,1,0:T(8,128)(2,1)S(1)} %get-tuple-element.47.spatial_ref, ...), custom_call_target="tpu_custom_call" | custom-call | flops 196608000 | bytes 2097152 | tf_op jit(solution)/shard_map/pallas_call | solution.py:493
  19.1 0.0 copy-start.12
  19.1 0.0 copy-start.13
  19.1 3.2 %collective-permute-start.4 = (bf16[1,800,128]{2,1,0:T(8,128)(2,1)S(1)}, bf16[1,800,128]{2,1,0:T(8,128)(2,1)S(1)}, u32[]{:S(2)}, u32[]{:S(2)}) collective-permute-start(bf16[1,800,128]{2,1,0:T(8,128)(2,1)S(1)} %shard_map.151.from_ref), channel_id=1, source_target_pairs={{0,12},{4,8},{8,4},{12,0},{1,13},{5,9},{9,5},{13,1},{2,14},{6,10},... | collective-permute-start | bytes 614408 | tf_op jit(solution)/shard_map/ppermute | solution.py:502
  22.3 0.0 copy-done.1
  22.3 0.0 copy-done.11
  22.3 4.2 %shard_map.149 = (bf16[4,320,320]{2,1,0:T(8,128)(2,1)S(1)}, bf16[4,320,320]{2,1,0:T(8,128)(2,1)S(1)}, bf16[4,320,640]{2,1,0:T(8,128)(2,1)S(1)}) custom-call(bf16[800,128]{1,0:T(8,128)(2,1)S(1)} %collective-permute-done.2.even_ref, bf16[800,128]{1,0:T(8,128)(2,1)S(1)} %collective-permute-done.3.odd_ref, ...), custom_call_target="tpu_custom_call" | custom-call | flops 1572864000 | bytes 2097152 | tf_op jit(solution)/shard_map/pallas_call | solution.py:503
  26.5 2.8 %collective-permute-start.6 = (bf16[1,800,128]{2,1,0:T(8,128)(2,1)S(1)}, bf16[1,800,128]{2,1,0:T(8,128)(2,1)S(1)}, u32[]{:S(2)}, u32[]{:S(2)}) collective-permute-start(bf16[1,800,128]{2,1,0:T(8,128)(2,1)S(1)} %shard_map.153), channel_id=1, source_target_pairs={{0,4},{4,0},{8,12},{12,8},{1,5},{5,1},{9,13},{13,9},{2,6},{6,2},{1... | collective-permute-start | bytes 614408 | tf_op jit(solution)/shard_map/ppermute | solution.py:511
  29.3 0.0 copy-done.12
  29.3 0.0 copy-done.13
  29.3 2.2 %shard_map.150 = (f32[2,320,128]{2,1,0:T(8,128)S(1)}, f32[2,320,128]{2,1,0:T(8,128)S(1)}, f32[2,320,384]{2,1,0:T(8,128)S(1)}, f32[8,128]{1,0:T(8,128)S(1)}) custom-call(s32[1,1]{1,0:T(1,128)S(6)} %copy.16.picks_ref, s32[1]{0:T(128)S(6)} %copy.17.window_ref, bf16[4,320,320]{2,1,0:T(8,128)(2,1)S(1)} %get-tuple-element.49.query_ref, ...), custom_call_target="tpu_custom_call" | custom-call | flops 1310720000 | bytes 2097152 | tf_op jit(solution)/shard_map/pallas_call | solution.py:517
  31.5 0.0 collective-permute-done.4.refs_0_.anchor_ref
  31.6 1.2 %collective-permute-start.5 = (bf16[1,800,128]{2,1,0:T(8,128)(2,1)S(1)}, bf16[1,800,128]{2,1,0:T(8,128)(2,1)S(1)}, u32[]{:S(2)}, u32[]{:S(2)}) collective-permute-start(bf16[1,800,128]{2,1,0:T(8,128)(2,1)S(1)} %get-tuple-element.52), channel_id=1, source_target_pairs={{0,4},{4,0},{8,12},{12,8},{1,5},{5,1},{9,13},{13,9},{2,6},{6,2},{1... | collective-permute-start | bytes 614408 | tf_op jit(solution)/shard_map/ppermute | solution.py:532
  32.8 2.2 %shard_map.154 = (f32[2,320,128]{2,1,0:T(8,128)S(1)}, f32[2,320,128]{2,1,0:T(8,128)S(1)}, f32[2,320,384]{2,1,0:T(8,128)S(1)}, f32[8,128]{1,0:T(8,128)}) custom-call(s32[1,1]{1,0:T(1,128)S(6)} %copy.16.picks_ref, s32[1]{0:T(128)S(6)} %copy.17.window_ref, bf16[4,320,320]{2,1,0:T(8,128)(2,1)S(1)} %get-tuple-element.49.query_ref, ...), custom_call_target="tpu_custom_call" | custom-call | flops 1310720000 | bytes 2097152 | tf_op jit(solution)/shard_map/pallas_call | solution.py:517
  35.0 0.0 collective-permute-done.6.anchor_ref
  35.0 0.0 copy-done.2
  35.0 0.0 copy-done.6
  35.0 1.5 %shard_map.155 = (f32[4,320,128]{2,1,0:T(8,128)S(1)}, f32[4,320,128]{2,1,0:T(8,128)S(1)}, f32[4,320,384]{2,1,0:T(8,128)S(1)}) custom-call(bf16[1,800,128]{2,1,0:T(8,128)(2,1)S(1)} %collective-permute-done.6.anchor_ref, bf16[320,640]{1,0:T(8,128)(2,1)S(1)} %copy-done.1, bf16[320,128]{1,0:T(8,128)(2,1)S(1)} %copy-done.6, bf16[640,128]{1,0:T(8,128)(2,1)S(1)} %copy-done.2, ...), custom_call_target="tpu_custom_call" | custom-call | flops 1048576000 | bytes 2097152 | tf_op jit(solution)/shard_map/pallas_call | solution.py:540
  36.5 0.0 copy-start.7
  36.6 1.3 %shard_map.156 = (f32[4,320,128]{2,1,0:T(8,128)S(1)}, f32[4,320,128]{2,1,0:T(8,128)S(1)}, f32[4,320,384]{2,1,0:T(8,128)S(1)}) custom-call(bf16[1,800,128]{2,1,0:T(8,128)(2,1)S(1)} %collective-permute-done.4.refs_0_.anchor_ref, bf16[320,640]{1,0:T(8,128)(2,1)S(1)} %copy-done.1, bf16[320,128]{1,0:T(8,128)(2,1)S(1)} %copy-done.6, ...), custom_call_target="tpu_custom_call" | custom-call | flops 1048576000 | bytes 2097152 | tf_op jit(solution)/shard_map/pallas_call | solution.py:540
  37.9 0.2 collective-permute-done.5.anchor_ref
  38.0 0.0 copy-done.7
  38.0 2.7 %shard_map.157 = bf16[4,5,64,320]{3,2,1,0:T(8,128)(2,1)} custom-call(bf16[1,800,128]{2,1,0:T(8,128)(2,1)S(1)} %collective-permute-done.5.anchor_ref, bf16[320,640]{1,0:T(8,128)(2,1)S(1)} %copy-done.1, bf16[320,128]{1,0:T(8,128)(2,1)S(1)} %copy-done.6, bf16[640,128]{1,0:T(8,128)(2,1)S(1)} %copy-done.2, bf16[4,320,320]{2,1,0:T(8,128)(2,1)S(1)} %get-tuple-element.49.query_ref, ...), custom_call_target="tpu_custom_call" | custom-call | flops 1310720000 | bytes 2097152 | tf_op jit(solution)/shard_map/pallas_call | solution.py:548
  (7 shorter events, 0.0 us)
Async XLA Ops:
  0.0 6.5 %copy-start = (bf16[3,3,320,320]{3,2,1,0:T(8,128)(2,1)S(1)}, bf16[3,3,320,320]{3,2,1,0:T(8,128)(2,1)}, u32[]{:S(2)}) copy-start(bf16[3,3,320,320]{3,2,1,0:T(8,128)(2,1)} %param.19) | copy-start | bytes 5529604
  0.0 1.4 %copy-start.3 = (bf16[4,5,64,320]{3,2,1,0:T(8,128)(2,1)S(1)}, bf16[4,5,64,320]{3,2,1,0:T(8,128)(2,1)}, u32[]{:S(2)}) copy-start(bf16[4,5,64,320]{3,2,1,0:T(8,128)(2,1)} %x_ref.5) | copy-start | bytes 2457604
  1.4 5.1 %copy-start.8 = (f32[320]{0:T(512)S(1)}, f32[320]{0:T(512)}, u32[]{:S(2)}) copy-start(f32[320]{0:T(512)} %g1_ref.5) | copy-start | bytes 3844
  1.4 5.1 %copy-start.9 = (f32[320]{0:T(512)S(1)}, f32[320]{0:T(512)}, u32[]{:S(2)}) copy-start(f32[320]{0:T(512)} %g2_ref.5) | copy-start | bytes 3844
  1.5 7.9 %collective-permute-start = (bf16[640,128]{1,0:T(8,128)(2,1)S(1)}, bf16[640,128]{1,0:T(8,128)(2,1)S(1)}, u32[]{:S(2)}, u32[]{:S(2)}) collective-permute-start(bf16[640,128]{1,0:T(8,128)(2,1)S(1)} %get-tuple-element.37), channel_id=1, source_target_pairs={{1,2},{2,1},{5,6},{6,5},{9,10},{10,9},{13,14},{14,13},{17,18},{18,... | collective-permute-start | bytes 491528 | tf_op jit(solution)/shard_map/ppermute | solution.py:438
  2.1 7.3 %collective-permute-start.1 = (bf16[640,128]{1,0:T(8,128)(2,1)S(1)}, bf16[640,128]{1,0:T(8,128)(2,1)S(1)}, u32[]{:S(2)}, u32[]{:S(2)}) collective-permute-start(bf16[640,128]{1,0:T(8,128)(2,1)S(1)} %get-tuple-element.38), channel_id=1, source_target_pairs={{0,1},{2,3},{1,0},{3,2},{4,5},{6,7},{5,4},{7,6},{8,9},{10,11},{9,8... | collective-permute-start | bytes 491528 | tf_op jit(solution)/shard_map/ppermute | solution.py:439
  9.4 5.0 %copy-start.4 = (bf16[4,5,64,320]{3,2,1,0:T(8,128)(2,1)S(1)}, bf16[4,5,64,320]{3,2,1,0:T(8,128)(2,1)}, u32[]{:S(2)}) copy-start(bf16[4,5,64,320]{3,2,1,0:T(8,128)(2,1)} %x_ref.5) | copy-start | bytes 2457604
  10.6 7.6 %collective-permute-start.2 = (bf16[800,128]{1,0:T(8,128)(2,1)S(1)}, bf16[800,128]{1,0:T(8,128)(2,1)S(1)}, u32[]{:S(2)}, u32[]{:S(2)}) collective-permute-start(bf16[800,128]{1,0:T(8,128)(2,1)S(1)} %get-tuple-element.43), channel_id=1, source_target_pairs={{0,4},{8,12},{4,0},{12,8},{1,5},{9,13},{5,1},{13,9},{2,6},{10,14},... | collective-permute-start | bytes 614408 | tf_op jit(solution)/shard_map/ppermute | solution.py:436
  12.2 5.9 %collective-permute-start.3 = (bf16[800,128]{1,0:T(8,128)(2,1)S(1)}, bf16[800,128]{1,0:T(8,128)(2,1)S(1)}, u32[]{:S(2)}, u32[]{:S(2)}) collective-permute-start(bf16[800,128]{1,0:T(8,128)(2,1)S(1)} %get-tuple-element.44), channel_id=1, source_target_pairs={{4,8},{8,4},{5,9},{9,5},{6,10},{10,6},{7,11},{11,7},{20,24},{24,20... | collective-permute-start | bytes 614408 | tf_op jit(solution)/shard_map/ppermute | solution.py:437
  14.4 3.8 %copy-start.5 = (bf16[3,320,320]{2,1,0:T(8,128)(2,1)S(1)}, bf16[3,320,320]{2,1,0:T(8,128)(2,1)}, u32[]{:S(2)}) copy-start(bf16[3,320,320]{2,1,0:T(8,128)(2,1)} %wt_ref.3) | copy-start | bytes 1843204
  14.4 3.8 %copy-start.10 = (f32[320]{0:T(512)S(1)}, f32[320]{0:T(512)}, u32[]{:S(2)}) copy-start(f32[320]{0:T(512)} %g3_ref.3) | copy-start | bytes 3844
  18.1 4.2 %copy-start.1 = (bf16[320,640]{1,0:T(8,128)(2,1)S(1)}, bf16[320,640]{1,0:T(8,128)(2,1)}, u32[]{:S(2)}) copy-start(bf16[320,640]{1,0:T(8,128)(2,1)} %wkv_ref.7) | copy-start | bytes 1228804
  18.1 4.2 %copy-start.11 = (bf16[320,320]{1,0:T(8,128)(2,1)S(1)}, bf16[320,320]{1,0:T(8,128)(2,1)}, u32[]{:S(2)}) copy-start(bf16[320,320]{1,0:T(8,128)(2,1)} %wq_ref.1) | copy-start | bytes 614404
  19.1 10.2 %copy-start.12 = (bf16[1280,128]{1,0:T(8,128)(2,1)S(1)}, bf16[1280,128]{1,0:T(8,128)(2,1)}, u32[]{:S(2)}) copy-start(bf16[1280,128]{1,0:T(8,128)(2,1)} %constant.9.clone.to_channels_ref) | copy-start | bytes 983044
  19.1 10.2 %copy-start.13 = (bf16[1280,128]{1,0:T(8,128)(2,1)S(1)}, bf16[1280,128]{1,0:T(8,128)(2,1)}, u32[]{:S(2)}) copy-start(bf16[1280,128]{1,0:T(8,128)(2,1)} %constant.8.clone.to_lanes_ref) | copy-start | bytes 983044
  19.1 12.4 %collective-permute-start.4 = (bf16[1,800,128]{2,1,0:T(8,128)(2,1)S(1)}, bf16[1,800,128]{2,1,0:T(8,128)(2,1)S(1)}, u32[]{:S(2)}, u32[]{:S(2)}) collective-permute-start(bf16[1,800,128]{2,1,0:T(8,128)(2,1)S(1)} %shard_map.151.from_ref), channel_id=1, source_target_pairs={{0,12},{4,8},{8,4},{12,0},{1,13},{5,9},{9,5},{13,1},{2,14},{6,10},... | collective-permute-start | bytes 614408 | tf_op jit(solution)/shard_map/ppermute | solution.py:502
  26.5 8.4 %collective-permute-start.6 = (bf16[1,800,128]{2,1,0:T(8,128)(2,1)S(1)}, bf16[1,800,128]{2,1,0:T(8,128)(2,1)S(1)}, u32[]{:S(2)}, u32[]{:S(2)}) collective-permute-start(bf16[1,800,128]{2,1,0:T(8,128)(2,1)S(1)} %shard_map.153), channel_id=1, source_target_pairs={{0,4},{4,0},{8,12},{12,8},{1,5},{5,1},{9,13},{13,9},{2,6},{6,2},{1... | collective-permute-start | bytes 614408 | tf_op jit(solution)/shard_map/ppermute | solution.py:511
  31.6 6.4 %collective-permute-start.5 = (bf16[1,800,128]{2,1,0:T(8,128)(2,1)S(1)}, bf16[1,800,128]{2,1,0:T(8,128)(2,1)S(1)}, u32[]{:S(2)}, u32[]{:S(2)}) collective-permute-start(bf16[1,800,128]{2,1,0:T(8,128)(2,1)S(1)} %get-tuple-element.52), channel_id=1, source_target_pairs={{0,4},{4,0},{8,12},{12,8},{1,5},{5,1},{9,13},{13,9},{2,6},{6,2},{1... | collective-permute-start | bytes 614408 | tf_op jit(solution)/shard_map/ppermute | solution.py:532
  32.8 2.2 %copy-start.2 = (bf16[640,128]{1,0:T(8,128)(2,1)S(1)}, bf16[640,128]{1,0:T(8,128)(2,1)}, u32[]{:S(2)}) copy-start(bf16[640,128]{1,0:T(8,128)(2,1)} %constant.11.clone.to_channels_ref) | copy-start | bytes 491524
  32.8 2.2 %copy-start.6 = (bf16[320,128]{1,0:T(8,128)(2,1)S(1)}, bf16[320,128]{1,0:T(8,128)(2,1)}, u32[]{:S(2)}) copy-start(bf16[320,128]{1,0:T(8,128)(2,1)} %constant.10.clone.to_lanes_ref) | copy-start | bytes 245764
  36.5 1.5 %copy-start.7 = (bf16[320,320]{1,0:T(8,128)(2,1)S(1)}, bf16[320,320]{1,0:T(8,128)(2,1)}, u32[]{:S(2)}) copy-start(bf16[320,320]{1,0:T(8,128)(2,1)} %wo_ref.1) | copy-start | bytes 614404

commit v12 on v10

--- a/solution.py
+++ b/solution.py
@@ -105,7 +105,7 @@
     return jnp.where(odd, second, first), jnp.where(odd, first, second)
 
 
-def edge_kernel(x_ref, odd_ref, even_ref):
+def edge_kernel(x_ref, even_ref, odd_ref):
     frames, height, width, channels = x_ref.shape
     odd = at_odd("strip")
     top = x_ref[:, 0].reshape(frames * width, channels)
@@ -182,7 +182,7 @@
 
 
 def outer_edge_kernel(
-    frames, edge_ref, odd_ref, even_ref, order_ref, mid_ref, mid2_ref, g1_ref, g2_ref, w_ref, rem_ref,
+    frames, edge_ref, even_ref, odd_ref, order_ref, mid_ref, mid2_ref, g1_ref, g2_ref, w_ref, rem_ref,
     spatial_ref, hidden_ref, even_clip_ref, odd_clip_ref,
 ):
     _, cells, channels = spatial_ref.shape
@@ -211,7 +211,7 @@
 
 
 def inner_kernel(
-    x_ref, odd_ref, even_ref, g1_ref, g2_ref, w_ref, rem_ref, outer_spatial_ref, outer_hidden_ref,
+    x_ref, even_ref, odd_ref, g1_ref, g2_ref, w_ref, rem_ref, outer_spatial_ref, outer_hidden_ref,
     spatial_ref, hidden_ref, col_ref,
 ):
     frames, height, width, channels = x_ref.shape
@@ -456,10 +456,10 @@
 
     x, g1, g2, g3, w = latents, gain_one, gain_two, gain_three, ws
 
-    strip_odd, strip_even = call(
+    strip_even, strip_odd = call(
         edge_kernel, [((edge_packed, LANES), BF)] * 2, [VMEM], flops=8 * frames * cells * one
     )(x)
-    strip_odd, strip_even = swapped(strip_odd, strip_even, "strip", False)
+    strip_odd, strip_even = swapped(strip_odd, strip_even, "strip", True)
     outer_col = pltpu.VMEM((2 * cells, 3 * channels), BF)
     inner_col = pltpu.VMEM(((frames - 2) * (cells + 2 * width), 3 * channels), BF)
     middle = (2, cells - 2 * width, channels)
@@ -481,7 +481,7 @@
         [((2, cells, channels), BF)] * 2 + [((packed, LANES), BF)] * 2,
         [VMEM] * 10,
         flops=6 * 2 * width * one,
-    )(edge, strip_odd, strip_even, order, mid, mid2, g1, g2, w, w_rem)
+    )(edge, strip_even, strip_odd, order, mid, mid2, g1, g2, w, w_rem)
     clip_odd, clip_even = swapped(clip_odd, clip_even, "clip", True)
     spatial, hidden = call(
         inner_kernel,
@@ -489,7 +489,7 @@
         [VMEM] * 9,
         [inner_col],
         flops=9 * (frames - 2) * cells * one,
-    )(x, strip_odd, strip_even, g1, g2, w, w_rem, outer_spatial, outer_hidden)
+    )(x, strip_even, strip_odd, g1, g2, w, w_rem, outer_spatial, outer_hidden)
     (chosen,) = call(
         chosen_kernel, [((count, packed, LANES), BF)], [VMEM] * 7, flops=3 * cells * one
     )(anchor_index, clip_even, clip_odd, spatial, hidden, g3, temporal_w)

time: 41.1 us -> 39.6 us (0.964)
  starting transfers between devices: 14.6 us -> 12.7 us
    ppermute x2 -> x0, starting transfers between devices: 5.03 us -> none  [the longest x1 4.36 us: swapped(): return (odd, lax.ppermute(even, axis, pairs[1]))]
    ppermute x1, starting transfers between devices: 1.21 us -> 3.08 us  [on_device(): arrived += [lax.ppermute(v, 'clip', routes[0]) for v in relayed]]
    ppermute x1 -> x2, starting transfers between devices: 1.64 us -> 3.18 us  [swapped(): even = lax.ppermute(even, axis, pairs[1])]
    ppermute x2, starting transfers between devices: 5.9 us -> 4.92 us  [on_device(): arrived = [lax.ppermute(v, 'clip', route) for v, route in zip(sent, routes)]]
    ppermute x1 -> x2, starting transfers between devices: 0.84 us -> 1.5 us  [swapped(): return (lax.ppermute(odd, axis, pairs[0]), even)]
  transfers between devices with their start and end apart: 7 -> 7, of which waited for: 1 -> 1; matrix products, arithmetic and copies ran while one was open for 0% -> 0% of each run, Pallas kernels for 44% -> 46%
where the time goes in v12:
time: 39.6 us; the launch traced here: 39.4 us
  Pallas kernels  23 us (58%)
  starting transfers between devices  12.7 us (32%)
  between operations  1.75 us (4%)
  local copies, waits for them, and re-layouts  1.42 us (4%)
  waiting for transfers between devices  0.51 us (1%)
    ppermute x2, starting transfers between devices, on_device(): arrived = [lax.ppermute(v, 'clip', route) for v, route in zip(sent, routes)]  4.92 us
    pallas_call x2, Pallas kernels, local(): call(functools.partial(local_kernel, start), [(shape + (LANES,), F32)] *...  4.5 us
    pallas_call x1, Pallas kernels, on_device(): call(temporal_kernel, [(some, BF), (some, BF), ((frames, cells, 2 * chann...  4.22 us
    pallas_call x1, Pallas kernels, on_device(): call(inner_kernel, [(some, BF), (some, BF)], [VMEM] * 9, [inner_col], flo...  3.69 us
    ppermute x2, starting transfers between devices, swapped(): even = lax.ppermute(even, axis, pairs[1])  3.18 us
    ppermute x1, starting transfers between devices, on_device(): arrived += [lax.ppermute(v, 'clip', routes[0]) for v in relayed]  3.08 us
    pallas_call x1, Pallas kernels, on_device(): call(outer_kernel, [(middle, BF), (middle, BF), ((2, 2, width, channels),...  2.87 us
    pallas_call x2, Pallas kernels, on_device(): call(functools.partial(anchor_kernel, pieces), states, [VMEM] * (5 + 3 *...  2.82 us
  transfers between devices with their start and end apart: 7, of which 1 were waited for; matrix products, arithmetic and copies ran while one was open for 0% of the time, Pallas kernels for 46%

profile of v12, /device:TPU:0, one launch (start us, length us, event | category | flops | bytes accessed | tf_op | source)
XLA Modules:
  0.0 39.4 jit_solution(17679001510729290566)
XLA Ops:
  0.0 0.0 copy-start.3
  0.0 1.3 %copy-done.3 = bf16[4,5,64,320]{3,2,1,0:T(8,128)(2,1)S(1)} copy-done((bf16[4,5,64,320]{3,2,1,0:T(8,128)(2,1)S(1)}, bf16[4,5,64,320]{3,2,1,0:T(8,128)(2,1)}, u32[]{:S(2)}) %copy-start.3) | copy-done | bytes 819224
  1.4 0.1 shard_map.146
  1.5 0.5 %collective-permute-start = (bf16[640,128]{1,0:T(8,128)(2,1)S(1)}, bf16[640,128]{1,0:T(8,128)(2,1)S(1)}, u32[]{:S(2)}, u32[]{:S(2)}) collective-permute-start(bf16[640,128]{1,0:T(8,128)(2,1)S(1)} %get-tuple-element.37), channel_id=1, source_target_pairs={{0,1},{2,3},{1,0},{3,2},{4,5},{6,7},{5,4},{7,6},{8,9},{10,11},{9,8... | collective-permute-start | bytes 491528 | tf_op jit(solution)/shard_map/ppermute | solution.py:436
  2.0 0.7 %collective-permute-start.1 = (bf16[640,128]{1,0:T(8,128)(2,1)S(1)}, bf16[640,128]{1,0:T(8,128)(2,1)S(1)}, u32[]{:S(2)}, u32[]{:S(2)}) collective-permute-start(bf16[640,128]{1,0:T(8,128)(2,1)S(1)} %get-tuple-element.38), channel_id=1, source_target_pairs={{1,2},{2,1},{5,6},{6,5},{9,10},{10,9},{13,14},{14,13},{17,18},{18,... | collective-permute-start | bytes 491528 | tf_op jit(solution)/shard_map/ppermute | solution.py:437
  2.6 0.0 copy-done
  2.7 0.0 copy-done.8
  2.7 0.0 copy-done.9
  2.7 2.9 %shard_map.145 = (bf16[2,192,320]{2,1,0:T(8,128)(2,1)S(1)}, bf16[2,192,320]{2,1,0:T(8,128)(2,1)S(1)}, f32[2,2,64,320]{3,2,1,0:T(8,128)S(1)}, bf16[960,192]{1,0:T(8,128)(2,1)S(1)}, f32[8,128]{1,0:T(8,128)S(1)}) custom-call(bf16[4,5,64,320]{3,2,1,0:T(8,128)(2,1)S(1)} %copy-done.3, f32[320]{0:T(512)S(1)} %copy-done.8, f32[320]{0:T(512)S(1)} %copy-done.9, ...), custom_call_target="tpu_custom_call" | custom-call | flops 1179648000 | bytes 2097152 | tf_op jit(solution)/shard_map/pallas_call | solution.py:466
  5.5 0.0 collective-permute-done.even_ref
  5.6 0.0 collective-permute-done.1.odd_ref
  5.6 0.0 copy-start.4
  5.6 1.2 %shard_map.147 = (bf16[2,320,320]{2,1,0:T(8,128)(2,1)S(1)}, bf16[2,320,320]{2,1,0:T(8,128)(2,1)S(1)}, bf16[800,128]{1,0:T(8,128)(2,1)S(1)}, bf16[800,128]{1,0:T(8,128)(2,1)S(1)}) custom-call(f32[2,2,64,320]{3,2,1,0:T(8,128)S(1)} %get-tuple-element.36.edge_ref, bf16[640,128]{1,0:T(8,128)(2,1)S(1)} %collective-permute-done.even_ref, ...), custom_call_target="tpu_custom_call" | custom-call | flops 157286400 | bytes 2097152 | tf_op jit(solution)/shard_map/pallas_call | solution.py:479
  6.7 2.7 %collective-permute-start.2 = (bf16[800,128]{1,0:T(8,128)(2,1)S(1)}, bf16[800,128]{1,0:T(8,128)(2,1)S(1)}, u32[]{:S(2)}, u32[]{:S(2)}) collective-permute-start(bf16[800,128]{1,0:T(8,128)(2,1)S(1)} %get-tuple-element.43), channel_id=1, source_target_pairs={{0,4},{8,12},{4,0},{12,8},{1,5},{9,13},{5,1},{13,9},{2,6},{10,14},... | collective-permute-start | bytes 614408 | tf_op jit(solution)/shard_map/ppermute | solution.py:436
  9.4 0.8 %collective-permute-start.3 = (bf16[800,128]{1,0:T(8,128)(2,1)S(1)}, bf16[800,128]{1,0:T(8,128)(2,1)S(1)}, u32[]{:S(2)}, u32[]{:S(2)}) collective-permute-start(bf16[800,128]{1,0:T(8,128)(2,1)S(1)} %get-tuple-element.44), channel_id=1, source_target_pairs={{4,8},{8,4},{5,9},{9,5},{6,10},{10,6},{7,11},{11,7},{20,24},{24,20... | collective-permute-start | bytes 614408 | tf_op jit(solution)/shard_map/ppermute | solution.py:437
  11.5 0.0 copy-done.4
  11.6 0.0 copy-start.5
  11.6 0.0 copy-start.10
  11.6 3.7 %shard_map.148 = (bf16[4,320,320]{2,1,0:T(8,128)(2,1)S(1)}, bf16[4,320,320]{2,1,0:T(8,128)(2,1)S(1)}) custom-call(bf16[4,5,64,320]{3,2,1,0:T(8,128)(2,1)S(1)} %copy-done.4, bf16[640,128]{1,0:T(8,128)(2,1)S(1)} %collective-permute-done.even_ref, bf16[640,128]{1,0:T(8,128)(2,1)S(1)} %collective-permute-done.1.odd_ref, f32[320]{0:T(512)S(1)} %copy-done.8, ...), custom_call_target="tpu_custom_call" | custom-call | flops 1179648000 | bytes 2097152 | tf_op jit(solution)/shard_map/pallas_call | solution.py:486
  15.3 0.0 copy-start.1
  15.3 0.0 copy-start.11
  15.3 0.0 collective-permute-done.2.even_ref
  15.3 0.0 collective-permute-done.3.odd_ref
  15.3 0.0 copy-done.5
  15.3 0.0 copy-done.10
  15.3 0.9 %shard_map.151.from_ref = bf16[1,800,128]{2,1,0:T(8,128)(2,1)S(1)} custom-call(s32[1,1]{1,0:T(1,128)S(6)} %copy.16.picks_ref, bf16[800,128]{1,0:T(8,128)(2,1)S(1)} %collective-permute-done.2.even_ref, bf16[800,128]{1,0:T(8,128)(2,1)S(1)} %collective-permute-done.3.odd_ref, bf16[4,320,320]{2,1,0:T(8,128)(2,1)S(1)} %get-tuple-element.47.spatial_ref, ...), custom_call_target="tpu_custom_call" | custom-call | flops 196608000 | bytes 2097152 | tf_op jit(solution)/shard_map/pallas_call | solution.py:493
  16.3 0.0 copy-start.12
  16.3 0.0 copy-start.13
  16.3 2.5 %collective-permute-start.4 = (bf16[1,800,128]{2,1,0:T(8,128)(2,1)S(1)}, bf16[1,800,128]{2,1,0:T(8,128)(2,1)S(1)}, u32[]{:S(2)}, u32[]{:S(2)}) collective-permute-start(bf16[1,800,128]{2,1,0:T(8,128)(2,1)S(1)} %shard_map.151.from_ref), channel_id=1, source_target_pairs={{0,12},{4,8},{8,4},{12,0},{1,13},{5,9},{9,5},{13,1},{2,14},{6,10},... | collective-permute-start | bytes 614408 | tf_op jit(solution)/shard_map/ppermute | solution.py:504
  18.9 2.4 %collective-permute-start.6 = (bf16[1,800,128]{2,1,0:T(8,128)(2,1)S(1)}, bf16[1,800,128]{2,1,0:T(8,128)(2,1)S(1)}, u32[]{:S(2)}, u32[]{:S(2)}) collective-permute-start(bf16[1,800,128]{2,1,0:T(8,128)(2,1)S(1)} %shard_map.153), channel_id=1, source_target_pairs={{0,4},{4,0},{8,12},{12,8},{1,5},{5,1},{9,13},{13,9},{2,6},{6,2},{1... | collective-permute-start | bytes 614408 | tf_op jit(solution)/shard_map/ppermute | solution.py:504
  21.3 0.0 copy-done.1
  21.3 0.0 copy-done.11
  21.3 4.2 %shard_map.149 = (bf16[4,320,320]{2,1,0:T(8,128)(2,1)S(1)}, bf16[4,320,320]{2,1,0:T(8,128)(2,1)S(1)}, bf16[4,320,640]{2,1,0:T(8,128)(2,1)S(1)}) custom-call(bf16[800,128]{1,0:T(8,128)(2,1)S(1)} %collective-permute-done.2.even_ref, bf16[800,128]{1,0:T(8,128)(2,1)S(1)} %collective-permute-done.3.odd_ref, ...), custom_call_target="tpu_custom_call" | custom-call | flops 1572864000 | bytes 2097152 | tf_op jit(solution)/shard_map/pallas_call | solution.py:505
  25.5 0.0 copy-done.12
  25.5 0.0 copy-done.13
  25.5 2.3 %shard_map.150 = (f32[2,320,128]{2,1,0:T(8,128)S(1)}, f32[2,320,128]{2,1,0:T(8,128)S(1)}, f32[2,320,384]{2,1,0:T(8,128)S(1)}, f32[8,128]{1,0:T(8,128)S(1)}) custom-call(s32[1,1]{1,0:T(1,128)S(6)} %copy.16.picks_ref, s32[1]{0:T(128)S(6)} %copy.17.window_ref, bf16[4,320,320]{2,1,0:T(8,128)(2,1)S(1)} %get-tuple-element.49.query_ref, ...), custom_call_target="tpu_custom_call" | custom-call | flops 1310720000 | bytes 2097152 | tf_op jit(solution)/shard_map/pallas_call | solution.py:517
  27.8 0.0 collective-permute-done.4.refs_0_.anchor_ref
  27.8 3.1 %collective-permute-start.5 = (bf16[1,800,128]{2,1,0:T(8,128)(2,1)S(1)}, bf16[1,800,128]{2,1,0:T(8,128)(2,1)S(1)}, u32[]{:S(2)}, u32[]{:S(2)}) collective-permute-start(bf16[1,800,128]{2,1,0:T(8,128)(2,1)S(1)} %get-tuple-element.52), channel_id=1, source_target_pairs={{0,4},{4,0},{8,12},{12,8},{1,5},{5,1},{9,13},{13,9},{2,6},{6,2},{1... | collective-permute-start | bytes 614408 | tf_op jit(solution)/shard_map/ppermute | solution.py:532
  30.9 2.2 %shard_map.154 = (f32[2,320,128]{2,1,0:T(8,128)S(1)}, f32[2,320,128]{2,1,0:T(8,128)S(1)}, f32[2,320,384]{2,1,0:T(8,128)S(1)}, f32[8,128]{1,0:T(8,128)}) custom-call(s32[1,1]{1,0:T(1,128)S(6)} %copy.16.picks_ref, s32[1]{0:T(128)S(6)} %copy.17.window_ref, bf16[4,320,320]{2,1,0:T(8,128)(2,1)S(1)} %get-tuple-element.49.query_ref, ...), custom_call_target="tpu_custom_call" | custom-call | flops 1310720000 | bytes 2097152 | tf_op jit(solution)/shard_map/pallas_call | solution.py:517
  33.1 0.0 collective-permute-done.6.anchor_ref
  33.1 0.0 copy-done.2
  33.1 0.0 copy-done.6
  33.2 1.5 %shard_map.155 = (f32[4,320,128]{2,1,0:T(8,128)S(1)}, f32[4,320,128]{2,1,0:T(8,128)S(1)}, f32[4,320,384]{2,1,0:T(8,128)S(1)}) custom-call(bf16[1,800,128]{2,1,0:T(8,128)(2,1)S(1)} %collective-permute-done.6.anchor_ref, bf16[320,640]{1,0:T(8,128)(2,1)S(1)} %copy-done.1, bf16[320,128]{1,0:T(8,128)(2,1)S(1)} %copy-done.6, bf16[640,128]{1,0:T(8,128)(2,1)S(1)} %copy-done.2, ...), custom_call_target="tpu_custom_call" | custom-call | flops 1048576000 | bytes 2097152 | tf_op jit(solution)/shard_map/pallas_call | solution.py:540
  34.7 0.0 copy-start.7
  34.7 1.3 %shard_map.156 = (f32[4,320,128]{2,1,0:T(8,128)S(1)}, f32[4,320,128]{2,1,0:T(8,128)S(1)}, f32[4,320,384]{2,1,0:T(8,128)S(1)}) custom-call(bf16[1,800,128]{2,1,0:T(8,128)(2,1)S(1)} %collective-permute-done.4.refs_0_.anchor_ref, bf16[320,640]{1,0:T(8,128)(2,1)S(1)} %copy-done.1, bf16[320,128]{1,0:T(8,128)(2,1)S(1)} %copy-done.6, ...), custom_call_target="tpu_custom_call" | custom-call | flops 1048576000 | bytes 2097152 | tf_op jit(solution)/shard_map/pallas_call | solution.py:540
  36.0 0.5 %collective-permute-done.5.anchor_ref = bf16[1,800,128]{2,1,0:T(8,128)(2,1)S(1)} collective-permute-done((bf16[1,800,128]{2,1,0:T(8,128)(2,1)S(1)}, bf16[1,800,128]{2,1,0:T(8,128)(2,1)S(1)}, u32[]{:S(2)}, u32[]{:S(2)}) %collective-permute-start.5) | collective-permute-done | bytes 204832 | tf_op jit(solution)/shard_map/ppermute | solution.py:532
  36.5 0.0 copy-done.7
  36.5 2.7 %shard_map.157 = bf16[4,5,64,320]{3,2,1,0:T(8,128)(2,1)} custom-call(bf16[1,800,128]{2,1,0:T(8,128)(2,1)S(1)} %collective-permute-done.5.anchor_ref, bf16[320,640]{1,0:T(8,128)(2,1)S(1)} %copy-done.1, bf16[320,128]{1,0:T(8,128)(2,1)S(1)} %copy-done.6, bf16[640,128]{1,0:T(8,128)(2,1)S(1)} %copy-done.2, bf16[4,320,320]{2,1,0:T(8,128)(2,1)S(1)} %get-tuple-element.49.query_ref, ...), custom_call_target="tpu_custom_call" | custom-call | flops 1310720000 | bytes 2097152 | tf_op jit(solution)/shard_map/pallas_call | solution.py:548
  (7 shorter events, 0.0 us)
Async XLA Ops:
  0.0 2.6 %copy-start = (bf16[3,3,320,320]{3,2,1,0:T(8,128)(2,1)S(1)}, bf16[3,3,320,320]{3,2,1,0:T(8,128)(2,1)}, u32[]{:S(2)}) copy-start(bf16[3,3,320,320]{3,2,1,0:T(8,128)(2,1)} %param.19) | copy-start | bytes 5529604
  0.0 1.4 %copy-start.3 = (bf16[4,5,64,320]{3,2,1,0:T(8,128)(2,1)S(1)}, bf16[4,5,64,320]{3,2,1,0:T(8,128)(2,1)}, u32[]{:S(2)}) copy-start(bf16[4,5,64,320]{3,2,1,0:T(8,128)(2,1)} %x_ref.5) | copy-start | bytes 2457604
  1.4 1.3 %copy-start.8 = (f32[320]{0:T(512)S(1)}, f32[320]{0:T(512)}, u32[]{:S(2)}) copy-start(f32[320]{0:T(512)} %g1_ref.5) | copy-start | bytes 3844
  1.4 1.3 %copy-start.9 = (f32[320]{0:T(512)S(1)}, f32[320]{0:T(512)}, u32[]{:S(2)}) copy-start(f32[320]{0:T(512)} %g2_ref.5) | copy-start | bytes 3844
  1.5 4.1 %collective-permute-start = (bf16[640,128]{1,0:T(8,128)(2,1)S(1)}, bf16[640,128]{1,0:T(8,128)(2,1)S(1)}, u32[]{:S(2)}, u32[]{:S(2)}) collective-permute-start(bf16[640,128]{1,0:T(8,128)(2,1)S(1)} %get-tuple-element.37), channel_id=1, source_target_pairs={{0,1},{2,3},{1,0},{3,2},{4,5},{6,7},{5,4},{7,6},{8,9},{10,11},{9,8... | collective-permute-start | bytes 491528 | tf_op jit(solution)/shard_map/ppermute | solution.py:436
  2.0 3.6 %collective-permute-start.1 = (bf16[640,128]{1,0:T(8,128)(2,1)S(1)}, bf16[640,128]{1,0:T(8,128)(2,1)S(1)}, u32[]{:S(2)}, u32[]{:S(2)}) collective-permute-start(bf16[640,128]{1,0:T(8,128)(2,1)S(1)} %get-tuple-element.38), channel_id=1, source_target_pairs={{1,2},{2,1},{5,6},{6,5},{9,10},{10,9},{13,14},{14,13},{17,18},{18,... | collective-permute-start | bytes 491528 | tf_op jit(solution)/shard_map/ppermute | solution.py:437
  5.6 6.0 %copy-start.4 = (bf16[4,5,64,320]{3,2,1,0:T(8,128)(2,1)S(1)}, bf16[4,5,64,320]{3,2,1,0:T(8,128)(2,1)}, u32[]{:S(2)}) copy-start(bf16[4,5,64,320]{3,2,1,0:T(8,128)(2,1)} %x_ref.5) | copy-start | bytes 2457604
  6.7 8.6 %collective-permute-start.2 = (bf16[800,128]{1,0:T(8,128)(2,1)S(1)}, bf16[800,128]{1,0:T(8,128)(2,1)S(1)}, u32[]{:S(2)}, u32[]{:S(2)}) collective-permute-start(bf16[800,128]{1,0:T(8,128)(2,1)S(1)} %get-tuple-element.43), channel_id=1, source_target_pairs={{0,4},{8,12},{4,0},{12,8},{1,5},{9,13},{5,1},{13,9},{2,6},{10,14},... | collective-permute-start | bytes 614408 | tf_op jit(solution)/shard_map/ppermute | solution.py:436
  9.4 5.9 %collective-permute-start.3 = (bf16[800,128]{1,0:T(8,128)(2,1)S(1)}, bf16[800,128]{1,0:T(8,128)(2,1)S(1)}, u32[]{:S(2)}, u32[]{:S(2)}) collective-permute-start(bf16[800,128]{1,0:T(8,128)(2,1)S(1)} %get-tuple-element.44), channel_id=1, source_target_pairs={{4,8},{8,4},{5,9},{9,5},{6,10},{10,6},{7,11},{11,7},{20,24},{24,20... | collective-permute-start | bytes 614408 | tf_op jit(solution)/shard_map/ppermute | solution.py:437
  11.6 3.8 %copy-start.5 = (bf16[3,320,320]{2,1,0:T(8,128)(2,1)S(1)}, bf16[3,320,320]{2,1,0:T(8,128)(2,1)}, u32[]{:S(2)}) copy-start(bf16[3,320,320]{2,1,0:T(8,128)(2,1)} %wt_ref.3) | copy-start | bytes 1843204
  11.6 3.8 %copy-start.10 = (f32[320]{0:T(512)S(1)}, f32[320]{0:T(512)}, u32[]{:S(2)}) copy-start(f32[320]{0:T(512)} %g3_ref.3) | copy-start | bytes 3844
  15.3 6.0 %copy-start.1 = (bf16[320,640]{1,0:T(8,128)(2,1)S(1)}, bf16[320,640]{1,0:T(8,128)(2,1)}, u32[]{:S(2)}) copy-start(bf16[320,640]{1,0:T(8,128)(2,1)} %wkv_ref.7) | copy-start | bytes 1228804
  15.3 6.0 %copy-start.11 = (bf16[320,320]{1,0:T(8,128)(2,1)S(1)}, bf16[320,320]{1,0:T(8,128)(2,1)}, u32[]{:S(2)}) copy-start(bf16[320,320]{1,0:T(8,128)(2,1)} %wq_ref.1) | copy-start | bytes 614404
  16.3 9.2 %copy-start.12 = (bf16[1280,128]{1,0:T(8,128)(2,1)S(1)}, bf16[1280,128]{1,0:T(8,128)(2,1)}, u32[]{:S(2)}) copy-start(bf16[1280,128]{1,0:T(8,128)(2,1)} %constant.9.clone.to_channels_ref) | copy-start | bytes 983044
  16.3 9.2 %copy-start.13 = (bf16[1280,128]{1,0:T(8,128)(2,1)S(1)}, bf16[1280,128]{1,0:T(8,128)(2,1)}, u32[]{:S(2)}) copy-start(bf16[1280,128]{1,0:T(8,128)(2,1)} %constant.8.clone.to_lanes_ref) | copy-start | bytes 983044
  16.3 11.4 %collective-permute-start.4 = (bf16[1,800,128]{2,1,0:T(8,128)(2,1)S(1)}, bf16[1,800,128]{2,1,0:T(8,128)(2,1)S(1)}, u32[]{:S(2)}, u32[]{:S(2)}) collective-permute-start(bf16[1,800,128]{2,1,0:T(8,128)(2,1)S(1)} %shard_map.151.from_ref), channel_id=1, source_target_pairs={{0,12},{4,8},{8,4},{12,0},{1,13},{5,9},{9,5},{13,1},{2,14},{6,10},... | collective-permute-start | bytes 614408 | tf_op jit(solution)/shard_map/ppermute | solution.py:504
  18.9 14.3 %collective-permute-start.6 = (bf16[1,800,128]{2,1,0:T(8,128)(2,1)S(1)}, bf16[1,800,128]{2,1,0:T(8,128)(2,1)S(1)}, u32[]{:S(2)}, u32[]{:S(2)}) collective-permute-start(bf16[1,800,128]{2,1,0:T(8,128)(2,1)S(1)} %shard_map.153), channel_id=1, source_target_pairs={{0,4},{4,0},{8,12},{12,8},{1,5},{5,1},{9,13},{13,9},{2,6},{6,2},{1... | collective-permute-start | bytes 614408 | tf_op jit(solution)/shard_map/ppermute | solution.py:504
  27.8 8.7 %collective-permute-start.5 = (bf16[1,800,128]{2,1,0:T(8,128)(2,1)S(1)}, bf16[1,800,128]{2,1,0:T(8,128)(2,1)S(1)}, u32[]{:S(2)}, u32[]{:S(2)}) collective-permute-start(bf16[1,800,128]{2,1,0:T(8,128)(2,1)S(1)} %get-tuple-element.52), channel_id=1, source_target_pairs={{0,4},{4,0},{8,12},{12,8},{1,5},{5,1},{9,13},{13,9},{2,6},{6,2},{1... | collective-permute-start | bytes 614408 | tf_op jit(solution)/shard_map/ppermute | solution.py:532
  30.9 2.3 %copy-start.2 = (bf16[640,128]{1,0:T(8,128)(2,1)S(1)}, bf16[640,128]{1,0:T(8,128)(2,1)}, u32[]{:S(2)}) copy-start(bf16[640,128]{1,0:T(8,128)(2,1)} %constant.11.clone.to_channels_ref) | copy-start | bytes 491524
  30.9 2.3 %copy-start.6 = (bf16[320,128]{1,0:T(8,128)(2,1)S(1)}, bf16[320,128]{1,0:T(8,128)(2,1)}, u32[]{:S(2)}) copy-start(bf16[320,128]{1,0:T(8,128)(2,1)} %constant.10.clone.to_lanes_ref) | copy-start | bytes 245764
  34.7 1.8 %copy-start.7 = (bf16[320,320]{1,0:T(8,128)(2,1)S(1)}, bf16[320,320]{1,0:T(8,128)(2,1)}, u32[]{:S(2)}) copy-start(bf16[320,320]{1,0:T(8,128)(2,1)} %wo_ref.1) | copy-start | bytes 614404

commit v13 on v12

--- a/solution.py
+++ b/solution.py
@@ -380,7 +380,7 @@
     return top, total, mix
 
 
-def copy_kernel(from_ref, to_ref):
+def copy_kernel(from_ref, order_ref, to_ref):
     to_ref[...] = from_ref[...]
 
 
@@ -499,9 +499,7 @@
         routes = [[(i, i ^ s) for i in range(clips)] for s in range(1, clips, 2)]
     else:
         routes = [[(i, (i + s) % clips) for i in range(clips)] for s in range(1, clips)]
-    (near,) = call(copy_kernel, [(chosen.shape, BF)], [VMEM])(chosen)
-    sent = [near] + [chosen] * (len(routes) - 1)
-    arrived = [lax.ppermute(v, "clip", route) for v, route in zip(sent, routes)]
+    far = [lax.ppermute(chosen, "clip", route) for route in routes[1:]]
     temporal, query, keyval = call(
         temporal_kernel,
         [(some, BF), (some, BF), ((frames, cells, 2 * channels), BF)],
@@ -509,6 +507,8 @@
         flops=6 * frames * cells * one,
         limit=32,
     )(clip_even, clip_odd, spatial, hidden, g3, temporal_w, w_query, w_keyval)
+    (near,) = call(copy_kernel, [(chosen.shape, BF)], [VMEM] * 2)(chosen, temporal)
+    arrived = [lax.ppermute(near, "clip", routes[0])] + far
     maps = head_maps(frames, channels)
     split = frames // 2 if frames > 1 else frames
 

time: 39.6 us -> 40.5 us (1.023); the launches traced: 39.4 us -> 39.7 us
  transfers between devices with their start and end apart: 7 -> 7, of which waited for: 1 -> 1; matrix products, arithmetic and copies ran while one was open for 0% -> 0% of each run, Pallas kernels for 46% -> 45%
where the time goes in v13:
time: 40.5 us; the launch traced here: 39.7 us
  Pallas kernels  23 us (57%)
  starting transfers between devices  12.9 us (32%)
  between operations  1.74 us (4%)
  local copies, waits for them, and re-layouts  1.42 us (4%)
  waiting for transfers between devices  0.71 us (2%)
    pallas_call x2, Pallas kernels, local(): call(functools.partial(local_kernel, start), [(shape + (LANES,), F32)] *...  4.44 us
    pallas_call x1, Pallas kernels, on_device(): call(temporal_kernel, [(some, BF), (some, BF), ((frames, cells, 2 * chann...  4.21 us
    pallas_call x1, Pallas kernels, on_device(): call(inner_kernel, [(some, BF), (some, BF)], [VMEM] * 9, [inner_col], flo...  3.69 us
    ppermute x1, starting transfers between devices, on_device(): arrived += [lax.ppermute(v, 'clip', routes[0]) for v in relayed]  3.23 us
    ppermute x2, starting transfers between devices, swapped(): even = lax.ppermute(even, axis, pairs[1])  3.18 us
    pallas_call x1, Pallas kernels, on_device(): call(outer_kernel, [(middle, BF), (middle, BF), ((2, 2, width, channels),...  2.87 us
    pallas_call x2, Pallas kernels, on_device(): call(functools.partial(anchor_kernel, pieces), states, [VMEM] * (5 + 3 *...  2.82 us
    pallas_call x1, Pallas kernels, on_device(): call(last_kernel, [(latents.shape, BF)], [VMEM] * 10, [pltpu.VMEM(latents...  2.72 us
  transfers between devices with their start and end apart: 7, of which 1 were waited for; matrix products, arithmetic and copies ran while one was open for 0% of the time, Pallas kernels for 45%

profile of v13, /device:TPU:0, one launch (start us, length us, event | category | flops | bytes accessed | tf_op | source)
XLA Modules:
  0.0 39.7 jit_solution(7152337179114372765)
XLA Ops:
  0.0 0.0 copy-start
  0.0 1.3 %copy-done.3 = bf16[4,5,64,320]{3,2,1,0:T(8,128)(2,1)S(1)} copy-done((bf16[4,5,64,320]{3,2,1,0:T(8,128)(2,1)S(1)}, bf16[4,5,64,320]{3,2,1,0:T(8,128)(2,1)}, u32[]{:S(2)}) %copy-start.3) | copy-done | bytes 819224
  1.4 0.1 shard_map.146
  1.5 0.5 %collective-permute-start = (bf16[640,128]{1,0:T(8,128)(2,1)S(1)}, bf16[640,128]{1,0:T(8,128)(2,1)S(1)}, u32[]{:S(2)}, u32[]{:S(2)}) collective-permute-start(bf16[640,128]{1,0:T(8,128)(2,1)S(1)} %get-tuple-element.37), channel_id=1, source_target_pairs={{0,1},{2,3},{1,0},{3,2},{4,5},{6,7},{5,4},{7,6},{8,9},{10,11},{9,8... | collective-permute-start | bytes 491528 | tf_op jit(solution)/shard_map/ppermute | solution.py:436
  2.0 0.7 %collective-permute-start.1 = (bf16[640,128]{1,0:T(8,128)(2,1)S(1)}, bf16[640,128]{1,0:T(8,128)(2,1)S(1)}, u32[]{:S(2)}, u32[]{:S(2)}) collective-permute-start(bf16[640,128]{1,0:T(8,128)(2,1)S(1)} %get-tuple-element.38), channel_id=1, source_target_pairs={{1,2},{2,1},{5,6},{6,5},{9,10},{10,9},{13,14},{14,13},{17,18},{18,... | collective-permute-start | bytes 491528 | tf_op jit(solution)/shard_map/ppermute | solution.py:437
  2.6 0.0 copy-done
  2.7 0.0 copy-done.8
  2.7 0.0 copy-done.9
  2.7 2.9 %shard_map.145 = (bf16[2,192,320]{2,1,0:T(8,128)(2,1)S(1)}, bf16[2,192,320]{2,1,0:T(8,128)(2,1)S(1)}, f32[2,2,64,320]{3,2,1,0:T(8,128)S(1)}, bf16[960,192]{1,0:T(8,128)(2,1)S(1)}, f32[8,128]{1,0:T(8,128)S(1)}) custom-call(bf16[4,5,64,320]{3,2,1,0:T(8,128)(2,1)S(1)} %copy-done.3, f32[320]{0:T(512)S(1)} %copy-done.8, f32[320]{0:T(512)S(1)} %copy-done.9, ...), custom_call_target="tpu_custom_call" | custom-call | flops 1179648000 | bytes 2097152 | tf_op jit(solution)/shard_map/pallas_call | solution.py:466
  5.5 0.0 collective-permute-done.even_ref
  5.6 0.0 collective-permute-done.1.odd_ref
  5.6 0.0 copy-start.4
  5.6 1.2 %shard_map.147 = (bf16[2,320,320]{2,1,0:T(8,128)(2,1)S(1)}, bf16[2,320,320]{2,1,0:T(8,128)(2,1)S(1)}, bf16[800,128]{1,0:T(8,128)(2,1)S(1)}, bf16[800,128]{1,0:T(8,128)(2,1)S(1)}) custom-call(f32[2,2,64,320]{3,2,1,0:T(8,128)S(1)} %get-tuple-element.36.edge_ref, bf16[640,128]{1,0:T(8,128)(2,1)S(1)} %collective-permute-done.even_ref, ...), custom_call_target="tpu_custom_call" | custom-call | flops 157286400 | bytes 2097152 | tf_op jit(solution)/shard_map/pallas_call | solution.py:479
  6.7 2.7 %collective-permute-start.2 = (bf16[800,128]{1,0:T(8,128)(2,1)S(1)}, bf16[800,128]{1,0:T(8,128)(2,1)S(1)}, u32[]{:S(2)}, u32[]{:S(2)}) collective-permute-start(bf16[800,128]{1,0:T(8,128)(2,1)S(1)} %get-tuple-element.43), channel_id=1, source_target_pairs={{0,4},{8,12},{4,0},{12,8},{1,5},{9,13},{5,1},{13,9},{2,6},{10,14},... | collective-permute-start | bytes 614408 | tf_op jit(solution)/shard_map/ppermute | solution.py:436
  9.4 0.8 %collective-permute-start.3 = (bf16[800,128]{1,0:T(8,128)(2,1)S(1)}, bf16[800,128]{1,0:T(8,128)(2,1)S(1)}, u32[]{:S(2)}, u32[]{:S(2)}) collective-permute-start(bf16[800,128]{1,0:T(8,128)(2,1)S(1)} %get-tuple-element.44), channel_id=1, source_target_pairs={{4,8},{8,4},{5,9},{9,5},{6,10},{10,6},{7,11},{11,7},{20,24},{24,20... | collective-permute-start | bytes 614408 | tf_op jit(solution)/shard_map/ppermute | solution.py:437
  11.5 0.0 copy-done.4
  11.6 0.0 copy-start.5
  11.6 0.0 copy-start.10
  11.6 3.7 %shard_map.148 = (bf16[4,320,320]{2,1,0:T(8,128)(2,1)S(1)}, bf16[4,320,320]{2,1,0:T(8,128)(2,1)S(1)}) custom-call(bf16[4,5,64,320]{3,2,1,0:T(8,128)(2,1)S(1)} %copy-done.4, bf16[640,128]{1,0:T(8,128)(2,1)S(1)} %collective-permute-done.even_ref, bf16[640,128]{1,0:T(8,128)(2,1)S(1)} %collective-permute-done.1.odd_ref, f32[320]{0:T(512)S(1)} %copy-done.8, ...), custom_call_target="tpu_custom_call" | custom-call | flops 1179648000 | bytes 2097152 | tf_op jit(solution)/shard_map/pallas_call | solution.py:486
  15.3 0.0 copy-start.1
  15.3 0.0 copy-start.11
  15.3 0.0 collective-permute-done.2.even_ref
  15.3 0.0 collective-permute-done.3.odd_ref
  15.3 0.0 copy-done.5
  15.3 0.0 copy-done.10
  15.3 0.9 %shard_map.151.from_ref = bf16[1,800,128]{2,1,0:T(8,128)(2,1)S(1)} custom-call(s32[1,1]{1,0:T(1,128)S(6)} %copy.16.picks_ref, bf16[800,128]{1,0:T(8,128)(2,1)S(1)} %collective-permute-done.2.even_ref, bf16[800,128]{1,0:T(8,128)(2,1)S(1)} %collective-permute-done.3.odd_ref, bf16[4,320,320]{2,1,0:T(8,128)(2,1)S(1)} %get-tuple-element.47.spatial_ref, ...), custom_call_target="tpu_custom_call" | custom-call | flops 196608000 | bytes 2097152 | tf_op jit(solution)/shard_map/pallas_call | solution.py:493
  16.3 0.0 copy-start.12
  16.3 0.0 copy-start.13
  16.3 2.6 %collective-permute-start.4 = (bf16[1,800,128]{2,1,0:T(8,128)(2,1)S(1)}, bf16[1,800,128]{2,1,0:T(8,128)(2,1)S(1)}, u32[]{:S(2)}, u32[]{:S(2)}) collective-permute-start(bf16[1,800,128]{2,1,0:T(8,128)(2,1)S(1)} %shard_map.151.from_ref), channel_id=1, source_target_pairs={{0,12},{4,8},{8,4},{12,0},{1,13},{5,9},{9,5},{13,1},{2,14},{6,10},... | collective-permute-start | bytes 614408 | tf_op jit(solution)/shard_map/ppermute | solution.py:502
  18.8 0.0 copy-done.1
  18.9 0.0 copy-done.11
  18.9 4.2 %shard_map.149 = (bf16[4,320,320]{2,1,0:T(8,128)(2,1)S(1)}, bf16[4,320,320]{2,1,0:T(8,128)(2,1)S(1)}, bf16[4,320,640]{2,1,0:T(8,128)(2,1)S(1)}) custom-call(bf16[800,128]{1,0:T(8,128)(2,1)S(1)} %collective-permute-done.2.even_ref, bf16[800,128]{1,0:T(8,128)(2,1)S(1)} %collective-permute-done.3.odd_ref, ...), custom_call_target="tpu_custom_call" | custom-call | flops 1572864000 | bytes 2097152 | tf_op jit(solution)/shard_map/pallas_call | solution.py:503
  23.1 2.4 %collective-permute-start.6 = (bf16[1,800,128]{2,1,0:T(8,128)(2,1)S(1)}, bf16[1,800,128]{2,1,0:T(8,128)(2,1)S(1)}, u32[]{:S(2)}, u32[]{:S(2)}) collective-permute-start(bf16[1,800,128]{2,1,0:T(8,128)(2,1)S(1)} %shard_map.153), channel_id=1, source_target_pairs={{0,4},{4,0},{8,12},{12,8},{1,5},{5,1},{9,13},{13,9},{2,6},{6,2},{1... | collective-permute-start | bytes 614408 | tf_op jit(solution)/shard_map/ppermute | solution.py:511
  25.5 0.0 copy-done.12
  25.5 0.0 copy-done.13
  25.5 2.2 %shard_map.150 = (f32[2,320,128]{2,1,0:T(8,128)S(1)}, f32[2,320,128]{2,1,0:T(8,128)S(1)}, f32[2,320,384]{2,1,0:T(8,128)S(1)}, f32[8,128]{1,0:T(8,128)S(1)}) custom-call(s32[1,1]{1,0:T(1,128)S(6)} %copy.16.picks_ref, s32[1]{0:T(128)S(6)} %copy.17.window_ref, bf16[4,320,320]{2,1,0:T(8,128)(2,1)S(1)} %get-tuple-element.49.query_ref, ...), custom_call_target="tpu_custom_call" | custom-call | flops 1310720000 | bytes 2097152 | tf_op jit(solution)/shard_map/pallas_call | solution.py:517
  27.8 0.0 collective-permute-done.4.refs_0_.anchor_ref
  27.8 3.2 %collective-permute-start.5 = (bf16[1,800,128]{2,1,0:T(8,128)(2,1)S(1)}, bf16[1,800,128]{2,1,0:T(8,128)(2,1)S(1)}, u32[]{:S(2)}, u32[]{:S(2)}) collective-permute-start(bf16[1,800,128]{2,1,0:T(8,128)(2,1)S(1)} %get-tuple-element.52), channel_id=1, source_target_pairs={{0,4},{4,0},{8,12},{12,8},{1,5},{5,1},{9,13},{13,9},{2,6},{6,2},{1... | collective-permute-start | bytes 614408 | tf_op jit(solution)/shard_map/ppermute | solution.py:532
  31.0 2.2 %shard_map.154 = (f32[2,320,128]{2,1,0:T(8,128)S(1)}, f32[2,320,128]{2,1,0:T(8,128)S(1)}, f32[2,320,384]{2,1,0:T(8,128)S(1)}, f32[8,128]{1,0:T(8,128)}) custom-call(s32[1,1]{1,0:T(1,128)S(6)} %copy.16.picks_ref, s32[1]{0:T(128)S(6)} %copy.17.window_ref, bf16[4,320,320]{2,1,0:T(8,128)(2,1)S(1)} %get-tuple-element.49.query_ref, ...), custom_call_target="tpu_custom_call" | custom-call | flops 1310720000 | bytes 2097152 | tf_op jit(solution)/shard_map/pallas_call | solution.py:517
  33.3 0.0 collective-permute-done.6.anchor_ref
  33.3 0.0 copy-done.2
  33.3 0.0 copy-done.6
  33.3 1.5 %shard_map.155 = (f32[4,320,128]{2,1,0:T(8,128)S(1)}, f32[4,320,128]{2,1,0:T(8,128)S(1)}, f32[4,320,384]{2,1,0:T(8,128)S(1)}) custom-call(bf16[1,800,128]{2,1,0:T(8,128)(2,1)S(1)} %collective-permute-done.6.anchor_ref, bf16[320,640]{1,0:T(8,128)(2,1)S(1)} %copy-done.1, bf16[320,128]{1,0:T(8,128)(2,1)S(1)} %copy-done.6, bf16[640,128]{1,0:T(8,128)(2,1)S(1)} %copy-done.2, ...), custom_call_target="tpu_custom_call" | custom-call | flops 1048576000 | bytes 2097152 | tf_op jit(solution)/shard_map/pallas_call | solution.py:540
  34.8 0.0 copy-start.7
  34.8 1.3 %shard_map.156 = (f32[4,320,128]{2,1,0:T(8,128)S(1)}, f32[4,320,128]{2,1,0:T(8,128)S(1)}, f32[4,320,384]{2,1,0:T(8,128)S(1)}) custom-call(bf16[1,800,128]{2,1,0:T(8,128)(2,1)S(1)} %collective-permute-done.4.refs_0_.anchor_ref, bf16[320,640]{1,0:T(8,128)(2,1)S(1)} %copy-done.1, bf16[320,128]{1,0:T(8,128)(2,1)S(1)} %copy-done.6, ...), custom_call_target="tpu_custom_call" | custom-call | flops 1048576000 | bytes 2097152 | tf_op jit(solution)/shard_map/pallas_call | solution.py:540
  36.1 0.7 %collective-permute-done.5.anchor_ref = bf16[1,800,128]{2,1,0:T(8,128)(2,1)S(1)} collective-permute-done((bf16[1,800,128]{2,1,0:T(8,128)(2,1)S(1)}, bf16[1,800,128]{2,1,0:T(8,128)(2,1)S(1)}, u32[]{:S(2)}, u32[]{:S(2)}) %collective-permute-start.5) | collective-permute-done | bytes 204832 | tf_op jit(solution)/shard_map/ppermute | solution.py:532
  36.8 0.0 copy-done.7
  36.8 2.7 %shard_map.157 = bf16[4,5,64,320]{3,2,1,0:T(8,128)(2,1)} custom-call(bf16[1,800,128]{2,1,0:T(8,128)(2,1)S(1)} %collective-permute-done.5.anchor_ref, bf16[320,640]{1,0:T(8,128)(2,1)S(1)} %copy-done.1, bf16[320,128]{1,0:T(8,128)(2,1)S(1)} %copy-done.6, bf16[640,128]{1,0:T(8,128)(2,1)S(1)} %copy-done.2, bf16[4,320,320]{2,1,0:T(8,128)(2,1)S(1)} %get-tuple-element.49.query_ref, ...), custom_call_target="tpu_custom_call" | custom-call | flops 1310720000 | bytes 2097152 | tf_op jit(solution)/shard_map/pallas_call | solution.py:548
  (7 shorter events, 0.0 us)
Async XLA Ops:
  0.0 2.6 %copy-start = (bf16[3,3,320,320]{3,2,1,0:T(8,128)(2,1)S(1)}, bf16[3,3,320,320]{3,2,1,0:T(8,128)(2,1)}, u32[]{:S(2)}) copy-start(bf16[3,3,320,320]{3,2,1,0:T(8,128)(2,1)} %param.19) | copy-start | bytes 5529604
  0.0 1.4 %copy-start.3 = (bf16[4,5,64,320]{3,2,1,0:T(8,128)(2,1)S(1)}, bf16[4,5,64,320]{3,2,1,0:T(8,128)(2,1)}, u32[]{:S(2)}) copy-start(bf16[4,5,64,320]{3,2,1,0:T(8,128)(2,1)} %x_ref.5) | copy-start | bytes 2457604
  1.4 1.3 %copy-start.8 = (f32[320]{0:T(512)S(1)}, f32[320]{0:T(512)}, u32[]{:S(2)}) copy-start(f32[320]{0:T(512)} %g1_ref.5) | copy-start | bytes 3844
  1.4 1.3 %copy-start.9 = (f32[320]{0:T(512)S(1)}, f32[320]{0:T(512)}, u32[]{:S(2)}) copy-start(f32[320]{0:T(512)} %g2_ref.5) | copy-start | bytes 3844
  1.5 4.1 %collective-permute-start = (bf16[640,128]{1,0:T(8,128)(2,1)S(1)}, bf16[640,128]{1,0:T(8,128)(2,1)S(1)}, u32[]{:S(2)}, u32[]{:S(2)}) collective-permute-start(bf16[640,128]{1,0:T(8,128)(2,1)S(1)} %get-tuple-element.37), channel_id=1, source_target_pairs={{0,1},{2,3},{1,0},{3,2},{4,5},{6,7},{5,4},{7,6},{8,9},{10,11},{9,8... | collective-permute-start | bytes 491528 | tf_op jit(solution)/shard_map/ppermute | solution.py:436
  2.0 3.6 %collective-permute-start.1 = (bf16[640,128]{1,0:T(8,128)(2,1)S(1)}, bf16[640,128]{1,0:T(8,128)(2,1)S(1)}, u32[]{:S(2)}, u32[]{:S(2)}) collective-permute-start(bf16[640,128]{1,0:T(8,128)(2,1)S(1)} %get-tuple-element.38), channel_id=1, source_target_pairs={{1,2},{2,1},{5,6},{6,5},{9,10},{10,9},{13,14},{14,13},{17,18},{18,... | collective-permute-start | bytes 491528 | tf_op jit(solution)/shard_map/ppermute | solution.py:437
  5.6 6.0 %copy-start.4 = (bf16[4,5,64,320]{3,2,1,0:T(8,128)(2,1)S(1)}, bf16[4,5,64,320]{3,2,1,0:T(8,128)(2,1)}, u32[]{:S(2)}) copy-start(bf16[4,5,64,320]{3,2,1,0:T(8,128)(2,1)} %x_ref.5) | copy-start | bytes 2457604
  6.7 8.6 %collective-permute-start.2 = (bf16[800,128]{1,0:T(8,128)(2,1)S(1)}, bf16[800,128]{1,0:T(8,128)(2,1)S(1)}, u32[]{:S(2)}, u32[]{:S(2)}) collective-permute-start(bf16[800,128]{1,0:T(8,128)(2,1)S(1)} %get-tuple-element.43), channel_id=1, source_target_pairs={{0,4},{8,12},{4,0},{12,8},{1,5},{9,13},{5,1},{13,9},{2,6},{10,14},... | collective-permute-start | bytes 614408 | tf_op jit(solution)/shard_map/ppermute | solution.py:436
  9.4 5.9 %collective-permute-start.3 = (bf16[800,128]{1,0:T(8,128)(2,1)S(1)}, bf16[800,128]{1,0:T(8,128)(2,1)S(1)}, u32[]{:S(2)}, u32[]{:S(2)}) collective-permute-start(bf16[800,128]{1,0:T(8,128)(2,1)S(1)} %get-tuple-element.44), channel_id=1, source_target_pairs={{4,8},{8,4},{5,9},{9,5},{6,10},{10,6},{7,11},{11,7},{20,24},{24,20... | collective-permute-start | bytes 614408 | tf_op jit(solution)/shard_map/ppermute | solution.py:437
  11.6 3.8 %copy-start.5 = (bf16[3,320,320]{2,1,0:T(8,128)(2,1)S(1)}, bf16[3,320,320]{2,1,0:T(8,128)(2,1)}, u32[]{:S(2)}) copy-start(bf16[3,320,320]{2,1,0:T(8,128)(2,1)} %wt_ref.3) | copy-start | bytes 1843204
  11.6 3.8 %copy-start.10 = (f32[320]{0:T(512)S(1)}, f32[320]{0:T(512)}, u32[]{:S(2)}) copy-start(f32[320]{0:T(512)} %g3_ref.3) | copy-start | bytes 3844
  15.3 3.6 %copy-start.1 = (bf16[320,640]{1,0:T(8,128)(2,1)S(1)}, bf16[320,640]{1,0:T(8,128)(2,1)}, u32[]{:S(2)}) copy-start(bf16[320,640]{1,0:T(8,128)(2,1)} %wkv_ref.7) | copy-start | bytes 1228804
  15.3 3.6 %copy-start.11 = (bf16[320,320]{1,0:T(8,128)(2,1)S(1)}, bf16[320,320]{1,0:T(8,128)(2,1)}, u32[]{:S(2)}) copy-start(bf16[320,320]{1,0:T(8,128)(2,1)} %wq_ref.1) | copy-start | bytes 614404
  16.3 9.3 %copy-start.12 = (bf16[1280,128]{1,0:T(8,128)(2,1)S(1)}, bf16[1280,128]{1,0:T(8,128)(2,1)}, u32[]{:S(2)}) copy-start(bf16[1280,128]{1,0:T(8,128)(2,1)} %constant.9.clone.to_channels_ref) | copy-start | bytes 983044
  16.3 9.3 %copy-start.13 = (bf16[1280,128]{1,0:T(8,128)(2,1)S(1)}, bf16[1280,128]{1,0:T(8,128)(2,1)}, u32[]{:S(2)}) copy-start(bf16[1280,128]{1,0:T(8,128)(2,1)} %constant.8.clone.to_lanes_ref) | copy-start | bytes 983044
  16.3 11.5 %collective-permute-start.4 = (bf16[1,800,128]{2,1,0:T(8,128)(2,1)S(1)}, bf16[1,800,128]{2,1,0:T(8,128)(2,1)S(1)}, u32[]{:S(2)}, u32[]{:S(2)}) collective-permute-start(bf16[1,800,128]{2,1,0:T(8,128)(2,1)S(1)} %shard_map.151.from_ref), channel_id=1, source_target_pairs={{0,12},{4,8},{8,4},{12,0},{1,13},{5,9},{9,5},{13,1},{2,14},{6,10},... | collective-permute-start | bytes 614408 | tf_op jit(solution)/shard_map/ppermute | solution.py:502
  23.1 10.2 %collective-permute-start.6 = (bf16[1,800,128]{2,1,0:T(8,128)(2,1)S(1)}, bf16[1,800,128]{2,1,0:T(8,128)(2,1)S(1)}, u32[]{:S(2)}, u32[]{:S(2)}) collective-permute-start(bf16[1,800,128]{2,1,0:T(8,128)(2,1)S(1)} %shard_map.153), channel_id=1, source_target_pairs={{0,4},{4,0},{8,12},{12,8},{1,5},{5,1},{9,13},{13,9},{2,6},{6,2},{1... | collective-permute-start | bytes 614408 | tf_op jit(solution)/shard_map/ppermute | solution.py:511
  27.8 9.0 %collective-permute-start.5 = (bf16[1,800,128]{2,1,0:T(8,128)(2,1)S(1)}, bf16[1,800,128]{2,1,0:T(8,128)(2,1)S(1)}, u32[]{:S(2)}, u32[]{:S(2)}) collective-permute-start(bf16[1,800,128]{2,1,0:T(8,128)(2,1)S(1)} %get-tuple-element.52), channel_id=1, source_target_pairs={{0,4},{4,0},{8,12},{12,8},{1,5},{5,1},{9,13},{13,9},{2,6},{6,2},{1... | collective-permute-start | bytes 614408 | tf_op jit(solution)/shard_map/ppermute | solution.py:532
  31.0 2.2 %copy-start.2 = (bf16[640,128]{1,0:T(8,128)(2,1)S(1)}, bf16[640,128]{1,0:T(8,128)(2,1)}, u32[]{:S(2)}) copy-start(bf16[640,128]{1,0:T(8,128)(2,1)} %constant.11.clone.to_channels_ref) | copy-start | bytes 491524
  31.0 2.2 %copy-start.6 = (bf16[320,128]{1,0:T(8,128)(2,1)S(1)}, bf16[320,128]{1,0:T(8,128)(2,1)}, u32[]{:S(2)}) copy-start(bf16[320,128]{1,0:T(8,128)(2,1)} %constant.10.clone.to_lanes_ref) | copy-start | bytes 245764
  34.8 2.0 %copy-start.7 = (bf16[320,320]{1,0:T(8,128)(2,1)S(1)}, bf16[320,320]{1,0:T(8,128)(2,1)}, u32[]{:S(2)}) copy-start(bf16[320,320]{1,0:T(8,128)(2,1)} %wo_ref.1) | copy-start | bytes 614404

commit v14 on v12

--- a/solution.py
+++ b/solution.py
@@ -510,7 +510,7 @@
         limit=32,
     )(clip_even, clip_odd, spatial, hidden, g3, temporal_w, w_query, w_keyval)
     maps = head_maps(frames, channels)
-    split = frames // 2 if frames > 1 else frames
+    split = max(frames - 1, 1)
 
     def local(start, part, after):
         shape = (part, cells)

time: 39.6 us -> 39.3 us (level)
  starting transfers between devices: 12.7 us -> 11.8 us
    ppermute x1, starting transfers between devices: 3.08 us -> 2.17 us  [on_device(): arrived += [lax.ppermute(v, 'clip', routes[0]) for v in relayed]]
  transfers between devices with their start and end apart: 7 -> 7, of which waited for: 1 -> 1; matrix products, arithmetic and copies ran while one was open for 0% -> 0% of each run, Pallas kernels for 46% -> 47%
where the time goes in v14:
time: 39.3 us; the launch traced here: 38.8 us
  Pallas kernels  23 us (59%)
  starting transfers between devices  11.8 us (30%)
  between operations  1.77 us (5%)
  local copies, waits for them, and re-layouts  1.43 us (4%)
  waiting for transfers between devices  0.81 us (2%)
    ppermute x2, starting transfers between devices, on_device(): arrived = [lax.ppermute(v, 'clip', route) for v, route in zip(sent, routes)]  4.92 us
    pallas_call x2, Pallas kernels, local(): call(functools.partial(local_kernel, start), [(shape + (LANES,), F32)] *...  4.4 us
    pallas_call x1, Pallas kernels, on_device(): call(temporal_kernel, [(some, BF), (some, BF), ((frames, cells, 2 * chann...  4.24 us
    pallas_call x1, Pallas kernels, on_device(): call(inner_kernel, [(some, BF), (some, BF)], [VMEM] * 9, [inner_col], flo...  3.69 us
    ppermute x2, starting transfers between devices, swapped(): even = lax.ppermute(even, axis, pairs[1])  3.18 us
    pallas_call x1, Pallas kernels, on_device(): call(outer_kernel, [(middle, BF), (middle, BF), ((2, 2, width, channels),...  2.87 us
    pallas_call x2, Pallas kernels, on_device(): call(functools.partial(anchor_kernel, pieces), states, [VMEM] * (5 + 3 *...  2.85 us
    pallas_call x1, Pallas kernels, on_device(): call(last_kernel, [(latents.shape, BF)], [VMEM] * 10, [pltpu.VMEM(latents...  2.73 us
  transfers between devices with their start and end apart: 7, of which 1 were waited for; matrix products, arithmetic and copies ran while one was open for 0% of the time, Pallas kernels for 47%

profile of v14, /device:TPU:0, one launch (start us, length us, event | category | flops | bytes accessed | tf_op | source)
XLA Modules:
  0.0 38.8 jit_solution(1720149147712450793)
XLA Ops:
  0.0 1.3 %copy-done.3 = bf16[4,5,64,320]{3,2,1,0:T(8,128)(2,1)S(1)} copy-done((bf16[4,5,64,320]{3,2,1,0:T(8,128)(2,1)S(1)}, bf16[4,5,64,320]{3,2,1,0:T(8,128)(2,1)}, u32[]{:S(2)}) %copy-start.3) | copy-done | bytes 819224
  1.4 0.1 shard_map.146
  1.5 0.5 %collective-permute-start = (bf16[640,128]{1,0:T(8,128)(2,1)S(1)}, bf16[640,128]{1,0:T(8,128)(2,1)S(1)}, u32[]{:S(2)}, u32[]{:S(2)}) collective-permute-start(bf16[640,128]{1,0:T(8,128)(2,1)S(1)} %get-tuple-element.37), channel_id=1, source_target_pairs={{0,1},{2,3},{1,0},{3,2},{4,5},{6,7},{5,4},{7,6},{8,9},{10,11},{9,8... | collective-permute-start | bytes 491528 | tf_op jit(solution)/shard_map/ppermute | solution.py:436
  2.0 0.7 %collective-permute-start.1 = (bf16[640,128]{1,0:T(8,128)(2,1)S(1)}, bf16[640,128]{1,0:T(8,128)(2,1)S(1)}, u32[]{:S(2)}, u32[]{:S(2)}) collective-permute-start(bf16[640,128]{1,0:T(8,128)(2,1)S(1)} %get-tuple-element.38), channel_id=1, source_target_pairs={{1,2},{2,1},{5,6},{6,5},{9,10},{10,9},{13,14},{14,13},{17,18},{18,... | collective-permute-start | bytes 491528 | tf_op jit(solution)/shard_map/ppermute | solution.py:437
  2.6 0.0 copy-done
  2.7 0.0 copy-done.10
  2.7 0.0 copy-done.11
  2.7 2.9 %shard_map.145 = (bf16[2,192,320]{2,1,0:T(8,128)(2,1)S(1)}, bf16[2,192,320]{2,1,0:T(8,128)(2,1)S(1)}, f32[2,2,64,320]{3,2,1,0:T(8,128)S(1)}, bf16[960,192]{1,0:T(8,128)(2,1)S(1)}, f32[8,128]{1,0:T(8,128)S(1)}) custom-call(bf16[4,5,64,320]{3,2,1,0:T(8,128)(2,1)S(1)} %copy-done.3, f32[320]{0:T(512)S(1)} %copy-done.10, f32[320]{0:T(512)S(1)} %copy-done.11, ...), custom_call_target="tpu_custom_call" | custom-call | flops 1179648000 | bytes 2097152 | tf_op jit(solution)/shard_map/pallas_call | solution.py:466
  5.5 0.0 collective-permute-done.even_ref
  5.6 0.0 collective-permute-done.1.odd_ref
  5.6 0.0 copy-start.4
  5.6 1.2 %shard_map.147 = (bf16[2,320,320]{2,1,0:T(8,128)(2,1)S(1)}, bf16[2,320,320]{2,1,0:T(8,128)(2,1)S(1)}, bf16[800,128]{1,0:T(8,128)(2,1)S(1)}, bf16[800,128]{1,0:T(8,128)(2,1)S(1)}) custom-call(f32[2,2,64,320]{3,2,1,0:T(8,128)S(1)} %get-tuple-element.36.edge_ref, bf16[640,128]{1,0:T(8,128)(2,1)S(1)} %collective-permute-done.even_ref, ...), custom_call_target="tpu_custom_call" | custom-call | flops 157286400 | bytes 2097152 | tf_op jit(solution)/shard_map/pallas_call | solution.py:479
  6.7 2.7 %collective-permute-start.2 = (bf16[800,128]{1,0:T(8,128)(2,1)S(1)}, bf16[800,128]{1,0:T(8,128)(2,1)S(1)}, u32[]{:S(2)}, u32[]{:S(2)}) collective-permute-start(bf16[800,128]{1,0:T(8,128)(2,1)S(1)} %get-tuple-element.43), channel_id=1, source_target_pairs={{0,4},{8,12},{4,0},{12,8},{1,5},{9,13},{5,1},{13,9},{2,6},{10,14},... | collective-permute-start | bytes 614408 | tf_op jit(solution)/shard_map/ppermute | solution.py:436
  9.4 0.8 %collective-permute-start.3 = (bf16[800,128]{1,0:T(8,128)(2,1)S(1)}, bf16[800,128]{1,0:T(8,128)(2,1)S(1)}, u32[]{:S(2)}, u32[]{:S(2)}) collective-permute-start(bf16[800,128]{1,0:T(8,128)(2,1)S(1)} %get-tuple-element.44), channel_id=1, source_target_pairs={{4,8},{8,4},{5,9},{9,5},{6,10},{10,6},{7,11},{11,7},{20,24},{24,20... | collective-permute-start | bytes 614408 | tf_op jit(solution)/shard_map/ppermute | solution.py:437
  11.5 0.0 copy-done.4
  11.6 0.0 copy-start.5
  11.6 0.0 copy-start.12
  11.6 3.7 %shard_map.148 = (bf16[4,320,320]{2,1,0:T(8,128)(2,1)S(1)}, bf16[4,320,320]{2,1,0:T(8,128)(2,1)S(1)}) custom-call(bf16[4,5,64,320]{3,2,1,0:T(8,128)(2,1)S(1)} %copy-done.4, bf16[640,128]{1,0:T(8,128)(2,1)S(1)} %collective-permute-done.even_ref, bf16[640,128]{1,0:T(8,128)(2,1)S(1)} %collective-permute-done.1.odd_ref, f32[320]{0:T(512)S(1)} %copy-done.10, ...), custom_call_target="tpu_custom_call" | custom-call | flops 1179648000 | bytes 2097152 | tf_op jit(solution)/shard_map/pallas_call | solution.py:486
  15.3 0.0 copy-start.1
  15.3 0.0 copy-start.13
  15.3 0.0 collective-permute-done.2.even_ref
  15.3 0.0 collective-permute-done.3.odd_ref
  15.3 0.0 copy-done.5
  15.3 0.0 copy-done.12
  15.3 0.9 %shard_map.151.from_ref = bf16[1,800,128]{2,1,0:T(8,128)(2,1)S(1)} custom-call(s32[1,1]{1,0:T(1,128)S(6)} %copy.16.picks_ref, bf16[800,128]{1,0:T(8,128)(2,1)S(1)} %collective-permute-done.2.even_ref, bf16[800,128]{1,0:T(8,128)(2,1)S(1)} %collective-permute-done.3.odd_ref, bf16[4,320,320]{2,1,0:T(8,128)(2,1)S(1)} %get-tuple-element.47.spatial_ref, ...), custom_call_target="tpu_custom_call" | custom-call | flops 196608000 | bytes 2097152 | tf_op jit(solution)/shard_map/pallas_call | solution.py:493
  16.3 0.0 copy-start.7
  16.3 0.0 copy-start.8
  16.3 2.5 %collective-permute-start.4 = (bf16[1,800,128]{2,1,0:T(8,128)(2,1)S(1)}, bf16[1,800,128]{2,1,0:T(8,128)(2,1)S(1)}, u32[]{:S(2)}, u32[]{:S(2)}) collective-permute-start(bf16[1,800,128]{2,1,0:T(8,128)(2,1)S(1)} %shard_map.151.from_ref), channel_id=1, source_target_pairs={{0,12},{4,8},{8,4},{12,0},{1,13},{5,9},{9,5},{13,1},{2,14},{6,10},... | collective-permute-start | bytes 614408 | tf_op jit(solution)/shard_map/ppermute | solution.py:504
  18.9 2.4 %collective-permute-start.6 = (bf16[1,800,128]{2,1,0:T(8,128)(2,1)S(1)}, bf16[1,800,128]{2,1,0:T(8,128)(2,1)S(1)}, u32[]{:S(2)}, u32[]{:S(2)}) collective-permute-start(bf16[1,800,128]{2,1,0:T(8,128)(2,1)S(1)} %shard_map.153), channel_id=1, source_target_pairs={{0,4},{4,0},{8,12},{12,8},{1,5},{5,1},{9,13},{13,9},{2,6},{6,2},{1... | collective-permute-start | bytes 614408 | tf_op jit(solution)/shard_map/ppermute | solution.py:504
  21.3 0.0 copy-done.1
  21.3 0.0 copy-done.13
  21.3 4.2 %shard_map.149 = (bf16[4,320,320]{2,1,0:T(8,128)(2,1)S(1)}, bf16[4,320,320]{2,1,0:T(8,128)(2,1)S(1)}, bf16[4,320,640]{2,1,0:T(8,128)(2,1)S(1)}) custom-call(bf16[800,128]{1,0:T(8,128)(2,1)S(1)} %collective-permute-done.2.even_ref, bf16[800,128]{1,0:T(8,128)(2,1)S(1)} %collective-permute-done.3.odd_ref, ...), custom_call_target="tpu_custom_call" | custom-call | flops 1572864000 | bytes 2097152 | tf_op jit(solution)/shard_map/pallas_call | solution.py:505
  25.5 0.0 copy-done.7
  25.5 0.0 copy-done.8
  25.5 3.1 %shard_map.150 = (f32[3,320,128]{2,1,0:T(8,128)S(1)}, f32[3,320,128]{2,1,0:T(8,128)S(1)}, f32[3,320,384]{2,1,0:T(8,128)S(1)}, f32[8,128]{1,0:T(8,128)S(1)}) custom-call(s32[1,1]{1,0:T(1,128)S(6)} %copy.16.picks_ref, s32[1]{0:T(128)S(6)} %copy.17.window_ref, bf16[4,320,320]{2,1,0:T(8,128)(2,1)S(1)} %get-tuple-element.49.query_ref, ...), custom_call_target="tpu_custom_call" | custom-call | flops 1966080000 | bytes 2097152 | tf_op jit(solution)/shard_map/pallas_call | solution.py:517
  28.6 0.0 copy-start.2
  28.7 0.0 copy-start.6
  28.7 0.0 collective-permute-done.4.refs_0_.anchor_ref
  28.7 2.2 %collective-permute-start.5 = (bf16[1,800,128]{2,1,0:T(8,128)(2,1)S(1)}, bf16[1,800,128]{2,1,0:T(8,128)(2,1)S(1)}, u32[]{:S(2)}, u32[]{:S(2)}) collective-permute-start(bf16[1,800,128]{2,1,0:T(8,128)(2,1)S(1)} %get-tuple-element.52), channel_id=1, source_target_pairs={{0,4},{4,0},{8,12},{12,8},{1,5},{5,1},{9,13},{13,9},{2,6},{6,2},{1... | collective-permute-start | bytes 614408 | tf_op jit(solution)/shard_map/ppermute | solution.py:532
  30.9 1.3 %shard_map.154 = (f32[1,320,128]{2,1,0:T(8,128)S(1)}, f32[1,320,128]{2,1,0:T(8,128)S(1)}, f32[1,320,384]{2,1,0:T(8,128)S(1)}, f32[8,128]{1,0:T(8,128)}) custom-call(s32[1,1]{1,0:T(1,128)S(6)} %copy.16.picks_ref, s32[1]{0:T(128)S(6)} %copy.17.window_ref, bf16[4,320,320]{2,1,0:T(8,128)(2,1)S(1)} %get-tuple-element.49.query_ref, ...), custom_call_target="tpu_custom_call" | custom-call | flops 655360000 | bytes 2097152 | tf_op jit(solution)/shard_map/pallas_call | solution.py:517
  32.2 0.0 collective-permute-done.6.anchor_ref
  32.2 0.0 copy-done.2
  32.2 0.0 copy-done.6
  32.2 1.5 %shard_map.155 = (f32[4,320,128]{2,1,0:T(8,128)S(1)}, f32[4,320,128]{2,1,0:T(8,128)S(1)}, f32[4,320,384]{2,1,0:T(8,128)S(1)}) custom-call(bf16[1,800,128]{2,1,0:T(8,128)(2,1)S(1)} %collective-permute-done.6.anchor_ref, bf16[320,640]{1,0:T(8,128)(2,1)S(1)} %copy-done.1, bf16[320,128]{1,0:T(8,128)(2,1)S(1)} %copy-done.6, bf16[640,128]{1,0:T(8,128)(2,1)S(1)} %copy-done.2, ...), custom_call_target="tpu_custom_call" | custom-call | flops 1048576000 | bytes 2097152 | tf_op jit(solution)/shard_map/pallas_call | solution.py:540
  33.7 0.0 copy-start.9
  33.7 1.3 %shard_map.156 = (f32[4,320,128]{2,1,0:T(8,128)S(1)}, f32[4,320,128]{2,1,0:T(8,128)S(1)}, f32[4,320,384]{2,1,0:T(8,128)S(1)}) custom-call(bf16[1,800,128]{2,1,0:T(8,128)(2,1)S(1)} %collective-permute-done.4.refs_0_.anchor_ref, bf16[320,640]{1,0:T(8,128)(2,1)S(1)} %copy-done.1, bf16[320,128]{1,0:T(8,128)(2,1)S(1)} %copy-done.6, ...), custom_call_target="tpu_custom_call" | custom-call | flops 1048576000 | bytes 2097152 | tf_op jit(solution)/shard_map/pallas_call | solution.py:540
  35.1 0.8 %collective-permute-done.5.anchor_ref = bf16[1,800,128]{2,1,0:T(8,128)(2,1)S(1)} collective-permute-done((bf16[1,800,128]{2,1,0:T(8,128)(2,1)S(1)}, bf16[1,800,128]{2,1,0:T(8,128)(2,1)S(1)}, u32[]{:S(2)}, u32[]{:S(2)}) %collective-permute-start.5) | collective-permute-done | bytes 204832 | tf_op jit(solution)/shard_map/ppermute | solution.py:532
  35.9 2.7 %shard_map.157 = bf16[4,5,64,320]{3,2,1,0:T(8,128)(2,1)} custom-call(bf16[1,800,128]{2,1,0:T(8,128)(2,1)S(1)} %collective-permute-done.5.anchor_ref, bf16[320,640]{1,0:T(8,128)(2,1)S(1)} %copy-done.1, bf16[320,128]{1,0:T(8,128)(2,1)S(1)} %copy-done.6, bf16[640,128]{1,0:T(8,128)(2,1)S(1)} %copy-done.2, bf16[4,320,320]{2,1,0:T(8,128)(2,1)S(1)} %get-tuple-element.49.query_ref, ...), custom_call_target="tpu_custom_call" | custom-call | flops 1310720000 | bytes 2097152 | tf_op jit(solution)/shard_map/pallas_call | solution.py:548
  (7 shorter events, 0.0 us)
Async XLA Ops:
  0.0 2.6 %copy-start = (bf16[3,3,320,320]{3,2,1,0:T(8,128)(2,1)S(1)}, bf16[3,3,320,320]{3,2,1,0:T(8,128)(2,1)}, u32[]{:S(2)}) copy-start(bf16[3,3,320,320]{3,2,1,0:T(8,128)(2,1)} %param.19) | copy-start | bytes 5529604
  0.0 1.4 %copy-start.3 = (bf16[4,5,64,320]{3,2,1,0:T(8,128)(2,1)S(1)}, bf16[4,5,64,320]{3,2,1,0:T(8,128)(2,1)}, u32[]{:S(2)}) copy-start(bf16[4,5,64,320]{3,2,1,0:T(8,128)(2,1)} %x_ref.5) | copy-start | bytes 2457604
  1.4 1.3 %copy-start.10 = (f32[320]{0:T(512)S(1)}, f32[320]{0:T(512)}, u32[]{:S(2)}) copy-start(f32[320]{0:T(512)} %g1_ref.5) | copy-start | bytes 3844
  1.4 1.3 %copy-start.11 = (f32[320]{0:T(512)S(1)}, f32[320]{0:T(512)}, u32[]{:S(2)}) copy-start(f32[320]{0:T(512)} %g2_ref.5) | copy-start | bytes 3844
  1.5 4.1 %collective-permute-start = (bf16[640,128]{1,0:T(8,128)(2,1)S(1)}, bf16[640,128]{1,0:T(8,128)(2,1)S(1)}, u32[]{:S(2)}, u32[]{:S(2)}) collective-permute-start(bf16[640,128]{1,0:T(8,128)(2,1)S(1)} %get-tuple-element.37), channel_id=1, source_target_pairs={{0,1},{2,3},{1,0},{3,2},{4,5},{6,7},{5,4},{7,6},{8,9},{10,11},{9,8... | collective-permute-start | bytes 491528 | tf_op jit(solution)/shard_map/ppermute | solution.py:436
  2.0 3.6 %collective-permute-start.1 = (bf16[640,128]{1,0:T(8,128)(2,1)S(1)}, bf16[640,128]{1,0:T(8,128)(2,1)S(1)}, u32[]{:S(2)}, u32[]{:S(2)}) collective-permute-start(bf16[640,128]{1,0:T(8,128)(2,1)S(1)} %get-tuple-element.38), channel_id=1, source_target_pairs={{1,2},{2,1},{5,6},{6,5},{9,10},{10,9},{13,14},{14,13},{17,18},{18,... | collective-permute-start | bytes 491528 | tf_op jit(solution)/shard_map/ppermute | solution.py:437
  5.6 6.0 %copy-start.4 = (bf16[4,5,64,320]{3,2,1,0:T(8,128)(2,1)S(1)}, bf16[4,5,64,320]{3,2,1,0:T(8,128)(2,1)}, u32[]{:S(2)}) copy-start(bf16[4,5,64,320]{3,2,1,0:T(8,128)(2,1)} %x_ref.5) | copy-start | bytes 2457604
  6.7 8.6 %collective-permute-start.2 = (bf16[800,128]{1,0:T(8,128)(2,1)S(1)}, bf16[800,128]{1,0:T(8,128)(2,1)S(1)}, u32[]{:S(2)}, u32[]{:S(2)}) collective-permute-start(bf16[800,128]{1,0:T(8,128)(2,1)S(1)} %get-tuple-element.43), channel_id=1, source_target_pairs={{0,4},{8,12},{4,0},{12,8},{1,5},{9,13},{5,1},{13,9},{2,6},{10,14},... | collective-permute-start | bytes 614408 | tf_op jit(solution)/shard_map/ppermute | solution.py:436
  9.4 5.9 %collective-permute-start.3 = (bf16[800,128]{1,0:T(8,128)(2,1)S(1)}, bf16[800,128]{1,0:T(8,128)(2,1)S(1)}, u32[]{:S(2)}, u32[]{:S(2)}) collective-permute-start(bf16[800,128]{1,0:T(8,128)(2,1)S(1)} %get-tuple-element.44), channel_id=1, source_target_pairs={{4,8},{8,4},{5,9},{9,5},{6,10},{10,6},{7,11},{11,7},{20,24},{24,20... | collective-permute-start | bytes 614408 | tf_op jit(solution)/shard_map/ppermute | solution.py:437
  11.6 3.8 %copy-start.5 = (bf16[3,320,320]{2,1,0:T(8,128)(2,1)S(1)}, bf16[3,320,320]{2,1,0:T(8,128)(2,1)}, u32[]{:S(2)}) copy-start(bf16[3,320,320]{2,1,0:T(8,128)(2,1)} %wt_ref.3) | copy-start | bytes 1843204
  11.6 3.8 %copy-start.12 = (f32[320]{0:T(512)S(1)}, f32[320]{0:T(512)}, u32[]{:S(2)}) copy-start(f32[320]{0:T(512)} %g3_ref.3) | copy-start | bytes 3844
  15.3 6.0 %copy-start.1 = (bf16[320,640]{1,0:T(8,128)(2,1)S(1)}, bf16[320,640]{1,0:T(8,128)(2,1)}, u32[]{:S(2)}) copy-start(bf16[320,640]{1,0:T(8,128)(2,1)} %wkv_ref.7) | copy-start | bytes 1228804
  15.3 6.0 %copy-start.13 = (bf16[320,320]{1,0:T(8,128)(2,1)S(1)}, bf16[320,320]{1,0:T(8,128)(2,1)}, u32[]{:S(2)}) copy-start(bf16[320,320]{1,0:T(8,128)(2,1)} %wq_ref.1) | copy-start | bytes 614404
  16.3 9.2 %copy-start.7 = (bf16[1280,128]{1,0:T(8,128)(2,1)S(1)}, bf16[1280,128]{1,0:T(8,128)(2,1)}, u32[]{:S(2)}) copy-start(bf16[1280,128]{1,0:T(8,128)(2,1)} %constant.9.clone.to_channels_ref) | copy-start | bytes 983044
  16.3 9.2 %copy-start.8 = (bf16[1280,128]{1,0:T(8,128)(2,1)S(1)}, bf16[1280,128]{1,0:T(8,128)(2,1)}, u32[]{:S(2)}) copy-start(bf16[1280,128]{1,0:T(8,128)(2,1)} %constant.8.clone.to_lanes_ref) | copy-start | bytes 983044
  16.3 12.3 %collective-permute-start.4 = (bf16[1,800,128]{2,1,0:T(8,128)(2,1)S(1)}, bf16[1,800,128]{2,1,0:T(8,128)(2,1)S(1)}, u32[]{:S(2)}, u32[]{:S(2)}) collective-permute-start(bf16[1,800,128]{2,1,0:T(8,128)(2,1)S(1)} %shard_map.151.from_ref), channel_id=1, source_target_pairs={{0,12},{4,8},{8,4},{12,0},{1,13},{5,9},{9,5},{13,1},{2,14},{6,10},... | collective-permute-start | bytes 614408 | tf_op jit(solution)/shard_map/ppermute | solution.py:504
  18.9 13.3 %collective-permute-start.6 = (bf16[1,800,128]{2,1,0:T(8,128)(2,1)S(1)}, bf16[1,800,128]{2,1,0:T(8,128)(2,1)S(1)}, u32[]{:S(2)}, u32[]{:S(2)}) collective-permute-start(bf16[1,800,128]{2,1,0:T(8,128)(2,1)S(1)} %shard_map.153), channel_id=1, source_target_pairs={{0,4},{4,0},{8,12},{12,8},{1,5},{5,1},{9,13},{13,9},{2,6},{6,2},{1... | collective-permute-start | bytes 614408 | tf_op jit(solution)/shard_map/ppermute | solution.py:504
  28.6 3.5 %copy-start.2 = (bf16[640,128]{1,0:T(8,128)(2,1)S(1)}, bf16[640,128]{1,0:T(8,128)(2,1)}, u32[]{:S(2)}) copy-start(bf16[640,128]{1,0:T(8,128)(2,1)} %constant.11.clone.to_channels_ref) | copy-start | bytes 491524
  28.7 3.5 %copy-start.6 = (bf16[320,128]{1,0:T(8,128)(2,1)S(1)}, bf16[320,128]{1,0:T(8,128)(2,1)}, u32[]{:S(2)}) copy-start(bf16[320,128]{1,0:T(8,128)(2,1)} %constant.10.clone.to_lanes_ref) | copy-start | bytes 245764
  28.7 7.2 %collective-permute-start.5 = (bf16[1,800,128]{2,1,0:T(8,128)(2,1)S(1)}, bf16[1,800,128]{2,1,0:T(8,128)(2,1)S(1)}, u32[]{:S(2)}, u32[]{:S(2)}) collective-permute-start(bf16[1,800,128]{2,1,0:T(8,128)(2,1)S(1)} %get-tuple-element.52), channel_id=1, source_target_pairs={{0,4},{4,0},{8,12},{12,8},{1,5},{5,1},{9,13},{13,9},{2,6},{6,2},{1... | collective-permute-start | bytes 614408 | tf_op jit(solution)/shard_map/ppermute | solution.py:532
  33.7 2.1 %copy-start.9 = (bf16[320,320]{1,0:T(8,128)(2,1)S(1)}, bf16[320,320]{1,0:T(8,128)(2,1)}, u32[]{:S(2)}) copy-start(bf16[320,320]{1,0:T(8,128)(2,1)} %wo_ref.1) | copy-start | bytes 614404
